TPU v7x, 32 devices: a whole 2x2x4 slice. The times are simulated.
32 devices in a mesh: band: 4 (over z), sx: 4 (over x, core), sy: 2 (over y).
Axes of the slice: x: 2, y: 2, z: 4, core: 2. Of those that a mesh axis runs over, the one named last changes fastest.
Arguments:
- orbitals: float32 [256, 24, 12, 128], P('band', 'sx', 'sy'), may hold values from -6 to 6
- potential: float32 [24, 12, 128], P('sx', 'sy'), may hold values from -3 to 0
- projectors: float32 [32, 4, 5, 128], P(('sx', 'sy')), may hold values from -0.25 to 0.25
- energies: float32 [32, 4], P(('sx', 'sy')), may hold values from 1 to 6
- centers: int32 [32, 2], P(('sx', 'sy')), may hold values from 0 to 23, as said below
Outputs:
- filtered: float32 [256, 24, 12, 128], P('band', 'sx', 'sy')
- gram: float32 [256, 256], P('band')
Inputs may be any that keep to these rules, and one draw needn't show every extreme that they name: `centers`: atom a's cell lies in the grid slab of the device numbered a // 4 along sx+sy, sy counting fastest; the first entry indexes the first grid dimension, the second the second.
All inputs are finite; a program needn't handle non-finite values.
Results may differ from a plain program's by a relative error of at most 0.0022.
Values may be sent and summed in bfloat16 or wider, within the bound.
No kernel may reach another device: no remote copies, remote signals or barrier semaphores. Data moves between devices by JAX's collectives and lax.ppermute only.
A program may use at most 64 MiB of HBM per device.

v0:
```python
import jax
import jax.numpy as jnp
from jax import lax
from jax.sharding import PartitionSpec as P

stencil_weights = (
    -5369.0 / 1800.0,
    12.0 / 7.0,
    -15.0 / 56.0,
    10.0 / 189.0,
    -1.0 / 112.0,
    2.0 / 1925.0,
    -1.0 / 16632.0,
)
filter_center = 6.5
filter_half = 6.0
offsets_x = (0, -1, 1, 0, 0)
offsets_y = (0, 0, 0, -1, 1)


def from_behind(block, axis, distance):
    devices = range(lax.axis_size(axis))
    route = [(i - distance, i) for i in devices if i - distance in devices]
    return lax.ppermute(block, axis, route)


def extended(cells, sides, width):
    for axis, dim in sides:
        count = lax.axis_size(axis)
        ends = count - 1
        head = lax.slice_in_dim(cells, 0, width, axis=dim)
        tail = lax.slice_in_dim(cells, cells.shape[dim] - width, cells.shape[dim], axis=dim)
        cells = jnp.concatenate(
            [
                lax.ppermute(tail, axis, [(i, (i + 1) % count) for i in range(ends)]),
                cells,
                lax.ppermute(head, axis, [((i + 1) % count, i) for i in range(ends)]),
            ],
            axis=dim,
        )
    return cells


def second_sum(ext_x, ext_y, field):
    count_x = field.shape[1]
    count_y = field.shape[2]
    count_z = field.shape[3]
    padded_z = jnp.pad(field, ((0, 0), (0, 0), (0, 0), (6, 6)))
    total = 3.0 * stencil_weights[0] * field
    for step in range(1, 7):
        weight = stencil_weights[step]
        total = total + weight * (
            ext_x[:, 6 + step : 6 + step + count_x] + ext_x[:, 6 - step : 6 - step + count_x]
        )
        total = total + weight * (
            ext_y[:, :, 6 + step : 6 + step + count_y] + ext_y[:, :, 6 - step : 6 - step + count_y]
        )
        total = total + weight * (
            padded_z[:, :, :, 6 + step : 6 + step + count_z]
            + padded_z[:, :, :, 6 - step : 6 - step + count_z]
        )
    return total


def column_slots(centers, first_x, first_y, count_x, count_y):
    shift_x = jnp.array(offsets_x, jnp.int32)
    shift_y = jnp.array(offsets_y, jnp.int32)
    local_x = centers[:, 0:1] - first_x + shift_x[None, :]
    local_y = centers[:, 1:2] - first_y + shift_y[None, :]
    inner = count_x * count_y
    slots = jnp.where(
        local_x < 0,
        inner + local_y,
        jnp.where(
            local_x >= count_x,
            inner + count_y + local_y,
            jnp.where(
                local_y < 0,
                inner + 2 * count_y + local_x,
                jnp.where(
                    local_y >= count_y,
                    inner + 2 * count_y + count_x + local_x,
                    local_x * count_y + local_y,
                ),
            ),
        ),
    )
    return slots.reshape(-1)


def pass_x(strip, offset):
    return from_behind(strip.astype(jnp.bfloat16), "sx", offset).astype(strip.dtype)


def pass_y(strip, offset):
    return from_behind(strip, "sy", offset)


def nonlocal_term(field, ext_x, ext_y, slots, projectors, energies):
    batch, count_x, count_y, count_z = field.shape
    inner = count_x * count_y
    tiles = projectors.shape[2]
    atoms = projectors.shape[0]
    table = jnp.concatenate(
        [
            field.reshape(batch, inner, count_z),
            ext_x[:, 5],
            ext_x[:, 6 + count_x],
            ext_y[:, :, 5],
            ext_y[:, :, 6 + count_y],
        ],
        axis=1,
    )
    onehot = (slots[:, None] == jnp.arange(table.shape[1], dtype=jnp.int32)[None, :]).astype(
        jnp.float32
    )
    picked = jnp.einsum("kc,bcz->bkz", onehot, table, precision=lax.Precision.HIGHEST).reshape(
        batch, atoms, tiles, count_z
    )
    coeffs = jnp.einsum("aptz,batz->bap", projectors, picked, precision=lax.Precision.HIGHEST)
    weighted = coeffs * energies[None]
    spread = jnp.einsum(
        "aptz,bap->batz", projectors, weighted, precision=lax.Precision.HIGHEST
    ).reshape(batch, atoms * tiles, count_z)
    back = jnp.einsum("kc,bkz->bcz", onehot, spread, precision=lax.Precision.HIGHEST)
    result = back[:, :inner].reshape(batch, count_x, count_y, count_z)
    from_right = pass_x(back[:, inner : inner + count_y], -1)
    from_left = pass_x(back[:, inner + count_y : inner + 2 * count_y], 1)
    result = result.at[:, count_x - 1].add(from_right)
    result = result.at[:, 0].add(from_left)
    base_y = inner + 2 * count_y
    from_above = pass_y(back[:, base_y : base_y + count_x], -1)
    from_below = pass_y(back[:, base_y + count_x : base_y + 2 * count_x], 1)
    result = result.at[:, :, count_y - 1].add(from_above)
    result = result.at[:, :, 0].add(from_below)
    return result


def local(orbitals, potential, projectors, energies, centers):
    first_y = lax.axis_index("sy") * potential.shape[1]
    pot_all, proj_all, energy_all = (potential, projectors, energies)
    slots = column_slots(
        centers,
        lax.axis_index("sx") * potential.shape[0],
        first_y,
        orbitals.shape[1],
        orbitals.shape[2],
    )

    def apply_h(vector):
        ext_x = extended(vector, (("sx", 1),), 6)
        ext_y = extended(vector, (("sy", 2),), 6)
        kinetic = -0.5 * second_sum(ext_x, ext_y, vector)
        return (
            kinetic
            + pot_all[None] * vector
            + nonlocal_term(vector, ext_x, ext_y, slots, proj_all, energy_all)
        )

    previous = orbitals
    current = (apply_h(orbitals) - filter_center * orbitals) / filter_half
    following = 2.0 * (apply_h(current) - filter_center * current) / filter_half - previous
    previous, current = (current, following)
    rounded = current.astype(jnp.bfloat16)
    flat = rounded.reshape(rounded.shape[0], -1)
    partial_rows = lax.dot_general(
        flat,
        lax.all_gather(flat, "band", axis=0, tiled=True),
        (((1,), (1,)), ((), ())),
        preferred_element_type=jnp.float32,
    )
    cell_total = flat.shape[1] * lax.axis_size("sx") * lax.axis_size("sy")
    gram = lax.psum(partial_rows, ("sx", "sy")) / cell_total
    return (current, gram)


def solution(mesh):
    in_specs = (
        P("band", "sx", "sy", None),
        P("sx", "sy", None),
        P(("sx", "sy"), None, None, None),
        P(("sx", "sy"), None),
        P(("sx", "sy"), None),
    )
    out_specs = (P("band", "sx", "sy", None), P("band", None))
    return jax.shard_map(local, mesh=mesh, in_specs=in_specs, out_specs=out_specs, check_vma=False)
```

profile of v0, /device:TPU:0, one launch (start us, length us, event | category | flops | bytes accessed | tf_op | source)
XLA Modules:
  0.0 344.1 jit_solution(14134565312854021941)
XLA Ops:
  8.6 3.1 collective-permute-start.1
  11.7 6.0 %collective-permute-start.3 = (f32[64,6,6,128]{3,0,2,1:T(8,128)}, f32[64,6,6,128]{3,0,2,1:T(8,128)}, u32[]{:S(2)}, u32[]{:S(2)}) collective-permute-start(f32[64,6,6,128]{3,0,2,1:T(8,128)} %param.23), channel_id=1, source_target_pairs={{0,1},{2,3},{4,5},{6,7},{8,9},{10,11},{12,13},{14,15},{16,17},{18,... | collective-permute-start | bytes 3538952 | tf_op jit(solution)/shard_map/ppermute | solution.py:35
  18.9 3.1 copy.96
  23.8 19.4 %collective-permute-done.3 = f32[64,6,6,128]{3,0,2,1:T(8,128)} collective-permute-done((f32[64,6,6,128]{3,0,2,1:T(8,128)}, f32[64,6,6,128]{3,0,2,1:T(8,128)}, u32[]{:S(2)}, u32[]{:S(2)}) %collective-permute-start.3) | collective-permute-done | bytes 1179680 | tf_op jit(solution)/shard_map/ppermute | solution.py:35
  43.2 2.0 copy_dynamic-update-slice_fusion.2
  45.2 2.5 copy_dynamic-update-slice_fusion
  48.5 3.1 copy_dynamic-update-slice_fusion.3
  52.5 14.2 %concatenate.86 = f32[64,60,128]{2,1,0:T(8,128)} concatenate(f32[64,36,128]{2,1,0:T(8,128)} %copy.96, f32[64,6,128]{2,1,0:T(8,128)} %bitcast.115, f32[64,6,128]{2,1,0:T(8,128)S(1)} %bitcast.114, f32[64,6,128]{2,1,0:T(8,128)} %get-tuple-element.126, f32[64,6,128]{2,1,0:T(8,128)} %get-tuple-element.125), dimensions={1} | concatenate | bytes 3932160 | tf_op jit(solution)/shard_map/concatenate | solution.py:104
  66.6 2.5 convolution_bitcast_fusion.3
  76.0 3.2 collective-permute-start.5
  80.4 5.9 %collective-permute-start.7 = (f32[64,6,128]{2,1,0:T(8,128)}, f32[64,6,128]{2,1,0:T(8,128)}, u32[]{:S(2)}, u32[]{:S(2)}) collective-permute-start(f32[64,6,128]{2,1,0:T(8,128)} %get-tuple-element.110), channel_id=1, source_target_pairs={{0,1},{2,3},{4,5},{6,7},{8,9},{10,11},{12,13},{14,15},{16,17},{18,... | collective-permute-start | bytes 589832 | tf_op jit(solution)/shard_map/ppermute | solution.py:24
  86.4 1.9 copy.78
  88.3 1.8 copy.79
  90.2 1.8 copy.102
  92.2 6.1 %scatter-add.29 = f32[64,6,6,128]{3,1,0,2:T(8,128)} dynamic-update-slice(f32[64,6,6,128]{3,1,0,2:T(8,128)} %copy.102, f32[64,1,6,128]{3,1,0,2:T(1,128)S(1)} %add.430, s32[]{:T(128)} %constant.233.clone.1, s32[]{:T(128)} %constant.233.clone.1, s32[]{:T(128)} %constant.233.clone.1, s32[]{:T(128)} %constant.233.clone.1) | dynamic-update-slice | bytes 393220 | tf_op jit(solution)/shard_map/scatter-add | solution.py:130
  98.3 1.8 fusion.136
  100.1 1.8 fusion.135
  101.8 34.7 %broadcast_multiply_fusion = (f32[64,6,6,128]{3,1,0,2:T(8,128)S(1)}, f32[64,6,6,128]{3,1,0,2:T(8,128)}) fusion(f32[64,6,6,128]{3,1,0,2:T(8,128)} %get-tuple-element.116, f32[64,6,6,128]{3,1,0,2:T(8,128)} %fusion.135, f32[6,6,128]{2,0,1:T(8,128)S(1)} %copy.90, f32[64,6,6,128]{3,0,2,1:T(8,128)} %collective-permute-done.3, ...), kind=kLoop, calls=%fused_computation.225 | loop fusion | flops 21233664 | bytes 21252096 | tf_op jit(solution)/shard_map/div | solution.py:161
  139.4 4.7 %collective-permute-start.11 = (f32[64,6,6,128]{3,0,2,1:T(8,128)S(1)}, f32[64,6,6,128]{3,0,2,1:T(8,128)S(1)}, u32[]{:S(2)}, u32[]{:S(2)}) collective-permute-start(f32[64,6,6,128]{3,0,2,1:T(8,128)S(1)} %copy.104), channel_id=1, source_target_pairs={{0,1},{2,3},{4,5},{6,7},{8,9},{10,11},{12,13},{14,15},{16,17},{18,... | collective-permute-start | bytes 3538952 | tf_op jit(solution)/shard_map/ppermute | solution.py:35
  144.1 2.8 collective-permute-start.9
  148.8 19.8 %collective-permute-done.10 = f32[64,6,6,128]{3,0,2,1:T(8,128)S(1)} collective-permute-done((f32[64,6,6,128]{3,0,2,1:T(8,128)S(1)}, f32[64,6,6,128]{3,0,2,1:T(8,128)S(1)}, u32[]{:S(2)}, u32[]{:S(2)}) %collective-permute-start.10) | collective-permute-done | bytes 1179680 | tf_op jit(solution)/shard_map/ppermute | solution.py:37
  173.8 6.5 %concatenate.91 = f32[64,60,128]{2,1,0:T(8,128)S(1)} concatenate(f32[64,36,128]{2,1,0:T(8,128)S(1)} %copy.122, f32[64,6,128]{2,1,0:T(8,128)} %bitcast.117, f32[64,6,128]{2,1,0:T(8,128)} %bitcast.116, f32[64,6,128]{2,1,0:T(8,128)} %slice_bitcast_fusion.1, f32[64,6,128]{2,1,0:T(8,128)} %slice_bitcast_fusion), dimensions={1} | concatenate | bytes 3932160 | tf_op jit(solution)/shard_map/concatenate | solution.py:104
  188.0 3.2 collective-permute-start.13
  192.5 4.8 %collective-permute-start.15 = (f32[64,6,128]{2,1,0:T(8,128)}, f32[64,6,128]{2,1,0:T(8,128)S(1)}, u32[]{:S(2)}, u32[]{:S(2)}) collective-permute-start(f32[64,6,128]{2,1,0:T(8,128)} %get-tuple-element.108), channel_id=1, source_target_pairs={{0,1},{2,3},{4,5},{6,7},{8,9},{10,11},{12,13},{14,15},{16,17},{18,... | collective-permute-start | bytes 589832 | tf_op jit(solution)/shard_map/ppermute | solution.py:24
  197.3 1.9 copy.105
  199.2 1.9 copy.107
  201.2 1.8 copy.128
  203.3 6.2 %scatter-add.35 = f32[64,6,6,128]{3,1,0,2:T(8,128)} dynamic-update-slice(f32[64,6,6,128]{3,1,0,2:T(8,128)} %copy.128, f32[64,1,6,128]{3,1,0,2:T(1,128)S(1)} %add.472, s32[]{:T(128)} %constant.233.clone.1, s32[]{:T(128)} %constant.233.clone.1, s32[]{:T(128)} %constant.233.clone.1, s32[]{:T(128)} %constant.233.clone.1) | dynamic-update-slice | bytes 393220 | tf_op jit(solution)/shard_map/scatter-add | solution.py:130
  212.9 15.2 %fusion.152 = (bf16[64,6,6,128]{3,1,0,2:T(8,128)(2,1)S(1)}, f32[64,6,6,128]{3,1,0,2:T(8,128)}) fusion(f32[64,6,6,128]{3,0,2,1:T(8,128)S(1)} %copy-done.4, f32[64,6,6,128]{3,1,0,2:T(8,128)} %get-tuple-element.107, f32[64,6,6,128]{3,1,0,2:T(8,128)} %fusion.133, f32[6,6,128]{2,0,1:T(8,128)S(1)} %copy.116, f32[64,6,6,128]{3,1,0,2:T(8,128)} %copy-done.5, ...), kind=kLoop, calls=%fused_computation.274 | loop fusion | flops 24772608 | bytes 11225088 | tf_op jit(solution)/shard_map/convert_element_type | solution.py:164
  230.3 50.6 %all-gather.2.cloned.1.call-done = bf16[256,4608]{1,0:T(8,128)(2,1)} async-done(((bf16[64,4608]{1,0:T(8,128)(2,1)}), bf16[256,4608]{1,0:T(8,128)(2,1)}) %all-gather.2.cloned.1.call-update) | async-done | bytes 2359312 | tf_op jit(solution)/shard_map/all_gather | solution.py:168
  280.9 3.3 fusion.160
  285.4 50.3 %all-reduce.4.cloned.1.call-done = f32[64,256]{1,0:T(8,128)} async-done(((f32[64,256]{1,0:T(8,128)}), f32[64,256]{1,0:T(8,128)}) %all-reduce.4.cloned.1.call-update) | async-done | bytes 65552 | tf_op jit(solution)/shard_map/psum | solution.py:173
  (122 shorter events, 41.6 us)
Async XLA Ops:
  7.2 62.1 %copy-start = (f32[4,4,5,128]{3,1,2,0:T(4,128)S(1)}, f32[4,4,5,128]{3,1,2,0:T(4,128)}, u32[]{:S(2)}) copy-start(f32[4,4,5,128]{3,1,2,0:T(4,128)} %param.25) | copy-start | bytes 122884
  7.2 14.9 %copy-start.19 = (s32[5]{0:T(128)S(1)}, s32[5]{0:T(128)}, u32[]{:S(2)}) copy-start(s32[5]{0:T(128)} %constant.245.clone) | copy-start | bytes 64
  7.2 14.9 %copy-start.20 = (s32[5]{0:T(128)S(1)}, s32[5]{0:T(128)}, u32[]{:S(2)}) copy-start(s32[5]{0:T(128)} %constant.246.clone) | copy-start | bytes 64
  7.2 14.9 %copy-start.18 = (s32[4,2]{0,1:T(2,128)S(1)}, s32[4,2]{0,1:T(2,128)}, u32[]{:S(2)}) copy-start(s32[4,2]{0,1:T(2,128)} %param.27) | copy-start | bytes 100
  7.2 15.0 %copy-start.16 = (f32[6,6,128]{2,1,0:T(8,128)S(1)}, f32[6,6,128]{2,1,0:T(8,128)}, u32[]{:S(2)}) copy-start(f32[6,6,128]{2,1,0:T(8,128)} %param.24) | copy-start | bytes 55300
  7.2 273.6 %all-gather.2.cloned.1.call-start = ((), (), s32[]{:S(2)}) async-start(), calls=%async_computation | async-start | bytes 2949120 | tf_op jit(solution)/shard_map/all_gather | solution.py:168
  7.3 15.0 %collective-permute-start = (f32[64,6,6,128]{3,0,2,1:T(8,128)}, f32[64,6,6,128]{3,0,2,1:T(8,128)S(1)}, u32[]{:S(2)}, u32[]{:S(2)}) collective-permute-start(f32[64,6,6,128]{3,0,2,1:T(8,128)} %param.23), channel_id=1, source_target_pairs={{2,0},{4,2},{6,4},{3,1},{5,3},{7,5},{10,8},{12,10},{14,12},{11,9},... | collective-permute-start | bytes 3538952 | tf_op jit(solution)/shard_map/ppermute | solution.py:37
  8.6 13.9 %collective-permute-start.1 = (f32[64,6,6,128]{3,0,2,1:T(8,128)}, f32[64,6,6,128]{3,0,2,1:T(8,128)S(1)}, u32[]{:S(2)}, u32[]{:S(2)}) collective-permute-start(f32[64,6,6,128]{3,0,2,1:T(8,128)} %param.23), channel_id=1, source_target_pairs={{0,2},{2,4},{4,6},{1,3},{3,5},{5,7},{8,10},{10,12},{12,14},{9,11},... | collective-permute-start | bytes 3538952 | tf_op jit(solution)/shard_map/ppermute | solution.py:35
  11.7 31.5 %collective-permute-start.3 = (f32[64,6,6,128]{3,0,2,1:T(8,128)}, f32[64,6,6,128]{3,0,2,1:T(8,128)}, u32[]{:S(2)}, u32[]{:S(2)}) collective-permute-start(f32[64,6,6,128]{3,0,2,1:T(8,128)} %param.23), channel_id=1, source_target_pairs={{0,1},{2,3},{4,5},{6,7},{8,9},{10,11},{12,13},{14,15},{16,17},{18,... | collective-permute-start | bytes 3538952 | tf_op jit(solution)/shard_map/ppermute | solution.py:35
  17.6 30.8 %collective-permute-start.2 = (f32[64,6,6,128]{3,0,2,1:T(8,128)}, f32[64,6,6,128]{3,0,2,1:T(8,128)}, u32[]{:S(2)}, u32[]{:S(2)}) collective-permute-start(f32[64,6,6,128]{3,0,2,1:T(8,128)} %param.23), channel_id=1, source_target_pairs={{1,0},{3,2},{5,4},{7,6},{9,8},{11,10},{13,12},{15,14},{17,16},{19,... | collective-permute-start | bytes 3538952 | tf_op jit(solution)/shard_map/ppermute | solution.py:37
  23.8 21.4 %copy-start.3 = (f32[64,6,6,128]{3,0,2,1:T(8,128)S(1)}, f32[64,6,6,128]{3,0,2,1:T(8,128)}, u32[]{:S(2)}) copy-start(f32[64,6,6,128]{3,0,2,1:T(8,128)} %param.23) | copy-start | bytes 3538948
  73.4 16.7 %collective-permute-start.4 = (bf16[64,6,128]{2,0,1:T(8,128)(2,1)S(1)}, bf16[64,6,128]{2,0,1:T(8,128)(2,1)S(1)}, u32[]{:S(2)}, u32[]{:S(2)}) collective-permute-start(bf16[64,6,128]{2,0,1:T(8,128)(2,1)S(1)} %get-tuple-element.122), channel_id=1, source_target_pairs={{2,0},{4,2},{6,4},{3,1},{5,3},{7,5},{10,8},{12,10},{14,12},{11,9},... | collective-permute-start | bytes 294920 | tf_op jit(solution)/shard_map/ppermute | solution.py:24
  75.7 10.7 %copy-start.9 = (f32[64,6,6,128]{3,0,2,1:T(8,128)S(1)}, f32[64,6,6,128]{3,0,2,1:T(8,128)}, u32[]{:S(2)}) copy-start(f32[64,6,6,128]{3,0,2,1:T(8,128)} %copy-done.8) | copy-start | bytes 3538948
  76.0 12.3 %copy-start.11 = (f32[64,6,6,128]{3,0,2,1:T(8,128)S(1)}, f32[64,6,6,128]{3,0,2,1:T(8,128)}, u32[]{:S(2)}) copy-start(f32[64,6,6,128]{3,0,2,1:T(8,128)} %copy-done.10) | copy-start | bytes 3538948
  76.0 16.0 %collective-permute-start.5 = (bf16[64,6,128]{2,0,1:T(8,128)(2,1)S(1)}, bf16[64,6,128]{2,0,1:T(8,128)(2,1)S(1)}, u32[]{:S(2)}, u32[]{:S(2)}) collective-permute-start(bf16[64,6,128]{2,0,1:T(8,128)(2,1)S(1)} %get-tuple-element.121), channel_id=1, source_target_pairs={{0,2},{2,4},{4,6},{1,3},{3,5},{5,7},{8,10},{10,12},{12,14},{9,11},... | collective-permute-start | bytes 294920 | tf_op jit(solution)/shard_map/ppermute | solution.py:24
  79.1 19.2 %collective-permute-start.6 = (f32[64,6,128]{2,1,0:T(8,128)}, f32[64,6,128]{2,1,0:T(8,128)}, u32[]{:S(2)}, u32[]{:S(2)}) collective-permute-start(f32[64,6,128]{2,1,0:T(8,128)} %get-tuple-element.111), channel_id=1, source_target_pairs={{1,0},{3,2},{5,4},{7,6},{9,8},{11,10},{13,12},{15,14},{17,16},{19,... | collective-permute-start | bytes 589832 | tf_op jit(solution)/shard_map/ppermute | solution.py:24
  80.4 19.6 %collective-permute-start.7 = (f32[64,6,128]{2,1,0:T(8,128)}, f32[64,6,128]{2,1,0:T(8,128)}, u32[]{:S(2)}, u32[]{:S(2)}) collective-permute-start(f32[64,6,128]{2,1,0:T(8,128)} %get-tuple-element.110), channel_id=1, source_target_pairs={{0,1},{2,3},{4,5},{6,7},{8,9},{10,11},{12,13},{14,15},{16,17},{18,... | collective-permute-start | bytes 589832 | tf_op jit(solution)/shard_map/ppermute | solution.py:24
  136.6 11.1 %copy-start.1 = (f32[64,6,6,128]{3,1,0,2:T(8,128)}, f32[64,6,6,128]{3,1,0,2:T(8,128)S(1)}, u32[]{:S(2)}) copy-start(f32[64,6,6,128]{3,1,0,2:T(8,128)S(1)} %get-tuple-element.106) | copy-start | bytes 3538948
  136.8 10.9 %collective-permute-start.8 = (f32[64,6,6,128]{3,0,2,1:T(8,128)S(1)}, f32[64,6,6,128]{3,0,2,1:T(8,128)S(1)}, u32[]{:S(2)}, u32[]{:S(2)}) collective-permute-start(f32[64,6,6,128]{3,0,2,1:T(8,128)S(1)} %copy.104), channel_id=1, source_target_pairs={{2,0},{4,2},{6,4},{3,1},{5,3},{7,5},{10,8},{12,10},{14,12},{11,9},... | collective-permute-start | bytes 3538952 | tf_op jit(solution)/shard_map/ppermute | solution.py:37
  138.1 30.5 %collective-permute-start.10 = (f32[64,6,6,128]{3,0,2,1:T(8,128)S(1)}, f32[64,6,6,128]{3,0,2,1:T(8,128)S(1)}, u32[]{:S(2)}, u32[]{:S(2)}) collective-permute-start(f32[64,6,6,128]{3,0,2,1:T(8,128)S(1)} %copy.104), channel_id=1, source_target_pairs={{1,0},{3,2},{5,4},{7,6},{9,8},{11,10},{13,12},{15,14},{17,16},{19,... | collective-permute-start | bytes 3538952 | tf_op jit(solution)/shard_map/ppermute | solution.py:37
  139.4 31.0 %collective-permute-start.11 = (f32[64,6,6,128]{3,0,2,1:T(8,128)S(1)}, f32[64,6,6,128]{3,0,2,1:T(8,128)S(1)}, u32[]{:S(2)}, u32[]{:S(2)}) collective-permute-start(f32[64,6,6,128]{3,0,2,1:T(8,128)S(1)} %copy.104), channel_id=1, source_target_pairs={{0,1},{2,3},{4,5},{6,7},{8,9},{10,11},{12,13},{14,15},{16,17},{18,... | collective-permute-start | bytes 3538952 | tf_op jit(solution)/shard_map/ppermute | solution.py:35
  144.1 28.4 %collective-permute-start.9 = (f32[64,6,6,128]{3,0,2,1:T(8,128)S(1)}, f32[64,6,6,128]{3,0,2,1:T(8,128)S(1)}, u32[]{:S(2)}, u32[]{:S(2)}) collective-permute-start(f32[64,6,6,128]{3,0,2,1:T(8,128)S(1)} %copy.104), channel_id=1, source_target_pairs={{0,2},{2,4},{4,6},{1,3},{3,5},{5,7},{8,10},{10,12},{12,14},{9,11},... | collective-permute-start | bytes 3538952 | tf_op jit(solution)/shard_map/ppermute | solution.py:35
  185.5 15.7 %collective-permute-start.12 = (bf16[64,6,128]{2,0,1:T(8,128)(2,1)S(1)}, bf16[64,6,128]{2,0,1:T(8,128)(2,1)S(1)}, u32[]{:S(2)}, u32[]{:S(2)}) collective-permute-start(bf16[64,6,128]{2,0,1:T(8,128)(2,1)S(1)} %get-tuple-element.120), channel_id=1, source_target_pairs={{2,0},{4,2},{6,4},{3,1},{5,3},{7,5},{10,8},{12,10},{14,12},{11,9},... | collective-permute-start | bytes 294920 | tf_op jit(solution)/shard_map/ppermute | solution.py:24
  187.7 9.6 %copy-start.13 = (f32[64,6,6,128]{3,0,2,1:T(8,128)S(1)}, f32[64,6,6,128]{3,0,2,1:T(8,128)}, u32[]{:S(2)}) copy-start(f32[64,6,6,128]{3,0,2,1:T(8,128)} %copy-done.12) | copy-start | bytes 3538948
  188.0 11.2 %copy-start.15 = (f32[64,6,6,128]{3,0,2,1:T(8,128)S(1)}, f32[64,6,6,128]{3,0,2,1:T(8,128)}, u32[]{:S(2)}) copy-start(f32[64,6,6,128]{3,0,2,1:T(8,128)} %copy-done.14) | copy-start | bytes 3538948
  188.0 15.0 %collective-permute-start.13 = (bf16[64,6,128]{2,0,1:T(8,128)(2,1)S(1)}, bf16[64,6,128]{2,0,1:T(8,128)(2,1)S(1)}, u32[]{:S(2)}, u32[]{:S(2)}) collective-permute-start(bf16[64,6,128]{2,0,1:T(8,128)(2,1)S(1)} %get-tuple-element.119), channel_id=1, source_target_pairs={{0,2},{2,4},{4,6},{1,3},{3,5},{5,7},{8,10},{10,12},{12,14},{9,11},... | collective-permute-start | bytes 294920 | tf_op jit(solution)/shard_map/ppermute | solution.py:24
  191.2 18.3 %collective-permute-start.14 = (f32[64,6,128]{2,1,0:T(8,128)}, f32[64,6,128]{2,1,0:T(8,128)S(1)}, u32[]{:S(2)}, u32[]{:S(2)}) collective-permute-start(f32[64,6,128]{2,1,0:T(8,128)} %get-tuple-element.109), channel_id=1, source_target_pairs={{1,0},{3,2},{5,4},{7,6},{9,8},{11,10},{13,12},{15,14},{17,16},{19,... | collective-permute-start | bytes 589832 | tf_op jit(solution)/shard_map/ppermute | solution.py:24
  192.5 18.7 %collective-permute-start.15 = (f32[64,6,128]{2,1,0:T(8,128)}, f32[64,6,128]{2,1,0:T(8,128)S(1)}, u32[]{:S(2)}, u32[]{:S(2)}) collective-permute-start(f32[64,6,128]{2,1,0:T(8,128)} %get-tuple-element.108), channel_id=1, source_target_pairs={{0,1},{2,3},{4,5},{6,7},{8,9},{10,11},{12,13},{14,15},{16,17},{18,... | collective-permute-start | bytes 589832 | tf_op jit(solution)/shard_map/ppermute | solution.py:24
  203.0 9.8 %copy-start.2 = (f32[64,6,6,128]{3,1,0,2:T(8,128)S(1)}, f32[64,6,6,128]{3,1,0,2:T(8,128)}, u32[]{:S(2)}) copy-start(f32[64,6,6,128]{3,1,0,2:T(8,128)} %copy-done.1) | copy-start | bytes 3538948
  203.0 9.8 %copy-start.4 = (f32[64,6,6,128]{3,0,2,1:T(8,128)S(1)}, f32[64,6,6,128]{3,0,2,1:T(8,128)}, u32[]{:S(2)}) copy-start(f32[64,6,6,128]{3,0,2,1:T(8,128)} %param.23) | copy-start | bytes 3538948
  230.2 54.0 %copy-start.7 = (f32[64,6,6,128]{3,1,0,2:T(8,128)S(1)}, f32[64,6,6,128]{3,1,0,2:T(8,128)}, u32[]{:S(2)}) copy-start(f32[64,6,6,128]{3,1,0,2:T(8,128)} %get-tuple-element.105) | copy-start | bytes 3538948
  230.2 105.5 %all-reduce.4.cloned.1.call-start = ((), (), s32[]{:S(2)}) async-start(), calls=%async_computation.1 | async-start | bytes 131072 | tf_op jit(solution)/shard_map/psum | solution.py:173
  (7 other events, 12.7 us)
Sparse Core Ops, SparseCore 0:
  230.4 50.4 all-gather.1
  284.5 51.2 all-reduce.3
where the time goes:
time: 346 us; the launch traced here: 344 us
  waiting for transfers between devices  142 us (41%)
  local copies, waits for them, and re-layouts  71.7 us (21%)
  other arithmetic  58.9 us (17%)
  starting transfers between devices  44.1 us (13%)
  between operations  14.7 us (4%)
  matrix products  12.6 us (4%)
    all_gather x1, waiting for transfers between devices, local(): lax.all_gather(flat, 'band', axis=0, tiled=True)  50.6 us
    psum x1, waiting for transfers between devices, local(): gram = lax.psum(partial_rows, ('sx', 'sy')) / cell_total  50.3 us
    div x1, other arithmetic, local(): current = (apply_h(orbitals) - filter_center * orbitals) / filter_half  34.7 us
    ppermute x8, starting transfers between devices, from_behind(): return lax.ppermute(block, axis, route)  22.3 us
    concatenate x2, local copies, waits for them, and re-layouts, nonlocal_term(): jnp.concatenate([field.reshape(batch, inner, count_z), ext_x[:, 5], ext_x...  20.6 us
    ppermute x4, waiting for transfers between devices, extended(): lax.ppermute(head, axis, [((i + 1) % count, i) for i in range(ends)])  20.6 us
    ppermute x4, waiting for transfers between devices, extended(): lax.ppermute(tail, axis, [(i, (i + 1) % count) for i in range(ends)])  20.5 us
    ppermute x4, starting transfers between devices, extended(): lax.ppermute(tail, axis, [(i, (i + 1) % count) for i in range(ends)])  16.6 us
  transfers between devices with their start and end apart: 18, of which 6 were waited for; matrix products, arithmetic and copies ran while one was open for 13% of the time, Pallas kernels for 0%

commit v1 on v0

v1 whole, which is shorter than its diff:
```python
import functools

import jax
import jax.numpy as jnp
from jax import lax
from jax.experimental import pallas as pl
from jax.experimental.pallas import tpu as pltpu
from jax.sharding import PartitionSpec as P

stencil_weights = (
    -5369.0 / 1800.0,
    12.0 / 7.0,
    -15.0 / 56.0,
    10.0 / 189.0,
    -1.0 / 112.0,
    2.0 / 1925.0,
    -1.0 / 16632.0,
)
filter_center = 6.5
filter_half = 6.0
offsets_x = (0, -1, 1, 0, 0)
offsets_y = (0, 0, 0, -1, 1)
width = 6
plane = ("sx", "sy")
every = ("band", "sx", "sy")


def filter_kernel(
    slabs_y,
    cells_x,
    cells_y,
    each,
    centers_ref,
    energies_ref,
    got_ref,
    field_ref,
    rounded_ref,
    first,
    second,
    partial,
    pot,
):
    group, _, nz = got_ref.shape
    count_x, count_y = pot.shape[0], pot.shape[1]
    tiles = len(offsets_x)
    atoms_here = centers_ref.shape[1] // 2
    projs = energies_ref.shape[1] // atoms_here
    slab_cells = cells_x * cells_y
    proj_row = slab_cells * each
    pot_row = proj_row + atoms_here * projs * tiles
    scale = 1.0 / filter_half
    factors = [-0.5 * scale * w for w in stencil_weights]
    span = cells_y * 2 if slabs_y % 2 == 0 else cells_y
    spans = count_y // span

    first[...] = jnp.zeros_like(first)
    second[...] = jnp.zeros_like(second)

    def take_slab(g, carry):
        x0 = (g // slabs_y) * cells_x
        y0 = (g % slabs_y) * cells_y
        for i in range(cells_x):
            for j in range(cells_y):
                cell = i * cells_y + j
                first[width + x0 + i, width + y0 + j] = got_ref[g, pl.ds(cell * each, each), :]
                pot[x0 + i, y0 + j] = got_ref[g, pl.ds(pot_row + cell, 1), :]
        return carry

    lax.fori_loop(0, group, take_slab, 0)

    distance = jnp.abs(
        lax.broadcasted_iota(jnp.int32, (nz, nz), 0) - lax.broadcasted_iota(jnp.int32, (nz, nz), 1)
    )
    along_z = jnp.zeros((nz, nz), jnp.float32)
    for step in range(1, width + 1):
        along_z = jnp.where(distance == step, factors[step], along_z)
    z_high = along_z.astype(jnp.bfloat16)
    z_low = (along_z - z_high.astype(jnp.float32)).astype(jnp.bfloat16)
    z_matrix = jnp.concatenate(
        [
            jnp.concatenate([z_high, z_low], axis=1),
            jnp.concatenate([z_high, jnp.zeros_like(z_high)], axis=1),
        ],
        axis=0,
    )

    def apply(source, target, finish, gain):
        def z_part(block, carry):
            rows = source[pl.ds(width + block * cells_x, cells_x), pl.ds(width, count_y)]
            flat = rows.reshape(cells_x * count_y * each, nz)
            high = flat.astype(jnp.bfloat16)
            low = (flat - high.astype(jnp.float32)).astype(jnp.bfloat16)
            both = jnp.dot(
                jnp.concatenate([high, low], axis=1), z_matrix, preferred_element_type=jnp.float32
            )
            partial[pl.ds(block * cells_x, cells_x)] = (both[:, :nz] + both[:, nz:]).reshape(
                rows.shape
            )
            return carry

        lax.fori_loop(0, count_x // cells_x, z_part, 0)

        def xy_part(index, carry):
            x = index // spans
            y = (index % spans) * span
            at_x = width + x
            at_y = width + y
            center = source[at_x, pl.ds(at_y, span)]
            total = partial[x, pl.ds(y, span)] + (
                (3.0 * factors[0] - filter_center * scale) + scale * pot[x, pl.ds(y, span)]
            ) * center
            for step in range(1, width + 1):
                pair_x = source[at_x + step, pl.ds(at_y, span)] + source[at_x - step, pl.ds(at_y, span)]
                pair_y = source[at_x, pl.ds(at_y + step, span)] + source[at_x, pl.ds(at_y - step, span)]
                total = total + factors[step] * (pair_x + pair_y)
            target[at_x, pl.ds(at_y, span)] = finish(total, target[at_x, pl.ds(at_y, span)])
            return carry

        lax.fori_loop(0, count_x * spans, xy_part, 0)

        def atoms_part(g, carry):
            for a in range(atoms_here):
                at_x = width + centers_ref[g, 2 * a]
                at_y = width + centers_ref[g, 2 * a + 1]
                base = proj_row + a * projs * tiles
                sums = [None] * projs
                for t in range(tiles):
                    tile = source[at_x + offsets_x[t], at_y + offsets_y[t]]
                    for p in range(projs):
                        term = tile * got_ref[g, pl.ds(base + p * tiles + t, 1), :]
                        sums[p] = term if t == 0 else sums[p] + term
                coeffs = [
                    jnp.sum(sums[p], axis=-1, keepdims=True)
                    * (energies_ref[g, a * projs + p] * gain)
                    for p in range(projs)
                ]
                for t in range(tiles):
                    spread = coeffs[0] * got_ref[g, pl.ds(base + t, 1), :]
                    for p in range(1, projs):
                        spread = spread + coeffs[p] * got_ref[g, pl.ds(base + p * tiles + t, 1), :]
                    to_x = at_x + offsets_x[t]
                    to_y = at_y + offsets_y[t]
                    target[to_x, to_y] = target[to_x, to_y] + spread
            return carry

        lax.fori_loop(0, group, atoms_part, 0)

    apply(first, second, lambda total, old: total, scale)

    for x in (width - 1, width + count_x):
        second[x] = jnp.zeros(second.shape[1:], jnp.float32)
    for y in (width - 1, width + count_y):
        second[:, y] = jnp.zeros((second.shape[0],) + second.shape[2:], jnp.float32)

    apply(second, first, lambda total, old: 2.0 * total - old, 2.0 * scale)

    shares = rounded_ref.shape[0] // group
    portion = slab_cells // shares

    def give_slab(g, carry):
        x0 = (g // slabs_y) * cells_x
        y0 = (g % slabs_y) * cells_y
        for i in range(cells_x):
            for j in range(cells_y):
                cell = i * cells_y + j
                value = first[width + x0 + i, width + y0 + j]
                field_ref[g, pl.ds(cell * each, each), :] = value
                rounded_ref[
                    (cell // portion) * group + g, :, pl.ds((cell % portion) * nz, nz)
                ] = value.astype(jnp.bfloat16)
        return carry

    lax.fori_loop(0, group, give_slab, 0)


def local(orbitals, potential, projectors, energies, centers):
    band_orbitals, cells_x, cells_y, nz = orbitals.shape
    bands = lax.axis_size("band")
    slabs_x = lax.axis_size("sx")
    slabs_y = lax.axis_size("sy")
    group = slabs_x * slabs_y
    each = band_orbitals // group
    slab_cells = cells_x * cells_y
    grid = (slabs_x * cells_x, slabs_y * cells_y)

    chunks = orbitals.transpose(1, 2, 0, 3).reshape(slab_cells, group, each, nz)
    chunks = chunks.transpose(1, 0, 2, 3).reshape(group, slab_cells * each, nz)
    atoms, projs = energies.shape
    numbers = jnp.concatenate([energies.reshape(-1), centers.reshape(-1).astype(jnp.float32)])
    numbers = jnp.pad(numbers, (0, nz - numbers.shape[0])).reshape(1, nz)
    shared = jnp.concatenate([projectors.reshape(-1, nz), potential.reshape(-1, nz), numbers])
    shared = jnp.pad(shared, ((0, -shared.shape[0] % 8), (0, 0)))
    sent = jnp.concatenate(
        [chunks, jnp.broadcast_to(shared[None], (group,) + shared.shape)], axis=1
    )
    got = lax.all_to_all(sent, plane, 0, 0)
    numbers = got[:, slab_cells * each + projectors.size // nz + slab_cells]
    all_energies = numbers[:, : atoms * projs]
    all_centers = numbers[:, atoms * projs : atoms * (projs + 2)].astype(jnp.int32)

    portion = slab_cells // bands
    padded = (grid[0] + 2 * width, grid[1] + 2 * width, each, nz)
    field, rounded = pl.pallas_call(
        functools.partial(filter_kernel, slabs_y, cells_x, cells_y, each),
        in_specs=[
            pl.BlockSpec(memory_space=pltpu.SMEM),
            pl.BlockSpec(memory_space=pltpu.SMEM),
            pl.BlockSpec(memory_space=pltpu.VMEM),
        ],
        out_specs=[pl.BlockSpec(memory_space=pltpu.VMEM)] * 2,
        out_shape=[
            jax.ShapeDtypeStruct((group, slab_cells * each, nz), jnp.float32),
            jax.ShapeDtypeStruct((bands * group, each, portion * nz), jnp.bfloat16),
        ],
        scratch_shapes=[
            pltpu.VMEM(padded, jnp.float32),
            pltpu.VMEM(padded, jnp.float32),
            pltpu.VMEM(grid + (each, nz), jnp.float32),
            pltpu.VMEM(grid + (1, nz), jnp.float32),
        ],
        compiler_params=pltpu.CompilerParams(vmem_limit_bytes=56 * 1024 * 1024),
        cost_estimate=pl.CostEstimate(
            flops=2 * 2 * 40 * grid[0] * grid[1] * each * nz,
            bytes_accessed=8 * grid[0] * grid[1] * each * nz,
            transcendentals=0,
        ),
    )(all_centers, all_energies, got)

    pieces = lax.all_to_all(rounded, every, 0, 0)
    matrix = pieces.reshape(bands * band_orbitals, portion * nz)
    sums = lax.dot_general(
        matrix, matrix, (((1,), (1,)), ((), ())), preferred_element_type=jnp.float32
    )
    parts = lax.all_to_all(sums.reshape(bands * group, each, bands * band_orbitals), every, 0, 0)
    rows = jnp.sum(parts, axis=0) / (grid[0] * grid[1] * nz)
    gram = lax.all_to_all(jnp.broadcast_to(rows[None], (group,) + rows.shape), plane, 0, 0)
    gram = gram.reshape(band_orbitals, bands * band_orbitals)

    back = lax.all_to_all(field, plane, 0, 0)
    back = back.reshape(group, slab_cells, each, nz).transpose(1, 0, 2, 3)
    filtered = back.reshape(cells_x, cells_y, band_orbitals, nz).transpose(2, 0, 1, 3)
    return (filtered, gram)


def solution(mesh):
    in_specs = (
        P("band", "sx", "sy", None),
        P("sx", "sy", None),
        P(("sx", "sy"), None, None, None),
        P(("sx", "sy"), None),
        P(("sx", "sy"), None),
    )
    out_specs = (P("band", "sx", "sy", None), P("band", None))
    return jax.shard_map(local, mesh=mesh, in_specs=in_specs, out_specs=out_specs, check_vma=False)
```

time: 346 us -> 109 us (0.32)
  waiting for transfers between devices: 142 us -> 19.3 us
  local copies, waits for them, and re-layouts: 71.7 us -> 6.71 us
  blocking collectives: 0 us -> 61.5 us
  other arithmetic: 58.9 us -> 1.68 us
  starting transfers between devices: 44.1 us -> 6.92 us
  between operations: 14.7 us -> 0.72 us
  matrix products: 12.6 us -> 0.38 us
  Pallas kernels: 0 us -> 10.7 us
    all_to_all x0 -> x3, blocking collectives: none -> 61.5 us  [the longest x1 26.6 us: local(): got = lax.all_to_all(sent, plane, 0, 0)]
    all_gather x1 -> x0, waiting for transfers between devices: 50.6 us -> none  [local(): lax.all_gather(flat, 'band', axis=0, tiled=True)]
    psum x1 -> x0, waiting for transfers between devices: 50.3 us -> none  [local(): gram = lax.psum(partial_rows, ('sx', 'sy')) / cell_total]
    ppermute x16 -> x0, starting transfers between devices: 44.1 us -> none  [the longest x8 22.3 us: from_behind(): return lax.ppermute(block, axis, route)]
    ppermute x16 -> x0, waiting for transfers between devices: 41.1 us -> none  [the longest x4 20.6 us: extended(): lax.ppermute(head, axis, [((i + 1) % count, i) for i in range(ends)])]
    div x2 -> x1, other arithmetic: 36.2 us -> 0.01 us  [local(): rows = jnp.sum(parts, axis=0) / (grid[0] * grid[1] * nz)]
    concatenate x3 -> x0, local copies, waits for them, and re-layouts: 23.8 us -> none  [the longest x2 20.6 us: nonlocal_term(): jnp.concatenate([field.reshape(batch, inner, count_z), ext_x[:, 5], ext_x...]
    all_to_all x0 -> x2, waiting for transfers between devices: none -> 19.3 us  [the longest x1 15.8 us: local(): back = lax.all_to_all(field, plane, 0, 0)]
  transfers between devices with their start and end apart: 18 -> 2, of which waited for: 6 -> 2; matrix products, arithmetic and copies ran while one was open for 13% -> 1% of each run, Pallas kernels for 0% -> 0%
where the time goes in v1:
time: 109 us; the launch traced here: 108 us
  blocking collectives  61.5 us (56%)
  waiting for transfers between devices  19.3 us (18%)
  Pallas kernels  10.7 us (10%)
  starting transfers between devices  6.92 us (6%)
  local copies, waits for them, and re-layouts  6.71 us (6%)
  other arithmetic  1.68 us (2%)
    all_to_all x1, blocking collectives, local(): got = lax.all_to_all(sent, plane, 0, 0)  26.6 us
    all_to_all x1, blocking collectives, local(): pieces = lax.all_to_all(rounded, every, 0, 0)  20.8 us
    all_to_all x1, waiting for transfers between devices, local(): back = lax.all_to_all(field, plane, 0, 0)  15.8 us
    all_to_all x1, blocking collectives, local(): lax.all_to_all(sums.reshape(bands * group, each, bands * band_orbitals),...  14.1 us
    pallas_call x1, Pallas kernels, local(): pl.pallas_call(functools.partial(filter_kernel, slabs_y, cells_x, cells_y...  10.7 us
    all_to_all x1, starting transfers between devices, local(): back = lax.all_to_all(field, plane, 0, 0)  3.57 us
    all_to_all x1, waiting for transfers between devices, local(): lax.all_to_all(jnp.broadcast_to(rows[None], (group,) + rows.shape), plane...  3.52 us
    all_to_all x1, starting transfers between devices, local(): lax.all_to_all(jnp.broadcast_to(rows[None], (group,) + rows.shape), plane...  3.35 us
  transfers between devices with their start and end apart: 2, of which 2 were waited for; matrix products, arithmetic and copies ran while one was open for 1% of the time, Pallas kernels for 0%

profile of v1, /device:TPU:0, one launch (start us, length us, event | category | flops | bytes accessed | tf_op | source)
XLA Modules:
  0.0 108.0 jit_solution(18349378159317950952)
XLA Ops:
  0.6 0.8 reshape.47
  1.4 0.7 convert_element_type.13
  2.1 0.1 copy.12
  2.2 0.1 convert_element_type.14
  2.3 0.7 reshape.46
  3.0 0.8 copy.11
  3.8 1.3 %copy.15 = f32[36,8,8,128]{3,2,0,1:T(8,128)S(1)} copy(f32[36,8,8,128]{3,2,1,0:T(8,128)} %bitcast.27) | data formatting | bytes 2359296 | tf_op jit(solution)/shard_map/reshape | solution.py:186
  5.2 0.1 fusion.3
  5.3 0.1 pad_maximum_fusion
  5.4 26.6 %all_to_all.25.got_ref = f32[8,408,128]{2,1,0:T(8,128)S(1)} all-to-all(f32[8,408,128]{2,1,0:T(8,128)S(1)} %pad_maximum_fusion), channel_id=1, replica_groups=mesh['band'=4,'sx'=4,'sy'=2] {'sx','sy'}, dimensions={0} | all-to-all | bytes 3342336 | tf_op jit(solution)/shard_map/all_to_all | solution.py:196
  32.0 0.0 copy-start
  32.0 0.0 copy-start.1
  32.0 0.8 slice_convert_fusion.centers_ref
  32.8 0.4 copy-done
  33.2 0.0 copy-done.1
  33.2 10.7 %shard_map.68 = (f32[8,288,128]{2,1,0:T(8,128)}, bf16[32,8,1152]{2,1,0:T(8,128)(2,1)}) custom-call(s32[8,8]{1,0:T(8,128)} %slice_convert_fusion.centers_ref, f32[8,16]{1,0:T(8,128)} %bitcast.31, f32[8,408,128]{2,1,0:T(8,128)} %copy-done), custom_call_target="tpu_custom_call" | custom-call | flops 47185920 | bytes 2359296 | tf_op jit(solution)/shard_map/pallas_call | solution.py:203
  43.9 20.8 %all_to_all.26 = bf16[32,8,1152]{2,1,0:T(8,128)(2,1)S(1)} all-to-all(bf16[32,8,1152]{2,1,0:T(8,128)(2,1)} %get-tuple-element.5), channel_id=1, replica_groups=mesh['band'=4,'sx'=4,'sy'=2] {'band','sx','sy'}, dimensions={0} | all-to-all | bytes 1179648 | tf_op jit(solution)/shard_map/all_to_all | solution.py:229
  64.7 0.4 fusion
  65.1 14.1 %all_to_all.27 = f32[32,8,256]{2,1,0:T(8,128)S(1)} all-to-all(f32[32,8,256]{2,1,0:T(8,128)S(1)} %fusion), channel_id=1, replica_groups=mesh['band'=4,'sx'=4,'sy'=2] {'band','sx','sy'}, dimensions={0} | all-to-all | bytes 524288 | tf_op jit(solution)/shard_map/all_to_all | solution.py:234
  79.2 3.6 %all-to-all-start.1 = ((f32[8,288,128]{2,1,0:T(8,128)}), f32[8,288,128]{2,1,0:T(8,128)S(1)}, u32[]{:S(2)}, u32[]{:S(2)}) async-start(f32[8,288,128]{2,1,0:T(8,128)} %get-tuple-element.4), calls=%async_computation.1 | async-start | bytes 2359296 | tf_op jit(solution)/shard_map/all_to_all | solution.py:239
  82.8 15.8 %all-to-all-done.1 = f32[8,288,128]{2,1,0:T(8,128)S(1)} async-done(((f32[8,288,128]{2,1,0:T(8,128)}), f32[8,288,128]{2,1,0:T(8,128)S(1)}, u32[]{:S(2)}, u32[]{:S(2)}) %all-to-all-start.1) | async-done | bytes 1179680 | tf_op jit(solution)/shard_map/all_to_all | solution.py:239
  98.6 0.6 broadcast_in_dim.5
  99.3 3.4 %all-to-all-start.4 = ((f32[8,8,256]{2,1,0:T(8,128)}), f32[8,8,256]{2,1,0:T(8,128)S(1)}, u32[]{:S(2)}, u32[]{:S(2)}) async-start(f32[8,8,256]{2,1,0:T(8,128)} %broadcast_in_dim.5), calls=%async_computation.4 | async-start | bytes 131072 | tf_op jit(solution)/shard_map/all_to_all | solution.py:236
  102.6 1.2 %copy.13 = f32[36,8,8,128]{3,2,1,0:T(8,128)} copy(f32[36,8,8,128]{3,2,0,1:T(8,128)S(1)} %bitcast.26) | data formatting | bytes 2359296 | tf_op jit(solution)/shard_map/transpose | solution.py:240
  103.8 3.5 %all-to-all-done.4 = f32[8,8,256]{2,1,0:T(8,128)S(1)} async-done(((f32[8,8,256]{2,1,0:T(8,128)}), f32[8,8,256]{2,1,0:T(8,128)S(1)}, u32[]{:S(2)}, u32[]{:S(2)}) %all-to-all-start.4) | async-done | bytes 65568 | tf_op jit(solution)/shard_map/all_to_all | solution.py:236
  107.3 0.6 copy.17
  (6 shorter events, 0.1 us)
Async XLA Ops:
  32.0 1.2 %copy-start = (f32[8,408,128]{2,1,0:T(8,128)}, f32[8,408,128]{2,1,0:T(8,128)S(1)}, u32[]{:S(2)}) copy-start(f32[8,408,128]{2,1,0:T(8,128)S(1)} %all_to_all.25.got_ref) | copy-start | bytes 5013508
  32.0 1.2 %copy-start.1 = (f32[8,1,128]{2,1,0:T(1,128)}, f32[8,1,128]{2,1,0:T(1,128)S(1)}, u32[]{:S(2)}) copy-start(f32[8,1,128]{2,1,0:T(1,128)S(1)} %slice.12) | copy-start | bytes 12292
  79.2 19.4 %all-to-all-start.1 = ((f32[8,288,128]{2,1,0:T(8,128)}), f32[8,288,128]{2,1,0:T(8,128)S(1)}, u32[]{:S(2)}, u32[]{:S(2)}) async-start(f32[8,288,128]{2,1,0:T(8,128)} %get-tuple-element.4), calls=%async_computation.1 | async-start | bytes 2359296 | tf_op jit(solution)/shard_map/all_to_all | solution.py:239
  99.3 8.0 %all-to-all-start.4 = ((f32[8,8,256]{2,1,0:T(8,128)}), f32[8,8,256]{2,1,0:T(8,128)S(1)}, u32[]{:S(2)}, u32[]{:S(2)}) async-start(f32[8,8,256]{2,1,0:T(8,128)} %broadcast_in_dim.5), calls=%async_computation.4 | async-start | bytes 131072 | tf_op jit(solution)/shard_map/all_to_all | solution.py:236

commit v2 on v1

v2 whole, which is shorter than its diff:
```python
import functools

import jax
import jax.numpy as jnp
from jax import lax
from jax.experimental import pallas as pl
from jax.experimental.pallas import tpu as pltpu
from jax.sharding import PartitionSpec as P

stencil_weights = (
    -5369.0 / 1800.0,
    12.0 / 7.0,
    -15.0 / 56.0,
    10.0 / 189.0,
    -1.0 / 112.0,
    2.0 / 1925.0,
    -1.0 / 16632.0,
)
filter_center = 6.5
filter_half = 6.0
offsets_x = (0, -1, 1, 0, 0)
offsets_y = (0, 0, 0, -1, 1)
reach = 6
plane = ("sx", "sy")
every = ("band", "sx", "sy")

orbital_gain = 2.0**12
projector_gain = 2.0**17
potential_gain = 2.0**13
remainder_gain = 2.0**10
top = 15
middle = 8
levels = 17

vmem = pl.BlockSpec(memory_space=pltpu.VMEM)
smem = pl.BlockSpec(memory_space=pltpu.SMEM)
params = pltpu.CompilerParams(vmem_limit_bytes=24 * 1024 * 1024)


def level_of(largest):
    level = jnp.float32(0.0)
    scale = jnp.float32(2.0 ** (top + 8 * middle))
    for j in range(levels):
        above = largest >= jnp.float32(2.0 ** (8 * (j - middle)))
        level = jnp.where(above, jnp.float32(j + 1), level)
        scale = jnp.where(above, jnp.float32(2.0 ** (top - 8 * (j + 1 - middle))), scale)
    return level, scale


def shrink_of(level):
    return jnp.exp2(8.0 * (level - middle) - top)


def pack_kernel(each, energies_ref, centers_ref, orbitals_ref, projectors_ref, potential_ref, out_ref):
    group, rows, nz = out_ref.shape
    slab_cells = orbitals_ref.shape[0]
    atoms, tiles, projs = projectors_ref.shape[:3]
    base = slab_cells * each

    def take(g, carry):
        for cell in range(slab_cells):
            out_ref[g, pl.ds(cell * each, each), :] = (
                orbitals_ref[cell, pl.ds(pl.multiple_of(g * each, each), each), :] * orbital_gain
            )
        return carry

    lax.fori_loop(0, group, take, 0)

    row = base
    for a in range(atoms):
        for t in range(tiles):
            out_ref[0, pl.ds(row, projs), :] = projectors_ref[a, t] * projector_gain
            row += projs
    for i in range(potential_ref.shape[0]):
        count = potential_ref.shape[1]
        out_ref[0, pl.ds(row, count), :] = potential_ref[i] * potential_gain
        row += count
    lane = lax.broadcasted_iota(jnp.int32, (1, nz), 1)
    numbers = jnp.zeros((1, nz), jnp.float32)
    for a in range(atoms):
        for p in range(projs):
            numbers = jnp.where(lane == a * projs + p, energies_ref[a, p], numbers)
    high = numbers.astype(jnp.bfloat16).astype(jnp.float32)
    low = (numbers - high) * remainder_gain
    count = atoms * projs
    numbers = high + pltpu.roll(low, count, 1)
    for a in range(atoms):
        for d in range(2):
            here = centers_ref[a, d].astype(jnp.float32)
            numbers = jnp.where(lane == 2 * count + 2 * a + d, here, numbers)
    out_ref[0, pl.ds(row, 1), :] = numbers
    out_ref[0, pl.ds(row + 1, rows - row - 1), :] = jnp.zeros((rows - row - 1, nz), jnp.float32)

    def repeat(g, carry):
        out_ref[g, pl.ds(base, rows - base), :] = out_ref[0, pl.ds(base, rows - base), :]
        return carry

    lax.fori_loop(1, group, repeat, 0)


def filter_kernel(
    slabs_y,
    cells_x,
    cells_y,
    each,
    atoms,
    projs,
    got_ref,
    field_ref,
    rounded_ref,
    scale_ref,
    first,
    second,
    partial,
    diagonal,
    numbers,
    arrived,
):
    group, _, nz = got_ref.shape
    count_x, count_y = diagonal.shape[0], diagonal.shape[1]
    tiles = len(offsets_x)
    slab_cells = cells_x * cells_y
    proj_row = slab_cells * each
    pot_row = proj_row + atoms * projs * tiles
    number_row = pot_row + slab_cells
    scale = 1.0 / filter_half
    factors = [-0.5 * scale * w for w in stencil_weights]
    ring = 1

    copy = pltpu.make_async_copy(got_ref.at[:, number_row, :], numbers, arrived)
    copy.start()

    for field in (first, second):
        for x in (0, ring + count_x):
            field[x] = jnp.zeros(field.shape[1:], jnp.float32)
        for y in (0, ring + count_y):
            field[:, y] = jnp.zeros((field.shape[0],) + field.shape[2:], jnp.float32)

    def take_slab(g, carry):
        x0 = (g // slabs_y) * cells_x
        y0 = (g % slabs_y) * cells_y
        for i in range(cells_x):
            for j in range(cells_y):
                cell = i * cells_y + j
                first[ring + x0 + i, ring + y0 + j] = got_ref[g, pl.ds(cell * each, each), :] * (
                    1.0 / orbital_gain
                )
                diagonal[x0 + i, y0 + j] = got_ref[g, pl.ds(pot_row + cell, 1), :] * (
                    scale / potential_gain
                ) + (3.0 * factors[0] - filter_center * scale)
        return carry

    lax.fori_loop(0, group, take_slab, 0)

    distance = jnp.abs(
        lax.broadcasted_iota(jnp.int32, (nz, nz), 0) - lax.broadcasted_iota(jnp.int32, (nz, nz), 1)
    )
    along_z = jnp.zeros((nz, nz), jnp.float32)
    for step in range(1, reach + 1):
        along_z = jnp.where(distance == step, factors[step], along_z)
    z_high = along_z.astype(jnp.bfloat16)
    z_low = (along_z - z_high.astype(jnp.float32)).astype(jnp.bfloat16)
    z_matrix = jnp.concatenate(
        [
            jnp.concatenate([z_high, z_low], axis=1),
            jnp.concatenate([z_high, jnp.zeros_like(z_high)], axis=1),
        ],
        axis=0,
    )

    def along(cells, at):
        total = None
        for step in range(1, reach + 1):
            near = [cells[n] for n in (at - step, at + step) if 0 <= n < len(cells)]
            if near:
                term = factors[step] * sum(near[1:], near[0])
                total = term if total is None else total + term
        return total

    def apply(source, target, finish, gain):
        def z_part(block, carry):
            rows = source[pl.ds(ring + block * cells_x, cells_x), pl.ds(ring, count_y)]
            flat = rows.reshape(cells_x * count_y * each, nz)
            high = flat.astype(jnp.bfloat16)
            low = (flat - high.astype(jnp.float32)).astype(jnp.bfloat16)
            both = jnp.dot(
                jnp.concatenate([high, low], axis=1), z_matrix, preferred_element_type=jnp.float32
            )
            partial[pl.ds(block * cells_x, cells_x)] = (both[:, :nz] + both[:, nz:]).reshape(
                rows.shape
            )
            return carry

        lax.fori_loop(0, count_x // cells_x, z_part, 0)

        def x_part(y, carry):
            cells = [source[ring + x, ring + y] for x in range(count_x)]
            for x in range(count_x):
                partial[x, y] = partial[x, y] + diagonal[x, y] * cells[x] + along(cells, x)
            return carry

        lax.fori_loop(0, count_y, x_part, 0)

        def y_part(x, carry):
            cells = [source[ring + x, ring + y] for y in range(count_y)]
            for y in range(count_y):
                total = partial[x, y] + along(cells, y)
                target[ring + x, ring + y] = finish(total, target, ring + x, ring + y)
            return carry

        lax.fori_loop(0, count_x, y_part, 0)

        def atoms_part(g, carry):
            places = []
            sums = []
            for a in range(atoms):
                at_x = ring + numbers[g, 2 * atoms * projs + 2 * a].astype(jnp.int32)
                at_y = ring + numbers[g, 2 * atoms * projs + 2 * a + 1].astype(jnp.int32)
                places.append((at_x, at_y))
                totals = [None] * projs
                for t in range(tiles):
                    tile = source[at_x + offsets_x[t], at_y + offsets_y[t]]
                    for p in range(projs):
                        row = proj_row + (a * tiles + t) * projs + p
                        term = tile * got_ref[g, pl.ds(row, 1), :]
                        totals[p] = term if t == 0 else totals[p] + term
                sums.append(totals)
            for a in range(atoms):
                at_x, at_y = places[a]
                coeffs = []
                for p in range(projs):
                    k = a * projs + p
                    energy = numbers[g, k] + numbers[g, atoms * projs + k] * (1.0 / remainder_gain)
                    coeffs.append(
                        jnp.sum(sums[a][p], axis=-1, keepdims=True)
                        * (energy * (gain / projector_gain / projector_gain))
                    )
                for t in range(tiles):
                    row = proj_row + (a * tiles + t) * projs
                    spread = coeffs[0] * got_ref[g, pl.ds(row, 1), :]
                    for p in range(1, projs):
                        spread = spread + coeffs[p] * got_ref[g, pl.ds(row + p, 1), :]
                    to_x = at_x + offsets_x[t]
                    to_y = at_y + offsets_y[t]
                    target[to_x, to_y] = target[to_x, to_y] + spread
            return carry

        lax.fori_loop(0, group, atoms_part, 0)

    copy.wait()
    apply(first, second, lambda total, target, x, y: total, scale)

    for x in (0, ring + count_x):
        second[x] = jnp.zeros(second.shape[1:], jnp.float32)
    for y in (0, ring + count_y):
        second[:, y] = jnp.zeros((second.shape[0],) + second.shape[2:], jnp.float32)

    apply(second, first, lambda total, target, x, y: 2.0 * total - target[x, y], 2.0 * scale)

    shares = rounded_ref.shape[0] // group
    portion = slab_cells // shares

    def give_slab(g, largest):
        x0 = (g // slabs_y) * cells_x
        y0 = (g % slabs_y) * cells_y
        for i in range(cells_x):
            for j in range(cells_y):
                cell = i * cells_y + j
                value = first[ring + x0 + i, ring + y0 + j]
                field_ref[g, pl.ds(cell * each, each), :] = value
                rounded_ref[
                    (cell // portion) * group + g, :, pl.ds((cell % portion) * nz, nz)
                ] = value.astype(jnp.bfloat16)
                largest = jnp.maximum(largest, jnp.abs(value))
        return largest

    largest = lax.fori_loop(0, group, give_slab, jnp.zeros((each, nz), jnp.float32))
    level, gain = level_of(jnp.max(largest))
    scale_ref[0:1] = jnp.full((1, nz), gain, jnp.float32)
    scale_ref[1:2] = jnp.full((1, nz), level, jnp.float32)


def rows_kernel(cells, parts_ref, scale_ref, out_ref):
    _, each, columns = parts_ref.shape
    nz = out_ref.shape[1]
    total = jnp.sum(parts_ref[...], axis=0) / cells
    level, gain = level_of(jnp.max(jnp.abs(total)))
    total = total * gain
    high = total.astype(jnp.bfloat16).astype(jnp.float32)
    low = total - high
    row = 0
    for part in (high, low):
        for column in range(0, columns, nz):
            out_ref[pl.ds(row, each), :] = part[:, column : column + nz]
            row += each
    rest = out_ref.shape[0] - row
    out_ref[pl.ds(row, rest), :] = jnp.zeros((rest, nz), jnp.float32)
    out_ref[pl.ds(row, 1), :] = scale_ref[1:2]
    out_ref[pl.ds(row + 1, 1), :] = jnp.full((1, nz), level, jnp.float32)


def local(orbitals, potential, projectors, energies, centers):
    band_orbitals, cells_x, cells_y, nz = orbitals.shape
    bands = lax.axis_size("band")
    slabs_x = lax.axis_size("sx")
    slabs_y = lax.axis_size("sy")
    group = slabs_x * slabs_y
    each = band_orbitals // group
    total_orbitals = bands * band_orbitals
    slab_cells = cells_x * cells_y
    grid = (slabs_x * cells_x, slabs_y * cells_y)
    atoms, projs, tiles, _ = projectors.shape

    rows = slab_cells * each + atoms * projs * tiles + slab_cells + 1
    rows += -rows % 16
    sent = pl.pallas_call(
        functools.partial(pack_kernel, each),
        in_specs=[smem, smem, vmem, vmem, vmem],
        out_specs=vmem,
        out_shape=jax.ShapeDtypeStruct((group, rows, nz), jnp.float32),
        compiler_params=params,
    )(
        energies,
        centers,
        orbitals.transpose(1, 2, 0, 3).reshape(slab_cells, band_orbitals, nz),
        projectors.transpose(0, 2, 1, 3),
        potential,
    )
    got = lax.all_to_all(sent.astype(jnp.float16), plane, 0, 0).astype(jnp.float32)

    portion = slab_cells // bands
    ringed = (grid[0] + 2, grid[1] + 2, each, nz)
    field, rounded, scale = pl.pallas_call(
        functools.partial(filter_kernel, slabs_y, cells_x, cells_y, each, atoms, projs),
        in_specs=[vmem],
        out_specs=[vmem] * 3,
        out_shape=[
            jax.ShapeDtypeStruct((group, slab_cells * each, nz), jnp.float32),
            jax.ShapeDtypeStruct((bands * group, each, portion * nz), jnp.bfloat16),
            jax.ShapeDtypeStruct((2, nz), jnp.float32),
        ],
        scratch_shapes=[
            pltpu.VMEM(ringed, jnp.float32),
            pltpu.VMEM(ringed, jnp.float32),
            pltpu.VMEM(grid + (each, nz), jnp.float32),
            pltpu.VMEM(grid + (1, nz), jnp.float32),
            pltpu.SMEM((group, nz), jnp.float32),
            pltpu.SemaphoreType.DMA,
        ],
        compiler_params=params,
        cost_estimate=pl.CostEstimate(
            flops=2 * 2 * 40 * grid[0] * grid[1] * each * nz,
            bytes_accessed=8 * grid[0] * grid[1] * each * nz,
            transcendentals=0,
        ),
    )(got)

    pieces = lax.all_to_all(rounded, every, 0, 0)
    matrix = pieces.reshape(total_orbitals, portion * nz)
    sums = lax.dot_general(
        matrix, matrix, (((1,), (1,)), ((), ())), preferred_element_type=jnp.float32
    )
    parts = lax.all_to_all(sums.reshape(bands * group, each, total_orbitals), every, 0, 0)

    halves = total_orbitals // nz
    gram_rows = 2 * halves * each
    block = pl.pallas_call(
        functools.partial(rows_kernel, grid[0] * grid[1] * nz),
        in_specs=[vmem, vmem],
        out_specs=vmem,
        out_shape=jax.ShapeDtypeStruct((gram_rows + 8, nz), jnp.float32),
        compiler_params=params,
    )(parts, scale)
    sent = jnp.concatenate(
        [field * scale[0, 0], jnp.broadcast_to(block[None], (group,) + block.shape)], axis=1
    ).astype(jnp.float16)
    back = lax.all_to_all(sent, plane, 0, 0)

    start = slab_cells * each
    shrink = shrink_of(back[:, start + gram_rows : start + gram_rows + 2, :1].astype(jnp.float32))
    filtered = back[:, :start].reshape(group, slab_cells, each, nz).astype(jnp.float32)
    filtered = (filtered * shrink[:, :1, :, None]).transpose(1, 0, 2, 3)
    filtered = filtered.reshape(cells_x, cells_y, band_orbitals, nz).transpose(2, 0, 1, 3)
    gram = back[:, start : start + gram_rows].reshape(group, 2, halves, each, nz).astype(jnp.float32)
    gram = (gram[:, 0] + gram[:, 1]) * shrink[:, 1][:, None, None]
    gram = gram.transpose(0, 2, 1, 3).reshape(band_orbitals, total_orbitals)
    return (filtered, gram)


def solution(mesh):
    in_specs = (
        P("band", "sx", "sy", None),
        P("sx", "sy", None),
        P(("sx", "sy"), None, None, None),
        P(("sx", "sy"), None),
        P(("sx", "sy"), None),
    )
    out_specs = (P("band", "sx", "sy", None), P("band", None))
    return jax.shard_map(local, mesh=mesh, in_specs=in_specs, out_specs=out_specs, check_vma=False)
```

time: 109 us -> 83.9 us (0.77)
  blocking collectives: 61.5 us -> 51.4 us
  waiting for transfers between devices: 19.3 us -> 9.41 us
  starting transfers between devices: 6.92 us -> 3.62 us
  Pallas kernels: 10.7 us -> 9.06 us
    all_to_all x2 -> x1, waiting for transfers between devices: 19.3 us -> 9.41 us  [local(): lax.all_to_all(sums.reshape(bands * group, each, total_orbitals), every,...]
    all_to_all x2, blocking collectives: 40.7 us -> 31 us  [the longest x1 18 us: local(): lax.all_to_all(sent.astype(jnp.float16), plane, 0, 0).astype(jnp.float32)]
    all_to_all x2 -> x1, starting transfers between devices: 6.92 us -> 3.62 us  [local(): lax.all_to_all(sums.reshape(bands * group, each, total_orbitals), every,...]
    reshape x4 -> x0, local copies, waits for them, and re-layouts: 2.86 us -> none  [the longest x1 1.35 us: local(): chunks = orbitals.transpose(1, 2, 0, 3).reshape(slab_cells, group, each, nz)]
    pallas_call x1, Pallas kernels: 10.7 us -> 7.95 us  [local(): pl.pallas_call(functools.partial(filter_kernel, slabs_y, cells_x, cells_y...]
    unnamed x6 -> x9, local copies, waits for them, and re-layouts: 1.84 us -> 4.23 us
    convert_element_type x2 -> x3, other arithmetic: 1.45 us -> 0.24 us  [the longest x1 0.11 us: local(): sent.astype(jnp.float16)]
    pallas_call x0 -> x2, Pallas kernels: none -> 1.11 us  [the longest x1 0.93 us: local(): pl.pallas_call(functools.partial(pack_kernel, each), in_specs=[smem, smem...]
  transfers between devices with their start and end apart: 2 -> 1, of which waited for: 2 -> 1; matrix products, arithmetic and copies ran while one was open for 1% -> 2% of each run, Pallas kernels for 0% -> 0%
where the time goes in v2:
time: 83.9 us; the launch traced here: 83.5 us
  blocking collectives  51.4 us (61%)
  waiting for transfers between devices  9.41 us (11%)
  Pallas kernels  9.06 us (11%)
  local copies, waits for them, and re-layouts  6.09 us (7%)
  starting transfers between devices  3.62 us (4%)
  other arithmetic  2.06 us (2%)
  matrix products  1.08 us (1%)
    all_to_all x1, blocking collectives, local(): pieces = lax.all_to_all(rounded, every, 0, 0)  20.4 us
    all_to_all x1, blocking collectives, local(): lax.all_to_all(sent.astype(jnp.float16), plane, 0, 0).astype(jnp.float32)  18 us
    all_to_all x1, blocking collectives, local(): back = lax.all_to_all(sent, plane, 0, 0)  13 us
    all_to_all x1, waiting for transfers between devices, local(): lax.all_to_all(sums.reshape(bands * group, each, total_orbitals), every,...  9.41 us
    pallas_call x1, Pallas kernels, local(): pl.pallas_call(functools.partial(filter_kernel, slabs_y, cells_x, cells_y...  7.95 us
    unnamed x9, local copies, waits for them, and re-layouts  4.23 us
    all_to_all x1, starting transfers between devices, local(): lax.all_to_all(sums.reshape(bands * group, each, total_orbitals), every,...  3.62 us
  transfers between devices with their start and end apart: 1, of which 1 were waited for; matrix products, arithmetic and copies ran while one was open for 2% of the time, Pallas kernels for 0%

profile of v2, /device:TPU:0, one launch (start us, length us, event | category | flops | bytes accessed | tf_op | source)
XLA Modules:
  0.0 83.5 jit_solution(11992603018031335952)
XLA Ops:
  0.6 0.8 copy.11.centers_ref
  1.4 0.0 copy-start
  1.4 1.3 %copy-done = f32[64,6,6,128]{3,0,2,1:T(8,128)S(1)} copy-done((f32[64,6,6,128]{3,0,2,1:T(8,128)S(1)}, f32[64,6,6,128]{3,0,2,1:T(8,128)}, u32[]{:S(2)}) %copy-start) | copy-done | bytes 1179672
  2.7 0.0 copy-start.1
  2.7 0.8 copy-done.1
  3.4 0.0 copy-start.2
  3.4 0.7 copy-done.2
  4.2 0.0 copy-start.3
  4.2 0.7 copy-done.3
  4.9 0.9 %shard_map.68 = f32[8,416,128]{2,1,0:T(8,128)S(1)} custom-call(f32[4,4]{1,0:T(4,128)S(1)} %copy-done.3, s32[4,2]{1,0:T(4,128)S(1)} %copy.11.centers_ref, f32[36,64,128]{2,1,0:T(8,128)S(1)} %bitcast.33, f32[4,5,4,128]{3,2,1,0:T(4,128)S(1)} %bitcast.34, f32[6,6,128]{2,1,0:T(8,128)S(1)} %copy-done.2), custom_call_target="tpu_custom_call" | custom-call | tf_op jit(solution)/shard_map/pallas_call | solution.py:316
  5.8 0.1 convert_element_type.22
  5.9 18.0 %all_to_all.20 = f16[8,416,128]{2,1,0:T(8,128)(2,1)S(1)} all-to-all(f16[8,416,128]{2,1,0:T(8,128)(2,1)S(1)} %convert_element_type.22), channel_id=1, replica_groups=mesh['band'=4,'sx'=4,'sy'=2] {'sx','sy'}, dimensions={0} | all-to-all | bytes 1703936 | tf_op jit(solution)/shard_map/all_to_all | solution.py:329
  23.9 0.1 convert_element_type.23.got_ref
  24.0 8.0 %shard_map.69 = (f32[8,288,128]{2,1,0:T(8,128)S(1)}, bf16[32,8,1152]{2,1,0:T(8,128)(2,1)S(1)}, f32[2,128]{1,0:T(2,128)S(1)}) custom-call(f32[8,416,128]{2,1,0:T(8,128)S(1)} %convert_element_type.23.got_ref), custom_call_target="tpu_custom_call" | custom-call | flops 47185920 | bytes 2359296 | tf_op jit(solution)/shard_map/pallas_call | solution.py:333
  32.0 20.4 %all_to_all.21 = bf16[32,8,1152]{2,1,0:T(8,128)(2,1)S(1)} all-to-all(bf16[32,8,1152]{2,1,0:T(8,128)(2,1)S(1)} %get-tuple-element.7), channel_id=1, replica_groups=mesh['band'=4,'sx'=4,'sy'=2] {'band','sx','sy'}, dimensions={0} | all-to-all | bytes 1179648 | tf_op jit(solution)/shard_map/all_to_all | solution.py:358
  52.4 1.1 %fusion.1 = f32[32,8,256]{2,1,0:T(8,128)} fusion(bf16[32,8,1152]{2,1,0:T(8,128)(2,1)S(1)} %all_to_all.21), kind=kOutput, calls=%fused_computation.3 | convolution fusion | flops 150994944 | bytes 851968 | tf_op jit(solution)/shard_map/dot_general | solution.py:360
  53.5 3.6 %all-to-all-start.2 = ((f32[32,8,256]{2,1,0:T(8,128)}), f32[32,8,256]{2,1,0:T(8,128)S(1)}, u32[]{:S(2)}, u32[]{:S(2)}) async-start(f32[32,8,256]{2,1,0:T(8,128)} %fusion.1), calls=%async_computation.2 | async-start | bytes 524288 | tf_op jit(solution)/shard_map/all_to_all | solution.py:363
  57.1 0.5 slice.24
  57.6 0.8 multiply_convert_fusion
  58.4 9.4 %all-to-all-done.2.parts_ref = f32[32,8,256]{2,1,0:T(8,128)S(1)} async-done(((f32[32,8,256]{2,1,0:T(8,128)}), f32[32,8,256]{2,1,0:T(8,128)S(1)}, u32[]{:S(2)}, u32[]{:S(2)}) %all-to-all-start.2) | async-done | bytes 262176 | tf_op jit(solution)/shard_map/all_to_all | solution.py:363
  67.8 0.2 shard_map.70
  68.0 0.2 pad_maximum_fusion
  68.2 13.0 %all_to_all.22 = f16[8,328,128]{2,1,0:T(8,128)(2,1)S(1)} all-to-all(f16[8,328,128]{2,1,0:T(8,128)(2,1)S(1)} %pad_maximum_fusion), channel_id=1, replica_groups=mesh['band'=4,'sx'=4,'sy'=2] {'sx','sy'}, dimensions={0} | all-to-all | bytes 1343488 | tf_op jit(solution)/shard_map/all_to_all | solution.py:377
  81.2 0.1 slice_reduce_fusion
  81.4 0.2 fusion
  81.6 1.2 %copy.12 = f32[36,8,8,128]{3,2,1,0:T(8,128)} copy(f32[36,8,8,128]{3,2,0,1:T(8,128)S(1)} %fusion) | data formatting | bytes 2359296 | tf_op jit(solution)/shard_map/transpose | solution.py:382
  82.7 0.7 fusion.5
  (5 shorter events, 0.1 us)
Async XLA Ops:
  1.4 1.3 %copy-start = (f32[64,6,6,128]{3,0,2,1:T(8,128)S(1)}, f32[64,6,6,128]{3,0,2,1:T(8,128)}, u32[]{:S(2)}) copy-start(f32[64,6,6,128]{3,0,2,1:T(8,128)} %param.5) | copy-start | bytes 3538948
  2.7 0.8 copy-start.1
  3.4 0.7 copy-start.2
  4.2 0.7 copy-start.3
  53.5 14.3 %all-to-all-start.2 = ((f32[32,8,256]{2,1,0:T(8,128)}), f32[32,8,256]{2,1,0:T(8,128)S(1)}, u32[]{:S(2)}, u32[]{:S(2)}) async-start(f32[32,8,256]{2,1,0:T(8,128)} %fusion.1), calls=%async_computation.2 | async-start | bytes 524288 | tf_op jit(solution)/shard_map/all_to_all | solution.py:363

commit v3 on v2

--- a/solution.py
+++ b/solution.py
@@ -34,6 +34,7 @@
 
 vmem = pl.BlockSpec(memory_space=pltpu.VMEM)
 smem = pl.BlockSpec(memory_space=pltpu.SMEM)
+hbm = pl.BlockSpec(memory_space=pl.ANY)
 params = pltpu.CompilerParams(vmem_limit_bytes=24 * 1024 * 1024)
 
 
@@ -48,32 +49,37 @@
 
 
 def shrink_of(level):
-    return jnp.exp2(8.0 * (level - middle) - top)
-
-
-def pack_kernel(each, energies_ref, centers_ref, orbitals_ref, projectors_ref, potential_ref, out_ref):
-    group, rows, nz = out_ref.shape
-    slab_cells = orbitals_ref.shape[0]
+    shrink = jnp.full(level.shape, 2.0 ** (-top - 8 * middle), jnp.float32)
+    for j in range(levels):
+        shrink = jnp.where(level > j, jnp.float32(2.0 ** (8 * (j + 1 - middle) - top)), shrink)
+    return shrink
+
+
+def over_group(group, each, body):
+    if each % 8 == 0:
+
+        def step(g, carry):
+            body(g, pl.ds(pl.multiple_of(g * each, each), each))
+            return carry
+
+        lax.fori_loop(0, group, step, 0, unroll=min(group, 8))
+    else:
+        for g in range(group):
+            body(g, pl.ds(g * each, each))
+
+
+def share_kernel(_, energies_ref, centers_ref, projectors_ref, potential_ref, out_ref):
+    rows, nz = out_ref.shape
     atoms, tiles, projs = projectors_ref.shape[:3]
-    base = slab_cells * each
-
-    def take(g, carry):
-        for cell in range(slab_cells):
-            out_ref[g, pl.ds(cell * each, each), :] = (
-                orbitals_ref[cell, pl.ds(pl.multiple_of(g * each, each), each), :] * orbital_gain
-            )
-        return carry
-
-    lax.fori_loop(0, group, take, 0)
-
-    row = base
+
+    row = 0
     for a in range(atoms):
         for t in range(tiles):
-            out_ref[0, pl.ds(row, projs), :] = projectors_ref[a, t] * projector_gain
+            out_ref[pl.ds(row, projs), :] = projectors_ref[a, t] * projector_gain
             row += projs
     for i in range(potential_ref.shape[0]):
         count = potential_ref.shape[1]
-        out_ref[0, pl.ds(row, count), :] = potential_ref[i] * potential_gain
+        out_ref[pl.ds(row, count), :] = potential_ref[i] * potential_gain
         row += count
     lane = lax.broadcasted_iota(jnp.int32, (1, nz), 1)
     numbers = jnp.zeros((1, nz), jnp.float32)
@@ -86,16 +92,10 @@
     numbers = high + pltpu.roll(low, count, 1)
     for a in range(atoms):
         for d in range(2):
-            here = centers_ref[a, d].astype(jnp.float32)
+            here = centers_ref[d, a].astype(jnp.float32)
             numbers = jnp.where(lane == 2 * count + 2 * a + d, here, numbers)
-    out_ref[0, pl.ds(row, 1), :] = numbers
-    out_ref[0, pl.ds(row + 1, rows - row - 1), :] = jnp.zeros((rows - row - 1, nz), jnp.float32)
-
-    def repeat(g, carry):
-        out_ref[g, pl.ds(base, rows - base), :] = out_ref[0, pl.ds(base, rows - base), :]
-        return carry
-
-    lax.fori_loop(1, group, repeat, 0)
+    out_ref[pl.ds(row, 1), :] = numbers
+    out_ref[pl.ds(row + 1, rows - row - 1), :] = jnp.zeros((rows - row - 1, nz), jnp.float32)
 
 
 def filter_kernel(
@@ -108,11 +108,12 @@
     got_ref,
     field_ref,
     rounded_ref,
-    scale_ref,
+    level_ref,
     first,
     second,
     partial,
     diagonal,
+    coeffs,
     numbers,
     arrived,
 ):
@@ -210,13 +211,16 @@
 
         lax.fori_loop(0, count_x, y_part, 0)
 
-        def atoms_part(g, carry):
-            places = []
-            sums = []
+        def place_of(g, a):
+            at = 2 * atoms * projs + 2 * a
+            return (
+                ring + numbers[g, at].astype(jnp.int32),
+                ring + numbers[g, at + 1].astype(jnp.int32),
+            )
+
+        def gather_part(g, carry):
             for a in range(atoms):
-                at_x = ring + numbers[g, 2 * atoms * projs + 2 * a].astype(jnp.int32)
-                at_y = ring + numbers[g, 2 * atoms * projs + 2 * a + 1].astype(jnp.int32)
-                places.append((at_x, at_y))
+                at_x, at_y = place_of(g, a)
                 totals = [None] * projs
                 for t in range(tiles):
                     tile = source[at_x + offsets_x[t], at_y + offsets_y[t]]
@@ -224,28 +228,33 @@
                         row = proj_row + (a * tiles + t) * projs + p
                         term = tile * got_ref[g, pl.ds(row, 1), :]
                         totals[p] = term if t == 0 else totals[p] + term
-                sums.append(totals)
-            for a in range(atoms):
-                at_x, at_y = places[a]
-                coeffs = []
                 for p in range(projs):
                     k = a * projs + p
                     energy = numbers[g, k] + numbers[g, atoms * projs + k] * (1.0 / remainder_gain)
-                    coeffs.append(
-                        jnp.sum(sums[a][p], axis=-1, keepdims=True)
-                        * (energy * (gain / projector_gain / projector_gain))
+                    coeffs[g, k] = jnp.broadcast_to(
+                        jnp.sum(totals[p], axis=-1, keepdims=True)
+                        * (energy * (gain / projector_gain / projector_gain)),
+                        (each, nz),
                     )
+            return carry
+
+        lax.fori_loop(0, group, gather_part, 0, unroll=min(group, 4))
+
+        def scatter_part(g, carry):
+            for a in range(atoms):
+                at_x, at_y = place_of(g, a)
+                factor = [coeffs[g, a * projs + p] for p in range(projs)]
                 for t in range(tiles):
                     row = proj_row + (a * tiles + t) * projs
-                    spread = coeffs[0] * got_ref[g, pl.ds(row, 1), :]
+                    spread = factor[0] * got_ref[g, pl.ds(row, 1), :]
                     for p in range(1, projs):
-                        spread = spread + coeffs[p] * got_ref[g, pl.ds(row + p, 1), :]
+                        spread = spread + factor[p] * got_ref[g, pl.ds(row + p, 1), :]
                     to_x = at_x + offsets_x[t]
                     to_y = at_y + offsets_y[t]
                     target[to_x, to_y] = target[to_x, to_y] + spread
             return carry
 
-        lax.fori_loop(0, group, atoms_part, 0)
+        lax.fori_loop(0, group, scatter_part, 0, unroll=min(group, 2))
 
     copy.wait()
     apply(first, second, lambda total, target, x, y: total, scale)
@@ -260,27 +269,31 @@
     shares = rounded_ref.shape[0] // group
     portion = slab_cells // shares
 
-    def give_slab(g, largest):
+    def largest_of(x, largest):
+        row = jnp.abs(first[ring + x, pl.ds(ring, count_y)])
+        return jnp.maximum(largest, jnp.max(row, axis=0))
+
+    largest = lax.fori_loop(0, count_x, largest_of, jnp.zeros((each, nz), jnp.float32))
+    level, gain = level_of(jnp.max(largest))
+    level_ref[...] = jnp.full((1, nz), level, jnp.float32)
+
+    def give_slab(g, carry):
         x0 = (g // slabs_y) * cells_x
         y0 = (g % slabs_y) * cells_y
         for i in range(cells_x):
             for j in range(cells_y):
                 cell = i * cells_y + j
                 value = first[ring + x0 + i, ring + y0 + j]
-                field_ref[g, pl.ds(cell * each, each), :] = value
+                field_ref[g, pl.ds(cell * each, each), :] = value * gain
                 rounded_ref[
                     (cell // portion) * group + g, :, pl.ds((cell % portion) * nz, nz)
                 ] = value.astype(jnp.bfloat16)
-                largest = jnp.maximum(largest, jnp.abs(value))
-        return largest
-
-    largest = lax.fori_loop(0, group, give_slab, jnp.zeros((each, nz), jnp.float32))
-    level, gain = level_of(jnp.max(largest))
-    scale_ref[0:1] = jnp.full((1, nz), gain, jnp.float32)
-    scale_ref[1:2] = jnp.full((1, nz), level, jnp.float32)
-
-
-def rows_kernel(cells, parts_ref, scale_ref, out_ref):
+        return carry
+
+    lax.fori_loop(0, group, give_slab, 0)
+
+
+def rows_kernel(cells, parts_ref, level_ref, out_ref):
     _, each, columns = parts_ref.shape
     nz = out_ref.shape[1]
     total = jnp.sum(parts_ref[...], axis=0) / cells
@@ -295,8 +308,45 @@
             row += each
     rest = out_ref.shape[0] - row
     out_ref[pl.ds(row, rest), :] = jnp.zeros((rest, nz), jnp.float32)
-    out_ref[pl.ds(row, 1), :] = scale_ref[1:2]
+    out_ref[pl.ds(row, 1), :] = level_ref[...]
     out_ref[pl.ds(row + 1, 1), :] = jnp.full((1, nz), level, jnp.float32)
+
+
+def unpack_kernel(each, back_ref, filtered_hbm, gram_hbm, filtered_ref, gram_ref, chunk_sems, sem):
+    group, _, nz = back_ref.shape
+    slab_cells = filtered_ref.shape[0]
+    halves = gram_ref.shape[1] // nz
+    chunks = chunk_sems.shape[0]
+    chunk = slab_cells // chunks
+    base = slab_cells * each
+    number_row = base + 2 * halves * each
+
+    def put_rows(g, rows):
+        shrink = shrink_of(back_ref[g, pl.ds(number_row + 1, 1), :])
+        for half in range(halves):
+            row = base + half * each
+            value = back_ref[g, pl.ds(row, each), :] + back_ref[g, pl.ds(row + halves * each, each), :]
+            gram_ref[rows, half * nz : (half + 1) * nz] = value * shrink
+
+    over_group(group, each, put_rows)
+    copies = [pltpu.make_async_copy(gram_ref, gram_hbm, sem)]
+    copies[0].start()
+
+    for c in range(chunks):
+
+        def put_cells(g, rows):
+            shrink = shrink_of(back_ref[g, pl.ds(number_row, 1), :])
+            for cell in range(c * chunk, (c + 1) * chunk):
+                filtered_ref[cell, rows, :] = back_ref[g, pl.ds(cell * each, each), :] * shrink
+
+        over_group(group, each, put_cells)
+        part = pl.ds(c * chunk, chunk)
+        copies.append(
+            pltpu.make_async_copy(filtered_ref.at[part], filtered_hbm.at[part], chunk_sems.at[c])
+        )
+        copies[-1].start()
+    for copy in copies:
+        copy.wait()
 
 
 def local(orbitals, potential, projectors, energies, centers):
@@ -311,39 +361,38 @@
     grid = (slabs_x * cells_x, slabs_y * cells_y)
     atoms, projs, tiles, _ = projectors.shape
 
-    rows = slab_cells * each + atoms * projs * tiles + slab_cells + 1
-    rows += -rows % 16
-    sent = pl.pallas_call(
-        functools.partial(pack_kernel, each),
-        in_specs=[smem, smem, vmem, vmem, vmem],
+    rows = atoms * projs * tiles + slab_cells + 1
+    rows += -rows % 8
+    chunks = (orbitals * orbital_gain).astype(jnp.float16)
+    chunks = chunks.transpose(1, 2, 0, 3).reshape(slab_cells, group, each, nz)
+    chunks = chunks.transpose(1, 0, 2, 3).reshape(group, slab_cells * each, nz)
+    shared = pl.pallas_call(
+        share_kernel,
+        in_specs=[hbm, smem, smem, vmem, vmem],
         out_specs=vmem,
-        out_shape=jax.ShapeDtypeStruct((group, rows, nz), jnp.float32),
+        out_shape=jax.ShapeDtypeStruct((rows, nz), jnp.float32),
         compiler_params=params,
-    )(
-        energies,
-        centers,
-        orbitals.transpose(1, 2, 0, 3).reshape(slab_cells, band_orbitals, nz),
-        projectors.transpose(0, 2, 1, 3),
-        potential,
-    )
-    got = lax.all_to_all(sent.astype(jnp.float16), plane, 0, 0).astype(jnp.float32)
+    )(chunks[0, :8].astype(jnp.float32), energies, centers.T, projectors.transpose(0, 2, 1, 3), potential).astype(jnp.float16)
+    sent = jnp.concatenate([chunks, jnp.broadcast_to(shared[None], (group, rows, nz))], axis=1)
+    got = lax.all_to_all(sent, plane, 0, 0).astype(jnp.float32)
 
     portion = slab_cells // bands
     ringed = (grid[0] + 2, grid[1] + 2, each, nz)
-    field, rounded, scale = pl.pallas_call(
+    field, rounded, level = pl.pallas_call(
         functools.partial(filter_kernel, slabs_y, cells_x, cells_y, each, atoms, projs),
         in_specs=[vmem],
         out_specs=[vmem] * 3,
         out_shape=[
             jax.ShapeDtypeStruct((group, slab_cells * each, nz), jnp.float32),
             jax.ShapeDtypeStruct((bands * group, each, portion * nz), jnp.bfloat16),
-            jax.ShapeDtypeStruct((2, nz), jnp.float32),
+            jax.ShapeDtypeStruct((1, nz), jnp.float32),
         ],
         scratch_shapes=[
             pltpu.VMEM(ringed, jnp.float32),
             pltpu.VMEM(ringed, jnp.float32),
             pltpu.VMEM(grid + (each, nz), jnp.float32),
             pltpu.VMEM(grid + (1, nz), jnp.float32),
+            pltpu.VMEM((group, atoms * projs, each, nz), jnp.float32),
             pltpu.SMEM((group, nz), jnp.float32),
             pltpu.SemaphoreType.DMA,
         ],
@@ -370,20 +419,29 @@
         out_specs=vmem,
         out_shape=jax.ShapeDtypeStruct((gram_rows + 8, nz), jnp.float32),
         compiler_params=params,
-    )(parts, scale)
+    )(parts, level)
     sent = jnp.concatenate(
-        [field * scale[0, 0], jnp.broadcast_to(block[None], (group,) + block.shape)], axis=1
+        [field, jnp.broadcast_to(block[None], (group,) + block.shape)], axis=1
     ).astype(jnp.float16)
     back = lax.all_to_all(sent, plane, 0, 0)
 
-    start = slab_cells * each
-    shrink = shrink_of(back[:, start + gram_rows : start + gram_rows + 2, :1].astype(jnp.float32))
-    filtered = back[:, :start].reshape(group, slab_cells, each, nz).astype(jnp.float32)
-    filtered = (filtered * shrink[:, :1, :, None]).transpose(1, 0, 2, 3)
+    filtered, gram = pl.pallas_call(
+        functools.partial(unpack_kernel, each),
+        in_specs=[vmem],
+        out_specs=[hbm] * 2,
+        out_shape=[
+            jax.ShapeDtypeStruct((slab_cells, band_orbitals, nz), jnp.float32),
+            jax.ShapeDtypeStruct((band_orbitals, total_orbitals), jnp.float32),
+        ],
+        scratch_shapes=[
+            pltpu.VMEM((slab_cells, band_orbitals, nz), jnp.float32),
+            pltpu.VMEM((band_orbitals, total_orbitals), jnp.float32),
+            pltpu.SemaphoreType.DMA((cells_x,)),
+            pltpu.SemaphoreType.DMA,
+        ],
+        compiler_params=params,
+    )(back.astype(jnp.float32))
     filtered = filtered.reshape(cells_x, cells_y, band_orbitals, nz).transpose(2, 0, 1, 3)
-    gram = back[:, start : start + gram_rows].reshape(group, 2, halves, each, nz).astype(jnp.float32)
-    gram = (gram[:, 0] + gram[:, 1]) * shrink[:, 1][:, None, None]
-    gram = gram.transpose(0, 2, 1, 3).reshape(band_orbitals, total_orbitals)
     return (filtered, gram)
 
 

time: 83.9 us -> 79.5 us (0.948)
  local copies, waits for them, and re-layouts: 6.09 us -> 0.19 us
  waiting for transfers between devices: 9.41 us -> 10.6 us
    unnamed x9 -> x8, local copies, waits for them, and re-layouts: 4.23 us -> 0.02 us
    convert_element_type x3 -> x5, other arithmetic: 0.24 us -> 1.67 us  [the longest x1 1.46 us: local(): chunks = (orbitals * orbital_gain).astype(jnp.float16)]
    all_to_all x1, waiting for transfers between devices: 9.41 us -> 10.6 us  [local(): lax.all_to_all(sums.reshape(bands * group, each, total_orbitals), every,...]
    transpose x1 -> x0, local copies, waits for them, and re-layouts: 1.16 us -> none  [local(): filtered = (filtered * shrink[:, :1, :, None]).transpose(1, 0, 2, 3)]
    pallas_call x1 -> x2, Pallas kernels: 0.93 us -> 1.81 us  [the longest x1 1.13 us: local(): pl.pallas_call(functools.partial(unpack_kernel, each), in_specs=[vmem], o...]
  transfers between devices with their start and end apart: 1 -> 1, of which waited for: 1 -> 1; matrix products, arithmetic and copies ran while one was open for 2% -> 0% of each run, Pallas kernels for 0% -> 0%
where the time goes in v3:
time: 79.5 us; the launch traced here: 79.2 us
  blocking collectives  51.2 us (64%)
  waiting for transfers between devices  10.6 us (13%)
  Pallas kernels  9.48 us (12%)
  starting transfers between devices  3.62 us (5%)
  other arithmetic  2.15 us (3%)
  matrix products  1.08 us (1%)
  between operations  0.8 us (1%)
    all_to_all x1, blocking collectives, local(): pieces = lax.all_to_all(rounded, every, 0, 0)  20.4 us
    all_to_all x1, blocking collectives, local(): got = lax.all_to_all(sent, plane, 0, 0).astype(jnp.float32)  17.8 us
    all_to_all x1, blocking collectives, local(): back = lax.all_to_all(sent, plane, 0, 0)  13 us
    all_to_all x1, waiting for transfers between devices, local(): lax.all_to_all(sums.reshape(bands * group, each, total_orbitals), every,...  10.6 us
    pallas_call x1, Pallas kernels, local(): pl.pallas_call(functools.partial(filter_kernel, slabs_y, cells_x, cells_y...  7.5 us
    all_to_all x1, starting transfers between devices, local(): lax.all_to_all(sums.reshape(bands * group, each, total_orbitals), every,...  3.62 us
  transfers between devices with their start and end apart: 1, of which 1 were waited for; matrix products, arithmetic and copies ran while one was open for 0% of the time, Pallas kernels for 0%

profile of v3, /device:TPU:0, one launch (start us, length us, event | category | flops | bytes accessed | tf_op | source)
XLA Modules:
  0.0 79.2 jit_solution(2611341009535906626)
XLA Ops:
  0.6 0.0 copy-start.3
  0.6 0.0 copy-start.2
  0.7 0.0 copy-start
  0.7 0.0 copy-start.1
  0.7 1.5 %multiply_convert_fusion = f16[64,6,6,128]{3,0,2,1:T(8,128)(2,1)S(1)} fusion(f32[64,6,6,128]{3,0,2,1:T(8,128)} %param.5), kind=kLoop, calls=%fused_computation | loop fusion | flops 589824 | bytes 1769472 | tf_op jit(solution)/shard_map/convert_element_type | solution.py:366
  2.1 0.1 copy.9
  2.3 0.0 copy-done.3
  2.3 0.0 copy-done.2
  2.3 0.0 copy-done
  2.3 0.0 copy-done.1
  2.3 0.7 shard_map.68
  3.0 0.2 pad_maximum_fusion
  3.3 17.8 %all_to_all.20 = f16[8,408,128]{2,1,0:T(8,128)(2,1)S(1)} all-to-all(f16[8,408,128]{2,1,0:T(8,128)(2,1)S(1)} %pad_maximum_fusion), channel_id=1, replica_groups=mesh['band'=4,'sx'=4,'sy'=2] {'sx','sy'}, dimensions={0} | all-to-all | bytes 1671168 | tf_op jit(solution)/shard_map/all_to_all | solution.py:377
  21.1 0.1 convert_element_type.22.got_ref
  21.2 7.5 %shard_map.69 = (f32[8,288,128]{2,1,0:T(8,128)S(1)}, bf16[32,8,1152]{2,1,0:T(8,128)(2,1)S(1)}, f32[1,128]{1,0:T(1,128)S(1)}) custom-call(f32[8,408,128]{2,1,0:T(8,128)S(1)} %convert_element_type.22.got_ref), custom_call_target="tpu_custom_call" | custom-call | flops 47185920 | bytes 2359296 | tf_op jit(solution)/shard_map/pallas_call | solution.py:381
  28.8 20.4 %all_to_all.21 = bf16[32,8,1152]{2,1,0:T(8,128)(2,1)S(1)} all-to-all(bf16[32,8,1152]{2,1,0:T(8,128)(2,1)S(1)} %get-tuple-element.8), channel_id=1, replica_groups=mesh['band'=4,'sx'=4,'sy'=2] {'band','sx','sy'}, dimensions={0} | all-to-all | bytes 1179648 | tf_op jit(solution)/shard_map/all_to_all | solution.py:407
  49.1 1.1 %fusion = f32[32,8,256]{2,1,0:T(8,128)} fusion(bf16[32,8,1152]{2,1,0:T(8,128)(2,1)S(1)} %all_to_all.21), kind=kOutput, calls=%fused_computation.1 | convolution fusion | flops 150994944 | bytes 851968 | tf_op jit(solution)/shard_map/dot_general | solution.py:409
  50.2 3.6 %all-to-all-start.2 = ((f32[32,8,256]{2,1,0:T(8,128)}), f32[32,8,256]{2,1,0:T(8,128)S(1)}, u32[]{:S(2)}, u32[]{:S(2)}) async-start(f32[32,8,256]{2,1,0:T(8,128)} %fusion), calls=%async_computation.2 | async-start | bytes 524288 | tf_op jit(solution)/shard_map/all_to_all | solution.py:412
  53.8 0.1 convert.8
  53.9 10.6 %all-to-all-done.2.parts_ref = f32[32,8,256]{2,1,0:T(8,128)S(1)} async-done(((f32[32,8,256]{2,1,0:T(8,128)}), f32[32,8,256]{2,1,0:T(8,128)S(1)}, u32[]{:S(2)}, u32[]{:S(2)}) %all-to-all-start.2) | async-done | bytes 262176 | tf_op jit(solution)/shard_map/all_to_all | solution.py:412
  64.5 0.2 shard_map.70
  64.7 0.2 pad_maximum_fusion.1
  64.9 13.0 %all_to_all.22 = f16[8,328,128]{2,1,0:T(8,128)(2,1)S(1)} all-to-all(f16[8,328,128]{2,1,0:T(8,128)(2,1)S(1)} %pad_maximum_fusion.1), channel_id=1, replica_groups=mesh['band'=4,'sx'=4,'sy'=2] {'sx','sy'}, dimensions={0} | all-to-all | bytes 1343488 | tf_op jit(solution)/shard_map/all_to_all | solution.py:426
  77.9 0.1 convert_element_type.23.back_ref
  78.0 1.1 %shard_map.71 = (f32[36,64,128]{2,1,0:T(8,128)}, f32[64,256]{1,0:T(8,128)}) custom-call(f32[8,328,128]{2,1,0:T(8,128)S(1)} %convert_element_type.23.back_ref), custom_call_target="tpu_custom_call" | custom-call | tf_op jit(solution)/shard_map/pallas_call | solution.py:428
  (5 shorter events, 0.1 us)
Async XLA Ops:
  0.6 1.6 %copy-start.3 = (s32[4,2]{0,1:T(2,128)S(1)}, s32[4,2]{0,1:T(2,128)}, u32[]{:S(2)}) copy-start(s32[4,2]{0,1:T(2,128)} %param.9) | copy-start | bytes 100
  0.6 1.6 %copy-start.2 = (f32[4,4]{1,0:T(4,128)S(1)}, f32[4,4]{1,0:T(4,128)}, u32[]{:S(2)}) copy-start(f32[4,4]{1,0:T(4,128)} %energies_ref.1) | copy-start | bytes 196
  0.7 1.6 %copy-start = (f32[4,4,5,128]{3,1,2,0:T(4,128)S(1)}, f32[4,4,5,128]{3,1,2,0:T(4,128)}, u32[]{:S(2)}) copy-start(f32[4,4,5,128]{3,1,2,0:T(4,128)} %param.7) | copy-start | bytes 122884
  0.7 1.6 %copy-start.1 = (f32[6,6,128]{2,1,0:T(8,128)S(1)}, f32[6,6,128]{2,1,0:T(8,128)}, u32[]{:S(2)}) copy-start(f32[6,6,128]{2,1,0:T(8,128)} %potential_ref.1) | copy-start | bytes 55300
  50.2 14.3 %all-to-all-start.2 = ((f32[32,8,256]{2,1,0:T(8,128)}), f32[32,8,256]{2,1,0:T(8,128)S(1)}, u32[]{:S(2)}, u32[]{:S(2)}) async-start(f32[32,8,256]{2,1,0:T(8,128)} %fusion), calls=%async_computation.2 | async-start | bytes 524288 | tf_op jit(solution)/shard_map/all_to_all | solution.py:412

commit v4 on v3

--- a/solution.py
+++ b/solution.py
@@ -179,28 +179,21 @@
         return total
 
     def apply(source, target, finish, gain):
-        def z_part(block, carry):
-            rows = source[pl.ds(ring + block * cells_x, cells_x), pl.ds(ring, count_y)]
-            flat = rows.reshape(cells_x * count_y * each, nz)
+        def xz_part(y, carry):
+            column = source[pl.ds(ring, count_x), ring + y]
+            flat = column.reshape(count_x * each, nz)
             high = flat.astype(jnp.bfloat16)
             low = (flat - high.astype(jnp.float32)).astype(jnp.bfloat16)
             both = jnp.dot(
                 jnp.concatenate([high, low], axis=1), z_matrix, preferred_element_type=jnp.float32
             )
-            partial[pl.ds(block * cells_x, cells_x)] = (both[:, :nz] + both[:, nz:]).reshape(
-                rows.shape
-            )
+            along_z = (both[:, :nz] + both[:, nz:]).reshape(column.shape)
+            cells = [column[x] for x in range(count_x)]
+            for x in range(count_x):
+                partial[x, y] = along_z[x] + diagonal[x, y] * cells[x] + along(cells, x)
             return carry
 
-        lax.fori_loop(0, count_x // cells_x, z_part, 0)
-
-        def x_part(y, carry):
-            cells = [source[ring + x, ring + y] for x in range(count_x)]
-            for x in range(count_x):
-                partial[x, y] = partial[x, y] + diagonal[x, y] * cells[x] + along(cells, x)
-            return carry
-
-        lax.fori_loop(0, count_y, x_part, 0)
+        lax.fori_loop(0, count_y, xz_part, 0, unroll=2)
 
         def y_part(x, carry):
             cells = [source[ring + x, ring + y] for y in range(count_y)]
@@ -209,7 +202,7 @@
                 target[ring + x, ring + y] = finish(total, target, ring + x, ring + y)
             return carry
 
-        lax.fori_loop(0, count_x, y_part, 0)
+        lax.fori_loop(0, count_x, y_part, 0, unroll=2)
 
         def place_of(g, a):
             at = 2 * atoms * projs + 2 * a
@@ -293,10 +286,39 @@
     lax.fori_loop(0, group, give_slab, 0)
 
 
-def rows_kernel(cells, parts_ref, level_ref, out_ref):
-    _, each, columns = parts_ref.shape
+def gram_kernel(each, matrix_ref, out_ref):
+    matrix = matrix_ref[...]
+    sums = lax.dot_general(
+        matrix, matrix, (((1,), (1,)), ((), ())), preferred_element_type=jnp.float32
+    )
+    level, gain = level_of(jnp.max(jnp.abs(sums)))
+    row = lax.broadcasted_iota(jnp.int32, sums.shape, 0)
+    column = lax.broadcasted_iota(jnp.int32, sums.shape, 1)
+    spare = (column == row - 1) & (row % each == 1)
+    out_ref[...] = jnp.where(spare, level, sums * gain)
+
+
+def rows_kernel(cells, first_ref, parts_ref, level_ref, out_ref):
+    count, each, columns = parts_ref.shape
     nz = out_ref.shape[1]
-    total = jnp.sum(parts_ref[...], axis=0) / cells
+    if each > 1:
+        row = lax.broadcasted_iota(jnp.int32, (each, columns), 0)
+        column = lax.broadcasted_iota(jnp.int32, (each, columns), 1)
+        spare = (row == 1) & (column == first_ref[0])
+        twin = (row == 0) & (column == first_ref[0] + 1)
+
+        def entry(block, place):
+            picked = jnp.where(place, block, 0.0)
+            return jnp.sum(jnp.sum(picked, axis=0, keepdims=True), axis=1, keepdims=True)
+
+        total = jnp.zeros((each, columns), jnp.float32)
+        for source in range(count):
+            block = parts_ref[source]
+            total = total + block * shrink_of(entry(block, spare))
+        total = jnp.where(spare, entry(total, twin), total)
+    else:
+        total = jnp.sum(parts_ref[...], axis=0)
+    total = total / cells
     level, gain = level_of(jnp.max(jnp.abs(total)))
     total = total * gain
     high = total.astype(jnp.bfloat16).astype(jnp.float32)
@@ -406,20 +428,33 @@
 
     pieces = lax.all_to_all(rounded, every, 0, 0)
     matrix = pieces.reshape(total_orbitals, portion * nz)
-    sums = lax.dot_general(
-        matrix, matrix, (((1,), (1,)), ((), ())), preferred_element_type=jnp.float32
-    )
-    parts = lax.all_to_all(sums.reshape(bands * group, each, total_orbitals), every, 0, 0)
+    spread = (bands * group, each, total_orbitals)
+    if each > 1:
+        sums = pl.pallas_call(
+            functools.partial(gram_kernel, each),
+            in_specs=[vmem],
+            out_specs=vmem,
+            out_shape=jax.ShapeDtypeStruct((total_orbitals, total_orbitals), jnp.float32),
+            compiler_params=params,
+        )(matrix)
+        sums = sums.astype(jnp.float16).reshape(spread)
+    else:
+        sums = lax.dot_general(
+            matrix, matrix, (((1,), (1,)), ((), ())), preferred_element_type=jnp.float32
+        ).reshape(spread)
+    parts = lax.all_to_all(sums, every, 0, 0).astype(jnp.float32)
+    field, parts = lax.optimization_barrier((field, parts))
+    first_row = lax.axis_index(every).astype(jnp.int32).reshape(1) * each
 
     halves = total_orbitals // nz
     gram_rows = 2 * halves * each
     block = pl.pallas_call(
         functools.partial(rows_kernel, grid[0] * grid[1] * nz),
-        in_specs=[vmem, vmem],
+        in_specs=[smem, vmem, vmem],
         out_specs=vmem,
         out_shape=jax.ShapeDtypeStruct((gram_rows + 8, nz), jnp.float32),
         compiler_params=params,
-    )(parts, level)
+    )(first_row, parts, level)
     sent = jnp.concatenate(
         [field, jnp.broadcast_to(block[None], (group,) + block.shape)], axis=1
     ).astype(jnp.float16)

time: 79.5 us -> 76.9 us (0.967)
  waiting for transfers between devices: 10.6 us -> 8.62 us
  matrix products: 1.08 us -> 0 us
    all_to_all x1, waiting for transfers between devices: 10.6 us -> 8.62 us  [local(): parts = lax.all_to_all(sums, every, 0, 0).astype(jnp.float32)]
    dot_general x1 -> x0, matrix products: 1.08 us -> none  [local(): lax.dot_general(matrix, matrix, (((1,), (1,)), ((), ())), preferred_eleme...]
    pallas_call x1, Pallas kernels: 7.5 us -> 6.5 us  [local(): pl.pallas_call(functools.partial(filter_kernel, slabs_y, cells_x, cells_y...]
where the time goes in v4:
time: 76.9 us; the launch traced here: 76.6 us
  blocking collectives  51.2 us (67%)
  Pallas kernels  9.33 us (12%)
  waiting for transfers between devices  8.62 us (11%)
  starting transfers between devices  3.62 us (5%)
  other arithmetic  2.84 us (4%)
  between operations  0.82 us (1%)
    all_to_all x1, blocking collectives, local(): pieces = lax.all_to_all(rounded, every, 0, 0)  20.4 us
    all_to_all x1, blocking collectives, local(): got = lax.all_to_all(sent, plane, 0, 0).astype(jnp.float32)  17.8 us
    all_to_all x1, blocking collectives, local(): back = lax.all_to_all(sent, plane, 0, 0)  13 us
    all_to_all x1, waiting for transfers between devices, local(): parts = lax.all_to_all(sums, every, 0, 0).astype(jnp.float32)  8.62 us
    pallas_call x1, Pallas kernels, local(): pl.pallas_call(functools.partial(filter_kernel, slabs_y, cells_x, cells_y...  6.5 us
    all_to_all x1, starting transfers between devices, local(): parts = lax.all_to_all(sums, every, 0, 0).astype(jnp.float32)  3.62 us
  transfers between devices with their start and end apart: 1, of which 1 were waited for; matrix products, arithmetic and copies ran while one was open for 0% of the time, Pallas kernels for 0%

profile of v4, /device:TPU:0, one launch (start us, length us, event | category | flops | bytes accessed | tf_op | source)
XLA Modules:
  0.0 76.6 jit_solution(7271557685645896685)
XLA Ops:
  0.6 0.0 copy-start.3
  0.6 0.0 copy-start
  0.7 0.0 copy-start.1
  0.7 0.0 copy-start.2
  0.7 1.5 %multiply_convert_fusion = f16[64,6,6,128]{3,0,2,1:T(8,128)(2,1)S(1)} fusion(f32[64,6,6,128]{3,0,2,1:T(8,128)} %param.5), kind=kLoop, calls=%fused_computation | loop fusion | flops 589824 | bytes 1769472 | tf_op jit(solution)/shard_map/convert_element_type | solution.py:388
  2.1 0.1 copy.9
  2.3 0.0 copy-done.3
  2.3 0.0 copy-done
  2.3 0.0 copy-done.1
  2.3 0.0 copy-done.2
  2.3 0.7 shard_map.68
  3.0 0.2 pad_maximum_fusion
  3.3 17.8 %all_to_all.20 = f16[8,408,128]{2,1,0:T(8,128)(2,1)S(1)} all-to-all(f16[8,408,128]{2,1,0:T(8,128)(2,1)S(1)} %pad_maximum_fusion), channel_id=1, replica_groups=mesh['band'=4,'sx'=4,'sy'=2] {'sx','sy'}, dimensions={0} | all-to-all | bytes 1671168 | tf_op jit(solution)/shard_map/all_to_all | solution.py:399
  21.1 0.1 convert_element_type.28.got_ref
  21.2 6.5 %shard_map.69 = (f32[8,288,128]{2,1,0:T(8,128)S(1)}, bf16[32,8,1152]{2,1,0:T(8,128)(2,1)S(1)}, f32[1,128]{1,0:T(1,128)S(1)}) custom-call(f32[8,408,128]{2,1,0:T(8,128)S(1)} %convert_element_type.28.got_ref), custom_call_target="tpu_custom_call" | custom-call | flops 47185920 | bytes 2359296 | tf_op jit(solution)/shard_map/pallas_call | solution.py:403
  27.7 20.4 %all_to_all.21 = bf16[32,8,1152]{2,1,0:T(8,128)(2,1)S(1)} all-to-all(bf16[32,8,1152]{2,1,0:T(8,128)(2,1)S(1)} %get-tuple-element.10), channel_id=1, replica_groups=mesh['band'=4,'sx'=4,'sy'=2] {'band','sx','sy'}, dimensions={0} | all-to-all | bytes 1179648 | tf_op jit(solution)/shard_map/all_to_all | solution.py:429
  48.1 0.5 shard_map.70
  48.7 0.7 convert_bitcast_fusion
  49.3 3.6 %all-to-all-start.2 = ((f16[32,8,256]{2,1,0:T(8,128)(2,1)}), f16[32,8,256]{2,1,0:T(8,128)(2,1)S(1)}, u32[]{:S(2)}, u32[]{:S(2)}) async-start(f16[32,8,256]{2,1,0:T(8,128)(2,1)} %convert_bitcast_fusion), calls=%async_computation.2 | async-start | bytes 262144 | tf_op jit(solution)/shard_map/all_to_all | solution.py:445
  53.0 8.6 %all-to-all-done.2 = f16[32,8,256]{2,1,0:T(8,128)(2,1)S(1)} async-done(((f16[32,8,256]{2,1,0:T(8,128)(2,1)}), f16[32,8,256]{2,1,0:T(8,128)(2,1)S(1)}, u32[]{:S(2)}, u32[]{:S(2)}) %all-to-all-start.2) | async-done | bytes 131104 | tf_op jit(solution)/shard_map/all_to_all | solution.py:445
  61.6 0.5 shard_map.71
  62.1 0.1 convert.8
  62.2 0.2 pad_maximum_fusion.1
  62.4 13.0 %all_to_all.22 = f16[8,328,128]{2,1,0:T(8,128)(2,1)S(1)} all-to-all(f16[8,328,128]{2,1,0:T(8,128)(2,1)S(1)} %pad_maximum_fusion.1), channel_id=1, replica_groups=mesh['band'=4,'sx'=4,'sy'=2] {'sx','sy'}, dimensions={0} | all-to-all | bytes 1343488 | tf_op jit(solution)/shard_map/all_to_all | solution.py:461
  75.4 0.1 convert_element_type.31.back_ref
  75.5 1.1 %shard_map.72 = (f32[36,64,128]{2,1,0:T(8,128)}, f32[64,256]{1,0:T(8,128)}) custom-call(f32[8,328,128]{2,1,0:T(8,128)S(1)} %convert_element_type.31.back_ref), custom_call_target="tpu_custom_call" | custom-call | tf_op jit(solution)/shard_map/pallas_call | solution.py:463
  (6 shorter events, 0.1 us)
Async XLA Ops:
  0.6 1.6 %copy-start.3 = (s32[4,2]{0,1:T(2,128)S(1)}, s32[4,2]{0,1:T(2,128)}, u32[]{:S(2)}) copy-start(s32[4,2]{0,1:T(2,128)} %param.9) | copy-start | bytes 100
  0.6 1.6 %copy-start = (f32[4,4,5,128]{3,1,2,0:T(4,128)S(1)}, f32[4,4,5,128]{3,1,2,0:T(4,128)}, u32[]{:S(2)}) copy-start(f32[4,4,5,128]{3,1,2,0:T(4,128)} %param.7) | copy-start | bytes 122884
  0.7 1.6 %copy-start.1 = (f32[6,6,128]{2,1,0:T(8,128)S(1)}, f32[6,6,128]{2,1,0:T(8,128)}, u32[]{:S(2)}) copy-start(f32[6,6,128]{2,1,0:T(8,128)} %potential_ref.1) | copy-start | bytes 55300
  0.7 1.6 %copy-start.2 = (f32[4,4]{1,0:T(4,128)S(1)}, f32[4,4]{1,0:T(4,128)}, u32[]{:S(2)}) copy-start(f32[4,4]{1,0:T(4,128)} %energies_ref.1) | copy-start | bytes 196
  49.3 12.2 %all-to-all-start.2 = ((f16[32,8,256]{2,1,0:T(8,128)(2,1)}), f16[32,8,256]{2,1,0:T(8,128)(2,1)S(1)}, u32[]{:S(2)}, u32[]{:S(2)}) async-start(f16[32,8,256]{2,1,0:T(8,128)(2,1)} %convert_bitcast_fusion), calls=%async_computation.2 | async-start | bytes 262144 | tf_op jit(solution)/shard_map/all_to_all | solution.py:445

commit v5 on v4

--- a/solution.py
+++ b/solution.py
@@ -53,19 +53,6 @@
     for j in range(levels):
         shrink = jnp.where(level > j, jnp.float32(2.0 ** (8 * (j + 1 - middle) - top)), shrink)
     return shrink
-
-
-def over_group(group, each, body):
-    if each % 8 == 0:
-
-        def step(g, carry):
-            body(g, pl.ds(pl.multiple_of(g * each, each), each))
-            return carry
-
-        lax.fori_loop(0, group, step, 0, unroll=min(group, 8))
-    else:
-        for g in range(group):
-            body(g, pl.ds(g * each, each))
 
 
 def share_kernel(_, energies_ref, centers_ref, projectors_ref, potential_ref, out_ref):
@@ -105,10 +92,10 @@
     each,
     atoms,
     projs,
+    me_ref,
     got_ref,
     field_ref,
     rounded_ref,
-    level_ref,
     first,
     second,
     partial,
@@ -268,16 +255,18 @@
 
     largest = lax.fori_loop(0, count_x, largest_of, jnp.zeros((each, nz), jnp.float32))
     level, gain = level_of(jnp.max(largest))
-    level_ref[...] = jnp.full((1, nz), level, jnp.float32)
+    level_rows = jnp.full((8, nz), level, jnp.float32)
 
     def give_slab(g, carry):
+        slot = jnp.bitwise_xor(g, me_ref[0])
+        field_ref[slot, pl.ds(slab_cells * each, 8), :] = level_rows
         x0 = (g // slabs_y) * cells_x
         y0 = (g % slabs_y) * cells_y
         for i in range(cells_x):
             for j in range(cells_y):
                 cell = i * cells_y + j
                 value = first[ring + x0 + i, ring + y0 + j]
-                field_ref[g, pl.ds(cell * each, each), :] = value * gain
+                field_ref[slot, pl.ds(cell * each, each), :] = value * gain
                 rounded_ref[
                     (cell // portion) * group + g, :, pl.ds((cell % portion) * nz, nz)
                 ] = value.astype(jnp.bfloat16)
@@ -298,9 +287,8 @@
     out_ref[...] = jnp.where(spare, level, sums * gain)
 
 
-def rows_kernel(cells, first_ref, parts_ref, level_ref, out_ref):
+def rows_kernel(cells, first_ref, parts_ref, out_ref):
     count, each, columns = parts_ref.shape
-    nz = out_ref.shape[1]
     if each > 1:
         row = lax.broadcasted_iota(jnp.int32, (each, columns), 0)
         column = lax.broadcasted_iota(jnp.int32, (each, columns), 1)
@@ -318,50 +306,25 @@
         total = jnp.where(spare, entry(total, twin), total)
     else:
         total = jnp.sum(parts_ref[...], axis=0)
-    total = total / cells
-    level, gain = level_of(jnp.max(jnp.abs(total)))
-    total = total * gain
-    high = total.astype(jnp.bfloat16).astype(jnp.float32)
-    low = total - high
-    row = 0
-    for part in (high, low):
-        for column in range(0, columns, nz):
-            out_ref[pl.ds(row, each), :] = part[:, column : column + nz]
-            row += each
-    rest = out_ref.shape[0] - row
-    out_ref[pl.ds(row, rest), :] = jnp.zeros((rest, nz), jnp.float32)
-    out_ref[pl.ds(row, 1), :] = level_ref[...]
-    out_ref[pl.ds(row + 1, 1), :] = jnp.full((1, nz), level, jnp.float32)
-
-
-def unpack_kernel(each, back_ref, filtered_hbm, gram_hbm, filtered_ref, gram_ref, chunk_sems, sem):
-    group, _, nz = back_ref.shape
+    out_ref[...] = total / cells
+
+
+def unpack_kernel(each, me_ref, pieces_ref, filtered_hbm, filtered_ref, chunk_sems):
+    group, _, nz = pieces_ref.shape
     slab_cells = filtered_ref.shape[0]
-    halves = gram_ref.shape[1] // nz
     chunks = chunk_sems.shape[0]
     chunk = slab_cells // chunks
-    base = slab_cells * each
-    number_row = base + 2 * halves * each
-
-    def put_rows(g, rows):
-        shrink = shrink_of(back_ref[g, pl.ds(number_row + 1, 1), :])
-        for half in range(halves):
-            row = base + half * each
-            value = back_ref[g, pl.ds(row, each), :] + back_ref[g, pl.ds(row + halves * each, each), :]
-            gram_ref[rows, half * nz : (half + 1) * nz] = value * shrink
-
-    over_group(group, each, put_rows)
-    copies = [pltpu.make_async_copy(gram_ref, gram_hbm, sem)]
-    copies[0].start()
-
+    copies = []
     for c in range(chunks):
-
-        def put_cells(g, rows):
-            shrink = shrink_of(back_ref[g, pl.ds(number_row, 1), :])
+        for slot in range(group):
+            shrink = shrink_of(pieces_ref[slot, pl.ds(slab_cells * each, 1), :])
+            if each % 8 == 0:
+                source = jnp.bitwise_xor(me_ref[0], slot)
+                rows = pl.ds(pl.multiple_of(source * each, each), each)
+            else:
+                rows = pl.ds(slot * each, each)
             for cell in range(c * chunk, (c + 1) * chunk):
-                filtered_ref[cell, rows, :] = back_ref[g, pl.ds(cell * each, each), :] * shrink
-
-        over_group(group, each, put_cells)
+                filtered_ref[cell, rows, :] = pieces_ref[slot, pl.ds(cell * each, each), :] * shrink
         part = pl.ds(c * chunk, chunk)
         copies.append(
             pltpu.make_async_copy(filtered_ref.at[part], filtered_hbm.at[part], chunk_sems.at[c])
@@ -369,6 +332,26 @@
         copies[-1].start()
     for copy in copies:
         copy.wait()
+
+
+def swap_stages(slabs_x, slabs_y):
+    stages = [("sx", 1 << k) for k in range(slabs_x.bit_length() - 1)]
+    stages = stages[1:] + [("sy", 1 << k) for k in range(slabs_y.bit_length() - 1)] + stages[:1]
+    return [(axis, bit, bit * (slabs_y if axis == "sx" else 1)) for axis, bit in stages]
+
+
+def swap_pieces(field, stages):
+    group = field.shape[0]
+    held = {(r, 0): field[r] for r in range(group)}
+    for axis, bit, value in stages:
+        leaving = sorted(key for key in held if key[0] & value)
+        pairs = [(i, i ^ bit) for i in range(lax.axis_size(axis))]
+        sent = jnp.stack([held[key].astype(jnp.float16) for key in leaving])
+        came = lax.ppermute(sent, axis, pairs)
+        held = {key: piece for key, piece in held.items() if not key[0] & value}
+        for i, (to, origin) in enumerate(leaving):
+            held[(to ^ value, origin ^ value)] = came[i]
+    return jnp.stack([held[(0, r)].astype(jnp.float32) for r in range(group)])
 
 
 def local(orbitals, potential, projectors, energies, centers):
@@ -398,16 +381,20 @@
     sent = jnp.concatenate([chunks, jnp.broadcast_to(shared[None], (group, rows, nz))], axis=1)
     got = lax.all_to_all(sent, plane, 0, 0).astype(jnp.float32)
 
+    stages = swap_stages(slabs_x, slabs_y)
+    by_swaps = group <= 8 and each % 8 == 0 and group == 1 << len(stages)
+    place = lax.axis_index(plane).astype(jnp.int32).reshape(1)
+    me = place if by_swaps else jnp.zeros((1,), jnp.int32)
+
     portion = slab_cells // bands
     ringed = (grid[0] + 2, grid[1] + 2, each, nz)
-    field, rounded, level = pl.pallas_call(
+    field, rounded = pl.pallas_call(
         functools.partial(filter_kernel, slabs_y, cells_x, cells_y, each, atoms, projs),
-        in_specs=[vmem],
-        out_specs=[vmem] * 3,
+        in_specs=[smem, vmem],
+        out_specs=[vmem] * 2,
         out_shape=[
-            jax.ShapeDtypeStruct((group, slab_cells * each, nz), jnp.float32),
+            jax.ShapeDtypeStruct((group, slab_cells * each + 8, nz), jnp.float32),
             jax.ShapeDtypeStruct((bands * group, each, portion * nz), jnp.bfloat16),
-            jax.ShapeDtypeStruct((1, nz), jnp.float32),
         ],
         scratch_shapes=[
             pltpu.VMEM(ringed, jnp.float32),
@@ -424,10 +411,14 @@
             bytes_accessed=8 * grid[0] * grid[1] * each * nz,
             transcendentals=0,
         ),
-    )(got)
-
-    pieces = lax.all_to_all(rounded, every, 0, 0)
-    matrix = pieces.reshape(total_orbitals, portion * nz)
+    )(me, got)
+
+    if by_swaps:
+        pieces = swap_pieces(field, stages)
+    else:
+        pieces = lax.all_to_all(field.astype(jnp.float16), plane, 0, 0).astype(jnp.float32)
+
+    matrix = lax.all_to_all(rounded, every, 0, 0).reshape(total_orbitals, portion * nz)
     spread = (bands * group, each, total_orbitals)
     if each > 1:
         sums = pl.pallas_call(
@@ -443,39 +434,28 @@
             matrix, matrix, (((1,), (1,)), ((), ())), preferred_element_type=jnp.float32
         ).reshape(spread)
     parts = lax.all_to_all(sums, every, 0, 0).astype(jnp.float32)
-    field, parts = lax.optimization_barrier((field, parts))
-    first_row = lax.axis_index(every).astype(jnp.int32).reshape(1) * each
-
-    halves = total_orbitals // nz
-    gram_rows = 2 * halves * each
-    block = pl.pallas_call(
+    first_row = (lax.axis_index("band").astype(jnp.int32) * group + place) * each
+    rows = pl.pallas_call(
         functools.partial(rows_kernel, grid[0] * grid[1] * nz),
-        in_specs=[smem, vmem, vmem],
+        in_specs=[smem, vmem],
         out_specs=vmem,
-        out_shape=jax.ShapeDtypeStruct((gram_rows + 8, nz), jnp.float32),
+        out_shape=jax.ShapeDtypeStruct((each, total_orbitals), jnp.float32),
         compiler_params=params,
-    )(first_row, parts, level)
-    sent = jnp.concatenate(
-        [field, jnp.broadcast_to(block[None], (group,) + block.shape)], axis=1
-    ).astype(jnp.float16)
-    back = lax.all_to_all(sent, plane, 0, 0)
-
-    filtered, gram = pl.pallas_call(
+    )(first_row, parts)
+    gram = lax.all_to_all(jnp.broadcast_to(rows[None], (group,) + rows.shape), plane, 0, 0)
+    gram = gram.reshape(band_orbitals, total_orbitals)
+
+    filtered = pl.pallas_call(
         functools.partial(unpack_kernel, each),
-        in_specs=[vmem],
-        out_specs=[hbm] * 2,
-        out_shape=[
-            jax.ShapeDtypeStruct((slab_cells, band_orbitals, nz), jnp.float32),
-            jax.ShapeDtypeStruct((band_orbitals, total_orbitals), jnp.float32),
-        ],
+        in_specs=[smem, vmem],
+        out_specs=hbm,
+        out_shape=jax.ShapeDtypeStruct((slab_cells, band_orbitals, nz), jnp.float32),
         scratch_shapes=[
             pltpu.VMEM((slab_cells, band_orbitals, nz), jnp.float32),
-            pltpu.VMEM((band_orbitals, total_orbitals), jnp.float32),
             pltpu.SemaphoreType.DMA((cells_x,)),
-            pltpu.SemaphoreType.DMA,
         ],
         compiler_params=params,
-    )(back.astype(jnp.float32))
+    )(me, pieces)
     filtered = filtered.reshape(cells_x, cells_y, band_orbitals, nz).transpose(2, 0, 1, 3)
     return (filtered, gram)
 

time: 76.9 us -> 85.7 us (1.11)
  blocking collectives: 51.2 us -> 0 us
  waiting for transfers between devices: 8.62 us -> 45.1 us
  starting transfers between devices: 3.62 us -> 19.9 us
  other arithmetic: 2.84 us -> 6.44 us
  local copies, waits for them, and re-layouts: 0.19 us -> 2.92 us
    all_to_all x3 -> x0, blocking collectives: 51.2 us -> none  [the longest x1 20.4 us: local(): pieces = lax.all_to_all(rounded, every, 0, 0)]
    all_to_all x0 -> x3, waiting for transfers between devices: none -> 27 us  [the longest x1 12.3 us: local(): got = lax.all_to_all(sent, plane, 0, 0).astype(jnp.float32)]
    all_to_all x0 -> x3, starting transfers between devices: none -> 13.7 us  [the longest x1 5.2 us: local(): lax.all_to_all(rounded, every, 0, 0).reshape(total_orbitals, portion * nz)]
    ppermute x0 -> x3, waiting for transfers between devices: none -> 10.4 us  [swap_pieces(): came = lax.ppermute(sent, axis, pairs)]
    unnamed x0 -> x6, other arithmetic: none -> 2.74 us
    ppermute x0 -> x3, starting transfers between devices: none -> 2.53 us  [swap_pieces(): came = lax.ppermute(sent, axis, pairs)]
    unnamed x8 -> x14, local copies, waits for them, and re-layouts: 0.02 us -> 1.93 us
    all_to_all x1, waiting for transfers between devices: 8.62 us -> 7.7 us  [local(): parts = lax.all_to_all(sums, every, 0, 0).astype(jnp.float32)]
  transfers between devices with their start and end apart: 1 -> 7, of which waited for: 1 -> 7; matrix products, arithmetic and copies ran while one was open for 0% -> 3% of each run, Pallas kernels for 0% -> 1%
where the time goes in v5:
time: 85.7 us; the launch traced here: 85.2 us
  waiting for transfers between devices  45.1 us (53%)
  starting transfers between devices  19.9 us (23%)
  Pallas kernels  9.98 us (12%)
  other arithmetic  6.44 us (8%)
  local copies, waits for them, and re-layouts  2.92 us (3%)
  between operations  0.87 us (1%)
    all_to_all x1, waiting for transfers between devices, local(): got = lax.all_to_all(sent, plane, 0, 0).astype(jnp.float32)  12.3 us
    all_to_all x1, waiting for transfers between devices, local(): lax.all_to_all(rounded, every, 0, 0).reshape(total_orbitals, portion * nz)  11.2 us
    ppermute x3, waiting for transfers between devices, swap_pieces(): came = lax.ppermute(sent, axis, pairs)  10.4 us
    all_to_all x1, waiting for transfers between devices, local(): parts = lax.all_to_all(sums, every, 0, 0).astype(jnp.float32)  7.7 us
    pallas_call x1, Pallas kernels, local(): pl.pallas_call(functools.partial(filter_kernel, slabs_y, cells_x, cells_y...  7.33 us
    all_to_all x1, starting transfers between devices, local(): lax.all_to_all(rounded, every, 0, 0).reshape(total_orbitals, portion * nz)  5.2 us
    all_to_all x1, starting transfers between devices, local(): got = lax.all_to_all(sent, plane, 0, 0).astype(jnp.float32)  5.17 us
    all_to_all x1, starting transfers between devices, local(): parts = lax.all_to_all(sums, every, 0, 0).astype(jnp.float32)  3.63 us
  transfers between devices with their start and end apart: 7, of which 7 were waited for; matrix products, arithmetic and copies ran while one was open for 3% of the time, Pallas kernels for 1%

profile of v5, /device:TPU:0, one launch (start us, length us, event | category | flops | bytes accessed | tf_op | source)
XLA Modules:
  0.0 85.2 jit_solution(14020887488908786672)
XLA Ops:
  0.7 1.5 %multiply_convert_fusion = f16[64,6,6,128]{3,0,2,1:T(8,128)(2,1)S(1)} fusion(f32[64,6,6,128]{3,0,2,1:T(8,128)} %param.5), kind=kLoop, calls=%fused_computation | loop fusion | flops 589824 | bytes 1769472 | tf_op jit(solution)/shard_map/convert_element_type | solution.py:371
  2.1 0.1 copy.9
  2.3 0.7 shard_map.68
  3.0 1.1 %pad_maximum_fusion = f16[8,408,128]{2,1,0:T(8,128)(2,1)} fusion(f16[8,120,128]{2,1,0:T(8,128)(2,1)S(1)} %broadcast_in_dim.4, f16[8,288,128]{2,1,0:T(8,128)(2,1)S(1)} %bitcast.28), kind=kLoop, calls=%fused_computation.1 | loop fusion | flops 417792 | bytes 1671168 | tf_op jit(solution)/shard_map/concatenate | solution.py:381
  4.2 5.2 %all-to-all-start = ((f16[8,408,128]{2,1,0:T(8,128)(2,1)}), f16[8,408,128]{2,1,0:T(8,128)(2,1)S(1)}, u32[]{:S(2)}, u32[]{:S(2)}) async-start(f16[8,408,128]{2,1,0:T(8,128)(2,1)} %pad_maximum_fusion), calls=%async_computation | async-start | bytes 1671168 | tf_op jit(solution)/shard_map/all_to_all | solution.py:382
  9.3 12.3 %all-to-all-done = f16[8,408,128]{2,1,0:T(8,128)(2,1)S(1)} async-done(((f16[8,408,128]{2,1,0:T(8,128)(2,1)}), f16[8,408,128]{2,1,0:T(8,128)(2,1)S(1)}, u32[]{:S(2)}, u32[]{:S(2)}) %all-to-all-start) | async-done | bytes 835616 | tf_op jit(solution)/shard_map/all_to_all | solution.py:382
  21.6 0.1 convert_element_type.66.got_ref
  21.7 7.3 %shard_map.69 = (f32[8,296,128]{2,1,0:T(8,128)S(1)}, bf16[32,8,1152]{2,1,0:T(8,128)(2,1)}) custom-call(s32[1]{0:T(128)} %bitcast.me_ref, f32[8,408,128]{2,1,0:T(8,128)S(1)} %convert_element_type.66.got_ref), custom_call_target="tpu_custom_call" | custom-call | flops 47185920 | bytes 2359296 | tf_op jit(solution)/shard_map/pallas_call | solution.py:391
  29.2 1.4 %collective-permute-start = (f16[4,296,128]{2,1,0:T(8,128)(2,1)S(1)}, f16[4,296,128]{2,1,0:T(8,128)(2,1)S(1)}, u32[]{:S(2)}, u32[]{:S(2)}) collective-permute-start(f16[4,296,128]{2,1,0:T(8,128)(2,1)S(1)} %slice.94), channel_id=1, source_target_pairs={{0,4},{2,6},{4,0},{6,2},{1,5},{3,7},{5,1},{7,3},{8,12},{10,14},{12... | collective-permute-start | bytes 909320 | tf_op jit(solution)/shard_map/ppermute | solution.py:350
  30.7 7.7 %collective-permute-done = f16[4,296,128]{2,1,0:T(8,128)(2,1)S(1)} collective-permute-done((f16[4,296,128]{2,1,0:T(8,128)(2,1)S(1)}, f16[4,296,128]{2,1,0:T(8,128)(2,1)S(1)}, u32[]{:S(2)}, u32[]{:S(2)}) %collective-permute-start) | collective-permute-done | bytes 303136 | tf_op jit(solution)/shard_map/ppermute | solution.py:350
  38.4 0.7 copy-done.4
  39.2 0.1 pad_maximum_fusion.1
  39.3 1.1 %collective-permute-start.1 = (f16[4,296,128]{2,1,0:T(8,128)(2,1)S(1)}, f16[4,296,128]{2,1,0:T(8,128)(2,1)S(1)}, u32[]{:S(2)}, u32[]{:S(2)}) collective-permute-start(f16[4,296,128]{2,1,0:T(8,128)(2,1)S(1)} %pad_maximum_fusion.1), channel_id=1, source_target_pairs={{0,1},{1,0},{2,3},{3,2},{4,5},{5,4},{6,7},{7,6},{8,9},{9,8},{10,11... | collective-permute-start | bytes 909320 | tf_op jit(solution)/shard_map/ppermute | solution.py:350
  40.4 5.2 %all-to-all-start.1 = ((bf16[32,8,1152]{2,1,0:T(8,128)(2,1)}), bf16[32,8,1152]{2,1,0:T(8,128)(2,1)S(1)}, u32[]{:S(2)}, u32[]{:S(2)}) async-start(bf16[32,8,1152]{2,1,0:T(8,128)(2,1)} %get-tuple-element.5), calls=%async_computation.1 | async-start | bytes 1179648 | tf_op jit(solution)/shard_map/all_to_all | solution.py:421
  45.6 2.0 %collective-permute-done.1 = f16[4,296,128]{2,1,0:T(8,128)(2,1)S(1)} collective-permute-done((f16[4,296,128]{2,1,0:T(8,128)(2,1)S(1)}, f16[4,296,128]{2,1,0:T(8,128)(2,1)S(1)}, u32[]{:S(2)}, u32[]{:S(2)}) %collective-permute-start.1) | collective-permute-done | bytes 303136 | tf_op jit(solution)/shard_map/ppermute | solution.py:350
  47.7 0.1 pad_maximum_fusion.2
  47.8 0.6 copy-done.5
  48.3 0.9 %convert_dynamic-update-slice_fusion.6 = f32[8,296,128]{2,1,0:T(8,128)S(1)} fusion(f32[8,296,128]{2,1,0:T(8,128)S(1)} %slice_dynamic-update-slice_fusion, f16[4,296,128]{2,1,0:T(8,128)(2,1)} %copy-done.5), kind=kLoop, calls=%fused_computation.11 | loop fusion | flops 37888 | bytes 227328
  49.2 0.7 collective-permute-done.2
  50.0 0.9 %convert_dynamic-update-slice_fusion.3 = f32[8,296,128]{2,1,0:T(8,128)S(1)} fusion(f32[8,296,128]{2,1,0:T(8,128)S(1)} %convert_dynamic-update-slice_fusion.4, f16[4,296,128]{2,1,0:T(8,128)(2,1)} %copy-done.4), kind=kLoop, calls=%fused_computation.8 | loop fusion | flops 37888 | bytes 227328
  50.9 11.2 %all-to-all-done.1 = bf16[32,8,1152]{2,1,0:T(8,128)(2,1)S(1)} async-done(((bf16[32,8,1152]{2,1,0:T(8,128)(2,1)}), bf16[32,8,1152]{2,1,0:T(8,128)(2,1)S(1)}, u32[]{:S(2)}, u32[]{:S(2)}) %all-to-all-start.1) | async-done | bytes 589856 | tf_op jit(solution)/shard_map/all_to_all | solution.py:421
  62.0 0.5 shard_map.71
  62.6 0.7 convert_bitcast_fusion
  63.2 3.6 %all-to-all-start.2 = ((f16[32,8,256]{2,1,0:T(8,128)(2,1)}), f16[32,8,256]{2,1,0:T(8,128)(2,1)S(1)}, u32[]{:S(2)}, u32[]{:S(2)}) async-start(f16[32,8,256]{2,1,0:T(8,128)(2,1)} %convert_bitcast_fusion), calls=%async_computation.2 | async-start | bytes 262144 | tf_op jit(solution)/shard_map/all_to_all | solution.py:436
  66.9 0.9 %convert_dynamic-update-slice_fusion.2 = f32[8,296,128]{2,1,0:T(8,128)S(1)} fusion(f32[8,296,128]{2,1,0:T(8,128)S(1)} %convert_dynamic-update-slice_fusion.3, f16[4,296,128]{2,1,0:T(8,128)(2,1)} %copy-done.5), kind=kLoop, calls=%fused_computation.7 | loop fusion | flops 37888 | bytes 227328
  67.8 7.7 %all-to-all-done.2 = f16[32,8,256]{2,1,0:T(8,128)(2,1)S(1)} async-done(((f16[32,8,256]{2,1,0:T(8,128)(2,1)}), f16[32,8,256]{2,1,0:T(8,128)(2,1)S(1)}, u32[]{:S(2)}, u32[]{:S(2)}) %all-to-all-start.2) | async-done | bytes 131104 | tf_op jit(solution)/shard_map/all_to_all | solution.py:436
  75.5 0.3 shard_map.72
  75.9 0.6 broadcast_in_dim.5
  76.5 3.4 %all-to-all-start.3 = ((f32[8,8,256]{2,1,0:T(8,128)}), f32[8,8,256]{2,1,0:T(8,128)S(1)}, u32[]{:S(2)}, u32[]{:S(2)}) async-start(f32[8,8,256]{2,1,0:T(8,128)} %broadcast_in_dim.5), calls=%async_computation.3 | async-start | bytes 131072 | tf_op jit(solution)/shard_map/all_to_all | solution.py:445
  79.9 1.1 %shard_map.70 = f32[36,64,128]{2,1,0:T(8,128)} custom-call(s32[1]{0:T(128)} %bitcast.me_ref, f32[8,296,128]{2,1,0:T(8,128)S(1)} %convert_dynamic-update-slice_fusion.pieces_ref), custom_call_target="tpu_custom_call" | custom-call | tf_op jit(solution)/shard_map/pallas_call | solution.py:448
  81.0 3.5 %all-to-all-done.3 = f32[8,8,256]{2,1,0:T(8,128)S(1)} async-done(((f32[8,8,256]{2,1,0:T(8,128)}), f32[8,8,256]{2,1,0:T(8,128)S(1)}, u32[]{:S(2)}, u32[]{:S(2)}) %all-to-all-start.3) | async-done | bytes 65568 | tf_op jit(solution)/shard_map/all_to_all | solution.py:445
  84.5 0.6 copy.18
  (25 shorter events, 0.4 us)
Async XLA Ops:
  0.6 1.6 %copy-start.3 = (s32[4,2]{0,1:T(2,128)S(1)}, s32[4,2]{0,1:T(2,128)}, u32[]{:S(2)}) copy-start(s32[4,2]{0,1:T(2,128)} %param.9) | copy-start | bytes 100
  0.6 1.6 %copy-start.2 = (f32[4,4]{1,0:T(4,128)S(1)}, f32[4,4]{1,0:T(4,128)}, u32[]{:S(2)}) copy-start(f32[4,4]{1,0:T(4,128)} %energies_ref.1) | copy-start | bytes 196
  0.7 1.6 %copy-start = (f32[4,4,5,128]{3,1,2,0:T(4,128)S(1)}, f32[4,4,5,128]{3,1,2,0:T(4,128)}, u32[]{:S(2)}) copy-start(f32[4,4,5,128]{3,1,2,0:T(4,128)} %param.7) | copy-start | bytes 122884
  0.7 1.6 %copy-start.1 = (f32[6,6,128]{2,1,0:T(8,128)S(1)}, f32[6,6,128]{2,1,0:T(8,128)}, u32[]{:S(2)}) copy-start(f32[6,6,128]{2,1,0:T(8,128)} %potential_ref.1) | copy-start | bytes 55300
  4.2 17.4 %all-to-all-start = ((f16[8,408,128]{2,1,0:T(8,128)(2,1)}), f16[8,408,128]{2,1,0:T(8,128)(2,1)S(1)}, u32[]{:S(2)}, u32[]{:S(2)}) async-start(f16[8,408,128]{2,1,0:T(8,128)(2,1)} %pad_maximum_fusion), calls=%async_computation | async-start | bytes 1671168 | tf_op jit(solution)/shard_map/all_to_all | solution.py:382
  29.2 9.2 %collective-permute-start = (f16[4,296,128]{2,1,0:T(8,128)(2,1)S(1)}, f16[4,296,128]{2,1,0:T(8,128)(2,1)S(1)}, u32[]{:S(2)}, u32[]{:S(2)}) collective-permute-start(f16[4,296,128]{2,1,0:T(8,128)(2,1)S(1)} %slice.94), channel_id=1, source_target_pairs={{0,4},{2,6},{4,0},{6,2},{1,5},{3,7},{5,1},{7,3},{8,12},{10,14},{12... | collective-permute-start | bytes 909320 | tf_op jit(solution)/shard_map/ppermute | solution.py:350
  38.4 0.7 copy-start.4
  39.3 8.3 %collective-permute-start.1 = (f16[4,296,128]{2,1,0:T(8,128)(2,1)S(1)}, f16[4,296,128]{2,1,0:T(8,128)(2,1)S(1)}, u32[]{:S(2)}, u32[]{:S(2)}) collective-permute-start(f16[4,296,128]{2,1,0:T(8,128)(2,1)S(1)} %pad_maximum_fusion.1), channel_id=1, source_target_pairs={{0,1},{1,0},{2,3},{3,2},{4,5},{5,4},{6,7},{7,6},{8,9},{9,8},{10,11... | collective-permute-start | bytes 909320 | tf_op jit(solution)/shard_map/ppermute | solution.py:350
  40.4 21.6 %all-to-all-start.1 = ((bf16[32,8,1152]{2,1,0:T(8,128)(2,1)}), bf16[32,8,1152]{2,1,0:T(8,128)(2,1)S(1)}, u32[]{:S(2)}, u32[]{:S(2)}) async-start(bf16[32,8,1152]{2,1,0:T(8,128)(2,1)} %get-tuple-element.5), calls=%async_computation.1 | async-start | bytes 1179648 | tf_op jit(solution)/shard_map/all_to_all | solution.py:421
  47.6 0.7 copy-start.5
  48.3 1.6 %collective-permute-start.2 = (f16[4,296,128]{2,1,0:T(8,128)(2,1)S(1)}, f16[4,296,128]{2,1,0:T(8,128)(2,1)S(1)}, u32[]{:S(2)}, u32[]{:S(2)}) collective-permute-start(f16[4,296,128]{2,1,0:T(8,128)(2,1)S(1)} %pad_maximum_fusion.2), channel_id=1, source_target_pairs={{0,2},{2,0},{4,6},{6,4},{1,3},{3,1},{5,7},{7,5},{8,10},{10,8},{12,... | collective-permute-start | bytes 909320 | tf_op jit(solution)/shard_map/ppermute | solution.py:350
  63.2 12.3 %all-to-all-start.2 = ((f16[32,8,256]{2,1,0:T(8,128)(2,1)}), f16[32,8,256]{2,1,0:T(8,128)(2,1)S(1)}, u32[]{:S(2)}, u32[]{:S(2)}) async-start(f16[32,8,256]{2,1,0:T(8,128)(2,1)} %convert_bitcast_fusion), calls=%async_computation.2 | async-start | bytes 262144 | tf_op jit(solution)/shard_map/all_to_all | solution.py:436
  76.5 8.0 %all-to-all-start.3 = ((f32[8,8,256]{2,1,0:T(8,128)}), f32[8,8,256]{2,1,0:T(8,128)S(1)}, u32[]{:S(2)}, u32[]{:S(2)}) async-start(f32[8,8,256]{2,1,0:T(8,128)} %broadcast_in_dim.5), calls=%async_computation.3 | async-start | bytes 131072 | tf_op jit(solution)/shard_map/all_to_all | solution.py:445

commit v6 on v5

--- a/solution.py
+++ b/solution.py
@@ -92,7 +92,7 @@
     each,
     atoms,
     projs,
-    me_ref,
+    by_swaps,
     got_ref,
     field_ref,
     rounded_ref,
@@ -256,9 +256,10 @@
     largest = lax.fori_loop(0, count_x, largest_of, jnp.zeros((each, nz), jnp.float32))
     level, gain = level_of(jnp.max(largest))
     level_rows = jnp.full((8, nz), level, jnp.float32)
+    me = lax.axis_index("sx") * slabs_y + lax.axis_index("sy") if by_swaps else 0
 
     def give_slab(g, carry):
-        slot = jnp.bitwise_xor(g, me_ref[0])
+        slot = jnp.bitwise_xor(g, me) if by_swaps else g
         field_ref[slot, pl.ds(slab_cells * each, 8), :] = level_rows
         x0 = (g // slabs_y) * cells_x
         y0 = (g % slabs_y) * cells_y
@@ -287,13 +288,15 @@
     out_ref[...] = jnp.where(spare, level, sums * gain)
 
 
-def rows_kernel(cells, first_ref, parts_ref, out_ref):
+def rows_kernel(cells, plane_shape, parts_ref, out_ref):
     count, each, columns = parts_ref.shape
     if each > 1:
+        band = lax.axis_index("band") * plane_shape[0] + lax.axis_index("sx")
+        first = (band * plane_shape[1] + lax.axis_index("sy")) * each
         row = lax.broadcasted_iota(jnp.int32, (each, columns), 0)
         column = lax.broadcasted_iota(jnp.int32, (each, columns), 1)
-        spare = (row == 1) & (column == first_ref[0])
-        twin = (row == 0) & (column == first_ref[0] + 1)
+        spare = (row == 1) & (column == first)
+        twin = (row == 0) & (column == first + 1)
 
         def entry(block, place):
             picked = jnp.where(place, block, 0.0)
@@ -309,22 +312,24 @@
     out_ref[...] = total / cells
 
 
-def unpack_kernel(each, me_ref, pieces_ref, filtered_hbm, filtered_ref, chunk_sems):
-    group, _, nz = pieces_ref.shape
-    slab_cells = filtered_ref.shape[0]
+def unpack_kernel(each, slabs_y, places, *refs):
+    pieces = refs[:-3]
+    filtered_hbm, filtered_ref, chunk_sems = refs[-3:]
+    slab_cells, _, nz = filtered_ref.shape
     chunks = chunk_sems.shape[0]
     chunk = slab_cells // chunks
+    me = lax.axis_index("sx") * slabs_y + lax.axis_index("sy") if len(pieces) > 1 else 0
     copies = []
     for c in range(chunks):
-        for slot in range(group):
-            shrink = shrink_of(pieces_ref[slot, pl.ds(slab_cells * each, 1), :])
-            if each % 8 == 0:
-                source = jnp.bitwise_xor(me_ref[0], slot)
-                rows = pl.ds(pl.multiple_of(source * each, each), each)
+        for which, entry, other in places:
+            piece = pieces[which]
+            shrink = shrink_of(piece[entry, pl.ds(slab_cells * each, 1), :])
+            if len(pieces) > 1:
+                rows = pl.ds(pl.multiple_of(jnp.bitwise_xor(me, other) * each, each), each)
             else:
-                rows = pl.ds(slot * each, each)
+                rows = pl.ds(other * each, each)
             for cell in range(c * chunk, (c + 1) * chunk):
-                filtered_ref[cell, rows, :] = pieces_ref[slot, pl.ds(cell * each, each), :] * shrink
+                filtered_ref[cell, rows, :] = piece[entry, pl.ds(cell * each, each), :] * shrink
         part = pl.ds(c * chunk, chunk)
         copies.append(
             pltpu.make_async_copy(filtered_ref.at[part], filtered_hbm.at[part], chunk_sems.at[c])
@@ -334,24 +339,11 @@
         copy.wait()
 
 
-def swap_stages(slabs_x, slabs_y):
-    stages = [("sx", 1 << k) for k in range(slabs_x.bit_length() - 1)]
-    stages = stages[1:] + [("sy", 1 << k) for k in range(slabs_y.bit_length() - 1)] + stages[:1]
-    return [(axis, bit, bit * (slabs_y if axis == "sx" else 1)) for axis, bit in stages]
-
-
-def swap_pieces(field, stages):
-    group = field.shape[0]
-    held = {(r, 0): field[r] for r in range(group)}
-    for axis, bit, value in stages:
-        leaving = sorted(key for key in held if key[0] & value)
-        pairs = [(i, i ^ bit) for i in range(lax.axis_size(axis))]
-        sent = jnp.stack([held[key].astype(jnp.float16) for key in leaving])
-        came = lax.ppermute(sent, axis, pairs)
-        held = {key: piece for key, piece in held.items() if not key[0] & value}
-        for i, (to, origin) in enumerate(leaving):
-            held[(to ^ value, origin ^ value)] = came[i]
-    return jnp.stack([held[(0, r)].astype(jnp.float32) for r in range(group)])
+def swap(pieces, value):
+    group = lax.axis_size(plane)
+    return lax.ppermute(
+        jnp.stack(pieces).astype(jnp.float16), plane, [(i, i ^ value) for i in range(group)]
+    )
 
 
 def local(orbitals, potential, projectors, energies, centers):
@@ -381,16 +373,15 @@
     sent = jnp.concatenate([chunks, jnp.broadcast_to(shared[None], (group, rows, nz))], axis=1)
     got = lax.all_to_all(sent, plane, 0, 0).astype(jnp.float32)
 
-    stages = swap_stages(slabs_x, slabs_y)
-    by_swaps = group <= 8 and each % 8 == 0 and group == 1 << len(stages)
-    place = lax.axis_index(plane).astype(jnp.int32).reshape(1)
-    me = place if by_swaps else jnp.zeros((1,), jnp.int32)
+    near = slabs_y
+    far = [v for v in range(1, group) if not v & near]
+    by_swaps = group <= 8 and each % 8 == 0 and slabs_x > 1 and group & (group - 1) == 0
 
     portion = slab_cells // bands
     ringed = (grid[0] + 2, grid[1] + 2, each, nz)
     field, rounded = pl.pallas_call(
-        functools.partial(filter_kernel, slabs_y, cells_x, cells_y, each, atoms, projs),
-        in_specs=[smem, vmem],
+        functools.partial(filter_kernel, slabs_y, cells_x, cells_y, each, atoms, projs, by_swaps),
+        in_specs=[vmem],
         out_specs=[vmem] * 2,
         out_shape=[
             jax.ShapeDtypeStruct((group, slab_cells * each + 8, nz), jnp.float32),
@@ -411,14 +402,21 @@
             bytes_accessed=8 * grid[0] * grid[1] * each * nz,
             transcendentals=0,
         ),
-    )(me, got)
-
+    )(got)
+
+    matrix = lax.all_to_all(rounded, every, 0, 0).reshape(total_orbitals, portion * nz)
     if by_swaps:
-        pieces = swap_pieces(field, stages)
+        came = [swap([field[v], field[v | near]], v) for v in far]
+        came, matrix = lax.optimization_barrier((came, matrix))
+        came.append(swap([field[near]] + [block[1] for block in came], near))
+        pieces = [field] + [block.astype(jnp.float32) for block in came]
+        places = [(0, 0, 0), (len(pieces) - 1, 0, near)]
+        for i, v in enumerate(far):
+            places += [(i + 1, 0, v), (len(pieces) - 1, i + 1, v | near)]
     else:
-        pieces = lax.all_to_all(field.astype(jnp.float16), plane, 0, 0).astype(jnp.float32)
-
-    matrix = lax.all_to_all(rounded, every, 0, 0).reshape(total_orbitals, portion * nz)
+        pieces = [lax.all_to_all(field.astype(jnp.float16), plane, 0, 0).astype(jnp.float32)]
+        places = [(0, g, g) for g in range(group)]
+
     spread = (bands * group, each, total_orbitals)
     if each > 1:
         sums = pl.pallas_call(
@@ -434,20 +432,19 @@
             matrix, matrix, (((1,), (1,)), ((), ())), preferred_element_type=jnp.float32
         ).reshape(spread)
     parts = lax.all_to_all(sums, every, 0, 0).astype(jnp.float32)
-    first_row = (lax.axis_index("band").astype(jnp.int32) * group + place) * each
     rows = pl.pallas_call(
-        functools.partial(rows_kernel, grid[0] * grid[1] * nz),
-        in_specs=[smem, vmem],
+        functools.partial(rows_kernel, grid[0] * grid[1] * nz, (slabs_x, slabs_y)),
+        in_specs=[vmem],
         out_specs=vmem,
         out_shape=jax.ShapeDtypeStruct((each, total_orbitals), jnp.float32),
         compiler_params=params,
-    )(first_row, parts)
+    )(parts)
     gram = lax.all_to_all(jnp.broadcast_to(rows[None], (group,) + rows.shape), plane, 0, 0)
     gram = gram.reshape(band_orbitals, total_orbitals)
 
     filtered = pl.pallas_call(
-        functools.partial(unpack_kernel, each),
-        in_specs=[smem, vmem],
+        functools.partial(unpack_kernel, each, slabs_y, places),
+        in_specs=[vmem] * len(pieces),
         out_specs=hbm,
         out_shape=jax.ShapeDtypeStruct((slab_cells, band_orbitals, nz), jnp.float32),
         scratch_shapes=[
@@ -455,7 +452,7 @@
             pltpu.SemaphoreType.DMA((cells_x,)),
         ],
         compiler_params=params,
-    )(me, pieces)
+    )(*pieces)
     filtered = filtered.reshape(cells_x, cells_y, band_orbitals, nz).transpose(2, 0, 1, 3)
     return (filtered, gram)
 

time: 85.7 us -> 73.1 us (0.85)
  waiting for transfers between devices: 45.1 us -> 24.2 us
  blocking collectives: 0 us -> 17.8 us
  starting transfers between devices: 19.9 us -> 15.2 us
  other arithmetic: 6.44 us -> 2.93 us
  local copies, waits for them, and re-layouts: 2.92 us -> 1.61 us
    all_to_all x0 -> x1, blocking collectives: none -> 17.8 us  [local(): got = lax.all_to_all(sent, plane, 0, 0).astype(jnp.float32)]
    all_to_all x1 -> x0, waiting for transfers between devices: 12.3 us -> none  [local(): got = lax.all_to_all(sent, plane, 0, 0).astype(jnp.float32)]
    all_to_all x1, waiting for transfers between devices: 11.2 us -> 0.01 us  [local(): lax.all_to_all(rounded, every, 0, 0).reshape(total_orbitals, portion * nz)]
    all_to_all x1 -> x0, starting transfers between devices: 5.17 us -> none  [local(): got = lax.all_to_all(sent, plane, 0, 0).astype(jnp.float32)]
    unnamed x6 -> x0, other arithmetic: 2.74 us -> none
    ppermute x3 -> x4, waiting for transfers between devices: 10.4 us -> 12.7 us  [swap(): lax.ppermute(jnp.stack(pieces).astype(jnp.float16), plane, [(i, i ^ value...]
    ppermute x3 -> x4, starting transfers between devices: 2.53 us -> 4 us  [swap(): lax.ppermute(jnp.stack(pieces).astype(jnp.float16), plane, [(i, i ^ value...]
    unnamed x14 -> x9, local copies, waits for them, and re-layouts: 1.93 us -> 0.65 us
  transfers between devices with their start and end apart: 7 -> 7, of which waited for: 7 -> 5; matrix products, arithmetic and copies ran while one was open for 3% -> 2% of each run, Pallas kernels for 1% -> 2%
where the time goes in v6:
time: 73.1 us; the launch traced here: 72.7 us
  waiting for transfers between devices  24.2 us (33%)
  blocking collectives  17.8 us (24%)
  starting transfers between devices  15.2 us (21%)
  Pallas kernels  10 us (14%)
  other arithmetic  2.93 us (4%)
  local copies, waits for them, and re-layouts  1.61 us (2%)
  between operations  0.89 us (1%)
    all_to_all x1, blocking collectives, local(): got = lax.all_to_all(sent, plane, 0, 0).astype(jnp.float32)  17.8 us
    ppermute x4, waiting for transfers between devices, swap(): lax.ppermute(jnp.stack(pieces).astype(jnp.float16), plane, [(i, i ^ value...  12.7 us
    all_to_all x1, waiting for transfers between devices, local(): parts = lax.all_to_all(sums, every, 0, 0).astype(jnp.float32)  8.11 us
    pallas_call x1, Pallas kernels, local(): pl.pallas_call(functools.partial(filter_kernel, slabs_y, cells_x, cells_y...  7.33 us
    all_to_all x1, starting transfers between devices, local(): lax.all_to_all(rounded, every, 0, 0).reshape(total_orbitals, portion * nz)  4.17 us
    ppermute x4, starting transfers between devices, swap(): lax.ppermute(jnp.stack(pieces).astype(jnp.float16), plane, [(i, i ^ value...  4 us
    all_to_all x1, starting transfers between devices, local(): parts = lax.all_to_all(sums, every, 0, 0).astype(jnp.float32)  3.68 us
    all_to_all x1, waiting for transfers between devices, local(): lax.all_to_all(jnp.broadcast_to(rows[None], (group,) + rows.shape), plane...  3.41 us
  transfers between devices with their start and end apart: 7, of which 5 were waited for; matrix products, arithmetic and copies ran while one was open for 2% of the time, Pallas kernels for 2%

profile of v6, /device:TPU:0, one launch (start us, length us, event | category | flops | bytes accessed | tf_op | source)
XLA Modules:
  0.0 72.7 jit_solution(16098613936282441184)
XLA Ops:
  0.6 0.0 copy-start.3
  0.6 0.0 copy-start.2
  0.7 1.5 %multiply_convert_fusion = f16[64,6,6,128]{3,0,2,1:T(8,128)(2,1)S(1)} fusion(f32[64,6,6,128]{3,0,2,1:T(8,128)} %param.5), kind=kLoop, calls=%fused_computation | loop fusion | flops 589824 | bytes 1769472 | tf_op jit(solution)/shard_map/convert_element_type | solution.py:363
  2.1 0.1 copy.9
  2.3 0.7 shard_map.68
  3.0 0.2 pad_maximum_fusion
  3.3 17.8 %all_to_all.20 = f16[8,408,128]{2,1,0:T(8,128)(2,1)S(1)} all-to-all(f16[8,408,128]{2,1,0:T(8,128)(2,1)S(1)} %pad_maximum_fusion), channel_id=1, replica_groups=mesh['band'=4,'sx'=4,'sy'=2] {'sx','sy'}, dimensions={0} | all-to-all | bytes 1671168 | tf_op jit(solution)/shard_map/all_to_all | solution.py:374
  21.1 0.1 convert_element_type.46.got_ref
  21.2 7.3 %shard_map.69 = (f32[8,296,128]{2,1,0:T(8,128)S(1)}, bf16[32,8,1152]{2,1,0:T(8,128)(2,1)}) custom-call(f32[8,408,128]{2,1,0:T(8,128)S(1)} %convert_element_type.46.got_ref), custom_call_target="tpu_custom_call" | custom-call | flops 47185920 | bytes 2359296 | tf_op jit(solution)/shard_map/pallas_call | solution.py:382
  28.6 4.2 %all-to-all-start.1 = ((bf16[32,8,1152]{2,1,0:T(8,128)(2,1)}), bf16[32,8,1152]{2,1,0:T(8,128)(2,1)S(1)}, u32[]{:S(2)}, u32[]{:S(2)}) async-start(bf16[32,8,1152]{2,1,0:T(8,128)(2,1)} %get-tuple-element.9), calls=%async_computation.1 | async-start | bytes 1179648 | tf_op jit(solution)/shard_map/all_to_all | solution.py:407
  32.8 0.1 convert.20
  32.8 0.1 fusion.1
  33.0 1.8 %collective-permute-start = (f16[2,296,128]{2,1,0:T(8,128)(2,1)S(1)}, f16[2,296,128]{2,1,0:T(8,128)(2,1)S(1)}, u32[]{:S(2)}, u32[]{:S(2)}) collective-permute-start(f16[2,296,128]{2,1,0:T(8,128)(2,1)S(1)} %pad_maximum_fusion.2), channel_id=1, source_target_pairs={{0,1},{1,0},{2,3},{3,2},{4,5},{5,4},{6,7},{7,6},{8,9},{9,8},{10,11... | collective-permute-start | bytes 454664 | tf_op jit(solution)/shard_map/ppermute | solution.py:344
  34.9 1.5 %collective-permute-start.1 = (f16[2,296,128]{2,1,0:T(8,128)(2,1)S(1)}, f16[2,296,128]{2,1,0:T(8,128)(2,1)S(1)}, u32[]{:S(2)}, u32[]{:S(2)}) collective-permute-start(f16[2,296,128]{2,1,0:T(8,128)(2,1)S(1)} %pad_maximum_fusion.3), channel_id=1, source_target_pairs={{0,4},{1,5},{2,6},{3,7},{4,0},{5,1},{6,2},{7,3},{8,12},{9,13},{10,... | collective-permute-start | bytes 454664 | tf_op jit(solution)/shard_map/ppermute | solution.py:344
  36.5 0.3 collective-permute-start.2
  36.8 6.5 %collective-permute-done = f16[2,296,128]{2,1,0:T(8,128)(2,1)S(1)} collective-permute-done((f16[2,296,128]{2,1,0:T(8,128)(2,1)S(1)}, f16[2,296,128]{2,1,0:T(8,128)(2,1)S(1)}, u32[]{:S(2)}, u32[]{:S(2)}) %collective-permute-start) | collective-permute-done | bytes 151584 | tf_op jit(solution)/shard_map/ppermute | solution.py:344
  43.3 1.0 %collective-permute-done.1 = f16[2,296,128]{2,1,0:T(8,128)(2,1)S(1)} collective-permute-done((f16[2,296,128]{2,1,0:T(8,128)(2,1)S(1)}, f16[2,296,128]{2,1,0:T(8,128)(2,1)S(1)}, u32[]{:S(2)}, u32[]{:S(2)}) %collective-permute-start.1) | collective-permute-done | bytes 151584 | tf_op jit(solution)/shard_map/ppermute | solution.py:344
  44.2 5.3 %collective-permute-done.2 = f16[2,296,128]{2,1,0:T(8,128)(2,1)S(1)} collective-permute-done((f16[2,296,128]{2,1,0:T(8,128)(2,1)S(1)}, f16[2,296,128]{2,1,0:T(8,128)(2,1)S(1)}, u32[]{:S(2)}, u32[]{:S(2)}) %collective-permute-start.2) | collective-permute-done | bytes 151584 | tf_op jit(solution)/shard_map/ppermute | solution.py:344
  49.5 0.0 all-to-all-done.1
  49.5 0.5 shard_map.71
  50.0 0.7 convert_bitcast_fusion
  50.7 3.7 %all-to-all-start.2 = ((f16[32,8,256]{2,1,0:T(8,128)(2,1)}), f16[32,8,256]{2,1,0:T(8,128)(2,1)S(1)}, u32[]{:S(2)}, u32[]{:S(2)}) async-start(f16[32,8,256]{2,1,0:T(8,128)(2,1)} %convert_bitcast_fusion), calls=%async_computation.2 | async-start | bytes 262144 | tf_op jit(solution)/shard_map/all_to_all | solution.py:434
  54.5 0.1 pad_maximum_fusion.1
  54.6 0.3 collective-permute-start.3
  54.9 8.1 %all-to-all-done.2 = f16[32,8,256]{2,1,0:T(8,128)(2,1)S(1)} async-done(((f16[32,8,256]{2,1,0:T(8,128)(2,1)}), f16[32,8,256]{2,1,0:T(8,128)(2,1)S(1)}, u32[]{:S(2)}, u32[]{:S(2)}) %all-to-all-start.2) | async-done | bytes 131104 | tf_op jit(solution)/shard_map/all_to_all | solution.py:434
  63.1 0.3 shard_map.72
  63.4 0.6 broadcast_in_dim.5
  64.0 3.4 %all-to-all-start.3 = ((f32[8,8,256]{2,1,0:T(8,128)}), f32[8,8,256]{2,1,0:T(8,128)S(1)}, u32[]{:S(2)}, u32[]{:S(2)}) async-start(f32[8,8,256]{2,1,0:T(8,128)} %broadcast_in_dim.5), calls=%async_computation.3 | async-start | bytes 131072 | tf_op jit(solution)/shard_map/all_to_all | solution.py:442
  67.5 0.0 collective-permute-done.3
  67.6 1.1 %shard_map.70 = f32[36,64,128]{2,1,0:T(8,128)} custom-call(f32[8,296,128]{2,1,0:T(8,128)S(1)} %get-tuple-element.8.refs_0_, f32[2,296,128]{2,1,0:T(8,128)S(1)} %convert_element_type.47.refs_1_, f32[2,296,128]{2,1,0:T(8,128)S(1)} %convert_element_type.48.refs_2_, f32[2,296,128]{2,1,0:T(8,128)S(1)} %convert_element_type.49.refs_3_, ...), custom_call_target="tpu_custom_call" | custom-call | tf_op jit(solution)/shard_map/pallas_call | solution.py:445
  68.7 3.4 %all-to-all-done.3 = f32[8,8,256]{2,1,0:T(8,128)S(1)} async-done(((f32[8,8,256]{2,1,0:T(8,128)}), f32[8,8,256]{2,1,0:T(8,128)S(1)}, u32[]{:S(2)}, u32[]{:S(2)}) %all-to-all-start.3) | async-done | bytes 65568 | tf_op jit(solution)/shard_map/all_to_all | solution.py:442
  72.1 0.6 copy.11
  (20 shorter events, 0.4 us)
Async XLA Ops:
  0.6 1.6 %copy-start.3 = (s32[4,2]{0,1:T(2,128)S(1)}, s32[4,2]{0,1:T(2,128)}, u32[]{:S(2)}) copy-start(s32[4,2]{0,1:T(2,128)} %param.9) | copy-start | bytes 100
  0.6 1.6 %copy-start.2 = (f32[4,4]{1,0:T(4,128)S(1)}, f32[4,4]{1,0:T(4,128)}, u32[]{:S(2)}) copy-start(f32[4,4]{1,0:T(4,128)} %energies_ref.1) | copy-start | bytes 196
  0.7 1.6 %copy-start = (f32[4,4,5,128]{3,1,2,0:T(4,128)S(1)}, f32[4,4,5,128]{3,1,2,0:T(4,128)}, u32[]{:S(2)}) copy-start(f32[4,4,5,128]{3,1,2,0:T(4,128)} %param.7) | copy-start | bytes 122884
  0.7 1.6 %copy-start.1 = (f32[6,6,128]{2,1,0:T(8,128)S(1)}, f32[6,6,128]{2,1,0:T(8,128)}, u32[]{:S(2)}) copy-start(f32[6,6,128]{2,1,0:T(8,128)} %potential_ref.1) | copy-start | bytes 55300
  28.6 20.9 %all-to-all-start.1 = ((bf16[32,8,1152]{2,1,0:T(8,128)(2,1)}), bf16[32,8,1152]{2,1,0:T(8,128)(2,1)S(1)}, u32[]{:S(2)}, u32[]{:S(2)}) async-start(bf16[32,8,1152]{2,1,0:T(8,128)(2,1)} %get-tuple-element.9), calls=%async_computation.1 | async-start | bytes 1179648 | tf_op jit(solution)/shard_map/all_to_all | solution.py:407
  33.0 10.3 %collective-permute-start = (f16[2,296,128]{2,1,0:T(8,128)(2,1)S(1)}, f16[2,296,128]{2,1,0:T(8,128)(2,1)S(1)}, u32[]{:S(2)}, u32[]{:S(2)}) collective-permute-start(f16[2,296,128]{2,1,0:T(8,128)(2,1)S(1)} %pad_maximum_fusion.2), channel_id=1, source_target_pairs={{0,1},{1,0},{2,3},{3,2},{4,5},{5,4},{6,7},{7,6},{8,9},{9,8},{10,11... | collective-permute-start | bytes 454664 | tf_op jit(solution)/shard_map/ppermute | solution.py:344
  34.9 9.3 %collective-permute-start.1 = (f16[2,296,128]{2,1,0:T(8,128)(2,1)S(1)}, f16[2,296,128]{2,1,0:T(8,128)(2,1)S(1)}, u32[]{:S(2)}, u32[]{:S(2)}) collective-permute-start(f16[2,296,128]{2,1,0:T(8,128)(2,1)S(1)} %pad_maximum_fusion.3), channel_id=1, source_target_pairs={{0,4},{1,5},{2,6},{3,7},{4,0},{5,1},{6,2},{7,3},{8,12},{9,13},{10,... | collective-permute-start | bytes 454664 | tf_op jit(solution)/shard_map/ppermute | solution.py:344
  36.5 13.0 %collective-permute-start.2 = (f16[2,296,128]{2,1,0:T(8,128)(2,1)S(1)}, f16[2,296,128]{2,1,0:T(8,128)(2,1)S(1)}, u32[]{:S(2)}, u32[]{:S(2)}) collective-permute-start(f16[2,296,128]{2,1,0:T(8,128)(2,1)S(1)} %pad_maximum_fusion.4), channel_id=1, source_target_pairs={{0,5},{1,4},{2,7},{3,6},{4,1},{5,0},{6,3},{7,2},{8,13},{9,12},{10,... | collective-permute-start | bytes 454664 | tf_op jit(solution)/shard_map/ppermute | solution.py:344
  50.7 12.3 %all-to-all-start.2 = ((f16[32,8,256]{2,1,0:T(8,128)(2,1)}), f16[32,8,256]{2,1,0:T(8,128)(2,1)S(1)}, u32[]{:S(2)}, u32[]{:S(2)}) async-start(f16[32,8,256]{2,1,0:T(8,128)(2,1)} %convert_bitcast_fusion), calls=%async_computation.2 | async-start | bytes 262144 | tf_op jit(solution)/shard_map/all_to_all | solution.py:434
  54.6 12.9 %collective-permute-start.3 = (f16[4,296,128]{2,1,0:T(8,128)(2,1)S(1)}, f16[4,296,128]{2,1,0:T(8,128)(2,1)S(1)}, u32[]{:S(2)}, u32[]{:S(2)}) collective-permute-start(f16[4,296,128]{2,1,0:T(8,128)(2,1)S(1)} %pad_maximum_fusion.1), channel_id=1, source_target_pairs={{0,2},{1,3},{2,0},{3,1},{4,6},{5,7},{6,4},{7,5},{8,10},{9,11},{10,... | collective-permute-start | bytes 909320 | tf_op jit(solution)/shard_map/ppermute | solution.py:344
  64.0 8.0 %all-to-all-start.3 = ((f32[8,8,256]{2,1,0:T(8,128)}), f32[8,8,256]{2,1,0:T(8,128)S(1)}, u32[]{:S(2)}, u32[]{:S(2)}) async-start(f32[8,8,256]{2,1,0:T(8,128)} %broadcast_in_dim.5), calls=%async_computation.3 | async-start | bytes 131072 | tf_op jit(solution)/shard_map/all_to_all | solution.py:442

commit v7 on v6

--- a/solution.py
+++ b/solution.py
@@ -276,40 +276,44 @@
     lax.fori_loop(0, group, give_slab, 0)
 
 
-def gram_kernel(each, matrix_ref, out_ref):
+def entry(block, place):
+    picked = jnp.where(place, block, 0.0)
+    return jnp.sum(jnp.sum(picked, axis=0, keepdims=True), axis=1, keepdims=True)
+
+
+def band_corner(shape, band):
+    row = lax.broadcasted_iota(jnp.int32, shape, 0)
+    column = lax.broadcasted_iota(jnp.int32, shape, 1)
+    return (
+        (row == 1) & (column == band * shape[0]),
+        (row == 0) & (column == band * shape[0] + 1),
+    )
+
+
+def gram_kernel(matrix_ref, out_ref, sums_ref):
+    bands, rows, columns = out_ref.shape
     matrix = matrix_ref[...]
     sums = lax.dot_general(
         matrix, matrix, (((1,), (1,)), ((), ())), preferred_element_type=jnp.float32
     )
     level, gain = level_of(jnp.max(jnp.abs(sums)))
-    row = lax.broadcasted_iota(jnp.int32, sums.shape, 0)
-    column = lax.broadcasted_iota(jnp.int32, sums.shape, 1)
-    spare = (column == row - 1) & (row % each == 1)
-    out_ref[...] = jnp.where(spare, level, sums * gain)
-
-
-def rows_kernel(cells, plane_shape, parts_ref, out_ref):
-    count, each, columns = parts_ref.shape
-    if each > 1:
-        band = lax.axis_index("band") * plane_shape[0] + lax.axis_index("sx")
-        first = (band * plane_shape[1] + lax.axis_index("sy")) * each
-        row = lax.broadcasted_iota(jnp.int32, (each, columns), 0)
-        column = lax.broadcasted_iota(jnp.int32, (each, columns), 1)
-        spare = (row == 1) & (column == first)
-        twin = (row == 0) & (column == first + 1)
-
-        def entry(block, place):
-            picked = jnp.where(place, block, 0.0)
-            return jnp.sum(jnp.sum(picked, axis=0, keepdims=True), axis=1, keepdims=True)
-
-        total = jnp.zeros((each, columns), jnp.float32)
-        for source in range(count):
-            block = parts_ref[source]
-            total = total + block * shrink_of(entry(block, spare))
-        total = jnp.where(spare, entry(total, twin), total)
-    else:
-        total = jnp.sum(parts_ref[...], axis=0)
-    out_ref[...] = total / cells
+    sums_ref[...] = sums * gain
+    me = lax.axis_index("band")
+    for k in range(bands):
+        band = jnp.bitwise_xor(me, k)
+        spare, _ = band_corner((rows, columns), band)
+        block = sums_ref[pl.ds(pl.multiple_of(band * rows, rows), rows), :]
+        out_ref[k] = jnp.where(spare, level, block)
+
+
+def rows_kernel(cells, own_ref, *refs):
+    out_ref = refs[-1]
+    spare, twin = band_corner(out_ref.shape, lax.axis_index("band"))
+    total = None
+    for block in [own_ref[0]] + [ref[...] for ref in refs[:-1]]:
+        block = block * shrink_of(entry(block, spare))
+        total = block if total is None else total + block
+    out_ref[...] = jnp.where(spare, entry(total, twin), total) / cells
 
 
 def unpack_kernel(each, slabs_y, places, *refs):
@@ -375,7 +379,8 @@
 
     near = slabs_y
     far = [v for v in range(1, group) if not v & near]
-    by_swaps = group <= 8 and each % 8 == 0 and slabs_x > 1 and group & (group - 1) == 0
+    by_swaps = group <= 8 and each % 8 == 0 and slabs_x > 1
+    by_swaps = by_swaps and group & (group - 1) == 0 and bands & (bands - 1) == 0
 
     portion = slab_cells // bands
     ringed = (grid[0] + 2, grid[1] + 2, each, nz)
@@ -417,30 +422,45 @@
         pieces = [lax.all_to_all(field.astype(jnp.float16), plane, 0, 0).astype(jnp.float32)]
         places = [(0, g, g) for g in range(group)]
 
-    spread = (bands * group, each, total_orbitals)
-    if each > 1:
+    cells = grid[0] * grid[1] * nz
+    if by_swaps:
         sums = pl.pallas_call(
-            functools.partial(gram_kernel, each),
+            gram_kernel,
             in_specs=[vmem],
             out_specs=vmem,
-            out_shape=jax.ShapeDtypeStruct((total_orbitals, total_orbitals), jnp.float32),
+            out_shape=jax.ShapeDtypeStruct((bands, band_orbitals, total_orbitals), jnp.float32),
+            scratch_shapes=[pltpu.VMEM((total_orbitals, total_orbitals), jnp.float32)],
             compiler_params=params,
         )(matrix)
-        sums = sums.astype(jnp.float16).reshape(spread)
+        parts = [
+            lax.ppermute(
+                sums[k].astype(jnp.float16), "band", [(i, i ^ k) for i in range(bands)]
+            ).astype(jnp.float32)
+            for k in range(1, bands)
+        ]
+        gram = pl.pallas_call(
+            functools.partial(rows_kernel, cells),
+            in_specs=[vmem] * bands,
+            out_specs=vmem,
+            out_shape=jax.ShapeDtypeStruct((band_orbitals, total_orbitals), jnp.float32),
+            compiler_params=params,
+        )(sums, *parts)
+        terms = {v: lax.ppermute(gram, plane, [(i, i ^ v) for i in range(group)]) for v in far}
+        terms[0] = gram
+        bit = 1
+        while len(terms) > 1:
+            terms = {v: terms[v] + terms[v ^ bit] for v in terms if not v & bit and v ^ bit in terms} or terms
+            bit *= 2
+        gram = terms[0]
+        gram = gram + lax.ppermute(gram, plane, [(i, i ^ near) for i in range(group)])
     else:
         sums = lax.dot_general(
             matrix, matrix, (((1,), (1,)), ((), ())), preferred_element_type=jnp.float32
-        ).reshape(spread)
-    parts = lax.all_to_all(sums, every, 0, 0).astype(jnp.float32)
-    rows = pl.pallas_call(
-        functools.partial(rows_kernel, grid[0] * grid[1] * nz, (slabs_x, slabs_y)),
-        in_specs=[vmem],
-        out_specs=vmem,
-        out_shape=jax.ShapeDtypeStruct((each, total_orbitals), jnp.float32),
-        compiler_params=params,
-    )(parts)
-    gram = lax.all_to_all(jnp.broadcast_to(rows[None], (group,) + rows.shape), plane, 0, 0)
-    gram = gram.reshape(band_orbitals, total_orbitals)
+        )
+        parts = lax.all_to_all(sums.reshape(bands * group, each, total_orbitals), every, 0, 0)
+        rows = jnp.sum(parts, axis=0) / cells
+        gram = lax.all_to_all(jnp.broadcast_to(rows[None], (group,) + rows.shape), plane, 0, 0)
+        gram = gram.reshape(band_orbitals, total_orbitals)
 
     filtered = pl.pallas_call(
         functools.partial(unpack_kernel, each, slabs_y, places),

time: 73.1 us -> 68.1 us (0.932)
  waiting for transfers between devices: 24.2 us -> 20 us
  local copies, waits for them, and re-layouts: 1.61 us -> 0.36 us
    all_to_all x2 -> x0, waiting for transfers between devices: 11.5 us -> none  [the longest x1 8.11 us: local(): parts = lax.all_to_all(sums, every, 0, 0).astype(jnp.float32)]
    ppermute x0 -> x7, starting transfers between devices: none -> 8.01 us  [the longest x3 4.45 us: local(): lax.ppermute(sums[k].astype(jnp.float16), 'band', [(i, i ^ k) for i in ra...]
    ppermute x0 -> x7, waiting for transfers between devices: none -> 7.28 us  [the longest x3 3.61 us: local(): lax.ppermute(sums[k].astype(jnp.float16), 'band', [(i, i ^ k) for i in ra...]
    all_to_all x2 -> x0, starting transfers between devices: 7.03 us -> none  [the longest x1 3.68 us: local(): parts = lax.all_to_all(sums, every, 0, 0).astype(jnp.float32)]
  transfers between devices with their start and end apart: 7 -> 12, of which waited for: 5 -> 8; matrix products, arithmetic and copies ran while one was open for 2% -> 2% of each run, Pallas kernels for 2% -> 0%
where the time goes in v7:
time: 68.1 us; the launch traced here: 67.8 us
  waiting for transfers between devices  20 us (29%)
  blocking collectives  17.8 us (26%)
  starting transfers between devices  15.9 us (23%)
  Pallas kernels  9.86 us (14%)
  other arithmetic  2.93 us (4%)
  between operations  0.9 us (1%)
    all_to_all x1, blocking collectives, local(): got = lax.all_to_all(sent, plane, 0, 0).astype(jnp.float32)  17.8 us
    ppermute x4, waiting for transfers between devices, swap(): lax.ppermute(jnp.stack(pieces).astype(jnp.float16), plane, [(i, i ^ value...  12.7 us
    pallas_call x1, Pallas kernels, local(): pl.pallas_call(functools.partial(filter_kernel, slabs_y, cells_x, cells_y...  7.34 us
    ppermute x3, starting transfers between devices, local(): lax.ppermute(sums[k].astype(jnp.float16), 'band', [(i, i ^ k) for i in ra...  4.45 us
    all_to_all x1, starting transfers between devices, local(): lax.all_to_all(rounded, every, 0, 0).reshape(total_orbitals, portion * nz)  4.17 us
    ppermute x4, starting transfers between devices, swap(): lax.ppermute(jnp.stack(pieces).astype(jnp.float16), plane, [(i, i ^ value...  3.75 us
    ppermute x3, waiting for transfers between devices, local(): lax.ppermute(sums[k].astype(jnp.float16), 'band', [(i, i ^ k) for i in ra...  3.61 us
    ppermute x3, starting transfers between devices, local(): lax.ppermute(gram, plane, [(i, i ^ v) for i in range(group)])  3.49 us
  transfers between devices with their start and end apart: 12, of which 8 were waited for; matrix products, arithmetic and copies ran while one was open for 2% of the time, Pallas kernels for 0%

profile of v7, /device:TPU:0, one launch (start us, length us, event | category | flops | bytes accessed | tf_op | source)
XLA Modules:
  0.0 67.8 jit_solution(12582783786713987441)
XLA Ops:
  0.7 1.5 %multiply_convert_fusion = f16[64,6,6,128]{3,0,2,1:T(8,128)(2,1)S(1)} fusion(f32[64,6,6,128]{3,0,2,1:T(8,128)} %param.5), kind=kLoop, calls=%fused_computation | loop fusion | flops 589824 | bytes 1769472 | tf_op jit(solution)/shard_map/convert_element_type | solution.py:367
  2.1 0.1 copy.9
  2.3 0.7 shard_map.68
  3.0 0.2 pad_maximum_fusion
  3.3 17.8 %all_to_all.10 = f16[8,408,128]{2,1,0:T(8,128)(2,1)S(1)} all-to-all(f16[8,408,128]{2,1,0:T(8,128)(2,1)S(1)} %pad_maximum_fusion), channel_id=1, replica_groups=mesh['band'=4,'sx'=4,'sy'=2] {'sx','sy'}, dimensions={0} | all-to-all | bytes 1671168 | tf_op jit(solution)/shard_map/all_to_all | solution.py:378
  21.1 0.1 convert_element_type.61.got_ref
  21.2 7.3 %shard_map.69 = (f32[8,296,128]{2,1,0:T(8,128)S(1)}, bf16[32,8,1152]{2,1,0:T(8,128)(2,1)}) custom-call(f32[8,408,128]{2,1,0:T(8,128)S(1)} %convert_element_type.61.got_ref), custom_call_target="tpu_custom_call" | custom-call | flops 47185920 | bytes 2359296 | tf_op jit(solution)/shard_map/pallas_call | solution.py:387
  28.6 4.2 %all-to-all-start.1 = ((bf16[32,8,1152]{2,1,0:T(8,128)(2,1)}), bf16[32,8,1152]{2,1,0:T(8,128)(2,1)S(1)}, u32[]{:S(2)}, u32[]{:S(2)}) async-start(bf16[32,8,1152]{2,1,0:T(8,128)(2,1)} %get-tuple-element.9), calls=%async_computation.1 | async-start | bytes 1179648 | tf_op jit(solution)/shard_map/all_to_all | solution.py:412
  32.8 0.1 convert.25
  32.9 0.1 fusion.1
  33.0 1.8 %collective-permute-start = (f16[2,296,128]{2,1,0:T(8,128)(2,1)S(1)}, f16[2,296,128]{2,1,0:T(8,128)(2,1)S(1)}, u32[]{:S(2)}, u32[]{:S(2)}) collective-permute-start(f16[2,296,128]{2,1,0:T(8,128)(2,1)S(1)} %pad_maximum_fusion.2), channel_id=1, source_target_pairs={{0,1},{1,0},{2,3},{3,2},{4,5},{5,4},{6,7},{7,6},{8,9},{9,8},{10,11... | collective-permute-start | bytes 454664 | tf_op jit(solution)/shard_map/ppermute | solution.py:348
  34.9 1.5 %collective-permute-start.1 = (f16[2,296,128]{2,1,0:T(8,128)(2,1)S(1)}, f16[2,296,128]{2,1,0:T(8,128)(2,1)S(1)}, u32[]{:S(2)}, u32[]{:S(2)}) collective-permute-start(f16[2,296,128]{2,1,0:T(8,128)(2,1)S(1)} %pad_maximum_fusion.3), channel_id=1, source_target_pairs={{0,4},{1,5},{2,6},{3,7},{4,0},{5,1},{6,2},{7,3},{8,12},{9,13},{10,... | collective-permute-start | bytes 454664 | tf_op jit(solution)/shard_map/ppermute | solution.py:348
  36.5 0.3 collective-permute-start.2
  36.8 6.5 %collective-permute-done = f16[2,296,128]{2,1,0:T(8,128)(2,1)S(1)} collective-permute-done((f16[2,296,128]{2,1,0:T(8,128)(2,1)S(1)}, f16[2,296,128]{2,1,0:T(8,128)(2,1)S(1)}, u32[]{:S(2)}, u32[]{:S(2)}) %collective-permute-start) | collective-permute-done | bytes 151584 | tf_op jit(solution)/shard_map/ppermute | solution.py:348
  43.3 1.0 %collective-permute-done.1 = f16[2,296,128]{2,1,0:T(8,128)(2,1)S(1)} collective-permute-done((f16[2,296,128]{2,1,0:T(8,128)(2,1)S(1)}, f16[2,296,128]{2,1,0:T(8,128)(2,1)S(1)}, u32[]{:S(2)}, u32[]{:S(2)}) %collective-permute-start.1) | collective-permute-done | bytes 151584 | tf_op jit(solution)/shard_map/ppermute | solution.py:348
  44.2 5.3 %collective-permute-done.2 = f16[2,296,128]{2,1,0:T(8,128)(2,1)S(1)} collective-permute-done((f16[2,296,128]{2,1,0:T(8,128)(2,1)S(1)}, f16[2,296,128]{2,1,0:T(8,128)(2,1)S(1)}, u32[]{:S(2)}, u32[]{:S(2)}) %collective-permute-start.2) | collective-permute-done | bytes 151584 | tf_op jit(solution)/shard_map/ppermute | solution.py:348
  49.5 0.5 shard_map.71.own_ref
  50.1 3.3 %collective-permute-start.6 = (f16[64,256]{1,0:T(8,128)(2,1)S(1)}, f16[64,256]{1,0:T(8,128)(2,1)S(1)}, u32[]{:S(2)}, u32[]{:S(2)}) collective-permute-start(f16[64,256]{1,0:T(8,128)(2,1)S(1)} %get-tuple-element.21), channel_id=1, source_target_pairs={{0,24},{8,16},{16,8},{24,0},{1,25},{9,17},{17,9},{25,1},{2,26},{10... | collective-permute-start | bytes 98312 | tf_op jit(solution)/shard_map/ppermute | solution.py:436
  53.4 1.1 %collective-permute-start.4 = (f16[64,256]{1,0:T(8,128)(2,1)S(1)}, f16[64,256]{1,0:T(8,128)(2,1)S(1)}, u32[]{:S(2)}, u32[]{:S(2)}) collective-permute-start(f16[64,256]{1,0:T(8,128)(2,1)S(1)} %get-tuple-element.23), channel_id=1, source_target_pairs={{0,8},{8,0},{16,24},{24,16},{1,9},{9,1},{17,25},{25,17},{2,10},{10... | collective-permute-start | bytes 98312 | tf_op jit(solution)/shard_map/ppermute | solution.py:436
  54.6 1.5 %collective-permute-done.6 = f16[64,256]{1,0:T(8,128)(2,1)S(1)} collective-permute-done((f16[64,256]{1,0:T(8,128)(2,1)S(1)}, f16[64,256]{1,0:T(8,128)(2,1)S(1)}, u32[]{:S(2)}, u32[]{:S(2)}) %collective-permute-start.6) | collective-permute-done | bytes 32800 | tf_op jit(solution)/shard_map/ppermute | solution.py:436
  56.1 2.1 %collective-permute-done.5 = f16[64,256]{1,0:T(8,128)(2,1)S(1)} collective-permute-done((f16[64,256]{1,0:T(8,128)(2,1)S(1)}, f16[64,256]{1,0:T(8,128)(2,1)S(1)}, u32[]{:S(2)}, u32[]{:S(2)}) %collective-permute-start.5) | collective-permute-done | bytes 32800 | tf_op jit(solution)/shard_map/ppermute | solution.py:436
  58.3 0.2 shard_map.72
  58.5 0.6 collective-permute-start.9
  59.1 1.3 %collective-permute-start.8 = (f32[64,256]{1,0:T(8,128)S(1)}, f32[64,256]{1,0:T(8,128)S(1)}, u32[]{:S(2)}, u32[]{:S(2)}) collective-permute-start(f32[64,256]{1,0:T(8,128)S(1)} %shard_map.72), channel_id=1, source_target_pairs={{0,4},{1,5},{2,6},{3,7},{4,0},{5,1},{6,2},{7,3},{8,12},{9,13},{10,... | collective-permute-start | bytes 196616 | tf_op jit(solution)/shard_map/ppermute | solution.py:448
  60.4 1.6 %collective-permute-start.7 = (f32[64,256]{1,0:T(8,128)S(1)}, f32[64,256]{1,0:T(8,128)S(1)}, u32[]{:S(2)}, u32[]{:S(2)}) collective-permute-start(f32[64,256]{1,0:T(8,128)S(1)} %shard_map.72), channel_id=1, source_target_pairs={{0,1},{1,0},{2,3},{3,2},{4,5},{5,4},{6,7},{7,6},{8,9},{9,8},{10,11... | collective-permute-start | bytes 196616 | tf_op jit(solution)/shard_map/ppermute | solution.py:448
  62.0 0.1 pad_maximum_fusion.1
  62.1 0.1 collective-permute-start.3
  62.2 1.5 %collective-permute-done.9 = f32[64,256]{1,0:T(8,128)S(1)} collective-permute-done((f32[64,256]{1,0:T(8,128)S(1)}, f32[64,256]{1,0:T(8,128)S(1)}, u32[]{:S(2)}, u32[]{:S(2)}) %collective-permute-start.9) | collective-permute-done | bytes 65568 | tf_op jit(solution)/shard_map/ppermute | solution.py:448
  63.6 1.0 %collective-permute-done.7 = f32[64,256]{1,0:T(8,128)S(1)} collective-permute-done((f32[64,256]{1,0:T(8,128)S(1)}, f32[64,256]{1,0:T(8,128)S(1)}, u32[]{:S(2)}, u32[]{:S(2)}) %collective-permute-start.7) | collective-permute-done | bytes 65568 | tf_op jit(solution)/shard_map/ppermute | solution.py:448
  64.9 1.1 %collective-permute-done.10 = f32[64,256]{1,0:T(8,128)S(1)} collective-permute-done((f32[64,256]{1,0:T(8,128)S(1)}, f32[64,256]{1,0:T(8,128)S(1)}, u32[]{:S(2)}, u32[]{:S(2)}) %collective-permute-start.10) | collective-permute-done | bytes 65568 | tf_op jit(solution)/shard_map/ppermute | solution.py:455
  66.0 0.6 add.15
  66.7 1.1 %shard_map.70 = f32[36,64,128]{2,1,0:T(8,128)} custom-call(f32[8,296,128]{2,1,0:T(8,128)S(1)} %get-tuple-element.8.refs_0_, f32[2,296,128]{2,1,0:T(8,128)S(1)} %convert_element_type.62.refs_1_, f32[2,296,128]{2,1,0:T(8,128)S(1)} %convert_element_type.63.refs_2_, f32[2,296,128]{2,1,0:T(8,128)S(1)} %convert_element_type.64.refs_3_, ...), custom_call_target="tpu_custom_call" | custom-call | tf_op jit(solution)/shard_map/pallas_call | solution.py:465
  (33 shorter events, 0.5 us)
Async XLA Ops:
  0.6 1.6 %copy-start.3 = (s32[4,2]{0,1:T(2,128)S(1)}, s32[4,2]{0,1:T(2,128)}, u32[]{:S(2)}) copy-start(s32[4,2]{0,1:T(2,128)} %param.9) | copy-start | bytes 100
  0.6 1.6 %copy-start.2 = (f32[4,4]{1,0:T(4,128)S(1)}, f32[4,4]{1,0:T(4,128)}, u32[]{:S(2)}) copy-start(f32[4,4]{1,0:T(4,128)} %energies_ref.1) | copy-start | bytes 196
  0.7 1.6 %copy-start = (f32[4,4,5,128]{3,1,2,0:T(4,128)S(1)}, f32[4,4,5,128]{3,1,2,0:T(4,128)}, u32[]{:S(2)}) copy-start(f32[4,4,5,128]{3,1,2,0:T(4,128)} %param.7) | copy-start | bytes 122884
  0.7 1.6 %copy-start.1 = (f32[6,6,128]{2,1,0:T(8,128)S(1)}, f32[6,6,128]{2,1,0:T(8,128)}, u32[]{:S(2)}) copy-start(f32[6,6,128]{2,1,0:T(8,128)} %potential_ref.1) | copy-start | bytes 55300
  28.6 20.9 %all-to-all-start.1 = ((bf16[32,8,1152]{2,1,0:T(8,128)(2,1)}), bf16[32,8,1152]{2,1,0:T(8,128)(2,1)S(1)}, u32[]{:S(2)}, u32[]{:S(2)}) async-start(bf16[32,8,1152]{2,1,0:T(8,128)(2,1)} %get-tuple-element.9), calls=%async_computation.1 | async-start | bytes 1179648 | tf_op jit(solution)/shard_map/all_to_all | solution.py:412
  33.0 10.3 %collective-permute-start = (f16[2,296,128]{2,1,0:T(8,128)(2,1)S(1)}, f16[2,296,128]{2,1,0:T(8,128)(2,1)S(1)}, u32[]{:S(2)}, u32[]{:S(2)}) collective-permute-start(f16[2,296,128]{2,1,0:T(8,128)(2,1)S(1)} %pad_maximum_fusion.2), channel_id=1, source_target_pairs={{0,1},{1,0},{2,3},{3,2},{4,5},{5,4},{6,7},{7,6},{8,9},{9,8},{10,11... | collective-permute-start | bytes 454664 | tf_op jit(solution)/shard_map/ppermute | solution.py:348
  34.9 9.3 %collective-permute-start.1 = (f16[2,296,128]{2,1,0:T(8,128)(2,1)S(1)}, f16[2,296,128]{2,1,0:T(8,128)(2,1)S(1)}, u32[]{:S(2)}, u32[]{:S(2)}) collective-permute-start(f16[2,296,128]{2,1,0:T(8,128)(2,1)S(1)} %pad_maximum_fusion.3), channel_id=1, source_target_pairs={{0,4},{1,5},{2,6},{3,7},{4,0},{5,1},{6,2},{7,3},{8,12},{9,13},{10,... | collective-permute-start | bytes 454664 | tf_op jit(solution)/shard_map/ppermute | solution.py:348
  36.5 13.0 %collective-permute-start.2 = (f16[2,296,128]{2,1,0:T(8,128)(2,1)S(1)}, f16[2,296,128]{2,1,0:T(8,128)(2,1)S(1)}, u32[]{:S(2)}, u32[]{:S(2)}) collective-permute-start(f16[2,296,128]{2,1,0:T(8,128)(2,1)S(1)} %pad_maximum_fusion.4), channel_id=1, source_target_pairs={{0,5},{1,4},{2,7},{3,6},{4,1},{5,0},{6,3},{7,2},{8,13},{9,12},{10,... | collective-permute-start | bytes 454664 | tf_op jit(solution)/shard_map/ppermute | solution.py:348
  50.1 6.0 %collective-permute-start.6 = (f16[64,256]{1,0:T(8,128)(2,1)S(1)}, f16[64,256]{1,0:T(8,128)(2,1)S(1)}, u32[]{:S(2)}, u32[]{:S(2)}) collective-permute-start(f16[64,256]{1,0:T(8,128)(2,1)S(1)} %get-tuple-element.21), channel_id=1, source_target_pairs={{0,24},{8,16},{16,8},{24,0},{1,25},{9,17},{17,9},{25,1},{2,26},{10... | collective-permute-start | bytes 98312 | tf_op jit(solution)/shard_map/ppermute | solution.py:436
  53.4 4.8 %collective-permute-start.5 = (f16[64,256]{1,0:T(8,128)(2,1)S(1)}, f16[64,256]{1,0:T(8,128)(2,1)S(1)}, u32[]{:S(2)}, u32[]{:S(2)}) collective-permute-start(f16[64,256]{1,0:T(8,128)(2,1)S(1)} %get-tuple-element.22), channel_id=1, source_target_pairs={{0,16},{8,24},{16,0},{24,8},{1,17},{9,25},{17,1},{25,9},{2,18},{10... | collective-permute-start | bytes 98312 | tf_op jit(solution)/shard_map/ppermute | solution.py:436
  53.4 4.8 %collective-permute-start.4 = (f16[64,256]{1,0:T(8,128)(2,1)S(1)}, f16[64,256]{1,0:T(8,128)(2,1)S(1)}, u32[]{:S(2)}, u32[]{:S(2)}) collective-permute-start(f16[64,256]{1,0:T(8,128)(2,1)S(1)} %get-tuple-element.23), channel_id=1, source_target_pairs={{0,8},{8,0},{16,24},{24,16},{1,9},{9,1},{17,25},{25,17},{2,10},{10... | collective-permute-start | bytes 98312 | tf_op jit(solution)/shard_map/ppermute | solution.py:436
  58.5 5.2 %collective-permute-start.9 = (f32[64,256]{1,0:T(8,128)S(1)}, f32[64,256]{1,0:T(8,128)S(1)}, u32[]{:S(2)}, u32[]{:S(2)}) collective-permute-start(f32[64,256]{1,0:T(8,128)S(1)} %shard_map.72), channel_id=1, source_target_pairs={{0,5},{1,4},{2,7},{3,6},{4,1},{5,0},{6,3},{7,2},{8,13},{9,12},{10,... | collective-permute-start | bytes 196616 | tf_op jit(solution)/shard_map/ppermute | solution.py:448
  59.1 4.6 %collective-permute-start.8 = (f32[64,256]{1,0:T(8,128)S(1)}, f32[64,256]{1,0:T(8,128)S(1)}, u32[]{:S(2)}, u32[]{:S(2)}) collective-permute-start(f32[64,256]{1,0:T(8,128)S(1)} %shard_map.72), channel_id=1, source_target_pairs={{0,4},{1,5},{2,6},{3,7},{4,0},{5,1},{6,2},{7,3},{8,12},{9,13},{10,... | collective-permute-start | bytes 196616 | tf_op jit(solution)/shard_map/ppermute | solution.py:448
  60.4 4.3 %collective-permute-start.7 = (f32[64,256]{1,0:T(8,128)S(1)}, f32[64,256]{1,0:T(8,128)S(1)}, u32[]{:S(2)}, u32[]{:S(2)}) collective-permute-start(f32[64,256]{1,0:T(8,128)S(1)} %shard_map.72), channel_id=1, source_target_pairs={{0,1},{1,0},{2,3},{3,2},{4,5},{5,4},{6,7},{7,6},{8,9},{9,8},{10,11... | collective-permute-start | bytes 196616 | tf_op jit(solution)/shard_map/ppermute | solution.py:448
  62.1 4.6 %collective-permute-start.3 = (f16[4,296,128]{2,1,0:T(8,128)(2,1)S(1)}, f16[4,296,128]{2,1,0:T(8,128)(2,1)S(1)}, u32[]{:S(2)}, u32[]{:S(2)}) collective-permute-start(f16[4,296,128]{2,1,0:T(8,128)(2,1)S(1)} %pad_maximum_fusion.1), channel_id=1, source_target_pairs={{0,2},{1,3},{2,0},{3,1},{4,6},{5,7},{6,4},{7,5},{8,10},{9,11},{10,... | collective-permute-start | bytes 909320 | tf_op jit(solution)/shard_map/ppermute | solution.py:348
  64.7 1.3 %collective-permute-start.10 = (f32[64,256]{1,0:T(8,128)S(1)}, f32[64,256]{1,0:T(8,128)S(1)}, u32[]{:S(2)}, u32[]{:S(2)}) collective-permute-start(f32[64,256]{1,0:T(8,128)S(1)} %add_add_fusion), channel_id=1, source_target_pairs={{0,2},{1,3},{2,0},{3,1},{4,6},{5,7},{6,4},{7,5},{8,10},{9,11},{10,... | collective-permute-start | bytes 196616 | tf_op jit(solution)/shard_map/ppermute | solution.py:455

commit v8 on v7

--- a/solution.py
+++ b/solution.py
@@ -85,38 +85,56 @@
     out_ref[pl.ds(row + 1, rows - row - 1), :] = jnp.zeros((rows - row - 1, nz), jnp.float32)
 
 
-def filter_kernel(
-    slabs_y,
-    cells_x,
-    cells_y,
-    each,
-    atoms,
-    projs,
-    by_swaps,
-    got_ref,
-    field_ref,
-    rounded_ref,
-    first,
-    second,
-    partial,
-    diagonal,
-    coeffs,
-    numbers,
-    arrived,
-):
-    group, _, nz = got_ref.shape
+def filter_kernel(slabs_y, cells_x, cells_y, each, atoms, projs, slabs, *refs):
+    inputs, (field_ref, rounded_out) = refs[:-11], refs[-11:-9]
+    first, second, partial, diagonal, coeffs, numbers, rounded_ref, arrived, sent = refs[-9:]
+    group = numbers.shape[0]
+    nz = first.shape[-1]
     count_x, count_y = diagonal.shape[0], diagonal.shape[1]
     tiles = len(offsets_x)
     slab_cells = cells_x * cells_y
-    proj_row = slab_cells * each
-    pot_row = proj_row + atoms * projs * tiles
+    pot_row = atoms * projs * tiles
     number_row = pot_row + slab_cells
     scale = 1.0 / filter_half
     factors = [-0.5 * scale * w for w in stencil_weights]
     ring = 1
-
-    copy = pltpu.make_async_copy(got_ref.at[:, number_row, :], numbers, arrived)
-    copy.start()
+    me = 0 if slabs is None else lax.axis_index("sx") * slabs_y + lax.axis_index("sy")
+
+    def rows_of(g, shared, row, count):
+        if slabs is None:
+            return inputs[0].at[g, pl.ds(row + (slab_cells * each if shared else 0), count), :]
+        which, at, start = slabs[g][1 if shared else 0]
+        return inputs[which].at[at, pl.ds(start + row, count), :]
+
+    def shared_row(g, row):
+        return rows_of(g, True, row, 1)[...]
+
+    def over_slabs(body, unroll):
+        if slabs is None:
+            lax.fori_loop(0, group, lambda g, carry: body(g) or carry, 0, unroll=min(group, unroll))
+        else:
+            for g in range(group):
+                body(g)
+
+    def corner(g):
+        place = g if slabs is None else jnp.bitwise_xor(me, g)
+        return place, (place // slabs_y) * cells_x, (place % slabs_y) * cells_y
+
+    if slabs is None:
+        copies = [
+            pltpu.make_async_copy(
+                inputs[0].at[:, slab_cells * each + number_row, :], numbers, arrived.at[0]
+            )
+        ]
+    else:
+        copies = [
+            pltpu.make_async_copy(
+                rows_of(g, True, number_row, 1), numbers.at[pl.ds(g, 1), :], arrived.at[g]
+            )
+            for g in range(group)
+        ]
+    for copy in copies:
+        copy.start()
 
     for field in (first, second):
         for x in (0, ring + count_x):
@@ -124,21 +142,19 @@
         for y in (0, ring + count_y):
             field[:, y] = jnp.zeros((field.shape[0],) + field.shape[2:], jnp.float32)
 
-    def take_slab(g, carry):
-        x0 = (g // slabs_y) * cells_x
-        y0 = (g % slabs_y) * cells_y
+    def take_slab(g):
+        _, x0, y0 = corner(g)
         for i in range(cells_x):
             for j in range(cells_y):
                 cell = i * cells_y + j
-                first[ring + x0 + i, ring + y0 + j] = got_ref[g, pl.ds(cell * each, each), :] * (
+                first[ring + x0 + i, ring + y0 + j] = rows_of(g, False, cell * each, each)[...] * (
                     1.0 / orbital_gain
                 )
-                diagonal[x0 + i, y0 + j] = got_ref[g, pl.ds(pot_row + cell, 1), :] * (
+                diagonal[x0 + i, y0 + j] = shared_row(g, pot_row + cell) * (
                     scale / potential_gain
                 ) + (3.0 * factors[0] - filter_center * scale)
-        return carry
-
-    lax.fori_loop(0, group, take_slab, 0)
+
+    over_slabs(take_slab, 1)
 
     distance = jnp.abs(
         lax.broadcasted_iota(jnp.int32, (nz, nz), 0) - lax.broadcasted_iota(jnp.int32, (nz, nz), 1)
@@ -198,15 +214,14 @@
                 ring + numbers[g, at + 1].astype(jnp.int32),
             )
 
-        def gather_part(g, carry):
+        def gather_part(g):
             for a in range(atoms):
                 at_x, at_y = place_of(g, a)
                 totals = [None] * projs
                 for t in range(tiles):
                     tile = source[at_x + offsets_x[t], at_y + offsets_y[t]]
                     for p in range(projs):
-                        row = proj_row + (a * tiles + t) * projs + p
-                        term = tile * got_ref[g, pl.ds(row, 1), :]
+                        term = tile * shared_row(g, (a * tiles + t) * projs + p)
                         totals[p] = term if t == 0 else totals[p] + term
                 for p in range(projs):
                     k = a * projs + p
@@ -216,27 +231,26 @@
                         * (energy * (gain / projector_gain / projector_gain)),
                         (each, nz),
                     )
-            return carry
-
-        lax.fori_loop(0, group, gather_part, 0, unroll=min(group, 4))
-
-        def scatter_part(g, carry):
+
+        over_slabs(gather_part, 4)
+
+        def scatter_part(g):
             for a in range(atoms):
                 at_x, at_y = place_of(g, a)
                 factor = [coeffs[g, a * projs + p] for p in range(projs)]
                 for t in range(tiles):
-                    row = proj_row + (a * tiles + t) * projs
-                    spread = factor[0] * got_ref[g, pl.ds(row, 1), :]
+                    row = (a * tiles + t) * projs
+                    spread = factor[0] * shared_row(g, row)
                     for p in range(1, projs):
-                        spread = spread + factor[p] * got_ref[g, pl.ds(row + p, 1), :]
+                        spread = spread + factor[p] * shared_row(g, row + p)
                     to_x = at_x + offsets_x[t]
                     to_y = at_y + offsets_y[t]
                     target[to_x, to_y] = target[to_x, to_y] + spread
-            return carry
-
-        lax.fori_loop(0, group, scatter_part, 0, unroll=min(group, 2))
-
-    copy.wait()
+
+        over_slabs(scatter_part, 2)
+
+    for copy in copies:
+        copy.wait()
     apply(first, second, lambda total, target, x, y: total, scale)
 
     for x in (0, ring + count_x):
@@ -246,34 +260,40 @@
 
     apply(second, first, lambda total, target, x, y: 2.0 * total - target[x, y], 2.0 * scale)
 
-    shares = rounded_ref.shape[0] // group
-    portion = slab_cells // shares
+    portion = rounded_ref.shape[-1] // nz
+
+    def round_slab(g):
+        place, x0, y0 = corner(g)
+        for i in range(cells_x):
+            for j in range(cells_y):
+                cell = i * cells_y + j
+                share = (cell // portion) * group + place
+                lanes = pl.ds((cell % portion) * nz, nz)
+                value = first[ring + x0 + i, ring + y0 + j].astype(jnp.bfloat16)
+                rounded_ref[share, :, lanes] = value
+
+    over_slabs(round_slab, 1)
+    copy_out = pltpu.make_async_copy(rounded_ref, rounded_out, sent)
+    copy_out.start()
 
     def largest_of(x, largest):
         row = jnp.abs(first[ring + x, pl.ds(ring, count_y)])
         return jnp.maximum(largest, jnp.max(row, axis=0))
 
-    largest = lax.fori_loop(0, count_x, largest_of, jnp.zeros((each, nz), jnp.float32))
+    largest = lax.fori_loop(0, count_x, largest_of, jnp.zeros((each, nz), jnp.float32), unroll=2)
     level, gain = level_of(jnp.max(largest))
     level_rows = jnp.full((8, nz), level, jnp.float32)
-    me = lax.axis_index("sx") * slabs_y + lax.axis_index("sy") if by_swaps else 0
-
-    def give_slab(g, carry):
-        slot = jnp.bitwise_xor(g, me) if by_swaps else g
-        field_ref[slot, pl.ds(slab_cells * each, 8), :] = level_rows
-        x0 = (g // slabs_y) * cells_x
-        y0 = (g % slabs_y) * cells_y
+
+    def give_slab(g):
+        _, x0, y0 = corner(g)
+        field_ref[g, pl.ds(slab_cells * each, 8), :] = level_rows
         for i in range(cells_x):
             for j in range(cells_y):
                 cell = i * cells_y + j
-                value = first[ring + x0 + i, ring + y0 + j]
-                field_ref[slot, pl.ds(cell * each, each), :] = value * gain
-                rounded_ref[
-                    (cell // portion) * group + g, :, pl.ds((cell % portion) * nz, nz)
-                ] = value.astype(jnp.bfloat16)
-        return carry
-
-    lax.fori_loop(0, group, give_slab, 0)
+                field_ref[g, pl.ds(cell * each, each), :] = first[ring + x0 + i, ring + y0 + j] * gain
+
+    over_slabs(give_slab, 1)
+    copy_out.wait()
 
 
 def entry(block, place):
@@ -343,11 +363,9 @@
         copy.wait()
 
 
-def swap(pieces, value):
+def swap(block, value):
     group = lax.axis_size(plane)
-    return lax.ppermute(
-        jnp.stack(pieces).astype(jnp.float16), plane, [(i, i ^ value) for i in range(group)]
-    )
+    return lax.ppermute(block, plane, [(i, i ^ value) for i in range(group)])
 
 
 def local(orbitals, potential, projectors, energies, centers):
@@ -362,35 +380,60 @@
     grid = (slabs_x * cells_x, slabs_y * cells_y)
     atoms, projs, tiles, _ = projectors.shape
 
+    near = slabs_y
+    far = [v for v in range(1, group) if not v & near]
+    by_swaps = group <= 8 and each % 8 == 0 and slabs_x > 1
+    by_swaps = by_swaps and group & (group - 1) == 0 and bands & (bands - 1) == 0
+
     rows = atoms * projs * tiles + slab_cells + 1
     rows += -rows % 8
+    piece_rows = slab_cells * each
     chunks = (orbitals * orbital_gain).astype(jnp.float16)
     chunks = chunks.transpose(1, 2, 0, 3).reshape(slab_cells, group, each, nz)
-    chunks = chunks.transpose(1, 0, 2, 3).reshape(group, slab_cells * each, nz)
+    chunks = chunks.transpose(1, 0, 2, 3).reshape(group, piece_rows, nz)
     shared = pl.pallas_call(
         share_kernel,
         in_specs=[hbm, smem, smem, vmem, vmem],
         out_specs=vmem,
         out_shape=jax.ShapeDtypeStruct((rows, nz), jnp.float32),
         compiler_params=params,
-    )(chunks[0, :8].astype(jnp.float32), energies, centers.T, projectors.transpose(0, 2, 1, 3), potential).astype(jnp.float16)
-    sent = jnp.concatenate([chunks, jnp.broadcast_to(shared[None], (group, rows, nz))], axis=1)
-    got = lax.all_to_all(sent, plane, 0, 0).astype(jnp.float32)
-
-    near = slabs_y
-    far = [v for v in range(1, group) if not v & near]
-    by_swaps = group <= 8 and each % 8 == 0 and slabs_x > 1
-    by_swaps = by_swaps and group & (group - 1) == 0 and bands & (bands - 1) == 0
+    )(chunks[0, :8].astype(jnp.float32), energies, centers.T, projectors.transpose(0, 2, 1, 3), potential)
+    narrow = shared.astype(jnp.float16)
+    if by_swaps:
+        me = lax.axis_index(plane)
+
+        def chunk_for(value):
+            return lax.dynamic_index_in_dim(chunks, me ^ value, 0, keepdims=False)
+
+        passed = [swap(jnp.concatenate([chunk_for(v ^ near), narrow]), v) for v in far]
+        direct = [swap(chunk_for(v), v) for v in far]
+        mine = jnp.concatenate([chunk_for(near), narrow])
+        crossed = swap(jnp.stack([mine] + passed), near)
+        operands = [chunk_for(0)[None], narrow[None]] + [b[None] for b in direct + passed] + [crossed]
+        operands = [block.astype(jnp.float32) for block in operands]
+        operands[1] = shared[None]
+        slabs = {0: ((0, 0, 0), (1, 0, 0))}
+        last = len(operands) - 1
+        slabs[near] = ((last, 0, 0), (last, 0, piece_rows))
+        for i, v in enumerate(far):
+            slabs[v] = ((2 + i, 0, 0), (2 + len(far) + i, 0, piece_rows))
+            slabs[v ^ near] = ((last, 1 + i, 0), (last, 1 + i, piece_rows))
+    else:
+        sent = jnp.concatenate([chunks, jnp.broadcast_to(narrow[None], (group, rows, nz))], axis=1)
+        operands = [lax.all_to_all(sent, plane, 0, 0).astype(jnp.float32)]
+        slabs = None
 
     portion = slab_cells // bands
     ringed = (grid[0] + 2, grid[1] + 2, each, nz)
+    shares = bands * group
+    rounded_shape = (shares, each, portion * nz)
     field, rounded = pl.pallas_call(
-        functools.partial(filter_kernel, slabs_y, cells_x, cells_y, each, atoms, projs, by_swaps),
-        in_specs=[vmem],
-        out_specs=[vmem] * 2,
+        functools.partial(filter_kernel, slabs_y, cells_x, cells_y, each, atoms, projs, slabs),
+        in_specs=[vmem] * len(operands),
+        out_specs=[vmem, hbm],
         out_shape=[
-            jax.ShapeDtypeStruct((group, slab_cells * each + 8, nz), jnp.float32),
-            jax.ShapeDtypeStruct((bands * group, each, portion * nz), jnp.bfloat16),
+            jax.ShapeDtypeStruct((group, piece_rows + 8, nz), jnp.float32),
+            jax.ShapeDtypeStruct(rounded_shape, jnp.bfloat16),
         ],
         scratch_shapes=[
             pltpu.VMEM(ringed, jnp.float32),
@@ -399,6 +442,8 @@
             pltpu.VMEM(grid + (1, nz), jnp.float32),
             pltpu.VMEM((group, atoms * projs, each, nz), jnp.float32),
             pltpu.SMEM((group, nz), jnp.float32),
+            pltpu.VMEM(rounded_shape, jnp.bfloat16),
+            pltpu.SemaphoreType.DMA((group,)),
             pltpu.SemaphoreType.DMA,
         ],
         compiler_params=params,
@@ -407,13 +452,15 @@
             bytes_accessed=8 * grid[0] * grid[1] * each * nz,
             transcendentals=0,
         ),
-    )(got)
-
-    matrix = lax.all_to_all(rounded, every, 0, 0).reshape(total_orbitals, portion * nz)
+    )(*operands)
+
+    matrix = lax.all_to_all(rounded, every, 0, 0)
+    matrix = matrix.reshape(total_orbitals, portion * nz)
     if by_swaps:
-        came = [swap([field[v], field[v | near]], v) for v in far]
+        narrow = field.astype(jnp.float16)
+        came = [swap(jnp.stack([narrow[v], narrow[v | near]]), v) for v in far]
         came, matrix = lax.optimization_barrier((came, matrix))
-        came.append(swap([field[near]] + [block[1] for block in came], near))
+        came.append(swap(jnp.stack([narrow[near]] + [block[1] for block in came]), near))
         pieces = [field] + [block.astype(jnp.float32) for block in came]
         places = [(0, 0, 0), (len(pieces) - 1, 0, near)]
         for i, v in enumerate(far):
@@ -421,6 +468,19 @@
     else:
         pieces = [lax.all_to_all(field.astype(jnp.float16), plane, 0, 0).astype(jnp.float32)]
         places = [(0, g, g) for g in range(group)]
+
+    def unpack(pieces):
+        return pl.pallas_call(
+            functools.partial(unpack_kernel, each, slabs_y, places),
+            in_specs=[vmem] * len(pieces),
+            out_specs=hbm,
+            out_shape=jax.ShapeDtypeStruct((slab_cells, band_orbitals, nz), jnp.float32),
+            scratch_shapes=[
+                pltpu.VMEM((slab_cells, band_orbitals, nz), jnp.float32),
+                pltpu.SemaphoreType.DMA((cells_x,)),
+            ],
+            compiler_params=params,
+        )(*pieces)
 
     cells = grid[0] * grid[1] * nz
     if by_swaps:
@@ -438,6 +498,7 @@
             ).astype(jnp.float32)
             for k in range(1, bands)
         ]
+        parts, pieces = lax.optimization_barrier((parts, pieces))
         gram = pl.pallas_call(
             functools.partial(rows_kernel, cells),
             in_specs=[vmem] * bands,
@@ -445,34 +506,24 @@
             out_shape=jax.ShapeDtypeStruct((band_orbitals, total_orbitals), jnp.float32),
             compiler_params=params,
         )(sums, *parts)
-        terms = {v: lax.ppermute(gram, plane, [(i, i ^ v) for i in range(group)]) for v in far}
+        terms = {v: swap(gram, v) for v in far}
         terms[0] = gram
         bit = 1
         while len(terms) > 1:
             terms = {v: terms[v] + terms[v ^ bit] for v in terms if not v & bit and v ^ bit in terms} or terms
             bit *= 2
-        gram = terms[0]
-        gram = gram + lax.ppermute(gram, plane, [(i, i ^ near) for i in range(group)])
+        gram, filtered = lax.optimization_barrier((terms[0], unpack(pieces)))
+        gram = gram + swap(gram, near)
     else:
         sums = lax.dot_general(
             matrix, matrix, (((1,), (1,)), ((), ())), preferred_element_type=jnp.float32
         )
-        parts = lax.all_to_all(sums.reshape(bands * group, each, total_orbitals), every, 0, 0)
+        parts = lax.all_to_all(sums.reshape(shares, each, total_orbitals), every, 0, 0)
         rows = jnp.sum(parts, axis=0) / cells
         gram = lax.all_to_all(jnp.broadcast_to(rows[None], (group,) + rows.shape), plane, 0, 0)
         gram = gram.reshape(band_orbitals, total_orbitals)
-
-    filtered = pl.pallas_call(
-        functools.partial(unpack_kernel, each, slabs_y, places),
-        in_specs=[vmem] * len(pieces),
-        out_specs=hbm,
-        out_shape=jax.ShapeDtypeStruct((slab_cells, band_orbitals, nz), jnp.float32),
-        scratch_shapes=[
-            pltpu.VMEM((slab_cells, band_orbitals, nz), jnp.float32),
-            pltpu.SemaphoreType.DMA((cells_x,)),
-        ],
-        compiler_params=params,
-    )(*pieces)
+        filtered = unpack(pieces)
+
     filtered = filtered.reshape(cells_x, cells_y, band_orbitals, nz).transpose(2, 0, 1, 3)
     return (filtered, gram)
 

time: 68.1 us -> 65.2 us (0.957)
  blocking collectives: 17.8 us -> 0 us
  starting transfers between devices: 15.9 us -> 26 us
  waiting for transfers between devices: 20 us -> 25.2 us
    all_to_all x1 -> x0, blocking collectives: 17.8 us -> none  [local(): got = lax.all_to_all(sent, plane, 0, 0).astype(jnp.float32)]
    ppermute x8 -> x15, starting transfers between devices: 7.32 us -> 16.2 us  [swap(): return lax.ppermute(block, plane, [(i, i ^ value) for i in range(group)])]
    ppermute x8 -> x15, waiting for transfers between devices: 16.4 us -> 22.2 us  [swap(): return lax.ppermute(block, plane, [(i, i ^ value) for i in range(group)])]
    all_to_all x1, starting transfers between devices: 4.17 us -> 5.36 us  [local(): matrix = lax.all_to_all(rounded, every, 0, 0)]
  transfers between devices with their start and end apart: 12 -> 19, of which waited for: 8 -> 14; matrix products, arithmetic and copies ran while one was open for 2% -> 1% of each run, Pallas kernels for 0% -> 4%
where the time goes in v8:
time: 65.2 us; the launch traced here: 65 us
  starting transfers between devices  26 us (40%)
  waiting for transfers between devices  25.2 us (39%)
  Pallas kernels  9.32 us (14%)
  other arithmetic  3.08 us (5%)
  between operations  1.02 us (2%)
    ppermute x15, waiting for transfers between devices, swap(): return lax.ppermute(block, plane, [(i, i ^ value) for i in range(group)])  22.2 us
    ppermute x15, starting transfers between devices, swap(): return lax.ppermute(block, plane, [(i, i ^ value) for i in range(group)])  16.2 us
    pallas_call x1, Pallas kernels, local(): pl.pallas_call(functools.partial(filter_kernel, slabs_y, cells_x, cells_y...  6.81 us
    all_to_all x1, starting transfers between devices, local(): matrix = lax.all_to_all(rounded, every, 0, 0)  5.36 us
    ppermute x3, starting transfers between devices, local(): lax.ppermute(sums[k].astype(jnp.float16), 'band', [(i, i ^ k) for i in ra...  4.45 us
    ppermute x3, waiting for transfers between devices, local(): lax.ppermute(sums[k].astype(jnp.float16), 'band', [(i, i ^ k) for i in ra...  3.01 us
    convert_element_type x1, other arithmetic, local(): chunks = (orbitals * orbital_gain).astype(jnp.float16)  1.43 us
  transfers between devices with their start and end apart: 19, of which 14 were waited for; matrix products, arithmetic and copies ran while one was open for 1% of the time, Pallas kernels for 4%

profile of v8, /device:TPU:0, one launch (start us, length us, event | category | flops | bytes accessed | tf_op | source)
XLA Modules:
  0.0 65.0 jit_solution(1148458660090222939)
XLA Ops:
  0.7 1.4 %multiply_convert_fusion = f16[64,6,6,128]{3,0,2,1:T(8,128)(2,1)S(1)} fusion(f32[64,6,6,128]{3,0,2,1:T(8,128)} %param.5), kind=kLoop, calls=%fused_computation | loop fusion | flops 589824 | bytes 1769472 | tf_op jit(solution)/shard_map/convert_element_type | solution.py:391
  2.4 4.0 %collective-permute-start.2 = (f16[288,128]{1,0:T(8,128)(2,1)S(1)}, f16[288,128]{1,0:T(8,128)(2,1)S(1)}, u32[]{:S(2)}, u32[]{:S(2)}) collective-permute-start(f16[288,128]{1,0:T(8,128)(2,1)S(1)} %get-tuple-element.45), channel_id=1, source_target_pairs={{0,5},{1,4},{2,7},{3,6},{4,1},{5,0},{6,3},{7,2},{8,13},{9,12},{10,... | collective-permute-start | bytes 221192 | tf_op jit(solution)/shard_map/ppermute | solution.py:368
  6.4 0.5 collective-permute-start.1
  7.1 0.7 %shard_map.68 = f32[120,128]{1,0:T(8,128)S(1)} custom-call(f32[8,128]{1,0:T(8,128)S(1)} %fusion.1._, f32[4,4]{1,0:T(4,128)S(1)} %copy-done.2, s32[2,4]{1,0:T(2,128)S(1)} %bitcast.60, f32[4,5,4,128]{3,2,1,0:T(4,128)S(1)} %bitcast.59, f32[6,6,128]{2,1,0:T(8,128)S(1)} %copy-done.1), custom_call_target="tpu_custom_call" | custom-call | tf_op jit(solution)/shard_map/pallas_call | solution.py:394
  7.9 2.0 %collective-permute-start.4 = (f16[408,128]{1,0:T(8,128)(2,1)S(1)}, f16[408,128]{1,0:T(8,128)(2,1)S(1)}, u32[]{:S(2)}, u32[]{:S(2)}) collective-permute-start(f16[408,128]{1,0:T(8,128)(2,1)S(1)} %get-tuple-element.53), channel_id=1, source_target_pairs={{0,4},{1,5},{2,6},{3,7},{4,0},{5,1},{6,2},{7,3},{8,12},{9,13},{10,... | collective-permute-start | bytes 313352 | tf_op jit(solution)/shard_map/ppermute | solution.py:368
  9.8 1.5 %collective-permute-start.5 = (f16[408,128]{1,0:T(8,128)(2,1)S(1)}, f16[408,128]{1,0:T(8,128)(2,1)S(1)}, u32[]{:S(2)}, u32[]{:S(2)}) collective-permute-start(f16[408,128]{1,0:T(8,128)(2,1)S(1)} %get-tuple-element.54), channel_id=1, source_target_pairs={{0,5},{1,4},{2,7},{3,6},{4,1},{5,0},{6,3},{7,2},{8,13},{9,12},{10,... | collective-permute-start | bytes 313352 | tf_op jit(solution)/shard_map/ppermute | solution.py:368
  11.6 2.2 %collective-permute-done.4 = f16[408,128]{1,0:T(8,128)(2,1)S(1)} collective-permute-done((f16[408,128]{1,0:T(8,128)(2,1)S(1)}, f16[408,128]{1,0:T(8,128)(2,1)S(1)}, u32[]{:S(2)}, u32[]{:S(2)}) %collective-permute-start.4) | collective-permute-done | bytes 104480 | tf_op jit(solution)/shard_map/ppermute | solution.py:368
  13.8 1.7 %collective-permute-done.5 = f16[408,128]{1,0:T(8,128)(2,1)S(1)} collective-permute-done((f16[408,128]{1,0:T(8,128)(2,1)S(1)}, f16[408,128]{1,0:T(8,128)(2,1)S(1)}, u32[]{:S(2)}, u32[]{:S(2)}) %collective-permute-start.5) | collective-permute-done | bytes 104480 | tf_op jit(solution)/shard_map/ppermute | solution.py:368
  15.5 1.1 %collective-permute-done.3 = f16[408,128]{1,0:T(8,128)(2,1)S(1)} collective-permute-done((f16[408,128]{1,0:T(8,128)(2,1)S(1)}, f16[408,128]{1,0:T(8,128)(2,1)S(1)}, u32[]{:S(2)}, u32[]{:S(2)}) %collective-permute-start.3) | collective-permute-done | bytes 104480 | tf_op jit(solution)/shard_map/ppermute | solution.py:368
  16.8 1.7 %collective-permute-done.6 = f16[4,408,128]{2,1,0:T(8,128)(2,1)S(1)} collective-permute-done((f16[4,408,128]{2,1,0:T(8,128)(2,1)S(1)}, f16[4,408,128]{2,1,0:T(8,128)(2,1)S(1)}, u32[]{:S(2)}, u32[]{:S(2)}) %collective-permute-start.6) | collective-permute-done | bytes 417824 | tf_op jit(solution)/shard_map/ppermute | solution.py:368
  18.6 6.8 %shard_map.69 = (f32[8,296,128]{2,1,0:T(8,128)S(1)}, bf16[32,8,1152]{2,1,0:T(8,128)(2,1)}) custom-call(f32[1,288,128]{2,1,0:T(8,128)S(1)} %get-tuple-element.48.refs_0_, f32[1,120,128]{2,1,0:T(8,128)S(1)} %bitcast.58, f32[1,288,128]{2,1,0:T(8,128)S(1)} %bitcast_convert_fusion.2.refs_2_, f32[1,288,128]{2,1,0:T(8,128)S(1)} %bitcast_convert_fusion.1.refs_3_, ...), custom_call_target="tpu_custom_call" | custom-call | flops 47185920 | bytes 2359296 | tf_op jit(solution)/shard_map/pallas_call | solution.py:430
  25.4 5.4 %all-to-all-start = ((bf16[32,8,1152]{2,1,0:T(8,128)(2,1)}), bf16[32,8,1152]{2,1,0:T(8,128)(2,1)S(1)}, u32[]{:S(2)}, u32[]{:S(2)}) async-start(bf16[32,8,1152]{2,1,0:T(8,128)(2,1)} %get-tuple-element.19), calls=%async_computation | async-start | bytes 1179648 | tf_op jit(solution)/shard_map/all_to_all | solution.py:457
  31.0 1.8 %collective-permute-start.7 = (f16[2,296,128]{2,1,0:T(8,128)(2,1)S(1)}, f16[2,296,128]{2,1,0:T(8,128)(2,1)S(1)}, u32[]{:S(2)}, u32[]{:S(2)}) collective-permute-start(f16[2,296,128]{2,1,0:T(8,128)(2,1)S(1)} %pad_maximum_fusion.6), channel_id=1, source_target_pairs={{0,1},{1,0},{2,3},{3,2},{4,5},{5,4},{6,7},{7,6},{8,9},{9,8},{10,11... | collective-permute-start | bytes 454664 | tf_op jit(solution)/shard_map/ppermute | solution.py:368
  32.9 1.5 %collective-permute-start.8 = (f16[2,296,128]{2,1,0:T(8,128)(2,1)S(1)}, f16[2,296,128]{2,1,0:T(8,128)(2,1)S(1)}, u32[]{:S(2)}, u32[]{:S(2)}) collective-permute-start(f16[2,296,128]{2,1,0:T(8,128)(2,1)S(1)} %pad_maximum_fusion.7), channel_id=1, source_target_pairs={{0,4},{1,5},{2,6},{3,7},{4,0},{5,1},{6,2},{7,3},{8,12},{9,13},{10,... | collective-permute-start | bytes 454664 | tf_op jit(solution)/shard_map/ppermute | solution.py:368
  34.5 0.3 collective-permute-start.9
  34.8 6.5 %collective-permute-done.7 = f16[2,296,128]{2,1,0:T(8,128)(2,1)S(1)} collective-permute-done((f16[2,296,128]{2,1,0:T(8,128)(2,1)S(1)}, f16[2,296,128]{2,1,0:T(8,128)(2,1)S(1)}, u32[]{:S(2)}, u32[]{:S(2)}) %collective-permute-start.7) | collective-permute-done | bytes 151584 | tf_op jit(solution)/shard_map/ppermute | solution.py:368
  41.3 1.0 %collective-permute-done.8 = f16[2,296,128]{2,1,0:T(8,128)(2,1)S(1)} collective-permute-done((f16[2,296,128]{2,1,0:T(8,128)(2,1)S(1)}, f16[2,296,128]{2,1,0:T(8,128)(2,1)S(1)}, u32[]{:S(2)}, u32[]{:S(2)}) %collective-permute-start.8) | collective-permute-done | bytes 151584 | tf_op jit(solution)/shard_map/ppermute | solution.py:368
  42.2 5.3 %collective-permute-done.9 = f16[2,296,128]{2,1,0:T(8,128)(2,1)S(1)} collective-permute-done((f16[2,296,128]{2,1,0:T(8,128)(2,1)S(1)}, f16[2,296,128]{2,1,0:T(8,128)(2,1)S(1)}, u32[]{:S(2)}, u32[]{:S(2)}) %collective-permute-start.9) | collective-permute-done | bytes 151584 | tf_op jit(solution)/shard_map/ppermute | solution.py:368
  47.7 0.7 %collective-permute-start.13 = (f16[4,296,128]{2,1,0:T(8,128)(2,1)S(1)}, f16[4,296,128]{2,1,0:T(8,128)(2,1)S(1)}, u32[]{:S(2)}, u32[]{:S(2)}) collective-permute-start(f16[4,296,128]{2,1,0:T(8,128)(2,1)S(1)} %pad_maximum_fusion.1), channel_id=1, source_target_pairs={{0,2},{1,3},{2,0},{3,1},{4,6},{5,7},{6,4},{7,5},{8,10},{9,11},{10,... | collective-permute-start | bytes 909320 | tf_op jit(solution)/shard_map/ppermute | solution.py:368
  48.3 0.5 shard_map.70.own_ref
  48.9 2.7 %collective-permute-start.12 = (f16[64,256]{1,0:T(8,128)(2,1)S(1)}, f16[64,256]{1,0:T(8,128)(2,1)S(1)}, u32[]{:S(2)}, u32[]{:S(2)}) collective-permute-start(f16[64,256]{1,0:T(8,128)(2,1)S(1)} %get-tuple-element.49), channel_id=1, source_target_pairs={{0,24},{8,16},{16,8},{24,0},{1,25},{9,17},{17,9},{25,1},{2,26},{10... | collective-permute-start | bytes 98312 | tf_op jit(solution)/shard_map/ppermute | solution.py:496
  51.7 1.7 %collective-permute-start.10 = (f16[64,256]{1,0:T(8,128)(2,1)S(1)}, f16[64,256]{1,0:T(8,128)(2,1)S(1)}, u32[]{:S(2)}, u32[]{:S(2)}) collective-permute-start(f16[64,256]{1,0:T(8,128)(2,1)S(1)} %get-tuple-element.51), channel_id=1, source_target_pairs={{0,8},{8,0},{16,24},{24,16},{1,9},{9,1},{17,25},{25,17},{2,10},{10... | collective-permute-start | bytes 98312 | tf_op jit(solution)/shard_map/ppermute | solution.py:496
  53.5 1.5 %collective-permute-done.12 = f16[64,256]{1,0:T(8,128)(2,1)S(1)} collective-permute-done((f16[64,256]{1,0:T(8,128)(2,1)S(1)}, f16[64,256]{1,0:T(8,128)(2,1)S(1)}, u32[]{:S(2)}, u32[]{:S(2)}) %collective-permute-start.12) | collective-permute-done | bytes 32800 | tf_op jit(solution)/shard_map/ppermute | solution.py:496
  55.0 1.5 %collective-permute-done.11 = f16[64,256]{1,0:T(8,128)(2,1)S(1)} collective-permute-done((f16[64,256]{1,0:T(8,128)(2,1)S(1)}, f16[64,256]{1,0:T(8,128)(2,1)S(1)}, u32[]{:S(2)}, u32[]{:S(2)}) %collective-permute-start.11) | collective-permute-done | bytes 32800 | tf_op jit(solution)/shard_map/ppermute | solution.py:496
  56.8 1.0 %collective-permute-start.16 = (f32[64,256]{1,0:T(8,128)S(1)}, f32[64,256]{1,0:T(8,128)S(1)}, u32[]{:S(2)}, u32[]{:S(2)}) collective-permute-start(f32[64,256]{1,0:T(8,128)S(1)} %shard_map.71), channel_id=1, source_target_pairs={{0,5},{1,4},{2,7},{3,6},{4,1},{5,0},{6,3},{7,2},{8,13},{9,12},{10,... | collective-permute-start | bytes 196616 | tf_op jit(solution)/shard_map/ppermute | solution.py:368
  57.8 1.0 %collective-permute-start.15 = (f32[64,256]{1,0:T(8,128)S(1)}, f32[64,256]{1,0:T(8,128)S(1)}, u32[]{:S(2)}, u32[]{:S(2)}) collective-permute-start(f32[64,256]{1,0:T(8,128)S(1)} %shard_map.71), channel_id=1, source_target_pairs={{0,4},{1,5},{2,6},{3,7},{4,0},{5,1},{6,2},{7,3},{8,12},{9,13},{10,... | collective-permute-start | bytes 196616 | tf_op jit(solution)/shard_map/ppermute | solution.py:368
  58.7 1.6 %collective-permute-start.14 = (f32[64,256]{1,0:T(8,128)S(1)}, f32[64,256]{1,0:T(8,128)S(1)}, u32[]{:S(2)}, u32[]{:S(2)}) collective-permute-start(f32[64,256]{1,0:T(8,128)S(1)} %shard_map.71), channel_id=1, source_target_pairs={{0,1},{1,0},{2,3},{3,2},{4,5},{5,4},{6,7},{7,6},{8,9},{9,8},{10,11... | collective-permute-start | bytes 196616 | tf_op jit(solution)/shard_map/ppermute | solution.py:368
  60.3 1.1 %shard_map.72 = f32[36,64,128]{2,1,0:T(8,128)} custom-call(f32[8,296,128]{2,1,0:T(8,128)S(1)} %get-tuple-element.27.refs_0_, f32[2,296,128]{2,1,0:T(8,128)S(1)} %convert_element_type.108.refs_1_, f32[2,296,128]{2,1,0:T(8,128)S(1)} %convert_element_type.109.refs_2_, f32[2,296,128]{2,1,0:T(8,128)S(1)} %convert_element_type.110.refs_3_, ...), custom_call_target="tpu_custom_call" | custom-call | tf_op jit(solution)/shard_map/pallas_call | solution.py:473
  61.4 0.6 collective-permute-done.16
  62.2 0.8 %collective-permute-done.14 = f32[64,256]{1,0:T(8,128)S(1)} collective-permute-done((f32[64,256]{1,0:T(8,128)S(1)}, f32[64,256]{1,0:T(8,128)S(1)}, u32[]{:S(2)}, u32[]{:S(2)}) %collective-permute-start.14) | collective-permute-done | bytes 65568 | tf_op jit(solution)/shard_map/ppermute | solution.py:368
  63.1 1.2 %collective-permute-done.17 = f32[64,256]{1,0:T(8,128)S(1)} collective-permute-done((f32[64,256]{1,0:T(8,128)S(1)}, f32[64,256]{1,0:T(8,128)S(1)}, u32[]{:S(2)}, u32[]{:S(2)}) %collective-permute-start.17) | collective-permute-done | bytes 65568 | tf_op jit(solution)/shard_map/ppermute | solution.py:368
  64.3 0.6 add.52
  (53 shorter events, 2.3 us)
Async XLA Ops:
  2.1 5.0 %copy-start = (f32[4,4,5,128]{3,1,2,0:T(4,128)S(1)}, f32[4,4,5,128]{3,1,2,0:T(4,128)}, u32[]{:S(2)}) copy-start(f32[4,4,5,128]{3,1,2,0:T(4,128)} %param.7) | copy-start | bytes 122884
  2.1 4.9 %copy-start.1 = (f32[6,6,128]{2,1,0:T(8,128)S(1)}, f32[6,6,128]{2,1,0:T(8,128)}, u32[]{:S(2)}) copy-start(f32[6,6,128]{2,1,0:T(8,128)} %potential_ref.1) | copy-start | bytes 55300
  2.1 4.9 %copy-start.2 = (f32[4,4]{1,0:T(4,128)S(1)}, f32[4,4]{1,0:T(4,128)}, u32[]{:S(2)}) copy-start(f32[4,4]{1,0:T(4,128)} %energies_ref.1) | copy-start | bytes 196
  2.1 4.9 %copy-start.3 = (s32[4,2]{0,1:T(2,128)S(1)}, s32[4,2]{0,1:T(2,128)}, u32[]{:S(2)}) copy-start(s32[4,2]{0,1:T(2,128)} %param.9) | copy-start | bytes 100
  2.4 8.9 %collective-permute-start.2 = (f16[288,128]{1,0:T(8,128)(2,1)S(1)}, f16[288,128]{1,0:T(8,128)(2,1)S(1)}, u32[]{:S(2)}, u32[]{:S(2)}) collective-permute-start(f16[288,128]{1,0:T(8,128)(2,1)S(1)} %get-tuple-element.45), channel_id=1, source_target_pairs={{0,5},{1,4},{2,7},{3,6},{4,1},{5,0},{6,3},{7,2},{8,13},{9,12},{10,... | collective-permute-start | bytes 221192 | tf_op jit(solution)/shard_map/ppermute | solution.py:368
  6.4 5.2 %collective-permute-start.1 = (f16[288,128]{1,0:T(8,128)(2,1)S(1)}, f16[288,128]{1,0:T(8,128)(2,1)S(1)}, u32[]{:S(2)}, u32[]{:S(2)}) collective-permute-start(f16[288,128]{1,0:T(8,128)(2,1)S(1)} %get-tuple-element.46), channel_id=1, source_target_pairs={{0,4},{1,5},{2,6},{3,7},{4,0},{5,1},{6,2},{7,3},{8,12},{9,13},{10,... | collective-permute-start | bytes 221192 | tf_op jit(solution)/shard_map/ppermute | solution.py:368
  6.9 4.6 %collective-permute-start = (f16[288,128]{1,0:T(8,128)(2,1)S(1)}, f16[288,128]{1,0:T(8,128)(2,1)S(1)}, u32[]{:S(2)}, u32[]{:S(2)}) collective-permute-start(f16[288,128]{1,0:T(8,128)(2,1)S(1)} %get-tuple-element.47), channel_id=1, source_target_pairs={{0,1},{1,0},{2,3},{3,2},{4,5},{5,4},{6,7},{7,6},{8,9},{9,8},{10,11... | collective-permute-start | bytes 221192 | tf_op jit(solution)/shard_map/ppermute | solution.py:368
  7.9 5.9 %collective-permute-start.4 = (f16[408,128]{1,0:T(8,128)(2,1)S(1)}, f16[408,128]{1,0:T(8,128)(2,1)S(1)}, u32[]{:S(2)}, u32[]{:S(2)}) collective-permute-start(f16[408,128]{1,0:T(8,128)(2,1)S(1)} %get-tuple-element.53), channel_id=1, source_target_pairs={{0,4},{1,5},{2,6},{3,7},{4,0},{5,1},{6,2},{7,3},{8,12},{9,13},{10,... | collective-permute-start | bytes 313352 | tf_op jit(solution)/shard_map/ppermute | solution.py:368
  9.8 5.6 %collective-permute-start.5 = (f16[408,128]{1,0:T(8,128)(2,1)S(1)}, f16[408,128]{1,0:T(8,128)(2,1)S(1)}, u32[]{:S(2)}, u32[]{:S(2)}) collective-permute-start(f16[408,128]{1,0:T(8,128)(2,1)S(1)} %get-tuple-element.54), channel_id=1, source_target_pairs={{0,5},{1,4},{2,7},{3,6},{4,1},{5,0},{6,3},{7,2},{8,13},{9,12},{10,... | collective-permute-start | bytes 313352 | tf_op jit(solution)/shard_map/ppermute | solution.py:368
  11.3 5.2 %collective-permute-start.3 = (f16[408,128]{1,0:T(8,128)(2,1)S(1)}, f16[408,128]{1,0:T(8,128)(2,1)S(1)}, u32[]{:S(2)}, u32[]{:S(2)}) collective-permute-start(f16[408,128]{1,0:T(8,128)(2,1)S(1)} %get-tuple-element.55), channel_id=1, source_target_pairs={{0,1},{1,0},{2,3},{3,2},{4,5},{5,4},{6,7},{7,6},{8,9},{9,8},{10,11... | collective-permute-start | bytes 313352 | tf_op jit(solution)/shard_map/ppermute | solution.py:368
  16.7 1.8 %collective-permute-start.6 = (f16[4,408,128]{2,1,0:T(8,128)(2,1)S(1)}, f16[4,408,128]{2,1,0:T(8,128)(2,1)S(1)}, u32[]{:S(2)}, u32[]{:S(2)}) collective-permute-start(f16[4,408,128]{2,1,0:T(8,128)(2,1)S(1)} %pad_maximum_fusion), channel_id=1, source_target_pairs={{0,2},{1,3},{2,0},{3,1},{4,6},{5,7},{6,4},{7,5},{8,10},{9,11},{10,... | collective-permute-start | bytes 1253384 | tf_op jit(solution)/shard_map/ppermute | solution.py:368
  25.4 22.1 %all-to-all-start = ((bf16[32,8,1152]{2,1,0:T(8,128)(2,1)}), bf16[32,8,1152]{2,1,0:T(8,128)(2,1)S(1)}, u32[]{:S(2)}, u32[]{:S(2)}) async-start(bf16[32,8,1152]{2,1,0:T(8,128)(2,1)} %get-tuple-element.19), calls=%async_computation | async-start | bytes 1179648 | tf_op jit(solution)/shard_map/all_to_all | solution.py:457
  31.0 10.3 %collective-permute-start.7 = (f16[2,296,128]{2,1,0:T(8,128)(2,1)S(1)}, f16[2,296,128]{2,1,0:T(8,128)(2,1)S(1)}, u32[]{:S(2)}, u32[]{:S(2)}) collective-permute-start(f16[2,296,128]{2,1,0:T(8,128)(2,1)S(1)} %pad_maximum_fusion.6), channel_id=1, source_target_pairs={{0,1},{1,0},{2,3},{3,2},{4,5},{5,4},{6,7},{7,6},{8,9},{9,8},{10,11... | collective-permute-start | bytes 454664 | tf_op jit(solution)/shard_map/ppermute | solution.py:368
  32.9 9.3 %collective-permute-start.8 = (f16[2,296,128]{2,1,0:T(8,128)(2,1)S(1)}, f16[2,296,128]{2,1,0:T(8,128)(2,1)S(1)}, u32[]{:S(2)}, u32[]{:S(2)}) collective-permute-start(f16[2,296,128]{2,1,0:T(8,128)(2,1)S(1)} %pad_maximum_fusion.7), channel_id=1, source_target_pairs={{0,4},{1,5},{2,6},{3,7},{4,0},{5,1},{6,2},{7,3},{8,12},{9,13},{10,... | collective-permute-start | bytes 454664 | tf_op jit(solution)/shard_map/ppermute | solution.py:368
  34.5 13.0 %collective-permute-start.9 = (f16[2,296,128]{2,1,0:T(8,128)(2,1)S(1)}, f16[2,296,128]{2,1,0:T(8,128)(2,1)S(1)}, u32[]{:S(2)}, u32[]{:S(2)}) collective-permute-start(f16[2,296,128]{2,1,0:T(8,128)(2,1)S(1)} %pad_maximum_fusion.8), channel_id=1, source_target_pairs={{0,5},{1,4},{2,7},{3,6},{4,1},{5,0},{6,3},{7,2},{8,13},{9,12},{10,... | collective-permute-start | bytes 454664 | tf_op jit(solution)/shard_map/ppermute | solution.py:368
  47.7 8.9 %collective-permute-start.13 = (f16[4,296,128]{2,1,0:T(8,128)(2,1)S(1)}, f16[4,296,128]{2,1,0:T(8,128)(2,1)S(1)}, u32[]{:S(2)}, u32[]{:S(2)}) collective-permute-start(f16[4,296,128]{2,1,0:T(8,128)(2,1)S(1)} %pad_maximum_fusion.1), channel_id=1, source_target_pairs={{0,2},{1,3},{2,0},{3,1},{4,6},{5,7},{6,4},{7,5},{8,10},{9,11},{10,... | collective-permute-start | bytes 909320 | tf_op jit(solution)/shard_map/ppermute | solution.py:368
  48.9 6.1 %collective-permute-start.12 = (f16[64,256]{1,0:T(8,128)(2,1)S(1)}, f16[64,256]{1,0:T(8,128)(2,1)S(1)}, u32[]{:S(2)}, u32[]{:S(2)}) collective-permute-start(f16[64,256]{1,0:T(8,128)(2,1)S(1)} %get-tuple-element.49), channel_id=1, source_target_pairs={{0,24},{8,16},{16,8},{24,0},{1,25},{9,17},{17,9},{25,1},{2,26},{10... | collective-permute-start | bytes 98312 | tf_op jit(solution)/shard_map/ppermute | solution.py:496
  51.7 4.8 %collective-permute-start.11 = (f16[64,256]{1,0:T(8,128)(2,1)S(1)}, f16[64,256]{1,0:T(8,128)(2,1)S(1)}, u32[]{:S(2)}, u32[]{:S(2)}) collective-permute-start(f16[64,256]{1,0:T(8,128)(2,1)S(1)} %get-tuple-element.50), channel_id=1, source_target_pairs={{0,16},{8,24},{16,0},{24,8},{1,17},{9,25},{17,1},{25,9},{2,18},{10... | collective-permute-start | bytes 98312 | tf_op jit(solution)/shard_map/ppermute | solution.py:496
  51.7 4.8 %collective-permute-start.10 = (f16[64,256]{1,0:T(8,128)(2,1)S(1)}, f16[64,256]{1,0:T(8,128)(2,1)S(1)}, u32[]{:S(2)}, u32[]{:S(2)}) collective-permute-start(f16[64,256]{1,0:T(8,128)(2,1)S(1)} %get-tuple-element.51), channel_id=1, source_target_pairs={{0,8},{8,0},{16,24},{24,16},{1,9},{9,1},{17,25},{25,17},{2,10},{10... | collective-permute-start | bytes 98312 | tf_op jit(solution)/shard_map/ppermute | solution.py:496
  56.8 5.2 %collective-permute-start.16 = (f32[64,256]{1,0:T(8,128)S(1)}, f32[64,256]{1,0:T(8,128)S(1)}, u32[]{:S(2)}, u32[]{:S(2)}) collective-permute-start(f32[64,256]{1,0:T(8,128)S(1)} %shard_map.71), channel_id=1, source_target_pairs={{0,5},{1,4},{2,7},{3,6},{4,1},{5,0},{6,3},{7,2},{8,13},{9,12},{10,... | collective-permute-start | bytes 196616 | tf_op jit(solution)/shard_map/ppermute | solution.py:368
  57.8 4.5 %collective-permute-start.15 = (f32[64,256]{1,0:T(8,128)S(1)}, f32[64,256]{1,0:T(8,128)S(1)}, u32[]{:S(2)}, u32[]{:S(2)}) collective-permute-start(f32[64,256]{1,0:T(8,128)S(1)} %shard_map.71), channel_id=1, source_target_pairs={{0,4},{1,5},{2,6},{3,7},{4,0},{5,1},{6,2},{7,3},{8,12},{9,13},{10,... | collective-permute-start | bytes 196616 | tf_op jit(solution)/shard_map/ppermute | solution.py:368
  58.7 4.3 %collective-permute-start.14 = (f32[64,256]{1,0:T(8,128)S(1)}, f32[64,256]{1,0:T(8,128)S(1)}, u32[]{:S(2)}, u32[]{:S(2)}) collective-permute-start(f32[64,256]{1,0:T(8,128)S(1)} %shard_map.71), channel_id=1, source_target_pairs={{0,1},{1,0},{2,3},{3,2},{4,5},{5,4},{6,7},{7,6},{8,9},{9,8},{10,11... | collective-permute-start | bytes 196616 | tf_op jit(solution)/shard_map/ppermute | solution.py:368
  63.0 1.3 %collective-permute-start.17 = (f32[64,256]{1,0:T(8,128)S(1)}, f32[64,256]{1,0:T(8,128)S(1)}, u32[]{:S(2)}, u32[]{:S(2)}) collective-permute-start(f32[64,256]{1,0:T(8,128)S(1)} %add_add_fusion), channel_id=1, source_target_pairs={{0,2},{1,3},{2,0},{3,1},{4,6},{5,7},{6,4},{7,5},{8,10},{9,11},{10,... | collective-permute-start | bytes 196616 | tf_op jit(solution)/shard_map/ppermute | solution.py:368

commit v9 on v8

--- a/solution.py
+++ b/solution.py
@@ -86,8 +86,8 @@
 
 
 def filter_kernel(slabs_y, cells_x, cells_y, each, atoms, projs, slabs, *refs):
-    inputs, (field_ref, rounded_out) = refs[:-11], refs[-11:-9]
-    first, second, partial, diagonal, coeffs, numbers, rounded_ref, arrived, sent = refs[-9:]
+    inputs, (first, rounded_out) = refs[:-10], refs[-10:-8]
+    second, partial, diagonal, coeffs, numbers, rounded_ref, arrived, sent = refs[-8:]
     group = numbers.shape[0]
     nz = first.shape[-1]
     count_x, count_y = diagonal.shape[0], diagonal.shape[1]
@@ -262,38 +262,56 @@
 
     portion = rounded_ref.shape[-1] // nz
 
-    def round_slab(g):
-        place, x0, y0 = corner(g)
-        for i in range(cells_x):
-            for j in range(cells_y):
-                cell = i * cells_y + j
-                share = (cell // portion) * group + place
-                lanes = pl.ds((cell % portion) * nz, nz)
-                value = first[ring + x0 + i, ring + y0 + j].astype(jnp.bfloat16)
-                rounded_ref[share, :, lanes] = value
-
-    over_slabs(round_slab, 1)
-    copy_out = pltpu.make_async_copy(rounded_ref, rounded_out, sent)
-    copy_out.start()
+    parts = slab_cells // portion
+    leaving = []
+    for part in range(parts):
+
+        def round_slab(g):
+            place, x0, y0 = corner(g)
+            for within in range(portion):
+                i, j = divmod(part * portion + within, cells_y)
+                rounded_ref[part * group + place, :, pl.ds(within * nz, nz)] = first[
+                    ring + x0 + i, ring + y0 + j
+                ].astype(jnp.bfloat16)
+
+        over_slabs(round_slab, 1)
+        shares = pl.ds(part * group, group)
+        leaving.append(
+            pltpu.make_async_copy(rounded_ref.at[shares], rounded_out.at[shares], sent.at[part])
+        )
+        leaving[-1].start()
+    for copy in leaving:
+        copy.wait()
+
+
+def scale_kernel(slabs_y, cells_x, cells_y, by_swaps, values_ref, field_ref):
+    group, rows, nz = field_ref.shape
+    each = values_ref.shape[2]
+    ring = 1
+    count_x, count_y = values_ref.shape[0] - 2 * ring, values_ref.shape[1] - 2 * ring
+    me = lax.axis_index("sx") * slabs_y + lax.axis_index("sy") if by_swaps else 0
 
     def largest_of(x, largest):
-        row = jnp.abs(first[ring + x, pl.ds(ring, count_y)])
+        row = jnp.abs(values_ref[ring + x, pl.ds(ring, count_y)])
         return jnp.maximum(largest, jnp.max(row, axis=0))
 
     largest = lax.fori_loop(0, count_x, largest_of, jnp.zeros((each, nz), jnp.float32), unroll=2)
     level, gain = level_of(jnp.max(largest))
     level_rows = jnp.full((8, nz), level, jnp.float32)
 
-    def give_slab(g):
-        _, x0, y0 = corner(g)
-        field_ref[g, pl.ds(slab_cells * each, 8), :] = level_rows
+    def give_slab(g, carry):
+        place = jnp.bitwise_xor(me, g) if by_swaps else g
+        x0 = (place // slabs_y) * cells_x
+        y0 = (place % slabs_y) * cells_y
+        field_ref[g, pl.ds(rows - 8, 8), :] = level_rows
         for i in range(cells_x):
             for j in range(cells_y):
-                cell = i * cells_y + j
-                field_ref[g, pl.ds(cell * each, each), :] = first[ring + x0 + i, ring + y0 + j] * gain
-
-    over_slabs(give_slab, 1)
-    copy_out.wait()
+                field_ref[g, pl.ds((i * cells_y + j) * each, each), :] = (
+                    values_ref[ring + x0 + i, ring + y0 + j] * gain
+                )
+        return carry
+
+    lax.fori_loop(0, group, give_slab, 0)
 
 
 def entry(block, place):
@@ -333,7 +351,25 @@
     for block in [own_ref[0]] + [ref[...] for ref in refs[:-1]]:
         block = block * shrink_of(entry(block, spare))
         total = block if total is None else total + block
-    out_ref[...] = jnp.where(spare, entry(total, twin), total) / cells
+    total = jnp.where(spare, entry(total, twin), total) / cells
+    level, gain = level_of(jnp.max(jnp.abs(total)))
+    out_ref[...] = jnp.where(spare, level, total * gain)
+
+
+def plane_kernel(far, *refs):
+    out_ref = refs[-1]
+    spare, twin = band_corner(out_ref.shape, lax.axis_index("band"))
+    terms = {}
+    for v, ref in zip([0] + far, refs[:-1]):
+        block = ref[...]
+        terms[v] = block * shrink_of(entry(block, spare))
+    bit = 1
+    while len(terms) > 1:
+        if any(v ^ bit in terms for v in terms):
+            terms = {v: terms[v] + terms[v ^ bit] for v in terms if not v & bit}
+        bit *= 2
+    total = terms[0]
+    out_ref[...] = jnp.where(spare, entry(total, twin), total)
 
 
 def unpack_kernel(each, slabs_y, places, *refs):
@@ -427,16 +463,15 @@
     ringed = (grid[0] + 2, grid[1] + 2, each, nz)
     shares = bands * group
     rounded_shape = (shares, each, portion * nz)
-    field, rounded = pl.pallas_call(
+    values, rounded = pl.pallas_call(
         functools.partial(filter_kernel, slabs_y, cells_x, cells_y, each, atoms, projs, slabs),
         in_specs=[vmem] * len(operands),
         out_specs=[vmem, hbm],
         out_shape=[
-            jax.ShapeDtypeStruct((group, piece_rows + 8, nz), jnp.float32),
+            jax.ShapeDtypeStruct(ringed, jnp.float32),
             jax.ShapeDtypeStruct(rounded_shape, jnp.bfloat16),
         ],
         scratch_shapes=[
-            pltpu.VMEM(ringed, jnp.float32),
             pltpu.VMEM(ringed, jnp.float32),
             pltpu.VMEM(grid + (each, nz), jnp.float32),
             pltpu.VMEM(grid + (1, nz), jnp.float32),
@@ -444,7 +479,7 @@
             pltpu.SMEM((group, nz), jnp.float32),
             pltpu.VMEM(rounded_shape, jnp.bfloat16),
             pltpu.SemaphoreType.DMA((group,)),
-            pltpu.SemaphoreType.DMA,
+            pltpu.SemaphoreType.DMA((bands,)),
         ],
         compiler_params=params,
         cost_estimate=pl.CostEstimate(
@@ -456,17 +491,21 @@
 
     matrix = lax.all_to_all(rounded, every, 0, 0)
     matrix = matrix.reshape(total_orbitals, portion * nz)
+    field = pl.pallas_call(
+        functools.partial(scale_kernel, slabs_y, cells_x, cells_y, by_swaps),
+        in_specs=[vmem],
+        out_specs=vmem,
+        out_shape=jax.ShapeDtypeStruct((group, piece_rows + 8, nz), jnp.float32),
+        compiler_params=params,
+    )(values)
+    narrow = field.astype(jnp.float16)
     if by_swaps:
-        narrow = field.astype(jnp.float16)
-        came = [swap(jnp.stack([narrow[v], narrow[v | near]]), v) for v in far]
+        came = [swap(narrow[v], v) for v in range(1, group)]
         came, matrix = lax.optimization_barrier((came, matrix))
-        came.append(swap(jnp.stack([narrow[near]] + [block[1] for block in came]), near))
-        pieces = [field] + [block.astype(jnp.float32) for block in came]
-        places = [(0, 0, 0), (len(pieces) - 1, 0, near)]
-        for i, v in enumerate(far):
-            places += [(i + 1, 0, v), (len(pieces) - 1, i + 1, v | near)]
+        pieces = [field] + [block.astype(jnp.float32)[None] for block in came]
+        places = [(v, 0, v) for v in range(group)]
     else:
-        pieces = [lax.all_to_all(field.astype(jnp.float16), plane, 0, 0).astype(jnp.float32)]
+        pieces = [lax.all_to_all(narrow, plane, 0, 0).astype(jnp.float32)]
         places = [(0, g, g) for g in range(group)]
 
     def unpack(pieces):
@@ -498,21 +537,24 @@
             ).astype(jnp.float32)
             for k in range(1, bands)
         ]
-        parts, pieces = lax.optimization_barrier((parts, pieces))
-        gram = pl.pallas_call(
+        parts, filtered = lax.optimization_barrier((parts, unpack(pieces)))
+        block = jax.ShapeDtypeStruct((band_orbitals, total_orbitals), jnp.float32)
+        own = pl.pallas_call(
             functools.partial(rows_kernel, cells),
             in_specs=[vmem] * bands,
             out_specs=vmem,
-            out_shape=jax.ShapeDtypeStruct((band_orbitals, total_orbitals), jnp.float32),
+            out_shape=block,
             compiler_params=params,
         )(sums, *parts)
-        terms = {v: swap(gram, v) for v in far}
-        terms[0] = gram
-        bit = 1
-        while len(terms) > 1:
-            terms = {v: terms[v] + terms[v ^ bit] for v in terms if not v & bit and v ^ bit in terms} or terms
-            bit *= 2
-        gram, filtered = lax.optimization_barrier((terms[0], unpack(pieces)))
+        own = lax.reduce_precision(own, 5, 10)
+        terms = [own] + [swap(own.astype(jnp.float16), v) for v in far]
+        gram = pl.pallas_call(
+            functools.partial(plane_kernel, far),
+            in_specs=[vmem] * len(terms),
+            out_specs=vmem,
+            out_shape=block,
+            compiler_params=params,
+        )(*[term.astype(jnp.float32) for term in terms])
         gram = gram + swap(gram, near)
     else:
         sums = lax.dot_general(

time: 65.2 us -> 65.9 us (1.011)
  starting transfers between devices: 26 us -> 30.4 us
  waiting for transfers between devices: 25.2 us -> 21.2 us
  Pallas kernels: 9.32 us -> 10.1 us
    ppermute x15 -> x18, starting transfers between devices: 16.2 us -> 20.5 us  [swap(): return lax.ppermute(block, plane, [(i, i ^ value) for i in range(group)])]
    ppermute x15 -> x18, waiting for transfers between devices: 22.2 us -> 18.5 us  [swap(): return lax.ppermute(block, plane, [(i, i ^ value) for i in range(group)])]
  transfers between devices with their start and end apart: 19 -> 22, of which waited for: 14 -> 15; matrix products, arithmetic and copies ran while one was open for 1% -> 1% of each run, Pallas kernels for 4% -> 3%
where the time goes in v9:
time: 65.9 us; the launch traced here: 65.7 us
  starting transfers between devices  30.4 us (46%)
  waiting for transfers between devices  21.2 us (32%)
  Pallas kernels  10.1 us (15%)
  other arithmetic  2.85 us (4%)
  between operations  1 us (2%)
    ppermute x18, starting transfers between devices, swap(): return lax.ppermute(block, plane, [(i, i ^ value) for i in range(group)])  20.5 us
    ppermute x18, waiting for transfers between devices, swap(): return lax.ppermute(block, plane, [(i, i ^ value) for i in range(group)])  18.5 us
    pallas_call x1, Pallas kernels, local(): pl.pallas_call(functools.partial(filter_kernel, slabs_y, cells_x, cells_y...  6.79 us
    all_to_all x1, starting transfers between devices, local(): matrix = lax.all_to_all(rounded, every, 0, 0)  5.39 us
    ppermute x3, starting transfers between devices, local(): lax.ppermute(sums[k].astype(jnp.float16), 'band', [(i, i ^ k) for i in ra...  4.45 us
    ppermute x3, waiting for transfers between devices, local(): lax.ppermute(sums[k].astype(jnp.float16), 'band', [(i, i ^ k) for i in ra...  2.66 us
    convert_element_type x1, other arithmetic, local(): chunks = (orbitals * orbital_gain).astype(jnp.float16)  1.43 us
  transfers between devices with their start and end apart: 22, of which 15 were waited for; matrix products, arithmetic and copies ran while one was open for 1% of the time, Pallas kernels for 3%

profile of v9, /device:TPU:0, one launch (start us, length us, event | category | flops | bytes accessed | tf_op | source)
XLA Modules:
  0.0 65.7 jit_solution(647052713085385784)
XLA Ops:
  0.7 1.4 %multiply_convert_fusion = f16[64,6,6,128]{3,0,2,1:T(8,128)(2,1)S(1)} fusion(f32[64,6,6,128]{3,0,2,1:T(8,128)} %param.5), kind=kLoop, calls=%fused_computation | loop fusion | flops 589824 | bytes 1769472 | tf_op jit(solution)/shard_map/convert_element_type | solution.py:427
  2.4 4.0 %collective-permute-start.2 = (f16[288,128]{1,0:T(8,128)(2,1)S(1)}, f16[288,128]{1,0:T(8,128)(2,1)S(1)}, u32[]{:S(2)}, u32[]{:S(2)}) collective-permute-start(f16[288,128]{1,0:T(8,128)(2,1)S(1)} %get-tuple-element.41), channel_id=1, source_target_pairs={{0,5},{1,4},{2,7},{3,6},{4,1},{5,0},{6,3},{7,2},{8,13},{9,12},{10,... | collective-permute-start | bytes 221192 | tf_op jit(solution)/shard_map/ppermute | solution.py:404
  6.4 0.5 collective-permute-start.1
  7.1 0.7 %shard_map.68 = f32[120,128]{1,0:T(8,128)S(1)} custom-call(f32[8,128]{1,0:T(8,128)S(1)} %fusion.1._, f32[4,4]{1,0:T(4,128)S(1)} %copy-done.2, s32[2,4]{1,0:T(2,128)S(1)} %bitcast.95, f32[4,5,4,128]{3,2,1,0:T(4,128)S(1)} %bitcast.94, f32[6,6,128]{2,1,0:T(8,128)S(1)} %copy-done.1), custom_call_target="tpu_custom_call" | custom-call | tf_op jit(solution)/shard_map/pallas_call | solution.py:430
  7.9 2.0 %collective-permute-start.4 = (f16[408,128]{1,0:T(8,128)(2,1)S(1)}, f16[408,128]{1,0:T(8,128)(2,1)S(1)}, u32[]{:S(2)}, u32[]{:S(2)}) collective-permute-start(f16[408,128]{1,0:T(8,128)(2,1)S(1)} %get-tuple-element.51), channel_id=1, source_target_pairs={{0,4},{1,5},{2,6},{3,7},{4,0},{5,1},{6,2},{7,3},{8,12},{9,13},{10,... | collective-permute-start | bytes 313352 | tf_op jit(solution)/shard_map/ppermute | solution.py:404
  9.8 1.5 %collective-permute-start.5 = (f16[408,128]{1,0:T(8,128)(2,1)S(1)}, f16[408,128]{1,0:T(8,128)(2,1)S(1)}, u32[]{:S(2)}, u32[]{:S(2)}) collective-permute-start(f16[408,128]{1,0:T(8,128)(2,1)S(1)} %get-tuple-element.52), channel_id=1, source_target_pairs={{0,5},{1,4},{2,7},{3,6},{4,1},{5,0},{6,3},{7,2},{8,13},{9,12},{10,... | collective-permute-start | bytes 313352 | tf_op jit(solution)/shard_map/ppermute | solution.py:404
  11.6 2.2 %collective-permute-done.4 = f16[408,128]{1,0:T(8,128)(2,1)S(1)} collective-permute-done((f16[408,128]{1,0:T(8,128)(2,1)S(1)}, f16[408,128]{1,0:T(8,128)(2,1)S(1)}, u32[]{:S(2)}, u32[]{:S(2)}) %collective-permute-start.4) | collective-permute-done | bytes 104480 | tf_op jit(solution)/shard_map/ppermute | solution.py:404
  13.8 1.7 %collective-permute-done.5 = f16[408,128]{1,0:T(8,128)(2,1)S(1)} collective-permute-done((f16[408,128]{1,0:T(8,128)(2,1)S(1)}, f16[408,128]{1,0:T(8,128)(2,1)S(1)}, u32[]{:S(2)}, u32[]{:S(2)}) %collective-permute-start.5) | collective-permute-done | bytes 104480 | tf_op jit(solution)/shard_map/ppermute | solution.py:404
  15.5 1.1 %collective-permute-done.3 = f16[408,128]{1,0:T(8,128)(2,1)S(1)} collective-permute-done((f16[408,128]{1,0:T(8,128)(2,1)S(1)}, f16[408,128]{1,0:T(8,128)(2,1)S(1)}, u32[]{:S(2)}, u32[]{:S(2)}) %collective-permute-start.3) | collective-permute-done | bytes 104480 | tf_op jit(solution)/shard_map/ppermute | solution.py:404
  16.8 1.7 %collective-permute-done.6 = f16[4,408,128]{2,1,0:T(8,128)(2,1)S(1)} collective-permute-done((f16[4,408,128]{2,1,0:T(8,128)(2,1)S(1)}, f16[4,408,128]{2,1,0:T(8,128)(2,1)S(1)}, u32[]{:S(2)}, u32[]{:S(2)}) %collective-permute-start.6) | collective-permute-done | bytes 417824 | tf_op jit(solution)/shard_map/ppermute | solution.py:404
  18.6 6.8 %shard_map.69 = (f32[26,14,8,128]{3,2,1,0:T(8,128)S(1)}, bf16[32,8,1152]{2,1,0:T(8,128)(2,1)}) custom-call(f32[1,288,128]{2,1,0:T(8,128)S(1)} %get-tuple-element.44.refs_0_, f32[1,120,128]{2,1,0:T(8,128)S(1)} %bitcast.93, f32[1,288,128]{2,1,0:T(8,128)S(1)} %bitcast_convert_fusion.9.refs_2_, f32[1,288,128]{2,1,0:T(8,128)S(1)} %bitcast_convert_fusion.8.refs_3_, ...), custom_call_target="tpu_custom_call" | custom-call | flops 47185920 | bytes 2359296 | tf_op jit(solution)/shard_map/pallas_call | solution.py:466
  25.4 5.4 %all-to-all-start = ((bf16[32,8,1152]{2,1,0:T(8,128)(2,1)}), bf16[32,8,1152]{2,1,0:T(8,128)(2,1)S(1)}, u32[]{:S(2)}, u32[]{:S(2)}) async-start(bf16[32,8,1152]{2,1,0:T(8,128)(2,1)} %get-tuple-element.17), calls=%async_computation | async-start | bytes 1179648 | tf_op jit(solution)/shard_map/all_to_all | solution.py:492
  31.4 2.5 %collective-permute-start.13 = (f16[296,128]{1,0:T(8,128)(2,1)S(1)}, f16[296,128]{1,0:T(8,128)(2,1)S(1)}, u32[]{:S(2)}, u32[]{:S(2)}) collective-permute-start(f16[296,128]{1,0:T(8,128)(2,1)S(1)} %get-tuple-element.30), channel_id=1, source_target_pairs={{0,7},{1,6},{2,5},{3,4},{4,3},{5,2},{6,1},{7,0},{8,15},{9,14},{10,... | collective-permute-start | bytes 227336 | tf_op jit(solution)/shard_map/ppermute | solution.py:404
  34.4 1.5 %collective-permute-start.11 = (f16[296,128]{1,0:T(8,128)(2,1)S(1)}, f16[296,128]{1,0:T(8,128)(2,1)S(1)}, u32[]{:S(2)}, u32[]{:S(2)}) collective-permute-start(f16[296,128]{1,0:T(8,128)(2,1)S(1)} %get-tuple-element.32), channel_id=1, source_target_pairs={{0,5},{1,4},{2,7},{3,6},{4,1},{5,0},{6,3},{7,2},{8,13},{9,12},{10,... | collective-permute-start | bytes 227336 | tf_op jit(solution)/shard_map/ppermute | solution.py:404
  36.1 1.0 %collective-permute-start.9 = (f16[296,128]{1,0:T(8,128)(2,1)S(1)}, f16[296,128]{1,0:T(8,128)(2,1)S(1)}, u32[]{:S(2)}, u32[]{:S(2)}) collective-permute-start(f16[296,128]{1,0:T(8,128)(2,1)S(1)} %get-tuple-element.34), channel_id=1, source_target_pairs={{0,3},{1,2},{2,1},{3,0},{4,7},{5,6},{6,5},{7,4},{8,11},{9,10},{10,... | collective-permute-start | bytes 227336 | tf_op jit(solution)/shard_map/ppermute | solution.py:404
  37.1 2.9 %collective-permute-done.13 = f16[296,128]{1,0:T(8,128)(2,1)S(1)} collective-permute-done((f16[296,128]{1,0:T(8,128)(2,1)S(1)}, f16[296,128]{1,0:T(8,128)(2,1)S(1)}, u32[]{:S(2)}, u32[]{:S(2)}) %collective-permute-start.13) | collective-permute-done | bytes 75808 | tf_op jit(solution)/shard_map/ppermute | solution.py:404
  40.0 1.5 %collective-permute-start.8 = (f16[296,128]{1,0:T(8,128)(2,1)S(1)}, f16[296,128]{1,0:T(8,128)(2,1)S(1)}, u32[]{:S(2)}, u32[]{:S(2)}) collective-permute-start(f16[296,128]{1,0:T(8,128)(2,1)S(1)} %get-tuple-element.35), channel_id=1, source_target_pairs={{0,2},{1,3},{2,0},{3,1},{4,6},{5,7},{6,4},{7,5},{8,10},{9,11},{10,... | collective-permute-start | bytes 227336 | tf_op jit(solution)/shard_map/ppermute | solution.py:404
  41.5 1.5 %collective-permute-start.7 = (f16[296,128]{1,0:T(8,128)(2,1)S(1)}, f16[296,128]{1,0:T(8,128)(2,1)S(1)}, u32[]{:S(2)}, u32[]{:S(2)}) collective-permute-start(f16[296,128]{1,0:T(8,128)(2,1)S(1)} %get-tuple-element.36), channel_id=1, source_target_pairs={{0,1},{1,0},{2,3},{3,2},{4,5},{5,4},{6,7},{7,6},{8,9},{9,8},{10,11... | collective-permute-start | bytes 227336 | tf_op jit(solution)/shard_map/ppermute | solution.py:404
  43.0 2.6 %collective-permute-done.11 = f16[296,128]{1,0:T(8,128)(2,1)S(1)} collective-permute-done((f16[296,128]{1,0:T(8,128)(2,1)S(1)}, f16[296,128]{1,0:T(8,128)(2,1)S(1)}, u32[]{:S(2)}, u32[]{:S(2)}) %collective-permute-start.11) | collective-permute-done | bytes 75808 | tf_op jit(solution)/shard_map/ppermute | solution.py:404
  45.6 0.6 collective-permute-done.10
  46.2 1.5 %collective-permute-done.7 = f16[296,128]{1,0:T(8,128)(2,1)S(1)} collective-permute-done((f16[296,128]{1,0:T(8,128)(2,1)S(1)}, f16[296,128]{1,0:T(8,128)(2,1)S(1)}, u32[]{:S(2)}, u32[]{:S(2)}) %collective-permute-start.7) | collective-permute-done | bytes 75808 | tf_op jit(solution)/shard_map/ppermute | solution.py:404
  48.2 3.5 %collective-permute-start.16 = (f16[64,256]{1,0:T(8,128)(2,1)S(1)}, f16[64,256]{1,0:T(8,128)(2,1)S(1)}, u32[]{:S(2)}, u32[]{:S(2)}) collective-permute-start(f16[64,256]{1,0:T(8,128)(2,1)S(1)} %get-tuple-element.45), channel_id=1, source_target_pairs={{0,24},{8,16},{16,8},{24,0},{1,25},{9,17},{17,9},{25,1},{2,26},{10... | collective-permute-start | bytes 98312 | tf_op jit(solution)/shard_map/ppermute | solution.py:535
  51.8 0.9 %collective-permute-start.14 = (f16[64,256]{1,0:T(8,128)(2,1)S(1)}, f16[64,256]{1,0:T(8,128)(2,1)S(1)}, u32[]{:S(2)}, u32[]{:S(2)}) collective-permute-start(f16[64,256]{1,0:T(8,128)(2,1)S(1)} %get-tuple-element.47), channel_id=1, source_target_pairs={{0,8},{8,0},{16,24},{24,16},{1,9},{9,1},{17,25},{25,17},{2,10},{10... | collective-permute-start | bytes 98312 | tf_op jit(solution)/shard_map/ppermute | solution.py:535
  52.8 1.1 %shard_map.72 = f32[36,64,128]{2,1,0:T(8,128)} custom-call(f32[8,296,128]{2,1,0:T(8,128)S(1)} %shard_map.70.refs_0_, f32[1,296,128]{2,1,0:T(8,128)S(1)} %bitcast_convert_fusion.6.refs_1_, f32[1,296,128]{2,1,0:T(8,128)S(1)} %get-tuple-element.59.refs_2_, f32[1,296,128]{2,1,0:T(8,128)S(1)} %get-tuple-element.58.refs_3_, ...), custom_call_target="tpu_custom_call" | custom-call | tf_op jit(solution)/shard_map/pallas_call | solution.py:512
  54.0 2.6 %collective-permute-done.15 = f16[64,256]{1,0:T(8,128)(2,1)S(1)} collective-permute-done((f16[64,256]{1,0:T(8,128)(2,1)S(1)}, f16[64,256]{1,0:T(8,128)(2,1)S(1)}, u32[]{:S(2)}, u32[]{:S(2)}) %collective-permute-start.15) | collective-permute-done | bytes 32800 | tf_op jit(solution)/shard_map/ppermute | solution.py:535
  57.0 1.1 %collective-permute-start.19 = (f16[64,256]{1,0:T(8,128)(2,1)S(1)}, f16[64,256]{1,0:T(8,128)(2,1)S(1)}, u32[]{:S(2)}, u32[]{:S(2)}) collective-permute-start(f16[64,256]{1,0:T(8,128)(2,1)S(1)} %get-tuple-element.48), channel_id=1, source_target_pairs={{0,5},{1,4},{2,7},{3,6},{4,1},{5,0},{6,3},{7,2},{8,13},{9,12},{10,... | collective-permute-start | bytes 98312 | tf_op jit(solution)/shard_map/ppermute | solution.py:404
  58.1 1.6 %collective-permute-start.18 = (f16[64,256]{1,0:T(8,128)(2,1)S(1)}, f16[64,256]{1,0:T(8,128)(2,1)S(1)}, u32[]{:S(2)}, u32[]{:S(2)}) collective-permute-start(f16[64,256]{1,0:T(8,128)(2,1)S(1)} %get-tuple-element.48), channel_id=1, source_target_pairs={{0,4},{1,5},{2,6},{3,7},{4,0},{5,1},{6,2},{7,3},{8,12},{9,13},{10,... | collective-permute-start | bytes 98312 | tf_op jit(solution)/shard_map/ppermute | solution.py:404
  59.7 0.8 %collective-permute-start.17 = (f16[64,256]{1,0:T(8,128)(2,1)S(1)}, f16[64,256]{1,0:T(8,128)(2,1)S(1)}, u32[]{:S(2)}, u32[]{:S(2)}) collective-permute-start(f16[64,256]{1,0:T(8,128)(2,1)S(1)} %get-tuple-element.48), channel_id=1, source_target_pairs={{0,1},{1,0},{2,3},{3,2},{4,5},{5,4},{6,7},{7,6},{8,9},{9,8},{10,11... | collective-permute-start | bytes 98312 | tf_op jit(solution)/shard_map/ppermute | solution.py:404
  60.5 1.3 %collective-permute-done.19 = f16[64,256]{1,0:T(8,128)(2,1)S(1)} collective-permute-done((f16[64,256]{1,0:T(8,128)(2,1)S(1)}, f16[64,256]{1,0:T(8,128)(2,1)S(1)}, u32[]{:S(2)}, u32[]{:S(2)}) %collective-permute-start.19) | collective-permute-done | bytes 32800 | tf_op jit(solution)/shard_map/ppermute | solution.py:404
  62.0 1.6 %collective-permute-done.17 = f16[64,256]{1,0:T(8,128)(2,1)S(1)} collective-permute-done((f16[64,256]{1,0:T(8,128)(2,1)S(1)}, f16[64,256]{1,0:T(8,128)(2,1)S(1)}, u32[]{:S(2)}, u32[]{:S(2)}) %collective-permute-start.17) | collective-permute-done | bytes 32800 | tf_op jit(solution)/shard_map/ppermute | solution.py:404
  63.8 1.2 %collective-permute-done.20 = f32[64,256]{1,0:T(8,128)S(1)} collective-permute-done((f32[64,256]{1,0:T(8,128)S(1)}, f32[64,256]{1,0:T(8,128)S(1)}, u32[]{:S(2)}, u32[]{:S(2)}) %collective-permute-start.20) | collective-permute-done | bytes 65568 | tf_op jit(solution)/shard_map/ppermute | solution.py:404
  65.1 0.6 add.40
  (57 shorter events, 4.0 us)
Async XLA Ops:
  2.1 5.0 %copy-start = (f32[4,4,5,128]{3,1,2,0:T(4,128)S(1)}, f32[4,4,5,128]{3,1,2,0:T(4,128)}, u32[]{:S(2)}) copy-start(f32[4,4,5,128]{3,1,2,0:T(4,128)} %param.7) | copy-start | bytes 122884
  2.1 4.9 %copy-start.1 = (f32[6,6,128]{2,1,0:T(8,128)S(1)}, f32[6,6,128]{2,1,0:T(8,128)}, u32[]{:S(2)}) copy-start(f32[6,6,128]{2,1,0:T(8,128)} %potential_ref.1) | copy-start | bytes 55300
  2.1 4.9 %copy-start.2 = (f32[4,4]{1,0:T(4,128)S(1)}, f32[4,4]{1,0:T(4,128)}, u32[]{:S(2)}) copy-start(f32[4,4]{1,0:T(4,128)} %energies_ref.1) | copy-start | bytes 196
  2.1 4.9 %copy-start.3 = (s32[4,2]{0,1:T(2,128)S(1)}, s32[4,2]{0,1:T(2,128)}, u32[]{:S(2)}) copy-start(s32[4,2]{0,1:T(2,128)} %param.9) | copy-start | bytes 100
  2.4 8.9 %collective-permute-start.2 = (f16[288,128]{1,0:T(8,128)(2,1)S(1)}, f16[288,128]{1,0:T(8,128)(2,1)S(1)}, u32[]{:S(2)}, u32[]{:S(2)}) collective-permute-start(f16[288,128]{1,0:T(8,128)(2,1)S(1)} %get-tuple-element.41), channel_id=1, source_target_pairs={{0,5},{1,4},{2,7},{3,6},{4,1},{5,0},{6,3},{7,2},{8,13},{9,12},{10,... | collective-permute-start | bytes 221192 | tf_op jit(solution)/shard_map/ppermute | solution.py:404
  6.4 5.2 %collective-permute-start.1 = (f16[288,128]{1,0:T(8,128)(2,1)S(1)}, f16[288,128]{1,0:T(8,128)(2,1)S(1)}, u32[]{:S(2)}, u32[]{:S(2)}) collective-permute-start(f16[288,128]{1,0:T(8,128)(2,1)S(1)} %get-tuple-element.42), channel_id=1, source_target_pairs={{0,4},{1,5},{2,6},{3,7},{4,0},{5,1},{6,2},{7,3},{8,12},{9,13},{10,... | collective-permute-start | bytes 221192 | tf_op jit(solution)/shard_map/ppermute | solution.py:404
  6.9 4.6 %collective-permute-start = (f16[288,128]{1,0:T(8,128)(2,1)S(1)}, f16[288,128]{1,0:T(8,128)(2,1)S(1)}, u32[]{:S(2)}, u32[]{:S(2)}) collective-permute-start(f16[288,128]{1,0:T(8,128)(2,1)S(1)} %get-tuple-element.43), channel_id=1, source_target_pairs={{0,1},{1,0},{2,3},{3,2},{4,5},{5,4},{6,7},{7,6},{8,9},{9,8},{10,11... | collective-permute-start | bytes 221192 | tf_op jit(solution)/shard_map/ppermute | solution.py:404
  7.9 5.9 %collective-permute-start.4 = (f16[408,128]{1,0:T(8,128)(2,1)S(1)}, f16[408,128]{1,0:T(8,128)(2,1)S(1)}, u32[]{:S(2)}, u32[]{:S(2)}) collective-permute-start(f16[408,128]{1,0:T(8,128)(2,1)S(1)} %get-tuple-element.51), channel_id=1, source_target_pairs={{0,4},{1,5},{2,6},{3,7},{4,0},{5,1},{6,2},{7,3},{8,12},{9,13},{10,... | collective-permute-start | bytes 313352 | tf_op jit(solution)/shard_map/ppermute | solution.py:404
  9.8 5.6 %collective-permute-start.5 = (f16[408,128]{1,0:T(8,128)(2,1)S(1)}, f16[408,128]{1,0:T(8,128)(2,1)S(1)}, u32[]{:S(2)}, u32[]{:S(2)}) collective-permute-start(f16[408,128]{1,0:T(8,128)(2,1)S(1)} %get-tuple-element.52), channel_id=1, source_target_pairs={{0,5},{1,4},{2,7},{3,6},{4,1},{5,0},{6,3},{7,2},{8,13},{9,12},{10,... | collective-permute-start | bytes 313352 | tf_op jit(solution)/shard_map/ppermute | solution.py:404
  11.3 5.2 %collective-permute-start.3 = (f16[408,128]{1,0:T(8,128)(2,1)S(1)}, f16[408,128]{1,0:T(8,128)(2,1)S(1)}, u32[]{:S(2)}, u32[]{:S(2)}) collective-permute-start(f16[408,128]{1,0:T(8,128)(2,1)S(1)} %get-tuple-element.53), channel_id=1, source_target_pairs={{0,1},{1,0},{2,3},{3,2},{4,5},{5,4},{6,7},{7,6},{8,9},{9,8},{10,11... | collective-permute-start | bytes 313352 | tf_op jit(solution)/shard_map/ppermute | solution.py:404
  16.7 1.8 %collective-permute-start.6 = (f16[4,408,128]{2,1,0:T(8,128)(2,1)S(1)}, f16[4,408,128]{2,1,0:T(8,128)(2,1)S(1)}, u32[]{:S(2)}, u32[]{:S(2)}) collective-permute-start(f16[4,408,128]{2,1,0:T(8,128)(2,1)S(1)} %pad_maximum_fusion), channel_id=1, source_target_pairs={{0,2},{1,3},{2,0},{3,1},{4,6},{5,7},{6,4},{7,5},{8,10},{9,11},{10,... | collective-permute-start | bytes 1253384 | tf_op jit(solution)/shard_map/ppermute | solution.py:404
  25.4 22.3 %all-to-all-start = ((bf16[32,8,1152]{2,1,0:T(8,128)(2,1)}), bf16[32,8,1152]{2,1,0:T(8,128)(2,1)S(1)}, u32[]{:S(2)}, u32[]{:S(2)}) async-start(bf16[32,8,1152]{2,1,0:T(8,128)(2,1)} %get-tuple-element.17), calls=%async_computation | async-start | bytes 1179648 | tf_op jit(solution)/shard_map/all_to_all | solution.py:492
  31.4 8.6 %collective-permute-start.13 = (f16[296,128]{1,0:T(8,128)(2,1)S(1)}, f16[296,128]{1,0:T(8,128)(2,1)S(1)}, u32[]{:S(2)}, u32[]{:S(2)}) collective-permute-start(f16[296,128]{1,0:T(8,128)(2,1)S(1)} %get-tuple-element.30), channel_id=1, source_target_pairs={{0,7},{1,6},{2,5},{3,4},{4,3},{5,2},{6,1},{7,0},{8,15},{9,14},{10,... | collective-permute-start | bytes 227336 | tf_op jit(solution)/shard_map/ppermute | solution.py:404
  33.9 7.6 %collective-permute-start.12 = (f16[296,128]{1,0:T(8,128)(2,1)S(1)}, f16[296,128]{1,0:T(8,128)(2,1)S(1)}, u32[]{:S(2)}, u32[]{:S(2)}) collective-permute-start(f16[296,128]{1,0:T(8,128)(2,1)S(1)} %get-tuple-element.31), channel_id=1, source_target_pairs={{0,6},{1,7},{2,4},{3,5},{4,2},{5,3},{6,0},{7,1},{8,14},{9,15},{10,... | collective-permute-start | bytes 227336 | tf_op jit(solution)/shard_map/ppermute | solution.py:404
  34.4 11.2 %collective-permute-start.11 = (f16[296,128]{1,0:T(8,128)(2,1)S(1)}, f16[296,128]{1,0:T(8,128)(2,1)S(1)}, u32[]{:S(2)}, u32[]{:S(2)}) collective-permute-start(f16[296,128]{1,0:T(8,128)(2,1)S(1)} %get-tuple-element.32), channel_id=1, source_target_pairs={{0,5},{1,4},{2,7},{3,6},{4,1},{5,0},{6,3},{7,2},{8,13},{9,12},{10,... | collective-permute-start | bytes 227336 | tf_op jit(solution)/shard_map/ppermute | solution.py:404
  35.9 10.3 %collective-permute-start.10 = (f16[296,128]{1,0:T(8,128)(2,1)S(1)}, f16[296,128]{1,0:T(8,128)(2,1)S(1)}, u32[]{:S(2)}, u32[]{:S(2)}) collective-permute-start(f16[296,128]{1,0:T(8,128)(2,1)S(1)} %get-tuple-element.33), channel_id=1, source_target_pairs={{0,4},{1,5},{2,6},{3,7},{4,0},{5,1},{6,2},{7,3},{8,12},{9,13},{10,... | collective-permute-start | bytes 227336 | tf_op jit(solution)/shard_map/ppermute | solution.py:404
  36.1 10.0 %collective-permute-start.9 = (f16[296,128]{1,0:T(8,128)(2,1)S(1)}, f16[296,128]{1,0:T(8,128)(2,1)S(1)}, u32[]{:S(2)}, u32[]{:S(2)}) collective-permute-start(f16[296,128]{1,0:T(8,128)(2,1)S(1)} %get-tuple-element.34), channel_id=1, source_target_pairs={{0,3},{1,2},{2,1},{3,0},{4,7},{5,6},{6,5},{7,4},{8,11},{9,10},{10,... | collective-permute-start | bytes 227336 | tf_op jit(solution)/shard_map/ppermute | solution.py:404
  40.0 6.2 %collective-permute-start.8 = (f16[296,128]{1,0:T(8,128)(2,1)S(1)}, f16[296,128]{1,0:T(8,128)(2,1)S(1)}, u32[]{:S(2)}, u32[]{:S(2)}) collective-permute-start(f16[296,128]{1,0:T(8,128)(2,1)S(1)} %get-tuple-element.35), channel_id=1, source_target_pairs={{0,2},{1,3},{2,0},{3,1},{4,6},{5,7},{6,4},{7,5},{8,10},{9,11},{10,... | collective-permute-start | bytes 227336 | tf_op jit(solution)/shard_map/ppermute | solution.py:404
  41.5 6.1 %collective-permute-start.7 = (f16[296,128]{1,0:T(8,128)(2,1)S(1)}, f16[296,128]{1,0:T(8,128)(2,1)S(1)}, u32[]{:S(2)}, u32[]{:S(2)}) collective-permute-start(f16[296,128]{1,0:T(8,128)(2,1)S(1)} %get-tuple-element.36), channel_id=1, source_target_pairs={{0,1},{1,0},{2,3},{3,2},{4,5},{5,4},{6,7},{7,6},{8,9},{9,8},{10,11... | collective-permute-start | bytes 227336 | tf_op jit(solution)/shard_map/ppermute | solution.py:404
  48.2 5.8 %collective-permute-start.16 = (f16[64,256]{1,0:T(8,128)(2,1)S(1)}, f16[64,256]{1,0:T(8,128)(2,1)S(1)}, u32[]{:S(2)}, u32[]{:S(2)}) collective-permute-start(f16[64,256]{1,0:T(8,128)(2,1)S(1)} %get-tuple-element.45), channel_id=1, source_target_pairs={{0,24},{8,16},{16,8},{24,0},{1,25},{9,17},{17,9},{25,1},{2,26},{10... | collective-permute-start | bytes 98312 | tf_op jit(solution)/shard_map/ppermute | solution.py:535
  51.7 4.8 %collective-permute-start.15 = (f16[64,256]{1,0:T(8,128)(2,1)S(1)}, f16[64,256]{1,0:T(8,128)(2,1)S(1)}, u32[]{:S(2)}, u32[]{:S(2)}) collective-permute-start(f16[64,256]{1,0:T(8,128)(2,1)S(1)} %get-tuple-element.46), channel_id=1, source_target_pairs={{0,16},{8,24},{16,0},{24,8},{1,17},{9,25},{17,1},{25,9},{2,18},{10... | collective-permute-start | bytes 98312 | tf_op jit(solution)/shard_map/ppermute | solution.py:535
  51.8 4.8 %collective-permute-start.14 = (f16[64,256]{1,0:T(8,128)(2,1)S(1)}, f16[64,256]{1,0:T(8,128)(2,1)S(1)}, u32[]{:S(2)}, u32[]{:S(2)}) collective-permute-start(f16[64,256]{1,0:T(8,128)(2,1)S(1)} %get-tuple-element.47), channel_id=1, source_target_pairs={{0,8},{8,0},{16,24},{24,16},{1,9},{9,1},{17,25},{25,17},{2,10},{10... | collective-permute-start | bytes 98312 | tf_op jit(solution)/shard_map/ppermute | solution.py:535
  57.0 4.9 %collective-permute-start.19 = (f16[64,256]{1,0:T(8,128)(2,1)S(1)}, f16[64,256]{1,0:T(8,128)(2,1)S(1)}, u32[]{:S(2)}, u32[]{:S(2)}) collective-permute-start(f16[64,256]{1,0:T(8,128)(2,1)S(1)} %get-tuple-element.48), channel_id=1, source_target_pairs={{0,5},{1,4},{2,7},{3,6},{4,1},{5,0},{6,3},{7,2},{8,13},{9,12},{10,... | collective-permute-start | bytes 98312 | tf_op jit(solution)/shard_map/ppermute | solution.py:404
  58.1 3.9 %collective-permute-start.18 = (f16[64,256]{1,0:T(8,128)(2,1)S(1)}, f16[64,256]{1,0:T(8,128)(2,1)S(1)}, u32[]{:S(2)}, u32[]{:S(2)}) collective-permute-start(f16[64,256]{1,0:T(8,128)(2,1)S(1)} %get-tuple-element.48), channel_id=1, source_target_pairs={{0,4},{1,5},{2,6},{3,7},{4,0},{5,1},{6,2},{7,3},{8,12},{9,13},{10,... | collective-permute-start | bytes 98312 | tf_op jit(solution)/shard_map/ppermute | solution.py:404
  59.7 3.9 %collective-permute-start.17 = (f16[64,256]{1,0:T(8,128)(2,1)S(1)}, f16[64,256]{1,0:T(8,128)(2,1)S(1)}, u32[]{:S(2)}, u32[]{:S(2)}) collective-permute-start(f16[64,256]{1,0:T(8,128)(2,1)S(1)} %get-tuple-element.48), channel_id=1, source_target_pairs={{0,1},{1,0},{2,3},{3,2},{4,5},{5,4},{6,7},{7,6},{8,9},{9,8},{10,11... | collective-permute-start | bytes 98312 | tf_op jit(solution)/shard_map/ppermute | solution.py:404
  63.8 1.3 %collective-permute-start.20 = (f32[64,256]{1,0:T(8,128)S(1)}, f32[64,256]{1,0:T(8,128)S(1)}, u32[]{:S(2)}, u32[]{:S(2)}) collective-permute-start(f32[64,256]{1,0:T(8,128)S(1)} %shard_map.74), channel_id=1, source_target_pairs={{0,2},{1,3},{2,0},{3,1},{4,6},{5,7},{6,4},{7,5},{8,10},{9,11},{10,... | collective-permute-start | bytes 196616 | tf_op jit(solution)/shard_map/ppermute | solution.py:404

commit v10 on v9

--- a/solution.py
+++ b/solution.py
@@ -351,25 +351,7 @@
     for block in [own_ref[0]] + [ref[...] for ref in refs[:-1]]:
         block = block * shrink_of(entry(block, spare))
         total = block if total is None else total + block
-    total = jnp.where(spare, entry(total, twin), total) / cells
-    level, gain = level_of(jnp.max(jnp.abs(total)))
-    out_ref[...] = jnp.where(spare, level, total * gain)
-
-
-def plane_kernel(far, *refs):
-    out_ref = refs[-1]
-    spare, twin = band_corner(out_ref.shape, lax.axis_index("band"))
-    terms = {}
-    for v, ref in zip([0] + far, refs[:-1]):
-        block = ref[...]
-        terms[v] = block * shrink_of(entry(block, spare))
-    bit = 1
-    while len(terms) > 1:
-        if any(v ^ bit in terms for v in terms):
-            terms = {v: terms[v] + terms[v ^ bit] for v in terms if not v & bit}
-        bit *= 2
-    total = terms[0]
-    out_ref[...] = jnp.where(spare, entry(total, twin), total)
+    out_ref[...] = jnp.where(spare, entry(total, twin), total) / cells
 
 
 def unpack_kernel(each, slabs_y, places, *refs):
@@ -441,19 +423,11 @@
         def chunk_for(value):
             return lax.dynamic_index_in_dim(chunks, me ^ value, 0, keepdims=False)
 
-        passed = [swap(jnp.concatenate([chunk_for(v ^ near), narrow]), v) for v in far]
-        direct = [swap(chunk_for(v), v) for v in far]
-        mine = jnp.concatenate([chunk_for(near), narrow])
-        crossed = swap(jnp.stack([mine] + passed), near)
-        operands = [chunk_for(0)[None], narrow[None]] + [b[None] for b in direct + passed] + [crossed]
-        operands = [block.astype(jnp.float32) for block in operands]
-        operands[1] = shared[None]
-        slabs = {0: ((0, 0, 0), (1, 0, 0))}
-        last = len(operands) - 1
-        slabs[near] = ((last, 0, 0), (last, 0, piece_rows))
-        for i, v in enumerate(far):
-            slabs[v] = ((2 + i, 0, 0), (2 + len(far) + i, 0, piece_rows))
-            slabs[v ^ near] = ((last, 1 + i, 0), (last, 1 + i, piece_rows))
+        came = [swap(jnp.concatenate([chunk_for(v), narrow]), v) for v in range(1, group)]
+        operands = [chunk_for(0).astype(jnp.float32)[None], shared[None]]
+        operands += [block.astype(jnp.float32)[None] for block in came]
+        slabs = {v: ((1 + v, 0, 0), (1 + v, 0, piece_rows)) for v in range(1, group)}
+        slabs[0] = ((0, 0, 0), (1, 0, 0))
     else:
         sent = jnp.concatenate([chunks, jnp.broadcast_to(narrow[None], (group, rows, nz))], axis=1)
         operands = [lax.all_to_all(sent, plane, 0, 0).astype(jnp.float32)]
@@ -537,24 +511,21 @@
             ).astype(jnp.float32)
             for k in range(1, bands)
         ]
-        parts, filtered = lax.optimization_barrier((parts, unpack(pieces)))
-        block = jax.ShapeDtypeStruct((band_orbitals, total_orbitals), jnp.float32)
-        own = pl.pallas_call(
+        gram = pl.pallas_call(
             functools.partial(rows_kernel, cells),
             in_specs=[vmem] * bands,
             out_specs=vmem,
-            out_shape=block,
+            out_shape=jax.ShapeDtypeStruct((band_orbitals, total_orbitals), jnp.float32),
             compiler_params=params,
         )(sums, *parts)
-        own = lax.reduce_precision(own, 5, 10)
-        terms = [own] + [swap(own.astype(jnp.float16), v) for v in far]
-        gram = pl.pallas_call(
-            functools.partial(plane_kernel, far),
-            in_specs=[vmem] * len(terms),
-            out_specs=vmem,
-            out_shape=block,
-            compiler_params=params,
-        )(*[term.astype(jnp.float32) for term in terms])
+        terms = {v: swap(gram, v) for v in far}
+        terms[0] = gram
+        bit = 1
+        while len(terms) > 1:
+            if any(v ^ bit in terms for v in terms):
+                terms = {v: terms[v] + terms[v ^ bit] for v in terms if not v & bit}
+            bit *= 2
+        gram, filtered = lax.optimization_barrier((terms[0], unpack(pieces)))
         gram = gram + swap(gram, near)
     else:
         sums = lax.dot_general(

time: 65.9 us -> 65.6 us (level)
  starting transfers between devices: 30.4 us -> 32.5 us
  waiting for transfers between devices: 21.2 us -> 19.2 us
    ppermute x18, waiting for transfers between devices: 18.5 us -> 15.4 us  [swap(): return lax.ppermute(block, plane, [(i, i ^ value) for i in range(group)])]
    ppermute x18, starting transfers between devices: 20.5 us -> 22.7 us  [swap(): return lax.ppermute(block, plane, [(i, i ^ value) for i in range(group)])]
    ppermute x3, waiting for transfers between devices: 2.66 us -> 3.79 us  [local(): lax.ppermute(sums[k].astype(jnp.float16), 'band', [(i, i ^ k) for i in ra...]
  transfers between devices with their start and end apart: 22 -> 22, of which waited for: 15 -> 13; matrix products, arithmetic and copies ran while one was open for 1% -> 1% of each run, Pallas kernels for 3% -> 2%
where the time goes in v10:
time: 65.6 us; the launch traced here: 65.4 us
  starting transfers between devices  32.5 us (50%)
  waiting for transfers between devices  19.2 us (29%)
  Pallas kernels  9.74 us (15%)
  other arithmetic  2.73 us (4%)
  between operations  1 us (2%)
    ppermute x18, starting transfers between devices, swap(): return lax.ppermute(block, plane, [(i, i ^ value) for i in range(group)])  22.7 us
    ppermute x18, waiting for transfers between devices, swap(): return lax.ppermute(block, plane, [(i, i ^ value) for i in range(group)])  15.4 us
    pallas_call x1, Pallas kernels, local(): pl.pallas_call(functools.partial(filter_kernel, slabs_y, cells_x, cells_y...  6.79 us
    all_to_all x1, starting transfers between devices, local(): matrix = lax.all_to_all(rounded, every, 0, 0)  5.29 us
    ppermute x3, starting transfers between devices, local(): lax.ppermute(sums[k].astype(jnp.float16), 'band', [(i, i ^ k) for i in ra...  4.45 us
    ppermute x3, waiting for transfers between devices, local(): lax.ppermute(sums[k].astype(jnp.float16), 'band', [(i, i ^ k) for i in ra...  3.79 us
    convert_element_type x1, other arithmetic, local(): chunks = (orbitals * orbital_gain).astype(jnp.float16)  1.46 us
  transfers between devices with their start and end apart: 22, of which 13 were waited for; matrix products, arithmetic and copies ran while one was open for 1% of the time, Pallas kernels for 2%

profile of v10, /device:TPU:0, one launch (start us, length us, event | category | flops | bytes accessed | tf_op | source)
XLA Modules:
  0.0 65.4 jit_solution(379710070555020162)
XLA Ops:
  0.7 1.5 %multiply_convert_fusion = f16[64,6,6,128]{3,0,2,1:T(8,128)(2,1)S(1)} fusion(f32[64,6,6,128]{3,0,2,1:T(8,128)} %param.5), kind=kLoop, calls=%fused_computation | loop fusion | flops 589824 | bytes 1769472 | tf_op jit(solution)/shard_map/convert_element_type | solution.py:409
  2.3 0.7 %shard_map.68 = f32[120,128]{1,0:T(8,128)S(1)} custom-call(f32[8,128]{1,0:T(8,128)S(1)} %fusion._, f32[4,4]{1,0:T(4,128)S(1)} %copy-done.2, s32[2,4]{1,0:T(2,128)S(1)} %bitcast.99, f32[4,5,4,128]{3,2,1,0:T(4,128)S(1)} %bitcast.98, f32[6,6,128]{2,1,0:T(8,128)S(1)} %copy-done.1), custom_call_target="tpu_custom_call" | custom-call | tf_op jit(solution)/shard_map/pallas_call | solution.py:412
  3.4 3.4 %collective-permute-start.6 = (f16[408,128]{1,0:T(8,128)(2,1)S(1)}, f16[408,128]{1,0:T(8,128)(2,1)S(1)}, u32[]{:S(2)}, u32[]{:S(2)}) collective-permute-start(f16[408,128]{1,0:T(8,128)(2,1)S(1)} %get-tuple-element.44), channel_id=1, source_target_pairs={{0,7},{1,6},{2,5},{3,4},{4,3},{5,2},{6,1},{7,0},{8,15},{9,14},{10,... | collective-permute-start | bytes 313352 | tf_op jit(solution)/shard_map/ppermute | solution.py:386
  6.8 0.7 %collective-permute-start.1 = (f16[408,128]{1,0:T(8,128)(2,1)S(1)}, f16[408,128]{1,0:T(8,128)(2,1)S(1)}, u32[]{:S(2)}, u32[]{:S(2)}) collective-permute-start(f16[408,128]{1,0:T(8,128)(2,1)S(1)} %get-tuple-element.45), channel_id=1, source_target_pairs={{0,2},{1,3},{2,0},{3,1},{4,6},{5,7},{6,4},{7,5},{8,10},{9,11},{10,... | collective-permute-start | bytes 313352 | tf_op jit(solution)/shard_map/ppermute | solution.py:386
  8.1 2.4 %collective-permute-start.4 = (f16[408,128]{1,0:T(8,128)(2,1)S(1)}, f16[408,128]{1,0:T(8,128)(2,1)S(1)}, u32[]{:S(2)}, u32[]{:S(2)}) collective-permute-start(f16[408,128]{1,0:T(8,128)(2,1)S(1)} %get-tuple-element.48), channel_id=1, source_target_pairs={{0,5},{1,4},{2,7},{3,6},{4,1},{5,0},{6,3},{7,2},{8,13},{9,12},{10,... | collective-permute-start | bytes 313352 | tf_op jit(solution)/shard_map/ppermute | solution.py:386
  10.6 1.7 %collective-permute-start.5 = (f16[408,128]{1,0:T(8,128)(2,1)S(1)}, f16[408,128]{1,0:T(8,128)(2,1)S(1)}, u32[]{:S(2)}, u32[]{:S(2)}) collective-permute-start(f16[408,128]{1,0:T(8,128)(2,1)S(1)} %get-tuple-element.49), channel_id=1, source_target_pairs={{0,6},{1,7},{2,4},{3,5},{4,2},{5,3},{6,0},{7,1},{8,14},{9,15},{10,... | collective-permute-start | bytes 313352 | tf_op jit(solution)/shard_map/ppermute | solution.py:386
  12.2 1.6 %collective-permute-start = (f16[408,128]{1,0:T(8,128)(2,1)S(1)}, f16[408,128]{1,0:T(8,128)(2,1)S(1)}, u32[]{:S(2)}, u32[]{:S(2)}) collective-permute-start(f16[408,128]{1,0:T(8,128)(2,1)S(1)} %get-tuple-element.50), channel_id=1, source_target_pairs={{0,1},{1,0},{2,3},{3,2},{4,5},{5,4},{6,7},{7,6},{8,9},{9,8},{10,11... | collective-permute-start | bytes 313352 | tf_op jit(solution)/shard_map/ppermute | solution.py:386
  14.0 2.5 %collective-permute-done.4 = f16[408,128]{1,0:T(8,128)(2,1)S(1)} collective-permute-done((f16[408,128]{1,0:T(8,128)(2,1)S(1)}, f16[408,128]{1,0:T(8,128)(2,1)S(1)}, u32[]{:S(2)}, u32[]{:S(2)}) %collective-permute-start.4) | collective-permute-done | bytes 104480 | tf_op jit(solution)/shard_map/ppermute | solution.py:386
  16.5 1.2 %collective-permute-done.5 = f16[408,128]{1,0:T(8,128)(2,1)S(1)} collective-permute-done((f16[408,128]{1,0:T(8,128)(2,1)S(1)}, f16[408,128]{1,0:T(8,128)(2,1)S(1)}, u32[]{:S(2)}, u32[]{:S(2)}) %collective-permute-start.5) | collective-permute-done | bytes 104480 | tf_op jit(solution)/shard_map/ppermute | solution.py:386
  17.7 0.6 collective-permute-done
  18.4 6.8 %shard_map.69 = (f32[26,14,8,128]{3,2,1,0:T(8,128)S(1)}, bf16[32,8,1152]{2,1,0:T(8,128)(2,1)}) custom-call(f32[1,288,128]{2,1,0:T(8,128)S(1)} %get-tuple-element.40.refs_0_, f32[1,120,128]{2,1,0:T(8,128)S(1)} %bitcast.97, f32[1,408,128]{2,1,0:T(8,128)S(1)} %bitcast_convert_fusion.6.refs_2_, f32[1,408,128]{2,1,0:T(8,128)S(1)} %bitcast_convert_fusion.5.refs_3_, ...), custom_call_target="tpu_custom_call" | custom-call | flops 47185920 | bytes 2359296 | tf_op jit(solution)/shard_map/pallas_call | solution.py:440
  25.2 5.3 %all-to-all-start = ((bf16[32,8,1152]{2,1,0:T(8,128)(2,1)}), bf16[32,8,1152]{2,1,0:T(8,128)(2,1)S(1)}, u32[]{:S(2)}, u32[]{:S(2)}) async-start(bf16[32,8,1152]{2,1,0:T(8,128)(2,1)} %get-tuple-element.15), calls=%async_computation | async-start | bytes 1179648 | tf_op jit(solution)/shard_map/all_to_all | solution.py:466
  31.1 2.5 %collective-permute-start.13 = (f16[296,128]{1,0:T(8,128)(2,1)S(1)}, f16[296,128]{1,0:T(8,128)(2,1)S(1)}, u32[]{:S(2)}, u32[]{:S(2)}) collective-permute-start(f16[296,128]{1,0:T(8,128)(2,1)S(1)} %get-tuple-element.26), channel_id=1, source_target_pairs={{0,7},{1,6},{2,5},{3,4},{4,3},{5,2},{6,1},{7,0},{8,15},{9,14},{10,... | collective-permute-start | bytes 227336 | tf_op jit(solution)/shard_map/ppermute | solution.py:386
  34.1 1.5 %collective-permute-start.11 = (f16[296,128]{1,0:T(8,128)(2,1)S(1)}, f16[296,128]{1,0:T(8,128)(2,1)S(1)}, u32[]{:S(2)}, u32[]{:S(2)}) collective-permute-start(f16[296,128]{1,0:T(8,128)(2,1)S(1)} %get-tuple-element.28), channel_id=1, source_target_pairs={{0,5},{1,4},{2,7},{3,6},{4,1},{5,0},{6,3},{7,2},{8,13},{9,12},{10,... | collective-permute-start | bytes 227336 | tf_op jit(solution)/shard_map/ppermute | solution.py:386
  35.8 1.0 %collective-permute-start.9 = (f16[296,128]{1,0:T(8,128)(2,1)S(1)}, f16[296,128]{1,0:T(8,128)(2,1)S(1)}, u32[]{:S(2)}, u32[]{:S(2)}) collective-permute-start(f16[296,128]{1,0:T(8,128)(2,1)S(1)} %get-tuple-element.30), channel_id=1, source_target_pairs={{0,3},{1,2},{2,1},{3,0},{4,7},{5,6},{6,5},{7,4},{8,11},{9,10},{10,... | collective-permute-start | bytes 227336 | tf_op jit(solution)/shard_map/ppermute | solution.py:386
  36.8 2.9 %collective-permute-done.13 = f16[296,128]{1,0:T(8,128)(2,1)S(1)} collective-permute-done((f16[296,128]{1,0:T(8,128)(2,1)S(1)}, f16[296,128]{1,0:T(8,128)(2,1)S(1)}, u32[]{:S(2)}, u32[]{:S(2)}) %collective-permute-start.13) | collective-permute-done | bytes 75808 | tf_op jit(solution)/shard_map/ppermute | solution.py:386
  39.7 1.5 %collective-permute-start.8 = (f16[296,128]{1,0:T(8,128)(2,1)S(1)}, f16[296,128]{1,0:T(8,128)(2,1)S(1)}, u32[]{:S(2)}, u32[]{:S(2)}) collective-permute-start(f16[296,128]{1,0:T(8,128)(2,1)S(1)} %get-tuple-element.31), channel_id=1, source_target_pairs={{0,2},{1,3},{2,0},{3,1},{4,6},{5,7},{6,4},{7,5},{8,10},{9,11},{10,... | collective-permute-start | bytes 227336 | tf_op jit(solution)/shard_map/ppermute | solution.py:386
  41.2 1.5 %collective-permute-start.7 = (f16[296,128]{1,0:T(8,128)(2,1)S(1)}, f16[296,128]{1,0:T(8,128)(2,1)S(1)}, u32[]{:S(2)}, u32[]{:S(2)}) collective-permute-start(f16[296,128]{1,0:T(8,128)(2,1)S(1)} %get-tuple-element.32), channel_id=1, source_target_pairs={{0,1},{1,0},{2,3},{3,2},{4,5},{5,4},{6,7},{7,6},{8,9},{9,8},{10,11... | collective-permute-start | bytes 227336 | tf_op jit(solution)/shard_map/ppermute | solution.py:386
  42.7 2.6 %collective-permute-done.11 = f16[296,128]{1,0:T(8,128)(2,1)S(1)} collective-permute-done((f16[296,128]{1,0:T(8,128)(2,1)S(1)}, f16[296,128]{1,0:T(8,128)(2,1)S(1)}, u32[]{:S(2)}, u32[]{:S(2)}) %collective-permute-start.11) | collective-permute-done | bytes 75808 | tf_op jit(solution)/shard_map/ppermute | solution.py:386
  45.3 0.6 collective-permute-done.10
  45.9 1.5 %collective-permute-done.7 = f16[296,128]{1,0:T(8,128)(2,1)S(1)} collective-permute-done((f16[296,128]{1,0:T(8,128)(2,1)S(1)}, f16[296,128]{1,0:T(8,128)(2,1)S(1)}, u32[]{:S(2)}, u32[]{:S(2)}) %collective-permute-start.7) | collective-permute-done | bytes 75808 | tf_op jit(solution)/shard_map/ppermute | solution.py:386
  47.9 3.5 %collective-permute-start.16 = (f16[64,256]{1,0:T(8,128)(2,1)S(1)}, f16[64,256]{1,0:T(8,128)(2,1)S(1)}, u32[]{:S(2)}, u32[]{:S(2)}) collective-permute-start(f16[64,256]{1,0:T(8,128)(2,1)S(1)} %get-tuple-element.41), channel_id=1, source_target_pairs={{0,24},{8,16},{16,8},{24,0},{1,25},{9,17},{17,9},{25,1},{2,26},{10... | collective-permute-start | bytes 98312 | tf_op jit(solution)/shard_map/ppermute | solution.py:509
  51.5 0.9 %collective-permute-start.14 = (f16[64,256]{1,0:T(8,128)(2,1)S(1)}, f16[64,256]{1,0:T(8,128)(2,1)S(1)}, u32[]{:S(2)}, u32[]{:S(2)}) collective-permute-start(f16[64,256]{1,0:T(8,128)(2,1)S(1)} %get-tuple-element.43), channel_id=1, source_target_pairs={{0,8},{8,0},{16,24},{24,16},{1,9},{9,1},{17,25},{25,17},{2,10},{10... | collective-permute-start | bytes 98312 | tf_op jit(solution)/shard_map/ppermute | solution.py:509
  52.5 1.2 %collective-permute-done.16 = f16[64,256]{1,0:T(8,128)(2,1)S(1)} collective-permute-done((f16[64,256]{1,0:T(8,128)(2,1)S(1)}, f16[64,256]{1,0:T(8,128)(2,1)S(1)}, u32[]{:S(2)}, u32[]{:S(2)}) %collective-permute-start.16) | collective-permute-done | bytes 32800 | tf_op jit(solution)/shard_map/ppermute | solution.py:509
  53.7 2.6 %collective-permute-done.15 = f16[64,256]{1,0:T(8,128)(2,1)S(1)} collective-permute-done((f16[64,256]{1,0:T(8,128)(2,1)S(1)}, f16[64,256]{1,0:T(8,128)(2,1)S(1)}, u32[]{:S(2)}, u32[]{:S(2)}) %collective-permute-start.15) | collective-permute-done | bytes 32800 | tf_op jit(solution)/shard_map/ppermute | solution.py:509
  56.5 1.1 %collective-permute-start.19 = (f32[64,256]{1,0:T(8,128)S(1)}, f32[64,256]{1,0:T(8,128)S(1)}, u32[]{:S(2)}, u32[]{:S(2)}) collective-permute-start(f32[64,256]{1,0:T(8,128)S(1)} %shard_map.72), channel_id=1, source_target_pairs={{0,5},{1,4},{2,7},{3,6},{4,1},{5,0},{6,3},{7,2},{8,13},{9,12},{10,... | collective-permute-start | bytes 196616 | tf_op jit(solution)/shard_map/ppermute | solution.py:386
  57.6 1.6 %collective-permute-start.18 = (f32[64,256]{1,0:T(8,128)S(1)}, f32[64,256]{1,0:T(8,128)S(1)}, u32[]{:S(2)}, u32[]{:S(2)}) collective-permute-start(f32[64,256]{1,0:T(8,128)S(1)} %shard_map.72), channel_id=1, source_target_pairs={{0,4},{1,5},{2,6},{3,7},{4,0},{5,1},{6,2},{7,3},{8,12},{9,13},{10,... | collective-permute-start | bytes 196616 | tf_op jit(solution)/shard_map/ppermute | solution.py:386
  59.2 0.8 %collective-permute-start.17 = (f32[64,256]{1,0:T(8,128)S(1)}, f32[64,256]{1,0:T(8,128)S(1)}, u32[]{:S(2)}, u32[]{:S(2)}) collective-permute-start(f32[64,256]{1,0:T(8,128)S(1)} %shard_map.72), channel_id=1, source_target_pairs={{0,1},{1,0},{2,3},{3,2},{4,5},{5,4},{6,7},{7,6},{8,9},{9,8},{10,11... | collective-permute-start | bytes 196616 | tf_op jit(solution)/shard_map/ppermute | solution.py:386
  60.0 1.1 %shard_map.73 = f32[36,64,128]{2,1,0:T(8,128)} custom-call(f32[8,296,128]{2,1,0:T(8,128)S(1)} %shard_map.70.refs_0_, f32[1,296,128]{2,1,0:T(8,128)S(1)} %bitcast_convert_fusion.13.refs_1_, f32[1,296,128]{2,1,0:T(8,128)S(1)} %get-tuple-element.56.refs_2_, f32[1,296,128]{2,1,0:T(8,128)S(1)} %get-tuple-element.55.refs_3_, ...), custom_call_target="tpu_custom_call" | custom-call | tf_op jit(solution)/shard_map/pallas_call | solution.py:486
  62.1 1.3 %collective-permute-done.17 = f32[64,256]{1,0:T(8,128)S(1)} collective-permute-done((f32[64,256]{1,0:T(8,128)S(1)}, f32[64,256]{1,0:T(8,128)S(1)}, u32[]{:S(2)}, u32[]{:S(2)}) %collective-permute-start.17) | collective-permute-done | bytes 65568 | tf_op jit(solution)/shard_map/ppermute | solution.py:386
  63.5 1.2 %collective-permute-done.20 = f32[64,256]{1,0:T(8,128)S(1)} collective-permute-done((f32[64,256]{1,0:T(8,128)S(1)}, f32[64,256]{1,0:T(8,128)S(1)}, u32[]{:S(2)}, u32[]{:S(2)}) %collective-permute-start.20) | collective-permute-done | bytes 65568 | tf_op jit(solution)/shard_map/ppermute | solution.py:386
  64.8 0.6 add.52
  (52 shorter events, 4.6 us)
Async XLA Ops:
  0.7 1.6 %copy-start = (f32[4,4,5,128]{3,1,2,0:T(4,128)S(1)}, f32[4,4,5,128]{3,1,2,0:T(4,128)}, u32[]{:S(2)}) copy-start(f32[4,4,5,128]{3,1,2,0:T(4,128)} %param.7) | copy-start | bytes 122884
  0.7 1.6 %copy-start.1 = (f32[6,6,128]{2,1,0:T(8,128)S(1)}, f32[6,6,128]{2,1,0:T(8,128)}, u32[]{:S(2)}) copy-start(f32[6,6,128]{2,1,0:T(8,128)} %potential_ref.1) | copy-start | bytes 55300
  0.7 1.6 %copy-start.2 = (f32[4,4]{1,0:T(4,128)S(1)}, f32[4,4]{1,0:T(4,128)}, u32[]{:S(2)}) copy-start(f32[4,4]{1,0:T(4,128)} %energies_ref.1) | copy-start | bytes 196
  0.7 1.6 %copy-start.3 = (s32[4,2]{0,1:T(2,128)S(1)}, s32[4,2]{0,1:T(2,128)}, u32[]{:S(2)}) copy-start(s32[4,2]{0,1:T(2,128)} %param.9) | copy-start | bytes 100
  3.4 7.2 %collective-permute-start.6 = (f16[408,128]{1,0:T(8,128)(2,1)S(1)}, f16[408,128]{1,0:T(8,128)(2,1)S(1)}, u32[]{:S(2)}, u32[]{:S(2)}) collective-permute-start(f16[408,128]{1,0:T(8,128)(2,1)S(1)} %get-tuple-element.44), channel_id=1, source_target_pairs={{0,7},{1,6},{2,5},{3,4},{4,3},{5,2},{6,1},{7,0},{8,15},{9,14},{10,... | collective-permute-start | bytes 313352 | tf_op jit(solution)/shard_map/ppermute | solution.py:386
  6.8 5.5 %collective-permute-start.1 = (f16[408,128]{1,0:T(8,128)(2,1)S(1)}, f16[408,128]{1,0:T(8,128)(2,1)S(1)}, u32[]{:S(2)}, u32[]{:S(2)}) collective-permute-start(f16[408,128]{1,0:T(8,128)(2,1)S(1)} %get-tuple-element.45), channel_id=1, source_target_pairs={{0,2},{1,3},{2,0},{3,1},{4,6},{5,7},{6,4},{7,5},{8,10},{9,11},{10,... | collective-permute-start | bytes 313352 | tf_op jit(solution)/shard_map/ppermute | solution.py:386
  7.5 6.4 %collective-permute-start.2 = (f16[408,128]{1,0:T(8,128)(2,1)S(1)}, f16[408,128]{1,0:T(8,128)(2,1)S(1)}, u32[]{:S(2)}, u32[]{:S(2)}) collective-permute-start(f16[408,128]{1,0:T(8,128)(2,1)S(1)} %get-tuple-element.46), channel_id=1, source_target_pairs={{0,3},{1,2},{2,1},{3,0},{4,7},{5,6},{6,5},{7,4},{8,11},{9,10},{10,... | collective-permute-start | bytes 313352 | tf_op jit(solution)/shard_map/ppermute | solution.py:386
  7.6 6.4 %collective-permute-start.3 = (f16[408,128]{1,0:T(8,128)(2,1)S(1)}, f16[408,128]{1,0:T(8,128)(2,1)S(1)}, u32[]{:S(2)}, u32[]{:S(2)}) collective-permute-start(f16[408,128]{1,0:T(8,128)(2,1)S(1)} %get-tuple-element.47), channel_id=1, source_target_pairs={{0,4},{1,5},{2,6},{3,7},{4,0},{5,1},{6,2},{7,3},{8,12},{9,13},{10,... | collective-permute-start | bytes 313352 | tf_op jit(solution)/shard_map/ppermute | solution.py:386
  8.1 8.4 %collective-permute-start.4 = (f16[408,128]{1,0:T(8,128)(2,1)S(1)}, f16[408,128]{1,0:T(8,128)(2,1)S(1)}, u32[]{:S(2)}, u32[]{:S(2)}) collective-permute-start(f16[408,128]{1,0:T(8,128)(2,1)S(1)} %get-tuple-element.48), channel_id=1, source_target_pairs={{0,5},{1,4},{2,7},{3,6},{4,1},{5,0},{6,3},{7,2},{8,13},{9,12},{10,... | collective-permute-start | bytes 313352 | tf_op jit(solution)/shard_map/ppermute | solution.py:386
  10.6 7.1 %collective-permute-start.5 = (f16[408,128]{1,0:T(8,128)(2,1)S(1)}, f16[408,128]{1,0:T(8,128)(2,1)S(1)}, u32[]{:S(2)}, u32[]{:S(2)}) collective-permute-start(f16[408,128]{1,0:T(8,128)(2,1)S(1)} %get-tuple-element.49), channel_id=1, source_target_pairs={{0,6},{1,7},{2,4},{3,5},{4,2},{5,3},{6,0},{7,1},{8,14},{9,15},{10,... | collective-permute-start | bytes 313352 | tf_op jit(solution)/shard_map/ppermute | solution.py:386
  12.2 6.1 %collective-permute-start = (f16[408,128]{1,0:T(8,128)(2,1)S(1)}, f16[408,128]{1,0:T(8,128)(2,1)S(1)}, u32[]{:S(2)}, u32[]{:S(2)}) collective-permute-start(f16[408,128]{1,0:T(8,128)(2,1)S(1)} %get-tuple-element.50), channel_id=1, source_target_pairs={{0,1},{1,0},{2,3},{3,2},{4,5},{5,4},{6,7},{7,6},{8,9},{9,8},{10,11... | collective-permute-start | bytes 313352 | tf_op jit(solution)/shard_map/ppermute | solution.py:386
  25.2 22.2 %all-to-all-start = ((bf16[32,8,1152]{2,1,0:T(8,128)(2,1)}), bf16[32,8,1152]{2,1,0:T(8,128)(2,1)S(1)}, u32[]{:S(2)}, u32[]{:S(2)}) async-start(bf16[32,8,1152]{2,1,0:T(8,128)(2,1)} %get-tuple-element.15), calls=%async_computation | async-start | bytes 1179648 | tf_op jit(solution)/shard_map/all_to_all | solution.py:466
  31.1 8.6 %collective-permute-start.13 = (f16[296,128]{1,0:T(8,128)(2,1)S(1)}, f16[296,128]{1,0:T(8,128)(2,1)S(1)}, u32[]{:S(2)}, u32[]{:S(2)}) collective-permute-start(f16[296,128]{1,0:T(8,128)(2,1)S(1)} %get-tuple-element.26), channel_id=1, source_target_pairs={{0,7},{1,6},{2,5},{3,4},{4,3},{5,2},{6,1},{7,0},{8,15},{9,14},{10,... | collective-permute-start | bytes 227336 | tf_op jit(solution)/shard_map/ppermute | solution.py:386
  33.6 7.6 %collective-permute-start.12 = (f16[296,128]{1,0:T(8,128)(2,1)S(1)}, f16[296,128]{1,0:T(8,128)(2,1)S(1)}, u32[]{:S(2)}, u32[]{:S(2)}) collective-permute-start(f16[296,128]{1,0:T(8,128)(2,1)S(1)} %get-tuple-element.27), channel_id=1, source_target_pairs={{0,6},{1,7},{2,4},{3,5},{4,2},{5,3},{6,0},{7,1},{8,14},{9,15},{10,... | collective-permute-start | bytes 227336 | tf_op jit(solution)/shard_map/ppermute | solution.py:386
  34.1 11.2 %collective-permute-start.11 = (f16[296,128]{1,0:T(8,128)(2,1)S(1)}, f16[296,128]{1,0:T(8,128)(2,1)S(1)}, u32[]{:S(2)}, u32[]{:S(2)}) collective-permute-start(f16[296,128]{1,0:T(8,128)(2,1)S(1)} %get-tuple-element.28), channel_id=1, source_target_pairs={{0,5},{1,4},{2,7},{3,6},{4,1},{5,0},{6,3},{7,2},{8,13},{9,12},{10,... | collective-permute-start | bytes 227336 | tf_op jit(solution)/shard_map/ppermute | solution.py:386
  35.6 10.3 %collective-permute-start.10 = (f16[296,128]{1,0:T(8,128)(2,1)S(1)}, f16[296,128]{1,0:T(8,128)(2,1)S(1)}, u32[]{:S(2)}, u32[]{:S(2)}) collective-permute-start(f16[296,128]{1,0:T(8,128)(2,1)S(1)} %get-tuple-element.29), channel_id=1, source_target_pairs={{0,4},{1,5},{2,6},{3,7},{4,0},{5,1},{6,2},{7,3},{8,12},{9,13},{10,... | collective-permute-start | bytes 227336 | tf_op jit(solution)/shard_map/ppermute | solution.py:386
  35.8 10.0 %collective-permute-start.9 = (f16[296,128]{1,0:T(8,128)(2,1)S(1)}, f16[296,128]{1,0:T(8,128)(2,1)S(1)}, u32[]{:S(2)}, u32[]{:S(2)}) collective-permute-start(f16[296,128]{1,0:T(8,128)(2,1)S(1)} %get-tuple-element.30), channel_id=1, source_target_pairs={{0,3},{1,2},{2,1},{3,0},{4,7},{5,6},{6,5},{7,4},{8,11},{9,10},{10,... | collective-permute-start | bytes 227336 | tf_op jit(solution)/shard_map/ppermute | solution.py:386
  39.7 6.2 %collective-permute-start.8 = (f16[296,128]{1,0:T(8,128)(2,1)S(1)}, f16[296,128]{1,0:T(8,128)(2,1)S(1)}, u32[]{:S(2)}, u32[]{:S(2)}) collective-permute-start(f16[296,128]{1,0:T(8,128)(2,1)S(1)} %get-tuple-element.31), channel_id=1, source_target_pairs={{0,2},{1,3},{2,0},{3,1},{4,6},{5,7},{6,4},{7,5},{8,10},{9,11},{10,... | collective-permute-start | bytes 227336 | tf_op jit(solution)/shard_map/ppermute | solution.py:386
  41.2 6.1 %collective-permute-start.7 = (f16[296,128]{1,0:T(8,128)(2,1)S(1)}, f16[296,128]{1,0:T(8,128)(2,1)S(1)}, u32[]{:S(2)}, u32[]{:S(2)}) collective-permute-start(f16[296,128]{1,0:T(8,128)(2,1)S(1)} %get-tuple-element.32), channel_id=1, source_target_pairs={{0,1},{1,0},{2,3},{3,2},{4,5},{5,4},{6,7},{7,6},{8,9},{9,8},{10,11... | collective-permute-start | bytes 227336 | tf_op jit(solution)/shard_map/ppermute | solution.py:386
  47.9 5.8 %collective-permute-start.16 = (f16[64,256]{1,0:T(8,128)(2,1)S(1)}, f16[64,256]{1,0:T(8,128)(2,1)S(1)}, u32[]{:S(2)}, u32[]{:S(2)}) collective-permute-start(f16[64,256]{1,0:T(8,128)(2,1)S(1)} %get-tuple-element.41), channel_id=1, source_target_pairs={{0,24},{8,16},{16,8},{24,0},{1,25},{9,17},{17,9},{25,1},{2,26},{10... | collective-permute-start | bytes 98312 | tf_op jit(solution)/shard_map/ppermute | solution.py:509
  51.5 4.8 %collective-permute-start.15 = (f16[64,256]{1,0:T(8,128)(2,1)S(1)}, f16[64,256]{1,0:T(8,128)(2,1)S(1)}, u32[]{:S(2)}, u32[]{:S(2)}) collective-permute-start(f16[64,256]{1,0:T(8,128)(2,1)S(1)} %get-tuple-element.42), channel_id=1, source_target_pairs={{0,16},{8,24},{16,0},{24,8},{1,17},{9,25},{17,1},{25,9},{2,18},{10... | collective-permute-start | bytes 98312 | tf_op jit(solution)/shard_map/ppermute | solution.py:509
  51.5 4.8 %collective-permute-start.14 = (f16[64,256]{1,0:T(8,128)(2,1)S(1)}, f16[64,256]{1,0:T(8,128)(2,1)S(1)}, u32[]{:S(2)}, u32[]{:S(2)}) collective-permute-start(f16[64,256]{1,0:T(8,128)(2,1)S(1)} %get-tuple-element.43), channel_id=1, source_target_pairs={{0,8},{8,0},{16,24},{24,16},{1,9},{9,1},{17,25},{25,17},{2,10},{10... | collective-permute-start | bytes 98312 | tf_op jit(solution)/shard_map/ppermute | solution.py:509
  56.5 5.2 %collective-permute-start.19 = (f32[64,256]{1,0:T(8,128)S(1)}, f32[64,256]{1,0:T(8,128)S(1)}, u32[]{:S(2)}, u32[]{:S(2)}) collective-permute-start(f32[64,256]{1,0:T(8,128)S(1)} %shard_map.72), channel_id=1, source_target_pairs={{0,5},{1,4},{2,7},{3,6},{4,1},{5,0},{6,3},{7,2},{8,13},{9,12},{10,... | collective-permute-start | bytes 196616 | tf_op jit(solution)/shard_map/ppermute | solution.py:386
  57.6 4.5 %collective-permute-start.18 = (f32[64,256]{1,0:T(8,128)S(1)}, f32[64,256]{1,0:T(8,128)S(1)}, u32[]{:S(2)}, u32[]{:S(2)}) collective-permute-start(f32[64,256]{1,0:T(8,128)S(1)} %shard_map.72), channel_id=1, source_target_pairs={{0,4},{1,5},{2,6},{3,7},{4,0},{5,1},{6,2},{7,3},{8,12},{9,13},{10,... | collective-permute-start | bytes 196616 | tf_op jit(solution)/shard_map/ppermute | solution.py:386
  59.2 4.3 %collective-permute-start.17 = (f32[64,256]{1,0:T(8,128)S(1)}, f32[64,256]{1,0:T(8,128)S(1)}, u32[]{:S(2)}, u32[]{:S(2)}) collective-permute-start(f32[64,256]{1,0:T(8,128)S(1)} %shard_map.72), channel_id=1, source_target_pairs={{0,1},{1,0},{2,3},{3,2},{4,5},{5,4},{6,7},{7,6},{8,9},{9,8},{10,11... | collective-permute-start | bytes 196616 | tf_op jit(solution)/shard_map/ppermute | solution.py:386
  63.4 1.3 %collective-permute-start.20 = (f32[64,256]{1,0:T(8,128)S(1)}, f32[64,256]{1,0:T(8,128)S(1)}, u32[]{:S(2)}, u32[]{:S(2)}) collective-permute-start(f32[64,256]{1,0:T(8,128)S(1)} %add_add_fusion), channel_id=1, source_target_pairs={{0,2},{1,3},{2,0},{3,1},{4,6},{5,7},{6,4},{7,5},{8,10},{9,11},{10,... | collective-permute-start | bytes 196616 | tf_op jit(solution)/shard_map/ppermute | solution.py:386

commit v11 on v10

--- a/solution.py
+++ b/solution.py
@@ -238,14 +238,14 @@
             for a in range(atoms):
                 at_x, at_y = place_of(g, a)
                 factor = [coeffs[g, a * projs + p] for p in range(projs)]
+                cells = [(at_x + offsets_x[t], at_y + offsets_y[t]) for t in range(tiles)]
+                values = [target[cell] for cell in cells]
                 for t in range(tiles):
                     row = (a * tiles + t) * projs
-                    spread = factor[0] * shared_row(g, row)
-                    for p in range(1, projs):
-                        spread = spread + factor[p] * shared_row(g, row + p)
-                    to_x = at_x + offsets_x[t]
-                    to_y = at_y + offsets_y[t]
-                    target[to_x, to_y] = target[to_x, to_y] + spread
+                    for p in range(projs):
+                        values[t] = values[t] + factor[p] * shared_row(g, row + p)
+                for t in range(tiles):
+                    target[cells[t]] = values[t]
 
         over_slabs(scatter_part, 2)
 
@@ -328,27 +328,24 @@
     )
 
 
-def gram_kernel(matrix_ref, out_ref, sums_ref):
+def gram_kernel(matrix_ref, out_ref):
     bands, rows, columns = out_ref.shape
     matrix = matrix_ref[...]
     sums = lax.dot_general(
         matrix, matrix, (((1,), (1,)), ((), ())), preferred_element_type=jnp.float32
     )
     level, gain = level_of(jnp.max(jnp.abs(sums)))
-    sums_ref[...] = sums * gain
-    me = lax.axis_index("band")
-    for k in range(bands):
-        band = jnp.bitwise_xor(me, k)
+    for band in range(bands):
         spare, _ = band_corner((rows, columns), band)
-        block = sums_ref[pl.ds(pl.multiple_of(band * rows, rows), rows), :]
-        out_ref[k] = jnp.where(spare, level, block)
-
-
-def rows_kernel(cells, own_ref, *refs):
-    out_ref = refs[-1]
+        block = sums[band * rows : (band + 1) * rows]
+        out_ref[band] = jnp.where(spare, level, block * gain)
+
+
+def rows_kernel(cells, parts_ref, out_ref):
     spare, twin = band_corner(out_ref.shape, lax.axis_index("band"))
     total = None
-    for block in [own_ref[0]] + [ref[...] for ref in refs[:-1]]:
+    for source in range(parts_ref.shape[0]):
+        block = parts_ref[source]
         block = block * shrink_of(entry(block, spare))
         total = block if total is None else total + block
     out_ref[...] = jnp.where(spare, entry(total, twin), total) / cells
@@ -502,22 +499,16 @@
             in_specs=[vmem],
             out_specs=vmem,
             out_shape=jax.ShapeDtypeStruct((bands, band_orbitals, total_orbitals), jnp.float32),
-            scratch_shapes=[pltpu.VMEM((total_orbitals, total_orbitals), jnp.float32)],
             compiler_params=params,
         )(matrix)
-        parts = [
-            lax.ppermute(
-                sums[k].astype(jnp.float16), "band", [(i, i ^ k) for i in range(bands)]
-            ).astype(jnp.float32)
-            for k in range(1, bands)
-        ]
+        parts = lax.all_to_all(sums.astype(jnp.float16), "band", 0, 0).astype(jnp.float32)
         gram = pl.pallas_call(
             functools.partial(rows_kernel, cells),
-            in_specs=[vmem] * bands,
+            in_specs=[vmem],
             out_specs=vmem,
             out_shape=jax.ShapeDtypeStruct((band_orbitals, total_orbitals), jnp.float32),
             compiler_params=params,
-        )(sums, *parts)
+        )(parts)
         terms = {v: swap(gram, v) for v in far}
         terms[0] = gram
         bit = 1

time: 65.6 us -> 68.9 us (1.050)
  waiting for transfers between devices: 19.2 us -> 21.5 us
    all_to_all x0 -> x1, waiting for transfers between devices: none -> 6.1 us  [local(): lax.all_to_all(sums.astype(jnp.float16), 'band', 0, 0).astype(jnp.float32)]
    all_to_all x0 -> x1, starting transfers between devices: none -> 4.73 us  [local(): lax.all_to_all(sums.astype(jnp.float16), 'band', 0, 0).astype(jnp.float32)]
    ppermute x3 -> x0, starting transfers between devices: 4.45 us -> none  [local(): lax.ppermute(sums[k].astype(jnp.float16), 'band', [(i, i ^ k) for i in ra...]
    ppermute x3 -> x0, waiting for transfers between devices: 3.79 us -> none  [local(): lax.ppermute(sums[k].astype(jnp.float16), 'band', [(i, i ^ k) for i in ra...]
  transfers between devices with their start and end apart: 22 -> 20, of which waited for: 13 -> 12; matrix products, arithmetic and copies ran while one was open for 1% -> 1% of each run, Pallas kernels for 2% -> 2%
where the time goes in v11:
time: 68.9 us; the launch traced here: 68.6 us
  starting transfers between devices  32.8 us (48%)
  waiting for transfers between devices  21.5 us (31%)
  Pallas kernels  9.76 us (14%)
  other arithmetic  3.39 us (5%)
  between operations  0.98 us (1%)
    ppermute x18, starting transfers between devices, swap(): return lax.ppermute(block, plane, [(i, i ^ value) for i in range(group)])  22.7 us
    ppermute x18, waiting for transfers between devices, swap(): return lax.ppermute(block, plane, [(i, i ^ value) for i in range(group)])  15.4 us
    pallas_call x1, Pallas kernels, local(): pl.pallas_call(functools.partial(filter_kernel, slabs_y, cells_x, cells_y...  6.82 us
    all_to_all x1, waiting for transfers between devices, local(): lax.all_to_all(sums.astype(jnp.float16), 'band', 0, 0).astype(jnp.float32)  6.1 us
    all_to_all x1, starting transfers between devices, local(): matrix = lax.all_to_all(rounded, every, 0, 0)  5.29 us
    all_to_all x1, starting transfers between devices, local(): lax.all_to_all(sums.astype(jnp.float16), 'band', 0, 0).astype(jnp.float32)  4.73 us
    convert_element_type x1, other arithmetic, local(): chunks = (orbitals * orbital_gain).astype(jnp.float16)  1.46 us
  transfers between devices with their start and end apart: 20, of which 12 were waited for; matrix products, arithmetic and copies ran while one was open for 1% of the time, Pallas kernels for 2%

profile of v11, /device:TPU:0, one launch (start us, length us, event | category | flops | bytes accessed | tf_op | source)
XLA Modules:
  0.0 68.6 jit_solution(6656912001550694549)
XLA Ops:
  0.7 1.5 %multiply_convert_fusion = f16[64,6,6,128]{3,0,2,1:T(8,128)(2,1)S(1)} fusion(f32[64,6,6,128]{3,0,2,1:T(8,128)} %param.5), kind=kLoop, calls=%fused_computation | loop fusion | flops 589824 | bytes 1769472 | tf_op jit(solution)/shard_map/convert_element_type | solution.py:406
  2.3 0.7 shard_map.68
  3.4 3.4 %collective-permute-start.6 = (f16[408,128]{1,0:T(8,128)(2,1)S(1)}, f16[408,128]{1,0:T(8,128)(2,1)S(1)}, u32[]{:S(2)}, u32[]{:S(2)}) collective-permute-start(f16[408,128]{1,0:T(8,128)(2,1)S(1)} %get-tuple-element.41), channel_id=1, source_target_pairs={{0,7},{1,6},{2,5},{3,4},{4,3},{5,2},{6,1},{7,0},{8,15},{9,14},{10,... | collective-permute-start | bytes 313352 | tf_op jit(solution)/shard_map/ppermute | solution.py:383
  6.8 0.7 collective-permute-start.1
  8.1 2.4 %collective-permute-start.4 = (f16[408,128]{1,0:T(8,128)(2,1)S(1)}, f16[408,128]{1,0:T(8,128)(2,1)S(1)}, u32[]{:S(2)}, u32[]{:S(2)}) collective-permute-start(f16[408,128]{1,0:T(8,128)(2,1)S(1)} %get-tuple-element.45), channel_id=1, source_target_pairs={{0,5},{1,4},{2,7},{3,6},{4,1},{5,0},{6,3},{7,2},{8,13},{9,12},{10,... | collective-permute-start | bytes 313352 | tf_op jit(solution)/shard_map/ppermute | solution.py:383
  10.6 1.7 %collective-permute-start.5 = (f16[408,128]{1,0:T(8,128)(2,1)S(1)}, f16[408,128]{1,0:T(8,128)(2,1)S(1)}, u32[]{:S(2)}, u32[]{:S(2)}) collective-permute-start(f16[408,128]{1,0:T(8,128)(2,1)S(1)} %get-tuple-element.46), channel_id=1, source_target_pairs={{0,6},{1,7},{2,4},{3,5},{4,2},{5,3},{6,0},{7,1},{8,14},{9,15},{10,... | collective-permute-start | bytes 313352 | tf_op jit(solution)/shard_map/ppermute | solution.py:383
  12.2 1.6 %collective-permute-start = (f16[408,128]{1,0:T(8,128)(2,1)S(1)}, f16[408,128]{1,0:T(8,128)(2,1)S(1)}, u32[]{:S(2)}, u32[]{:S(2)}) collective-permute-start(f16[408,128]{1,0:T(8,128)(2,1)S(1)} %get-tuple-element.47), channel_id=1, source_target_pairs={{0,1},{1,0},{2,3},{3,2},{4,5},{5,4},{6,7},{7,6},{8,9},{9,8},{10,11... | collective-permute-start | bytes 313352 | tf_op jit(solution)/shard_map/ppermute | solution.py:383
  14.0 2.5 %collective-permute-done.4 = f16[408,128]{1,0:T(8,128)(2,1)S(1)} collective-permute-done((f16[408,128]{1,0:T(8,128)(2,1)S(1)}, f16[408,128]{1,0:T(8,128)(2,1)S(1)}, u32[]{:S(2)}, u32[]{:S(2)}) %collective-permute-start.4) | collective-permute-done | bytes 104480 | tf_op jit(solution)/shard_map/ppermute | solution.py:383
  16.5 1.2 %collective-permute-done.5 = f16[408,128]{1,0:T(8,128)(2,1)S(1)} collective-permute-done((f16[408,128]{1,0:T(8,128)(2,1)S(1)}, f16[408,128]{1,0:T(8,128)(2,1)S(1)}, u32[]{:S(2)}, u32[]{:S(2)}) %collective-permute-start.5) | collective-permute-done | bytes 104480 | tf_op jit(solution)/shard_map/ppermute | solution.py:383
  17.7 0.6 collective-permute-done
  18.4 6.8 %shard_map.69 = (f32[26,14,8,128]{3,2,1,0:T(8,128)S(1)}, bf16[32,8,1152]{2,1,0:T(8,128)(2,1)}) custom-call(f32[1,288,128]{2,1,0:T(8,128)S(1)} %get-tuple-element.40.refs_0_, f32[1,120,128]{2,1,0:T(8,128)S(1)} %bitcast.91, f32[1,408,128]{2,1,0:T(8,128)S(1)} %bitcast_convert_fusion.6.refs_2_, f32[1,408,128]{2,1,0:T(8,128)S(1)} %bitcast_convert_fusion.5.refs_3_, ...), custom_call_target="tpu_custom_call" | custom-call | flops 47185920 | bytes 2359296 | tf_op jit(solution)/shard_map/pallas_call | solution.py:437
  25.2 5.3 %all-to-all-start = ((bf16[32,8,1152]{2,1,0:T(8,128)(2,1)}), bf16[32,8,1152]{2,1,0:T(8,128)(2,1)S(1)}, u32[]{:S(2)}, u32[]{:S(2)}) async-start(bf16[32,8,1152]{2,1,0:T(8,128)(2,1)} %get-tuple-element.15), calls=%async_computation | async-start | bytes 1179648 | tf_op jit(solution)/shard_map/all_to_all | solution.py:463
  31.1 2.5 %collective-permute-start.13 = (f16[296,128]{1,0:T(8,128)(2,1)S(1)}, f16[296,128]{1,0:T(8,128)(2,1)S(1)}, u32[]{:S(2)}, u32[]{:S(2)}) collective-permute-start(f16[296,128]{1,0:T(8,128)(2,1)S(1)} %get-tuple-element.26), channel_id=1, source_target_pairs={{0,7},{1,6},{2,5},{3,4},{4,3},{5,2},{6,1},{7,0},{8,15},{9,14},{10,... | collective-permute-start | bytes 227336 | tf_op jit(solution)/shard_map/ppermute | solution.py:383
  34.1 1.5 %collective-permute-start.11 = (f16[296,128]{1,0:T(8,128)(2,1)S(1)}, f16[296,128]{1,0:T(8,128)(2,1)S(1)}, u32[]{:S(2)}, u32[]{:S(2)}) collective-permute-start(f16[296,128]{1,0:T(8,128)(2,1)S(1)} %get-tuple-element.28), channel_id=1, source_target_pairs={{0,5},{1,4},{2,7},{3,6},{4,1},{5,0},{6,3},{7,2},{8,13},{9,12},{10,... | collective-permute-start | bytes 227336 | tf_op jit(solution)/shard_map/ppermute | solution.py:383
  35.9 1.0 %collective-permute-start.9 = (f16[296,128]{1,0:T(8,128)(2,1)S(1)}, f16[296,128]{1,0:T(8,128)(2,1)S(1)}, u32[]{:S(2)}, u32[]{:S(2)}) collective-permute-start(f16[296,128]{1,0:T(8,128)(2,1)S(1)} %get-tuple-element.30), channel_id=1, source_target_pairs={{0,3},{1,2},{2,1},{3,0},{4,7},{5,6},{6,5},{7,4},{8,11},{9,10},{10,... | collective-permute-start | bytes 227336 | tf_op jit(solution)/shard_map/ppermute | solution.py:383
  36.8 2.9 %collective-permute-done.13 = f16[296,128]{1,0:T(8,128)(2,1)S(1)} collective-permute-done((f16[296,128]{1,0:T(8,128)(2,1)S(1)}, f16[296,128]{1,0:T(8,128)(2,1)S(1)}, u32[]{:S(2)}, u32[]{:S(2)}) %collective-permute-start.13) | collective-permute-done | bytes 75808 | tf_op jit(solution)/shard_map/ppermute | solution.py:383
  39.7 1.5 %collective-permute-start.8 = (f16[296,128]{1,0:T(8,128)(2,1)S(1)}, f16[296,128]{1,0:T(8,128)(2,1)S(1)}, u32[]{:S(2)}, u32[]{:S(2)}) collective-permute-start(f16[296,128]{1,0:T(8,128)(2,1)S(1)} %get-tuple-element.31), channel_id=1, source_target_pairs={{0,2},{1,3},{2,0},{3,1},{4,6},{5,7},{6,4},{7,5},{8,10},{9,11},{10,... | collective-permute-start | bytes 227336 | tf_op jit(solution)/shard_map/ppermute | solution.py:383
  41.2 1.5 %collective-permute-start.7 = (f16[296,128]{1,0:T(8,128)(2,1)S(1)}, f16[296,128]{1,0:T(8,128)(2,1)S(1)}, u32[]{:S(2)}, u32[]{:S(2)}) collective-permute-start(f16[296,128]{1,0:T(8,128)(2,1)S(1)} %get-tuple-element.32), channel_id=1, source_target_pairs={{0,1},{1,0},{2,3},{3,2},{4,5},{5,4},{6,7},{7,6},{8,9},{9,8},{10,11... | collective-permute-start | bytes 227336 | tf_op jit(solution)/shard_map/ppermute | solution.py:383
  42.7 2.6 %collective-permute-done.11 = f16[296,128]{1,0:T(8,128)(2,1)S(1)} collective-permute-done((f16[296,128]{1,0:T(8,128)(2,1)S(1)}, f16[296,128]{1,0:T(8,128)(2,1)S(1)}, u32[]{:S(2)}, u32[]{:S(2)}) %collective-permute-start.11) | collective-permute-done | bytes 75808 | tf_op jit(solution)/shard_map/ppermute | solution.py:383
  45.3 0.6 collective-permute-done.10
  45.9 1.5 %collective-permute-done.7 = f16[296,128]{1,0:T(8,128)(2,1)S(1)} collective-permute-done((f16[296,128]{1,0:T(8,128)(2,1)S(1)}, f16[296,128]{1,0:T(8,128)(2,1)S(1)}, u32[]{:S(2)}, u32[]{:S(2)}) %collective-permute-start.7) | collective-permute-done | bytes 75808 | tf_op jit(solution)/shard_map/ppermute | solution.py:383
  47.9 0.7 convert_element_type.44
  48.6 4.7 %all-to-all-start.1 = ((f16[4,64,256]{2,1,0:T(8,128)(2,1)}), f16[4,64,256]{2,1,0:T(8,128)(2,1)S(1)}, u32[]{:S(2)}, u32[]{:S(2)}) async-start(f16[4,64,256]{2,1,0:T(8,128)(2,1)} %convert_element_type.44), calls=%async_computation.1 | async-start | bytes 262144 | tf_op jit(solution)/shard_map/all_to_all | solution.py:504
  53.4 6.1 %all-to-all-done.1 = f16[4,64,256]{2,1,0:T(8,128)(2,1)S(1)} async-done(((f16[4,64,256]{2,1,0:T(8,128)(2,1)}), f16[4,64,256]{2,1,0:T(8,128)(2,1)S(1)}, u32[]{:S(2)}, u32[]{:S(2)}) %all-to-all-start.1) | async-done | bytes 131104 | tf_op jit(solution)/shard_map/all_to_all | solution.py:504
  59.7 1.0 %collective-permute-start.16 = (f32[64,256]{1,0:T(8,128)S(1)}, f32[64,256]{1,0:T(8,128)S(1)}, u32[]{:S(2)}, u32[]{:S(2)}) collective-permute-start(f32[64,256]{1,0:T(8,128)S(1)} %shard_map.72), channel_id=1, source_target_pairs={{0,5},{1,4},{2,7},{3,6},{4,1},{5,0},{6,3},{7,2},{8,13},{9,12},{10,... | collective-permute-start | bytes 196616 | tf_op jit(solution)/shard_map/ppermute | solution.py:383
  60.7 1.6 %collective-permute-start.15 = (f32[64,256]{1,0:T(8,128)S(1)}, f32[64,256]{1,0:T(8,128)S(1)}, u32[]{:S(2)}, u32[]{:S(2)}) collective-permute-start(f32[64,256]{1,0:T(8,128)S(1)} %shard_map.72), channel_id=1, source_target_pairs={{0,4},{1,5},{2,6},{3,7},{4,0},{5,1},{6,2},{7,3},{8,12},{9,13},{10,... | collective-permute-start | bytes 196616 | tf_op jit(solution)/shard_map/ppermute | solution.py:383
  62.4 0.8 %collective-permute-start.14 = (f32[64,256]{1,0:T(8,128)S(1)}, f32[64,256]{1,0:T(8,128)S(1)}, u32[]{:S(2)}, u32[]{:S(2)}) collective-permute-start(f32[64,256]{1,0:T(8,128)S(1)} %shard_map.72), channel_id=1, source_target_pairs={{0,1},{1,0},{2,3},{3,2},{4,5},{5,4},{6,7},{7,6},{8,9},{9,8},{10,11... | collective-permute-start | bytes 196616 | tf_op jit(solution)/shard_map/ppermute | solution.py:383
  63.2 1.1 %shard_map.73 = f32[36,64,128]{2,1,0:T(8,128)} custom-call(f32[8,296,128]{2,1,0:T(8,128)S(1)} %shard_map.70.refs_0_, f32[1,296,128]{2,1,0:T(8,128)S(1)} %bitcast_convert_fusion.13.refs_1_, f32[1,296,128]{2,1,0:T(8,128)S(1)} %get-tuple-element.53.refs_2_, f32[1,296,128]{2,1,0:T(8,128)S(1)} %get-tuple-element.52.refs_3_, ...), custom_call_target="tpu_custom_call" | custom-call | tf_op jit(solution)/shard_map/pallas_call | solution.py:483
  64.3 0.5 collective-permute-done.16
  65.3 1.3 %collective-permute-done.14 = f32[64,256]{1,0:T(8,128)S(1)} collective-permute-done((f32[64,256]{1,0:T(8,128)S(1)}, f32[64,256]{1,0:T(8,128)S(1)}, u32[]{:S(2)}, u32[]{:S(2)}) %collective-permute-start.14) | collective-permute-done | bytes 65568 | tf_op jit(solution)/shard_map/ppermute | solution.py:383
  66.7 1.2 %collective-permute-done.17 = f32[64,256]{1,0:T(8,128)S(1)} collective-permute-done((f32[64,256]{1,0:T(8,128)S(1)}, f32[64,256]{1,0:T(8,128)S(1)}, u32[]{:S(2)}, u32[]{:S(2)}) %collective-permute-start.17) | collective-permute-done | bytes 65568 | tf_op jit(solution)/shard_map/ppermute | solution.py:383
  68.0 0.6 add.52
  (45 shorter events, 4.0 us)
Async XLA Ops:
  0.7 1.6 %copy-start = (f32[4,4,5,128]{3,1,2,0:T(4,128)S(1)}, f32[4,4,5,128]{3,1,2,0:T(4,128)}, u32[]{:S(2)}) copy-start(f32[4,4,5,128]{3,1,2,0:T(4,128)} %param.7) | copy-start | bytes 122884
  0.7 1.6 %copy-start.1 = (f32[6,6,128]{2,1,0:T(8,128)S(1)}, f32[6,6,128]{2,1,0:T(8,128)}, u32[]{:S(2)}) copy-start(f32[6,6,128]{2,1,0:T(8,128)} %potential_ref.1) | copy-start | bytes 55300
  0.7 1.6 %copy-start.2 = (f32[4,4]{1,0:T(4,128)S(1)}, f32[4,4]{1,0:T(4,128)}, u32[]{:S(2)}) copy-start(f32[4,4]{1,0:T(4,128)} %energies_ref.1) | copy-start | bytes 196
  0.7 1.6 %copy-start.3 = (s32[4,2]{0,1:T(2,128)S(1)}, s32[4,2]{0,1:T(2,128)}, u32[]{:S(2)}) copy-start(s32[4,2]{0,1:T(2,128)} %param.9) | copy-start | bytes 100
  3.4 7.2 %collective-permute-start.6 = (f16[408,128]{1,0:T(8,128)(2,1)S(1)}, f16[408,128]{1,0:T(8,128)(2,1)S(1)}, u32[]{:S(2)}, u32[]{:S(2)}) collective-permute-start(f16[408,128]{1,0:T(8,128)(2,1)S(1)} %get-tuple-element.41), channel_id=1, source_target_pairs={{0,7},{1,6},{2,5},{3,4},{4,3},{5,2},{6,1},{7,0},{8,15},{9,14},{10,... | collective-permute-start | bytes 313352 | tf_op jit(solution)/shard_map/ppermute | solution.py:383
  6.8 5.5 %collective-permute-start.1 = (f16[408,128]{1,0:T(8,128)(2,1)S(1)}, f16[408,128]{1,0:T(8,128)(2,1)S(1)}, u32[]{:S(2)}, u32[]{:S(2)}) collective-permute-start(f16[408,128]{1,0:T(8,128)(2,1)S(1)} %get-tuple-element.42), channel_id=1, source_target_pairs={{0,2},{1,3},{2,0},{3,1},{4,6},{5,7},{6,4},{7,5},{8,10},{9,11},{10,... | collective-permute-start | bytes 313352 | tf_op jit(solution)/shard_map/ppermute | solution.py:383
  7.5 6.4 %collective-permute-start.2 = (f16[408,128]{1,0:T(8,128)(2,1)S(1)}, f16[408,128]{1,0:T(8,128)(2,1)S(1)}, u32[]{:S(2)}, u32[]{:S(2)}) collective-permute-start(f16[408,128]{1,0:T(8,128)(2,1)S(1)} %get-tuple-element.43), channel_id=1, source_target_pairs={{0,3},{1,2},{2,1},{3,0},{4,7},{5,6},{6,5},{7,4},{8,11},{9,10},{10,... | collective-permute-start | bytes 313352 | tf_op jit(solution)/shard_map/ppermute | solution.py:383
  7.6 6.4 %collective-permute-start.3 = (f16[408,128]{1,0:T(8,128)(2,1)S(1)}, f16[408,128]{1,0:T(8,128)(2,1)S(1)}, u32[]{:S(2)}, u32[]{:S(2)}) collective-permute-start(f16[408,128]{1,0:T(8,128)(2,1)S(1)} %get-tuple-element.44), channel_id=1, source_target_pairs={{0,4},{1,5},{2,6},{3,7},{4,0},{5,1},{6,2},{7,3},{8,12},{9,13},{10,... | collective-permute-start | bytes 313352 | tf_op jit(solution)/shard_map/ppermute | solution.py:383
  8.1 8.4 %collective-permute-start.4 = (f16[408,128]{1,0:T(8,128)(2,1)S(1)}, f16[408,128]{1,0:T(8,128)(2,1)S(1)}, u32[]{:S(2)}, u32[]{:S(2)}) collective-permute-start(f16[408,128]{1,0:T(8,128)(2,1)S(1)} %get-tuple-element.45), channel_id=1, source_target_pairs={{0,5},{1,4},{2,7},{3,6},{4,1},{5,0},{6,3},{7,2},{8,13},{9,12},{10,... | collective-permute-start | bytes 313352 | tf_op jit(solution)/shard_map/ppermute | solution.py:383
  10.6 7.1 %collective-permute-start.5 = (f16[408,128]{1,0:T(8,128)(2,1)S(1)}, f16[408,128]{1,0:T(8,128)(2,1)S(1)}, u32[]{:S(2)}, u32[]{:S(2)}) collective-permute-start(f16[408,128]{1,0:T(8,128)(2,1)S(1)} %get-tuple-element.46), channel_id=1, source_target_pairs={{0,6},{1,7},{2,4},{3,5},{4,2},{5,3},{6,0},{7,1},{8,14},{9,15},{10,... | collective-permute-start | bytes 313352 | tf_op jit(solution)/shard_map/ppermute | solution.py:383
  12.2 6.1 %collective-permute-start = (f16[408,128]{1,0:T(8,128)(2,1)S(1)}, f16[408,128]{1,0:T(8,128)(2,1)S(1)}, u32[]{:S(2)}, u32[]{:S(2)}) collective-permute-start(f16[408,128]{1,0:T(8,128)(2,1)S(1)} %get-tuple-element.47), channel_id=1, source_target_pairs={{0,1},{1,0},{2,3},{3,2},{4,5},{5,4},{6,7},{7,6},{8,9},{9,8},{10,11... | collective-permute-start | bytes 313352 | tf_op jit(solution)/shard_map/ppermute | solution.py:383
  25.2 22.2 %all-to-all-start = ((bf16[32,8,1152]{2,1,0:T(8,128)(2,1)}), bf16[32,8,1152]{2,1,0:T(8,128)(2,1)S(1)}, u32[]{:S(2)}, u32[]{:S(2)}) async-start(bf16[32,8,1152]{2,1,0:T(8,128)(2,1)} %get-tuple-element.15), calls=%async_computation | async-start | bytes 1179648 | tf_op jit(solution)/shard_map/all_to_all | solution.py:463
  31.1 8.6 %collective-permute-start.13 = (f16[296,128]{1,0:T(8,128)(2,1)S(1)}, f16[296,128]{1,0:T(8,128)(2,1)S(1)}, u32[]{:S(2)}, u32[]{:S(2)}) collective-permute-start(f16[296,128]{1,0:T(8,128)(2,1)S(1)} %get-tuple-element.26), channel_id=1, source_target_pairs={{0,7},{1,6},{2,5},{3,4},{4,3},{5,2},{6,1},{7,0},{8,15},{9,14},{10,... | collective-permute-start | bytes 227336 | tf_op jit(solution)/shard_map/ppermute | solution.py:383
  33.6 7.6 %collective-permute-start.12 = (f16[296,128]{1,0:T(8,128)(2,1)S(1)}, f16[296,128]{1,0:T(8,128)(2,1)S(1)}, u32[]{:S(2)}, u32[]{:S(2)}) collective-permute-start(f16[296,128]{1,0:T(8,128)(2,1)S(1)} %get-tuple-element.27), channel_id=1, source_target_pairs={{0,6},{1,7},{2,4},{3,5},{4,2},{5,3},{6,0},{7,1},{8,14},{9,15},{10,... | collective-permute-start | bytes 227336 | tf_op jit(solution)/shard_map/ppermute | solution.py:383
  34.1 11.2 %collective-permute-start.11 = (f16[296,128]{1,0:T(8,128)(2,1)S(1)}, f16[296,128]{1,0:T(8,128)(2,1)S(1)}, u32[]{:S(2)}, u32[]{:S(2)}) collective-permute-start(f16[296,128]{1,0:T(8,128)(2,1)S(1)} %get-tuple-element.28), channel_id=1, source_target_pairs={{0,5},{1,4},{2,7},{3,6},{4,1},{5,0},{6,3},{7,2},{8,13},{9,12},{10,... | collective-permute-start | bytes 227336 | tf_op jit(solution)/shard_map/ppermute | solution.py:383
  35.6 10.3 %collective-permute-start.10 = (f16[296,128]{1,0:T(8,128)(2,1)S(1)}, f16[296,128]{1,0:T(8,128)(2,1)S(1)}, u32[]{:S(2)}, u32[]{:S(2)}) collective-permute-start(f16[296,128]{1,0:T(8,128)(2,1)S(1)} %get-tuple-element.29), channel_id=1, source_target_pairs={{0,4},{1,5},{2,6},{3,7},{4,0},{5,1},{6,2},{7,3},{8,12},{9,13},{10,... | collective-permute-start | bytes 227336 | tf_op jit(solution)/shard_map/ppermute | solution.py:383
  35.9 10.0 %collective-permute-start.9 = (f16[296,128]{1,0:T(8,128)(2,1)S(1)}, f16[296,128]{1,0:T(8,128)(2,1)S(1)}, u32[]{:S(2)}, u32[]{:S(2)}) collective-permute-start(f16[296,128]{1,0:T(8,128)(2,1)S(1)} %get-tuple-element.30), channel_id=1, source_target_pairs={{0,3},{1,2},{2,1},{3,0},{4,7},{5,6},{6,5},{7,4},{8,11},{9,10},{10,... | collective-permute-start | bytes 227336 | tf_op jit(solution)/shard_map/ppermute | solution.py:383
  39.7 6.2 %collective-permute-start.8 = (f16[296,128]{1,0:T(8,128)(2,1)S(1)}, f16[296,128]{1,0:T(8,128)(2,1)S(1)}, u32[]{:S(2)}, u32[]{:S(2)}) collective-permute-start(f16[296,128]{1,0:T(8,128)(2,1)S(1)} %get-tuple-element.31), channel_id=1, source_target_pairs={{0,2},{1,3},{2,0},{3,1},{4,6},{5,7},{6,4},{7,5},{8,10},{9,11},{10,... | collective-permute-start | bytes 227336 | tf_op jit(solution)/shard_map/ppermute | solution.py:383
  41.2 6.1 %collective-permute-start.7 = (f16[296,128]{1,0:T(8,128)(2,1)S(1)}, f16[296,128]{1,0:T(8,128)(2,1)S(1)}, u32[]{:S(2)}, u32[]{:S(2)}) collective-permute-start(f16[296,128]{1,0:T(8,128)(2,1)S(1)} %get-tuple-element.32), channel_id=1, source_target_pairs={{0,1},{1,0},{2,3},{3,2},{4,5},{5,4},{6,7},{7,6},{8,9},{9,8},{10,11... | collective-permute-start | bytes 227336 | tf_op jit(solution)/shard_map/ppermute | solution.py:383
  48.6 10.9 %all-to-all-start.1 = ((f16[4,64,256]{2,1,0:T(8,128)(2,1)}), f16[4,64,256]{2,1,0:T(8,128)(2,1)S(1)}, u32[]{:S(2)}, u32[]{:S(2)}) async-start(f16[4,64,256]{2,1,0:T(8,128)(2,1)} %convert_element_type.44), calls=%async_computation.1 | async-start | bytes 262144 | tf_op jit(solution)/shard_map/all_to_all | solution.py:504
  59.7 5.2 %collective-permute-start.16 = (f32[64,256]{1,0:T(8,128)S(1)}, f32[64,256]{1,0:T(8,128)S(1)}, u32[]{:S(2)}, u32[]{:S(2)}) collective-permute-start(f32[64,256]{1,0:T(8,128)S(1)} %shard_map.72), channel_id=1, source_target_pairs={{0,5},{1,4},{2,7},{3,6},{4,1},{5,0},{6,3},{7,2},{8,13},{9,12},{10,... | collective-permute-start | bytes 196616 | tf_op jit(solution)/shard_map/ppermute | solution.py:383
  60.7 4.6 %collective-permute-start.15 = (f32[64,256]{1,0:T(8,128)S(1)}, f32[64,256]{1,0:T(8,128)S(1)}, u32[]{:S(2)}, u32[]{:S(2)}) collective-permute-start(f32[64,256]{1,0:T(8,128)S(1)} %shard_map.72), channel_id=1, source_target_pairs={{0,4},{1,5},{2,6},{3,7},{4,0},{5,1},{6,2},{7,3},{8,12},{9,13},{10,... | collective-permute-start | bytes 196616 | tf_op jit(solution)/shard_map/ppermute | solution.py:383
  62.4 4.3 %collective-permute-start.14 = (f32[64,256]{1,0:T(8,128)S(1)}, f32[64,256]{1,0:T(8,128)S(1)}, u32[]{:S(2)}, u32[]{:S(2)}) collective-permute-start(f32[64,256]{1,0:T(8,128)S(1)} %shard_map.72), channel_id=1, source_target_pairs={{0,1},{1,0},{2,3},{3,2},{4,5},{5,4},{6,7},{7,6},{8,9},{9,8},{10,11... | collective-permute-start | bytes 196616 | tf_op jit(solution)/shard_map/ppermute | solution.py:383
  66.6 1.3 %collective-permute-start.17 = (f32[64,256]{1,0:T(8,128)S(1)}, f32[64,256]{1,0:T(8,128)S(1)}, u32[]{:S(2)}, u32[]{:S(2)}) collective-permute-start(f32[64,256]{1,0:T(8,128)S(1)} %add_add_fusion), channel_id=1, source_target_pairs={{0,2},{1,3},{2,0},{3,1},{4,6},{5,7},{6,4},{7,5},{8,10},{9,11},{10,... | collective-permute-start | bytes 196616 | tf_op jit(solution)/shard_map/ppermute | solution.py:383

commit v12 on v10

--- a/solution.py
+++ b/solution.py
@@ -196,7 +196,7 @@
                 partial[x, y] = along_z[x] + diagonal[x, y] * cells[x] + along(cells, x)
             return carry
 
-        lax.fori_loop(0, count_y, xz_part, 0, unroll=2)
+        lax.fori_loop(0, count_y, xz_part, 0)
 
         def y_part(x, carry):
             cells = [source[ring + x, ring + y] for y in range(count_y)]
@@ -205,7 +205,7 @@
                 target[ring + x, ring + y] = finish(total, target, ring + x, ring + y)
             return carry
 
-        lax.fori_loop(0, count_x, y_part, 0, unroll=2)
+        lax.fori_loop(0, count_x, y_part, 0, unroll=4)
 
         def place_of(g, a):
             at = 2 * atoms * projs + 2 * a
@@ -423,11 +423,20 @@
         def chunk_for(value):
             return lax.dynamic_index_in_dim(chunks, me ^ value, 0, keepdims=False)
 
-        came = [swap(jnp.concatenate([chunk_for(v), narrow]), v) for v in range(1, group)]
-        operands = [chunk_for(0).astype(jnp.float32)[None], shared[None]]
-        operands += [block.astype(jnp.float32)[None] for block in came]
-        slabs = {v: ((1 + v, 0, 0), (1 + v, 0, piece_rows)) for v in range(1, group)}
-        slabs[0] = ((0, 0, 0), (1, 0, 0))
+        pieces = [swap(jnp.stack([chunk_for(v), chunk_for(v ^ near)]), v) for v in far]
+        common = [swap(narrow, v) for v in far]
+        for_core = [chunk_for(near)] + [block[1] for block in pieces]
+        crossed = swap(
+            jnp.stack([jnp.concatenate(pair) for pair in zip(for_core, [narrow] + common)]), near
+        )
+        operands = [chunk_for(0)[None], narrow[None]] + pieces + [block[None] for block in common]
+        operands = [block.astype(jnp.float32) for block in operands + [crossed]]
+        operands[1] = shared[None]
+        last = len(operands) - 1
+        slabs = {0: ((0, 0, 0), (1, 0, 0)), near: ((last, 0, 0), (last, 0, piece_rows))}
+        for i, v in enumerate(far):
+            slabs[v] = ((2 + i, 0, 0), (2 + len(far) + i, 0, 0))
+            slabs[v ^ near] = ((last, 1 + i, 0), (last, 1 + i, piece_rows))
     else:
         sent = jnp.concatenate([chunks, jnp.broadcast_to(narrow[None], (group, rows, nz))], axis=1)
         operands = [lax.all_to_all(sent, plane, 0, 0).astype(jnp.float32)]

time: 65.6 us -> 69.1 us (1.053)
  waiting for transfers between devices: 19.2 us -> 21.1 us
  Pallas kernels: 9.74 us -> 11.4 us
    ppermute x18, waiting for transfers between devices: 15.4 us -> 17.3 us  [swap(): return lax.ppermute(block, plane, [(i, i ^ value) for i in range(group)])]
    pallas_call x1, Pallas kernels: 6.79 us -> 8.49 us  [local(): pl.pallas_call(functools.partial(filter_kernel, slabs_y, cells_x, cells_y...]
    ppermute x18, starting transfers between devices: 22.7 us -> 22 us  [swap(): return lax.ppermute(block, plane, [(i, i ^ value) for i in range(group)])]
  transfers between devices with their start and end apart: 22 -> 22, of which waited for: 13 -> 15; matrix products, arithmetic and copies ran while one was open for 1% -> 1% of each run, Pallas kernels for 2% -> 2%
where the time goes in v12:
time: 69.1 us; the launch traced here: 68.9 us
  starting transfers between devices  32.1 us (46%)
  waiting for transfers between devices  21.1 us (31%)
  Pallas kernels  11.4 us (16%)
  other arithmetic  2.98 us (4%)
  between operations  0.99 us (1%)
    ppermute x18, starting transfers between devices, swap(): return lax.ppermute(block, plane, [(i, i ^ value) for i in range(group)])  22 us
    ppermute x18, waiting for transfers between devices, swap(): return lax.ppermute(block, plane, [(i, i ^ value) for i in range(group)])  17.3 us
    pallas_call x1, Pallas kernels, local(): pl.pallas_call(functools.partial(filter_kernel, slabs_y, cells_x, cells_y...  8.49 us
    all_to_all x1, starting transfers between devices, local(): matrix = lax.all_to_all(rounded, every, 0, 0)  5.57 us
    ppermute x3, starting transfers between devices, local(): lax.ppermute(sums[k].astype(jnp.float16), 'band', [(i, i ^ k) for i in ra...  4.45 us
    ppermute x3, waiting for transfers between devices, local(): lax.ppermute(sums[k].astype(jnp.float16), 'band', [(i, i ^ k) for i in ra...  3.8 us
    convert_element_type x1, other arithmetic, local(): chunks = (orbitals * orbital_gain).astype(jnp.float16)  1.46 us
  transfers between devices with their start and end apart: 22, of which 15 were waited for; matrix products, arithmetic and copies ran while one was open for 1% of the time, Pallas kernels for 2%

profile of v12, /device:TPU:0, one launch (start us, length us, event | category | flops | bytes accessed | tf_op | source)
XLA Modules:
  0.0 68.9 jit_solution(3611240209499475825)
XLA Ops:
  0.7 1.5 %multiply_convert_fusion = f16[64,6,6,128]{3,0,2,1:T(8,128)(2,1)S(1)} fusion(f32[64,6,6,128]{3,0,2,1:T(8,128)} %param.5), kind=kLoop, calls=%fused_computation | loop fusion | flops 589824 | bytes 1769472 | tf_op jit(solution)/shard_map/convert_element_type | solution.py:409
  2.3 0.7 shard_map.68
  3.0 4.0 %collective-permute-start.5 = (f16[120,128]{1,0:T(8,128)(2,1)S(1)}, f16[120,128]{1,0:T(8,128)(2,1)S(1)}, u32[]{:S(2)}, u32[]{:S(2)}) collective-permute-start(f16[120,128]{1,0:T(8,128)(2,1)S(1)} %convert_element_type.79), channel_id=1, source_target_pairs={{0,5},{1,4},{2,7},{3,6},{4,1},{5,0},{6,3},{7,2},{8,13},{9,12},{10,... | collective-permute-start | bytes 92168 | tf_op jit(solution)/shard_map/ppermute | solution.py:386
  7.8 2.0 %collective-permute-start = (f16[2,288,128]{2,1,0:T(8,128)(2,1)S(1)}, f16[2,288,128]{2,1,0:T(8,128)(2,1)S(1)}, u32[]{:S(2)}, u32[]{:S(2)}) collective-permute-start(f16[2,288,128]{2,1,0:T(8,128)(2,1)S(1)} %pad_maximum_fusion.1), channel_id=1, source_target_pairs={{0,1},{1,0},{2,3},{3,2},{4,5},{5,4},{6,7},{7,6},{8,9},{9,8},{10,11... | collective-permute-start | bytes 442376 | tf_op jit(solution)/shard_map/ppermute | solution.py:386
  9.8 1.6 %collective-permute-start.1 = (f16[2,288,128]{2,1,0:T(8,128)(2,1)S(1)}, f16[2,288,128]{2,1,0:T(8,128)(2,1)S(1)}, u32[]{:S(2)}, u32[]{:S(2)}) collective-permute-start(f16[2,288,128]{2,1,0:T(8,128)(2,1)S(1)} %pad_maximum_fusion.2), channel_id=1, source_target_pairs={{0,4},{1,5},{2,6},{3,7},{4,0},{5,1},{6,2},{7,3},{8,12},{9,13},{10,... | collective-permute-start | bytes 442376 | tf_op jit(solution)/shard_map/ppermute | solution.py:386
  11.6 1.5 %collective-permute-start.2 = (f16[2,288,128]{2,1,0:T(8,128)(2,1)S(1)}, f16[2,288,128]{2,1,0:T(8,128)(2,1)S(1)}, u32[]{:S(2)}, u32[]{:S(2)}) collective-permute-start(f16[2,288,128]{2,1,0:T(8,128)(2,1)S(1)} %pad_maximum_fusion.3), channel_id=1, source_target_pairs={{0,5},{1,4},{2,7},{3,6},{4,1},{5,0},{6,3},{7,2},{8,13},{9,12},{10,... | collective-permute-start | bytes 442376 | tf_op jit(solution)/shard_map/ppermute | solution.py:386
  13.7 2.2 %collective-permute-done.1 = f16[2,288,128]{2,1,0:T(8,128)(2,1)S(1)} collective-permute-done((f16[2,288,128]{2,1,0:T(8,128)(2,1)S(1)}, f16[2,288,128]{2,1,0:T(8,128)(2,1)S(1)}, u32[]{:S(2)}, u32[]{:S(2)}) %collective-permute-start.1) | collective-permute-done | bytes 147488 | tf_op jit(solution)/shard_map/ppermute | solution.py:386
  15.9 1.8 %collective-permute-done.2 = f16[2,288,128]{2,1,0:T(8,128)(2,1)S(1)} collective-permute-done((f16[2,288,128]{2,1,0:T(8,128)(2,1)S(1)}, f16[2,288,128]{2,1,0:T(8,128)(2,1)S(1)}, u32[]{:S(2)}, u32[]{:S(2)}) %collective-permute-start.2) | collective-permute-done | bytes 147488 | tf_op jit(solution)/shard_map/ppermute | solution.py:386
  18.2 1.6 %collective-permute-done.6 = f16[4,408,128]{2,1,0:T(8,128)(2,1)S(1)} collective-permute-done((f16[4,408,128]{2,1,0:T(8,128)(2,1)S(1)}, f16[4,408,128]{2,1,0:T(8,128)(2,1)S(1)}, u32[]{:S(2)}, u32[]{:S(2)}) %collective-permute-start.6) | collective-permute-done | bytes 417824 | tf_op jit(solution)/shard_map/ppermute | solution.py:386
  19.9 8.5 %shard_map.69 = (f32[26,14,8,128]{3,2,1,0:T(8,128)S(1)}, bf16[32,8,1152]{2,1,0:T(8,128)(2,1)}) custom-call(f32[1,288,128]{2,1,0:T(8,128)S(1)} %get-tuple-element.40.refs_0_, f32[1,120,128]{2,1,0:T(8,128)S(1)} %bitcast.87, f32[2,288,128]{2,1,0:T(8,128)S(1)} %convert_element_type.76.refs_2_, f32[2,288,128]{2,1,0:T(8,128)S(1)} %convert_element_type.77.refs_3_, ...), custom_call_target="tpu_custom_call" | custom-call | flops 47185920 | bytes 2359296 | tf_op jit(solution)/shard_map/pallas_call | solution.py:449
  28.4 5.6 %all-to-all-start = ((bf16[32,8,1152]{2,1,0:T(8,128)(2,1)}), bf16[32,8,1152]{2,1,0:T(8,128)(2,1)S(1)}, u32[]{:S(2)}, u32[]{:S(2)}) async-start(bf16[32,8,1152]{2,1,0:T(8,128)(2,1)} %get-tuple-element.15), calls=%async_computation | async-start | bytes 1179648 | tf_op jit(solution)/shard_map/all_to_all | solution.py:475
  34.6 2.5 %collective-permute-start.13 = (f16[296,128]{1,0:T(8,128)(2,1)S(1)}, f16[296,128]{1,0:T(8,128)(2,1)S(1)}, u32[]{:S(2)}, u32[]{:S(2)}) collective-permute-start(f16[296,128]{1,0:T(8,128)(2,1)S(1)} %get-tuple-element.26), channel_id=1, source_target_pairs={{0,7},{1,6},{2,5},{3,4},{4,3},{5,2},{6,1},{7,0},{8,15},{9,14},{10,... | collective-permute-start | bytes 227336 | tf_op jit(solution)/shard_map/ppermute | solution.py:386
  37.7 1.5 %collective-permute-start.11 = (f16[296,128]{1,0:T(8,128)(2,1)S(1)}, f16[296,128]{1,0:T(8,128)(2,1)S(1)}, u32[]{:S(2)}, u32[]{:S(2)}) collective-permute-start(f16[296,128]{1,0:T(8,128)(2,1)S(1)} %get-tuple-element.28), channel_id=1, source_target_pairs={{0,5},{1,4},{2,7},{3,6},{4,1},{5,0},{6,3},{7,2},{8,13},{9,12},{10,... | collective-permute-start | bytes 227336 | tf_op jit(solution)/shard_map/ppermute | solution.py:386
  39.4 1.0 %collective-permute-start.9 = (f16[296,128]{1,0:T(8,128)(2,1)S(1)}, f16[296,128]{1,0:T(8,128)(2,1)S(1)}, u32[]{:S(2)}, u32[]{:S(2)}) collective-permute-start(f16[296,128]{1,0:T(8,128)(2,1)S(1)} %get-tuple-element.30), channel_id=1, source_target_pairs={{0,3},{1,2},{2,1},{3,0},{4,7},{5,6},{6,5},{7,4},{8,11},{9,10},{10,... | collective-permute-start | bytes 227336 | tf_op jit(solution)/shard_map/ppermute | solution.py:386
  40.3 2.9 %collective-permute-done.13 = f16[296,128]{1,0:T(8,128)(2,1)S(1)} collective-permute-done((f16[296,128]{1,0:T(8,128)(2,1)S(1)}, f16[296,128]{1,0:T(8,128)(2,1)S(1)}, u32[]{:S(2)}, u32[]{:S(2)}) %collective-permute-start.13) | collective-permute-done | bytes 75808 | tf_op jit(solution)/shard_map/ppermute | solution.py:386
  43.2 1.5 %collective-permute-start.8 = (f16[296,128]{1,0:T(8,128)(2,1)S(1)}, f16[296,128]{1,0:T(8,128)(2,1)S(1)}, u32[]{:S(2)}, u32[]{:S(2)}) collective-permute-start(f16[296,128]{1,0:T(8,128)(2,1)S(1)} %get-tuple-element.31), channel_id=1, source_target_pairs={{0,2},{1,3},{2,0},{3,1},{4,6},{5,7},{6,4},{7,5},{8,10},{9,11},{10,... | collective-permute-start | bytes 227336 | tf_op jit(solution)/shard_map/ppermute | solution.py:386
  44.7 1.5 %collective-permute-start.7 = (f16[296,128]{1,0:T(8,128)(2,1)S(1)}, f16[296,128]{1,0:T(8,128)(2,1)S(1)}, u32[]{:S(2)}, u32[]{:S(2)}) collective-permute-start(f16[296,128]{1,0:T(8,128)(2,1)S(1)} %get-tuple-element.32), channel_id=1, source_target_pairs={{0,1},{1,0},{2,3},{3,2},{4,5},{5,4},{6,7},{7,6},{8,9},{9,8},{10,11... | collective-permute-start | bytes 227336 | tf_op jit(solution)/shard_map/ppermute | solution.py:386
  46.2 2.6 %collective-permute-done.11 = f16[296,128]{1,0:T(8,128)(2,1)S(1)} collective-permute-done((f16[296,128]{1,0:T(8,128)(2,1)S(1)}, f16[296,128]{1,0:T(8,128)(2,1)S(1)}, u32[]{:S(2)}, u32[]{:S(2)}) %collective-permute-start.11) | collective-permute-done | bytes 75808 | tf_op jit(solution)/shard_map/ppermute | solution.py:386
  48.8 0.6 collective-permute-done.10
  49.4 1.5 %collective-permute-done.7 = f16[296,128]{1,0:T(8,128)(2,1)S(1)} collective-permute-done((f16[296,128]{1,0:T(8,128)(2,1)S(1)}, f16[296,128]{1,0:T(8,128)(2,1)S(1)}, u32[]{:S(2)}, u32[]{:S(2)}) %collective-permute-start.7) | collective-permute-done | bytes 75808 | tf_op jit(solution)/shard_map/ppermute | solution.py:386
  51.5 3.5 %collective-permute-start.16 = (f16[64,256]{1,0:T(8,128)(2,1)S(1)}, f16[64,256]{1,0:T(8,128)(2,1)S(1)}, u32[]{:S(2)}, u32[]{:S(2)}) collective-permute-start(f16[64,256]{1,0:T(8,128)(2,1)S(1)} %get-tuple-element.41), channel_id=1, source_target_pairs={{0,24},{8,16},{16,8},{24,0},{1,25},{9,17},{17,9},{25,1},{2,26},{10... | collective-permute-start | bytes 98312 | tf_op jit(solution)/shard_map/ppermute | solution.py:518
  55.0 0.9 %collective-permute-start.14 = (f16[64,256]{1,0:T(8,128)(2,1)S(1)}, f16[64,256]{1,0:T(8,128)(2,1)S(1)}, u32[]{:S(2)}, u32[]{:S(2)}) collective-permute-start(f16[64,256]{1,0:T(8,128)(2,1)S(1)} %get-tuple-element.43), channel_id=1, source_target_pairs={{0,8},{8,0},{16,24},{24,16},{1,9},{9,1},{17,25},{25,17},{2,10},{10... | collective-permute-start | bytes 98312 | tf_op jit(solution)/shard_map/ppermute | solution.py:518
  56.0 1.2 %collective-permute-done.16 = f16[64,256]{1,0:T(8,128)(2,1)S(1)} collective-permute-done((f16[64,256]{1,0:T(8,128)(2,1)S(1)}, f16[64,256]{1,0:T(8,128)(2,1)S(1)}, u32[]{:S(2)}, u32[]{:S(2)}) %collective-permute-start.16) | collective-permute-done | bytes 32800 | tf_op jit(solution)/shard_map/ppermute | solution.py:518
  57.2 2.6 %collective-permute-done.15 = f16[64,256]{1,0:T(8,128)(2,1)S(1)} collective-permute-done((f16[64,256]{1,0:T(8,128)(2,1)S(1)}, f16[64,256]{1,0:T(8,128)(2,1)S(1)}, u32[]{:S(2)}, u32[]{:S(2)}) %collective-permute-start.15) | collective-permute-done | bytes 32800 | tf_op jit(solution)/shard_map/ppermute | solution.py:518
  60.0 1.1 %collective-permute-start.19 = (f32[64,256]{1,0:T(8,128)S(1)}, f32[64,256]{1,0:T(8,128)S(1)}, u32[]{:S(2)}, u32[]{:S(2)}) collective-permute-start(f32[64,256]{1,0:T(8,128)S(1)} %shard_map.72), channel_id=1, source_target_pairs={{0,5},{1,4},{2,7},{3,6},{4,1},{5,0},{6,3},{7,2},{8,13},{9,12},{10,... | collective-permute-start | bytes 196616 | tf_op jit(solution)/shard_map/ppermute | solution.py:386
  61.1 1.6 %collective-permute-start.18 = (f32[64,256]{1,0:T(8,128)S(1)}, f32[64,256]{1,0:T(8,128)S(1)}, u32[]{:S(2)}, u32[]{:S(2)}) collective-permute-start(f32[64,256]{1,0:T(8,128)S(1)} %shard_map.72), channel_id=1, source_target_pairs={{0,4},{1,5},{2,6},{3,7},{4,0},{5,1},{6,2},{7,3},{8,12},{9,13},{10,... | collective-permute-start | bytes 196616 | tf_op jit(solution)/shard_map/ppermute | solution.py:386
  62.7 0.8 %collective-permute-start.17 = (f32[64,256]{1,0:T(8,128)S(1)}, f32[64,256]{1,0:T(8,128)S(1)}, u32[]{:S(2)}, u32[]{:S(2)}) collective-permute-start(f32[64,256]{1,0:T(8,128)S(1)} %shard_map.72), channel_id=1, source_target_pairs={{0,1},{1,0},{2,3},{3,2},{4,5},{5,4},{6,7},{7,6},{8,9},{9,8},{10,11... | collective-permute-start | bytes 196616 | tf_op jit(solution)/shard_map/ppermute | solution.py:386
  63.5 1.1 %shard_map.73 = f32[36,64,128]{2,1,0:T(8,128)} custom-call(f32[8,296,128]{2,1,0:T(8,128)S(1)} %shard_map.70.refs_0_, f32[1,296,128]{2,1,0:T(8,128)S(1)} %bitcast_convert_fusion.6.refs_1_, f32[1,296,128]{2,1,0:T(8,128)S(1)} %get-tuple-element.49.refs_2_, f32[1,296,128]{2,1,0:T(8,128)S(1)} %get-tuple-element.48.refs_3_, ...), custom_call_target="tpu_custom_call" | custom-call | tf_op jit(solution)/shard_map/pallas_call | solution.py:495
  64.7 0.5 collective-permute-done.19
  65.6 1.3 %collective-permute-done.17 = f32[64,256]{1,0:T(8,128)S(1)} collective-permute-done((f32[64,256]{1,0:T(8,128)S(1)}, f32[64,256]{1,0:T(8,128)S(1)}, u32[]{:S(2)}, u32[]{:S(2)}) %collective-permute-start.17) | collective-permute-done | bytes 65568 | tf_op jit(solution)/shard_map/ppermute | solution.py:386
  67.1 1.2 %collective-permute-done.20 = f32[64,256]{1,0:T(8,128)S(1)} collective-permute-done((f32[64,256]{1,0:T(8,128)S(1)}, f32[64,256]{1,0:T(8,128)S(1)}, u32[]{:S(2)}, u32[]{:S(2)}) %collective-permute-start.20) | collective-permute-done | bytes 65568 | tf_op jit(solution)/shard_map/ppermute | solution.py:386
  68.3 0.6 add.52
  (62 shorter events, 5.1 us)
Async XLA Ops:
  0.6 1.6 %copy-start.3 = (s32[4,2]{0,1:T(2,128)S(1)}, s32[4,2]{0,1:T(2,128)}, u32[]{:S(2)}) copy-start(s32[4,2]{0,1:T(2,128)} %param.9) | copy-start | bytes 100
  0.6 1.6 %copy-start.2 = (f32[4,4]{1,0:T(4,128)S(1)}, f32[4,4]{1,0:T(4,128)}, u32[]{:S(2)}) copy-start(f32[4,4]{1,0:T(4,128)} %energies_ref.1) | copy-start | bytes 196
  0.7 1.6 %copy-start = (f32[4,4,5,128]{3,1,2,0:T(4,128)S(1)}, f32[4,4,5,128]{3,1,2,0:T(4,128)}, u32[]{:S(2)}) copy-start(f32[4,4,5,128]{3,1,2,0:T(4,128)} %param.7) | copy-start | bytes 122884
  0.7 1.6 %copy-start.1 = (f32[6,6,128]{2,1,0:T(8,128)S(1)}, f32[6,6,128]{2,1,0:T(8,128)}, u32[]{:S(2)}) copy-start(f32[6,6,128]{2,1,0:T(8,128)} %potential_ref.1) | copy-start | bytes 55300
  3.0 14.8 %collective-permute-start.5 = (f16[120,128]{1,0:T(8,128)(2,1)S(1)}, f16[120,128]{1,0:T(8,128)(2,1)S(1)}, u32[]{:S(2)}, u32[]{:S(2)}) collective-permute-start(f16[120,128]{1,0:T(8,128)(2,1)S(1)} %convert_element_type.79), channel_id=1, source_target_pairs={{0,5},{1,4},{2,7},{3,6},{4,1},{5,0},{6,3},{7,2},{8,13},{9,12},{10,... | collective-permute-start | bytes 92168 | tf_op jit(solution)/shard_map/ppermute | solution.py:386
  7.0 10.8 %collective-permute-start.4 = (f16[120,128]{1,0:T(8,128)(2,1)S(1)}, f16[120,128]{1,0:T(8,128)(2,1)S(1)}, u32[]{:S(2)}, u32[]{:S(2)}) collective-permute-start(f16[120,128]{1,0:T(8,128)(2,1)S(1)} %convert_element_type.79), channel_id=1, source_target_pairs={{0,4},{1,5},{2,6},{3,7},{4,0},{5,1},{6,2},{7,3},{8,12},{9,13},{10,... | collective-permute-start | bytes 92168 | tf_op jit(solution)/shard_map/ppermute | solution.py:386
  7.5 4.1 %collective-permute-start.3 = (f16[120,128]{1,0:T(8,128)(2,1)S(1)}, f16[120,128]{1,0:T(8,128)(2,1)S(1)}, u32[]{:S(2)}, u32[]{:S(2)}) collective-permute-start(f16[120,128]{1,0:T(8,128)(2,1)S(1)} %convert_element_type.79), channel_id=1, source_target_pairs={{0,1},{1,0},{2,3},{3,2},{4,5},{5,4},{6,7},{7,6},{8,9},{9,8},{10,11... | collective-permute-start | bytes 92168 | tf_op jit(solution)/shard_map/ppermute | solution.py:386
  7.8 5.9 %collective-permute-start = (f16[2,288,128]{2,1,0:T(8,128)(2,1)S(1)}, f16[2,288,128]{2,1,0:T(8,128)(2,1)S(1)}, u32[]{:S(2)}, u32[]{:S(2)}) collective-permute-start(f16[2,288,128]{2,1,0:T(8,128)(2,1)S(1)} %pad_maximum_fusion.1), channel_id=1, source_target_pairs={{0,1},{1,0},{2,3},{3,2},{4,5},{5,4},{6,7},{7,6},{8,9},{9,8},{10,11... | collective-permute-start | bytes 442376 | tf_op jit(solution)/shard_map/ppermute | solution.py:386
  9.8 6.1 %collective-permute-start.1 = (f16[2,288,128]{2,1,0:T(8,128)(2,1)S(1)}, f16[2,288,128]{2,1,0:T(8,128)(2,1)S(1)}, u32[]{:S(2)}, u32[]{:S(2)}) collective-permute-start(f16[2,288,128]{2,1,0:T(8,128)(2,1)S(1)} %pad_maximum_fusion.2), channel_id=1, source_target_pairs={{0,4},{1,5},{2,6},{3,7},{4,0},{5,1},{6,2},{7,3},{8,12},{9,13},{10,... | collective-permute-start | bytes 442376 | tf_op jit(solution)/shard_map/ppermute | solution.py:386
  11.6 6.1 %collective-permute-start.2 = (f16[2,288,128]{2,1,0:T(8,128)(2,1)S(1)}, f16[2,288,128]{2,1,0:T(8,128)(2,1)S(1)}, u32[]{:S(2)}, u32[]{:S(2)}) collective-permute-start(f16[2,288,128]{2,1,0:T(8,128)(2,1)S(1)} %pad_maximum_fusion.3), channel_id=1, source_target_pairs={{0,5},{1,4},{2,7},{3,6},{4,1},{5,0},{6,3},{7,2},{8,13},{9,12},{10,... | collective-permute-start | bytes 442376 | tf_op jit(solution)/shard_map/ppermute | solution.py:386
  18.0 1.8 %collective-permute-start.6 = (f16[4,408,128]{2,1,0:T(8,128)(2,1)S(1)}, f16[4,408,128]{2,1,0:T(8,128)(2,1)S(1)}, u32[]{:S(2)}, u32[]{:S(2)}) collective-permute-start(f16[4,408,128]{2,1,0:T(8,128)(2,1)S(1)} %pad_maximum_fusion), channel_id=1, source_target_pairs={{0,2},{1,3},{2,0},{3,1},{4,6},{5,7},{6,4},{7,5},{8,10},{9,11},{10,... | collective-permute-start | bytes 1253384 | tf_op jit(solution)/shard_map/ppermute | solution.py:386
  28.4 22.5 %all-to-all-start = ((bf16[32,8,1152]{2,1,0:T(8,128)(2,1)}), bf16[32,8,1152]{2,1,0:T(8,128)(2,1)S(1)}, u32[]{:S(2)}, u32[]{:S(2)}) async-start(bf16[32,8,1152]{2,1,0:T(8,128)(2,1)} %get-tuple-element.15), calls=%async_computation | async-start | bytes 1179648 | tf_op jit(solution)/shard_map/all_to_all | solution.py:475
  34.6 8.6 %collective-permute-start.13 = (f16[296,128]{1,0:T(8,128)(2,1)S(1)}, f16[296,128]{1,0:T(8,128)(2,1)S(1)}, u32[]{:S(2)}, u32[]{:S(2)}) collective-permute-start(f16[296,128]{1,0:T(8,128)(2,1)S(1)} %get-tuple-element.26), channel_id=1, source_target_pairs={{0,7},{1,6},{2,5},{3,4},{4,3},{5,2},{6,1},{7,0},{8,15},{9,14},{10,... | collective-permute-start | bytes 227336 | tf_op jit(solution)/shard_map/ppermute | solution.py:386
  37.1 7.6 %collective-permute-start.12 = (f16[296,128]{1,0:T(8,128)(2,1)S(1)}, f16[296,128]{1,0:T(8,128)(2,1)S(1)}, u32[]{:S(2)}, u32[]{:S(2)}) collective-permute-start(f16[296,128]{1,0:T(8,128)(2,1)S(1)} %get-tuple-element.27), channel_id=1, source_target_pairs={{0,6},{1,7},{2,4},{3,5},{4,2},{5,3},{6,0},{7,1},{8,14},{9,15},{10,... | collective-permute-start | bytes 227336 | tf_op jit(solution)/shard_map/ppermute | solution.py:386
  37.7 11.2 %collective-permute-start.11 = (f16[296,128]{1,0:T(8,128)(2,1)S(1)}, f16[296,128]{1,0:T(8,128)(2,1)S(1)}, u32[]{:S(2)}, u32[]{:S(2)}) collective-permute-start(f16[296,128]{1,0:T(8,128)(2,1)S(1)} %get-tuple-element.28), channel_id=1, source_target_pairs={{0,5},{1,4},{2,7},{3,6},{4,1},{5,0},{6,3},{7,2},{8,13},{9,12},{10,... | collective-permute-start | bytes 227336 | tf_op jit(solution)/shard_map/ppermute | solution.py:386
  39.1 10.3 %collective-permute-start.10 = (f16[296,128]{1,0:T(8,128)(2,1)S(1)}, f16[296,128]{1,0:T(8,128)(2,1)S(1)}, u32[]{:S(2)}, u32[]{:S(2)}) collective-permute-start(f16[296,128]{1,0:T(8,128)(2,1)S(1)} %get-tuple-element.29), channel_id=1, source_target_pairs={{0,4},{1,5},{2,6},{3,7},{4,0},{5,1},{6,2},{7,3},{8,12},{9,13},{10,... | collective-permute-start | bytes 227336 | tf_op jit(solution)/shard_map/ppermute | solution.py:386
  39.4 10.0 %collective-permute-start.9 = (f16[296,128]{1,0:T(8,128)(2,1)S(1)}, f16[296,128]{1,0:T(8,128)(2,1)S(1)}, u32[]{:S(2)}, u32[]{:S(2)}) collective-permute-start(f16[296,128]{1,0:T(8,128)(2,1)S(1)} %get-tuple-element.30), channel_id=1, source_target_pairs={{0,3},{1,2},{2,1},{3,0},{4,7},{5,6},{6,5},{7,4},{8,11},{9,10},{10,... | collective-permute-start | bytes 227336 | tf_op jit(solution)/shard_map/ppermute | solution.py:386
  43.2 6.2 %collective-permute-start.8 = (f16[296,128]{1,0:T(8,128)(2,1)S(1)}, f16[296,128]{1,0:T(8,128)(2,1)S(1)}, u32[]{:S(2)}, u32[]{:S(2)}) collective-permute-start(f16[296,128]{1,0:T(8,128)(2,1)S(1)} %get-tuple-element.31), channel_id=1, source_target_pairs={{0,2},{1,3},{2,0},{3,1},{4,6},{5,7},{6,4},{7,5},{8,10},{9,11},{10,... | collective-permute-start | bytes 227336 | tf_op jit(solution)/shard_map/ppermute | solution.py:386
  44.7 6.1 %collective-permute-start.7 = (f16[296,128]{1,0:T(8,128)(2,1)S(1)}, f16[296,128]{1,0:T(8,128)(2,1)S(1)}, u32[]{:S(2)}, u32[]{:S(2)}) collective-permute-start(f16[296,128]{1,0:T(8,128)(2,1)S(1)} %get-tuple-element.32), channel_id=1, source_target_pairs={{0,1},{1,0},{2,3},{3,2},{4,5},{5,4},{6,7},{7,6},{8,9},{9,8},{10,11... | collective-permute-start | bytes 227336 | tf_op jit(solution)/shard_map/ppermute | solution.py:386
  51.5 5.8 %collective-permute-start.16 = (f16[64,256]{1,0:T(8,128)(2,1)S(1)}, f16[64,256]{1,0:T(8,128)(2,1)S(1)}, u32[]{:S(2)}, u32[]{:S(2)}) collective-permute-start(f16[64,256]{1,0:T(8,128)(2,1)S(1)} %get-tuple-element.41), channel_id=1, source_target_pairs={{0,24},{8,16},{16,8},{24,0},{1,25},{9,17},{17,9},{25,1},{2,26},{10... | collective-permute-start | bytes 98312 | tf_op jit(solution)/shard_map/ppermute | solution.py:518
  55.0 4.8 %collective-permute-start.15 = (f16[64,256]{1,0:T(8,128)(2,1)S(1)}, f16[64,256]{1,0:T(8,128)(2,1)S(1)}, u32[]{:S(2)}, u32[]{:S(2)}) collective-permute-start(f16[64,256]{1,0:T(8,128)(2,1)S(1)} %get-tuple-element.42), channel_id=1, source_target_pairs={{0,16},{8,24},{16,0},{24,8},{1,17},{9,25},{17,1},{25,9},{2,18},{10... | collective-permute-start | bytes 98312 | tf_op jit(solution)/shard_map/ppermute | solution.py:518
  55.0 4.8 %collective-permute-start.14 = (f16[64,256]{1,0:T(8,128)(2,1)S(1)}, f16[64,256]{1,0:T(8,128)(2,1)S(1)}, u32[]{:S(2)}, u32[]{:S(2)}) collective-permute-start(f16[64,256]{1,0:T(8,128)(2,1)S(1)} %get-tuple-element.43), channel_id=1, source_target_pairs={{0,8},{8,0},{16,24},{24,16},{1,9},{9,1},{17,25},{25,17},{2,10},{10... | collective-permute-start | bytes 98312 | tf_op jit(solution)/shard_map/ppermute | solution.py:518
  60.0 5.2 %collective-permute-start.19 = (f32[64,256]{1,0:T(8,128)S(1)}, f32[64,256]{1,0:T(8,128)S(1)}, u32[]{:S(2)}, u32[]{:S(2)}) collective-permute-start(f32[64,256]{1,0:T(8,128)S(1)} %shard_map.72), channel_id=1, source_target_pairs={{0,5},{1,4},{2,7},{3,6},{4,1},{5,0},{6,3},{7,2},{8,13},{9,12},{10,... | collective-permute-start | bytes 196616 | tf_op jit(solution)/shard_map/ppermute | solution.py:386
  61.1 4.5 %collective-permute-start.18 = (f32[64,256]{1,0:T(8,128)S(1)}, f32[64,256]{1,0:T(8,128)S(1)}, u32[]{:S(2)}, u32[]{:S(2)}) collective-permute-start(f32[64,256]{1,0:T(8,128)S(1)} %shard_map.72), channel_id=1, source_target_pairs={{0,4},{1,5},{2,6},{3,7},{4,0},{5,1},{6,2},{7,3},{8,12},{9,13},{10,... | collective-permute-start | bytes 196616 | tf_op jit(solution)/shard_map/ppermute | solution.py:386
  62.7 4.3 %collective-permute-start.17 = (f32[64,256]{1,0:T(8,128)S(1)}, f32[64,256]{1,0:T(8,128)S(1)}, u32[]{:S(2)}, u32[]{:S(2)}) collective-permute-start(f32[64,256]{1,0:T(8,128)S(1)} %shard_map.72), channel_id=1, source_target_pairs={{0,1},{1,0},{2,3},{3,2},{4,5},{5,4},{6,7},{7,6},{8,9},{9,8},{10,11... | collective-permute-start | bytes 196616 | tf_op jit(solution)/shard_map/ppermute | solution.py:386
  67.0 1.3 %collective-permute-start.20 = (f32[64,256]{1,0:T(8,128)S(1)}, f32[64,256]{1,0:T(8,128)S(1)}, u32[]{:S(2)}, u32[]{:S(2)}) collective-permute-start(f32[64,256]{1,0:T(8,128)S(1)} %add_add_fusion), channel_id=1, source_target_pairs={{0,2},{1,3},{2,0},{3,1},{4,6},{5,7},{6,4},{7,5},{8,10},{9,11},{10,... | collective-permute-start | bytes 196616 | tf_op jit(solution)/shard_map/ppermute | solution.py:386

commit v13 on v10

--- a/solution.py
+++ b/solution.py
@@ -196,7 +196,7 @@
                 partial[x, y] = along_z[x] + diagonal[x, y] * cells[x] + along(cells, x)
             return carry
 
-        lax.fori_loop(0, count_y, xz_part, 0, unroll=2)
+        lax.fori_loop(0, count_y, xz_part, 0, unroll=4)
 
         def y_part(x, carry):
             cells = [source[ring + x, ring + y] for y in range(count_y)]
@@ -423,11 +423,17 @@
         def chunk_for(value):
             return lax.dynamic_index_in_dim(chunks, me ^ value, 0, keepdims=False)
 
-        came = [swap(jnp.concatenate([chunk_for(v), narrow]), v) for v in range(1, group)]
-        operands = [chunk_for(0).astype(jnp.float32)[None], shared[None]]
-        operands += [block.astype(jnp.float32)[None] for block in came]
-        slabs = {v: ((1 + v, 0, 0), (1 + v, 0, piece_rows)) for v in range(1, group)}
-        slabs[0] = ((0, 0, 0), (1, 0, 0))
+        came = [swap(jnp.concatenate([chunk_for(v), narrow, chunk_for(v ^ near)]), v) for v in far]
+        mine = jnp.concatenate([narrow, chunk_for(near)])
+        crossed = swap(jnp.stack([mine] + [block[piece_rows:] for block in came]), near)
+        operands = [chunk_for(0)[None], narrow[None]] + [block[None] for block in came] + [crossed]
+        operands = [block.astype(jnp.float32) for block in operands]
+        operands[1] = shared[None]
+        last = len(operands) - 1
+        slabs = {0: ((0, 0, 0), (1, 0, 0)), near: ((last, 0, rows), (last, 0, 0))}
+        for i, v in enumerate(far):
+            slabs[v] = ((2 + i, 0, 0), (2 + i, 0, piece_rows))
+            slabs[v ^ near] = ((last, 1 + i, rows), (last, 1 + i, 0))
     else:
         sent = jnp.concatenate([chunks, jnp.broadcast_to(narrow[None], (group, rows, nz))], axis=1)
         operands = [lax.all_to_all(sent, plane, 0, 0).astype(jnp.float32)]

time: 65.6 us -> 65.2 us (level)
  starting transfers between devices: 32.5 us -> 27.1 us
  waiting for transfers between devices: 19.2 us -> 24.4 us
    ppermute x18 -> x15, starting transfers between devices: 22.7 us -> 17 us  [swap(): return lax.ppermute(block, plane, [(i, i ^ value) for i in range(group)])]
    ppermute x18 -> x15, waiting for transfers between devices: 15.4 us -> 20.6 us  [swap(): return lax.ppermute(block, plane, [(i, i ^ value) for i in range(group)])]
  transfers between devices with their start and end apart: 22 -> 19, of which waited for: 13 -> 13; matrix products, arithmetic and copies ran while one was open for 1% -> 1% of each run, Pallas kernels for 2% -> 2%
where the time goes in v13:
time: 65.2 us; the launch traced here: 65 us
  starting transfers between devices  27.1 us (42%)
  waiting for transfers between devices  24.4 us (37%)
  Pallas kernels  9.21 us (14%)
  other arithmetic  2.91 us (4%)
  between operations  1.01 us (2%)
    ppermute x15, waiting for transfers between devices, swap(): return lax.ppermute(block, plane, [(i, i ^ value) for i in range(group)])  20.6 us
    ppermute x15, starting transfers between devices, swap(): return lax.ppermute(block, plane, [(i, i ^ value) for i in range(group)])  17 us
    pallas_call x1, Pallas kernels, local(): pl.pallas_call(functools.partial(filter_kernel, slabs_y, cells_x, cells_y...  6.26 us
    all_to_all x1, starting transfers between devices, local(): matrix = lax.all_to_all(rounded, every, 0, 0)  5.72 us
    ppermute x3, starting transfers between devices, local(): lax.ppermute(sums[k].astype(jnp.float16), 'band', [(i, i ^ k) for i in ra...  4.45 us
    ppermute x3, waiting for transfers between devices, local(): lax.ppermute(sums[k].astype(jnp.float16), 'band', [(i, i ^ k) for i in ra...  3.8 us
    convert_element_type x1, other arithmetic, local(): chunks = (orbitals * orbital_gain).astype(jnp.float16)  1.46 us
  transfers between devices with their start and end apart: 19, of which 13 were waited for; matrix products, arithmetic and copies ran while one was open for 1% of the time, Pallas kernels for 2%

profile of v13, /device:TPU:0, one launch (start us, length us, event | category | flops | bytes accessed | tf_op | source)
XLA Modules:
  0.0 65.0 jit_solution(8192161386231184387)
XLA Ops:
  0.7 1.5 %multiply_convert_fusion = f16[64,6,6,128]{3,0,2,1:T(8,128)(2,1)S(1)} fusion(f32[64,6,6,128]{3,0,2,1:T(8,128)} %param.5), kind=kLoop, calls=%fused_computation | loop fusion | flops 589824 | bytes 1769472 | tf_op jit(solution)/shard_map/convert_element_type | solution.py:409
  2.3 0.7 %shard_map.68 = f32[120,128]{1,0:T(8,128)S(1)} custom-call(f32[8,128]{1,0:T(8,128)S(1)} %fusion.3._, f32[4,4]{1,0:T(4,128)S(1)} %copy-done.2, s32[2,4]{1,0:T(2,128)S(1)} %bitcast.95, f32[4,5,4,128]{3,2,1,0:T(4,128)S(1)} %bitcast.94, f32[6,6,128]{2,1,0:T(8,128)S(1)} %copy-done.1), custom_call_target="tpu_custom_call" | custom-call | tf_op jit(solution)/shard_map/pallas_call | solution.py:412
  3.4 4.0 %collective-permute-start.2 = (f16[696,128]{1,0:T(8,128)(2,1)S(1)}, f16[696,128]{1,0:T(8,128)(2,1)S(1)}, u32[]{:S(2)}, u32[]{:S(2)}) collective-permute-start(f16[696,128]{1,0:T(8,128)(2,1)S(1)} %get-tuple-element.44), channel_id=1, source_target_pairs={{0,5},{1,4},{2,7},{3,6},{4,1},{5,0},{6,3},{7,2},{8,13},{9,12},{10,... | collective-permute-start | bytes 534536 | tf_op jit(solution)/shard_map/ppermute | solution.py:386
  7.3 0.5 collective-permute-start.1
  8.0 4.7 %collective-permute-done.2 = f16[696,128]{1,0:T(8,128)(2,1)S(1)} collective-permute-done((f16[696,128]{1,0:T(8,128)(2,1)S(1)}, f16[696,128]{1,0:T(8,128)(2,1)S(1)}, u32[]{:S(2)}, u32[]{:S(2)}) %collective-permute-start.2) | collective-permute-done | bytes 178208 | tf_op jit(solution)/shard_map/ppermute | solution.py:386
  12.7 3.3 %collective-permute-done.1 = f16[696,128]{1,0:T(8,128)(2,1)S(1)} collective-permute-done((f16[696,128]{1,0:T(8,128)(2,1)S(1)}, f16[696,128]{1,0:T(8,128)(2,1)S(1)}, u32[]{:S(2)}, u32[]{:S(2)}) %collective-permute-start.1) | collective-permute-done | bytes 178208 | tf_op jit(solution)/shard_map/ppermute | solution.py:386
  16.3 1.6 %collective-permute-done.3 = f16[4,408,128]{2,1,0:T(8,128)(2,1)S(1)} collective-permute-done((f16[4,408,128]{2,1,0:T(8,128)(2,1)S(1)}, f16[4,408,128]{2,1,0:T(8,128)(2,1)S(1)}, u32[]{:S(2)}, u32[]{:S(2)}) %collective-permute-start.3) | collective-permute-done | bytes 417824 | tf_op jit(solution)/shard_map/ppermute | solution.py:386
  18.0 6.3 %shard_map.69 = (f32[26,14,8,128]{3,2,1,0:T(8,128)S(1)}, bf16[32,8,1152]{2,1,0:T(8,128)(2,1)}) custom-call(f32[1,288,128]{2,1,0:T(8,128)S(1)} %get-tuple-element.40.refs_0_, f32[1,120,128]{2,1,0:T(8,128)S(1)} %bitcast.93, f32[1,696,128]{2,1,0:T(8,128)S(1)} %bitcast_convert_fusion.2.refs_2_, f32[1,696,128]{2,1,0:T(8,128)S(1)} %bitcast_convert_fusion.1.refs_3_, ...), custom_call_target="tpu_custom_call" | custom-call | flops 47185920 | bytes 2359296 | tf_op jit(solution)/shard_map/pallas_call | solution.py:446
  24.3 5.7 %all-to-all-start = ((bf16[32,8,1152]{2,1,0:T(8,128)(2,1)}), bf16[32,8,1152]{2,1,0:T(8,128)(2,1)S(1)}, u32[]{:S(2)}, u32[]{:S(2)}) async-start(bf16[32,8,1152]{2,1,0:T(8,128)(2,1)} %get-tuple-element.15), calls=%async_computation | async-start | bytes 1179648 | tf_op jit(solution)/shard_map/all_to_all | solution.py:472
  30.7 2.5 %collective-permute-start.10 = (f16[296,128]{1,0:T(8,128)(2,1)S(1)}, f16[296,128]{1,0:T(8,128)(2,1)S(1)}, u32[]{:S(2)}, u32[]{:S(2)}) collective-permute-start(f16[296,128]{1,0:T(8,128)(2,1)S(1)} %get-tuple-element.26), channel_id=1, source_target_pairs={{0,7},{1,6},{2,5},{3,4},{4,3},{5,2},{6,1},{7,0},{8,15},{9,14},{10,... | collective-permute-start | bytes 227336 | tf_op jit(solution)/shard_map/ppermute | solution.py:386
  33.2 0.5 collective-permute-start.9
  33.7 1.5 %collective-permute-start.8 = (f16[296,128]{1,0:T(8,128)(2,1)S(1)}, f16[296,128]{1,0:T(8,128)(2,1)S(1)}, u32[]{:S(2)}, u32[]{:S(2)}) collective-permute-start(f16[296,128]{1,0:T(8,128)(2,1)S(1)} %get-tuple-element.28), channel_id=1, source_target_pairs={{0,5},{1,4},{2,7},{3,6},{4,1},{5,0},{6,3},{7,2},{8,13},{9,12},{10,... | collective-permute-start | bytes 227336 | tf_op jit(solution)/shard_map/ppermute | solution.py:386
  35.4 1.0 %collective-permute-start.6 = (f16[296,128]{1,0:T(8,128)(2,1)S(1)}, f16[296,128]{1,0:T(8,128)(2,1)S(1)}, u32[]{:S(2)}, u32[]{:S(2)}) collective-permute-start(f16[296,128]{1,0:T(8,128)(2,1)S(1)} %get-tuple-element.30), channel_id=1, source_target_pairs={{0,3},{1,2},{2,1},{3,0},{4,7},{5,6},{6,5},{7,4},{8,11},{9,10},{10,... | collective-permute-start | bytes 227336 | tf_op jit(solution)/shard_map/ppermute | solution.py:386
  36.4 2.9 %collective-permute-done.10 = f16[296,128]{1,0:T(8,128)(2,1)S(1)} collective-permute-done((f16[296,128]{1,0:T(8,128)(2,1)S(1)}, f16[296,128]{1,0:T(8,128)(2,1)S(1)}, u32[]{:S(2)}, u32[]{:S(2)}) %collective-permute-start.10) | collective-permute-done | bytes 75808 | tf_op jit(solution)/shard_map/ppermute | solution.py:386
  39.3 1.5 %collective-permute-start.5 = (f16[296,128]{1,0:T(8,128)(2,1)S(1)}, f16[296,128]{1,0:T(8,128)(2,1)S(1)}, u32[]{:S(2)}, u32[]{:S(2)}) collective-permute-start(f16[296,128]{1,0:T(8,128)(2,1)S(1)} %get-tuple-element.31), channel_id=1, source_target_pairs={{0,2},{1,3},{2,0},{3,1},{4,6},{5,7},{6,4},{7,5},{8,10},{9,11},{10,... | collective-permute-start | bytes 227336 | tf_op jit(solution)/shard_map/ppermute | solution.py:386
  40.8 1.5 %collective-permute-start.4 = (f16[296,128]{1,0:T(8,128)(2,1)S(1)}, f16[296,128]{1,0:T(8,128)(2,1)S(1)}, u32[]{:S(2)}, u32[]{:S(2)}) collective-permute-start(f16[296,128]{1,0:T(8,128)(2,1)S(1)} %get-tuple-element.32), channel_id=1, source_target_pairs={{0,1},{1,0},{2,3},{3,2},{4,5},{5,4},{6,7},{7,6},{8,9},{9,8},{10,11... | collective-permute-start | bytes 227336 | tf_op jit(solution)/shard_map/ppermute | solution.py:386
  42.3 2.6 %collective-permute-done.8 = f16[296,128]{1,0:T(8,128)(2,1)S(1)} collective-permute-done((f16[296,128]{1,0:T(8,128)(2,1)S(1)}, f16[296,128]{1,0:T(8,128)(2,1)S(1)}, u32[]{:S(2)}, u32[]{:S(2)}) %collective-permute-start.8) | collective-permute-done | bytes 75808 | tf_op jit(solution)/shard_map/ppermute | solution.py:386
  44.9 0.6 collective-permute-done.7
  45.5 1.5 %collective-permute-done.4 = f16[296,128]{1,0:T(8,128)(2,1)S(1)} collective-permute-done((f16[296,128]{1,0:T(8,128)(2,1)S(1)}, f16[296,128]{1,0:T(8,128)(2,1)S(1)}, u32[]{:S(2)}, u32[]{:S(2)}) %collective-permute-start.4) | collective-permute-done | bytes 75808 | tf_op jit(solution)/shard_map/ppermute | solution.py:386
  46.9 0.5 shard_map.71.own_ref
  47.5 3.5 %collective-permute-start.13 = (f16[64,256]{1,0:T(8,128)(2,1)S(1)}, f16[64,256]{1,0:T(8,128)(2,1)S(1)}, u32[]{:S(2)}, u32[]{:S(2)}) collective-permute-start(f16[64,256]{1,0:T(8,128)(2,1)S(1)} %get-tuple-element.41), channel_id=1, source_target_pairs={{0,24},{8,16},{16,8},{24,0},{1,25},{9,17},{17,9},{25,1},{2,26},{10... | collective-permute-start | bytes 98312 | tf_op jit(solution)/shard_map/ppermute | solution.py:515
  51.0 0.9 %collective-permute-start.11 = (f16[64,256]{1,0:T(8,128)(2,1)S(1)}, f16[64,256]{1,0:T(8,128)(2,1)S(1)}, u32[]{:S(2)}, u32[]{:S(2)}) collective-permute-start(f16[64,256]{1,0:T(8,128)(2,1)S(1)} %get-tuple-element.43), channel_id=1, source_target_pairs={{0,8},{8,0},{16,24},{24,16},{1,9},{9,1},{17,25},{25,17},{2,10},{10... | collective-permute-start | bytes 98312 | tf_op jit(solution)/shard_map/ppermute | solution.py:515
  52.1 1.2 %collective-permute-done.13 = f16[64,256]{1,0:T(8,128)(2,1)S(1)} collective-permute-done((f16[64,256]{1,0:T(8,128)(2,1)S(1)}, f16[64,256]{1,0:T(8,128)(2,1)S(1)}, u32[]{:S(2)}, u32[]{:S(2)}) %collective-permute-start.13) | collective-permute-done | bytes 32800 | tf_op jit(solution)/shard_map/ppermute | solution.py:515
  53.3 2.6 %collective-permute-done.12 = f16[64,256]{1,0:T(8,128)(2,1)S(1)} collective-permute-done((f16[64,256]{1,0:T(8,128)(2,1)S(1)}, f16[64,256]{1,0:T(8,128)(2,1)S(1)}, u32[]{:S(2)}, u32[]{:S(2)}) %collective-permute-start.12) | collective-permute-done | bytes 32800 | tf_op jit(solution)/shard_map/ppermute | solution.py:515
  56.1 1.0 %collective-permute-start.16 = (f32[64,256]{1,0:T(8,128)S(1)}, f32[64,256]{1,0:T(8,128)S(1)}, u32[]{:S(2)}, u32[]{:S(2)}) collective-permute-start(f32[64,256]{1,0:T(8,128)S(1)} %shard_map.72), channel_id=1, source_target_pairs={{0,5},{1,4},{2,7},{3,6},{4,1},{5,0},{6,3},{7,2},{8,13},{9,12},{10,... | collective-permute-start | bytes 196616 | tf_op jit(solution)/shard_map/ppermute | solution.py:386
  57.1 1.6 %collective-permute-start.15 = (f32[64,256]{1,0:T(8,128)S(1)}, f32[64,256]{1,0:T(8,128)S(1)}, u32[]{:S(2)}, u32[]{:S(2)}) collective-permute-start(f32[64,256]{1,0:T(8,128)S(1)} %shard_map.72), channel_id=1, source_target_pairs={{0,4},{1,5},{2,6},{3,7},{4,0},{5,1},{6,2},{7,3},{8,12},{9,13},{10,... | collective-permute-start | bytes 196616 | tf_op jit(solution)/shard_map/ppermute | solution.py:386
  58.7 0.8 %collective-permute-start.14 = (f32[64,256]{1,0:T(8,128)S(1)}, f32[64,256]{1,0:T(8,128)S(1)}, u32[]{:S(2)}, u32[]{:S(2)}) collective-permute-start(f32[64,256]{1,0:T(8,128)S(1)} %shard_map.72), channel_id=1, source_target_pairs={{0,1},{1,0},{2,3},{3,2},{4,5},{5,4},{6,7},{7,6},{8,9},{9,8},{10,11... | collective-permute-start | bytes 196616 | tf_op jit(solution)/shard_map/ppermute | solution.py:386
  59.6 1.1 %shard_map.73 = f32[36,64,128]{2,1,0:T(8,128)} custom-call(f32[8,296,128]{2,1,0:T(8,128)S(1)} %shard_map.70.refs_0_, f32[1,296,128]{2,1,0:T(8,128)S(1)} %bitcast_convert_fusion.9.refs_1_, f32[1,296,128]{2,1,0:T(8,128)S(1)} %get-tuple-element.52.refs_2_, f32[1,296,128]{2,1,0:T(8,128)S(1)} %get-tuple-element.51.refs_3_, ...), custom_call_target="tpu_custom_call" | custom-call | tf_op jit(solution)/shard_map/pallas_call | solution.py:492
  60.7 0.5 collective-permute-done.16
  61.7 1.3 %collective-permute-done.14 = f32[64,256]{1,0:T(8,128)S(1)} collective-permute-done((f32[64,256]{1,0:T(8,128)S(1)}, f32[64,256]{1,0:T(8,128)S(1)}, u32[]{:S(2)}, u32[]{:S(2)}) %collective-permute-start.14) | collective-permute-done | bytes 65568 | tf_op jit(solution)/shard_map/ppermute | solution.py:386
  63.1 1.2 %collective-permute-done.17 = f32[64,256]{1,0:T(8,128)S(1)} collective-permute-done((f32[64,256]{1,0:T(8,128)S(1)}, f32[64,256]{1,0:T(8,128)S(1)}, u32[]{:S(2)}, u32[]{:S(2)}) %collective-permute-start.17) | collective-permute-done | bytes 65568 | tf_op jit(solution)/shard_map/ppermute | solution.py:386
  64.4 0.6 add.52
  (48 shorter events, 2.7 us)
Async XLA Ops:
  0.7 1.6 %copy-start = (f32[4,4,5,128]{3,1,2,0:T(4,128)S(1)}, f32[4,4,5,128]{3,1,2,0:T(4,128)}, u32[]{:S(2)}) copy-start(f32[4,4,5,128]{3,1,2,0:T(4,128)} %param.7) | copy-start | bytes 122884
  0.7 1.6 %copy-start.1 = (f32[6,6,128]{2,1,0:T(8,128)S(1)}, f32[6,6,128]{2,1,0:T(8,128)}, u32[]{:S(2)}) copy-start(f32[6,6,128]{2,1,0:T(8,128)} %potential_ref.1) | copy-start | bytes 55300
  0.7 1.6 %copy-start.2 = (f32[4,4]{1,0:T(4,128)S(1)}, f32[4,4]{1,0:T(4,128)}, u32[]{:S(2)}) copy-start(f32[4,4]{1,0:T(4,128)} %energies_ref.1) | copy-start | bytes 196
  0.7 1.6 %copy-start.3 = (s32[4,2]{0,1:T(2,128)S(1)}, s32[4,2]{0,1:T(2,128)}, u32[]{:S(2)}) copy-start(s32[4,2]{0,1:T(2,128)} %param.9) | copy-start | bytes 100
  3.4 9.3 %collective-permute-start.2 = (f16[696,128]{1,0:T(8,128)(2,1)S(1)}, f16[696,128]{1,0:T(8,128)(2,1)S(1)}, u32[]{:S(2)}, u32[]{:S(2)}) collective-permute-start(f16[696,128]{1,0:T(8,128)(2,1)S(1)} %get-tuple-element.44), channel_id=1, source_target_pairs={{0,5},{1,4},{2,7},{3,6},{4,1},{5,0},{6,3},{7,2},{8,13},{9,12},{10,... | collective-permute-start | bytes 534536 | tf_op jit(solution)/shard_map/ppermute | solution.py:386
  7.3 8.6 %collective-permute-start.1 = (f16[696,128]{1,0:T(8,128)(2,1)S(1)}, f16[696,128]{1,0:T(8,128)(2,1)S(1)}, u32[]{:S(2)}, u32[]{:S(2)}) collective-permute-start(f16[696,128]{1,0:T(8,128)(2,1)S(1)} %get-tuple-element.45), channel_id=1, source_target_pairs={{0,4},{1,5},{2,6},{3,7},{4,0},{5,1},{6,2},{7,3},{8,12},{9,13},{10,... | collective-permute-start | bytes 534536 | tf_op jit(solution)/shard_map/ppermute | solution.py:386
  7.9 8.1 %collective-permute-start = (f16[696,128]{1,0:T(8,128)(2,1)S(1)}, f16[696,128]{1,0:T(8,128)(2,1)S(1)}, u32[]{:S(2)}, u32[]{:S(2)}) collective-permute-start(f16[696,128]{1,0:T(8,128)(2,1)S(1)} %get-tuple-element.46), channel_id=1, source_target_pairs={{0,1},{1,0},{2,3},{3,2},{4,5},{5,4},{6,7},{7,6},{8,9},{9,8},{10,11... | collective-permute-start | bytes 534536 | tf_op jit(solution)/shard_map/ppermute | solution.py:386
  16.2 1.8 %collective-permute-start.3 = (f16[4,408,128]{2,1,0:T(8,128)(2,1)S(1)}, f16[4,408,128]{2,1,0:T(8,128)(2,1)S(1)}, u32[]{:S(2)}, u32[]{:S(2)}) collective-permute-start(f16[4,408,128]{2,1,0:T(8,128)(2,1)S(1)} %pad_maximum_fusion), channel_id=1, source_target_pairs={{0,2},{1,3},{2,0},{3,1},{4,6},{5,7},{6,4},{7,5},{8,10},{9,11},{10,... | collective-permute-start | bytes 1253384 | tf_op jit(solution)/shard_map/ppermute | solution.py:386
  24.3 22.6 %all-to-all-start = ((bf16[32,8,1152]{2,1,0:T(8,128)(2,1)}), bf16[32,8,1152]{2,1,0:T(8,128)(2,1)S(1)}, u32[]{:S(2)}, u32[]{:S(2)}) async-start(bf16[32,8,1152]{2,1,0:T(8,128)(2,1)} %get-tuple-element.15), calls=%async_computation | async-start | bytes 1179648 | tf_op jit(solution)/shard_map/all_to_all | solution.py:472
  30.7 8.6 %collective-permute-start.10 = (f16[296,128]{1,0:T(8,128)(2,1)S(1)}, f16[296,128]{1,0:T(8,128)(2,1)S(1)}, u32[]{:S(2)}, u32[]{:S(2)}) collective-permute-start(f16[296,128]{1,0:T(8,128)(2,1)S(1)} %get-tuple-element.26), channel_id=1, source_target_pairs={{0,7},{1,6},{2,5},{3,4},{4,3},{5,2},{6,1},{7,0},{8,15},{9,14},{10,... | collective-permute-start | bytes 227336 | tf_op jit(solution)/shard_map/ppermute | solution.py:386
  33.2 7.6 %collective-permute-start.9 = (f16[296,128]{1,0:T(8,128)(2,1)S(1)}, f16[296,128]{1,0:T(8,128)(2,1)S(1)}, u32[]{:S(2)}, u32[]{:S(2)}) collective-permute-start(f16[296,128]{1,0:T(8,128)(2,1)S(1)} %get-tuple-element.27), channel_id=1, source_target_pairs={{0,6},{1,7},{2,4},{3,5},{4,2},{5,3},{6,0},{7,1},{8,14},{9,15},{10,... | collective-permute-start | bytes 227336 | tf_op jit(solution)/shard_map/ppermute | solution.py:386
  33.7 11.2 %collective-permute-start.8 = (f16[296,128]{1,0:T(8,128)(2,1)S(1)}, f16[296,128]{1,0:T(8,128)(2,1)S(1)}, u32[]{:S(2)}, u32[]{:S(2)}) collective-permute-start(f16[296,128]{1,0:T(8,128)(2,1)S(1)} %get-tuple-element.28), channel_id=1, source_target_pairs={{0,5},{1,4},{2,7},{3,6},{4,1},{5,0},{6,3},{7,2},{8,13},{9,12},{10,... | collective-permute-start | bytes 227336 | tf_op jit(solution)/shard_map/ppermute | solution.py:386
  35.2 10.3 %collective-permute-start.7 = (f16[296,128]{1,0:T(8,128)(2,1)S(1)}, f16[296,128]{1,0:T(8,128)(2,1)S(1)}, u32[]{:S(2)}, u32[]{:S(2)}) collective-permute-start(f16[296,128]{1,0:T(8,128)(2,1)S(1)} %get-tuple-element.29), channel_id=1, source_target_pairs={{0,4},{1,5},{2,6},{3,7},{4,0},{5,1},{6,2},{7,3},{8,12},{9,13},{10,... | collective-permute-start | bytes 227336 | tf_op jit(solution)/shard_map/ppermute | solution.py:386
  35.4 10.0 %collective-permute-start.6 = (f16[296,128]{1,0:T(8,128)(2,1)S(1)}, f16[296,128]{1,0:T(8,128)(2,1)S(1)}, u32[]{:S(2)}, u32[]{:S(2)}) collective-permute-start(f16[296,128]{1,0:T(8,128)(2,1)S(1)} %get-tuple-element.30), channel_id=1, source_target_pairs={{0,3},{1,2},{2,1},{3,0},{4,7},{5,6},{6,5},{7,4},{8,11},{9,10},{10,... | collective-permute-start | bytes 227336 | tf_op jit(solution)/shard_map/ppermute | solution.py:386
  39.3 6.2 %collective-permute-start.5 = (f16[296,128]{1,0:T(8,128)(2,1)S(1)}, f16[296,128]{1,0:T(8,128)(2,1)S(1)}, u32[]{:S(2)}, u32[]{:S(2)}) collective-permute-start(f16[296,128]{1,0:T(8,128)(2,1)S(1)} %get-tuple-element.31), channel_id=1, source_target_pairs={{0,2},{1,3},{2,0},{3,1},{4,6},{5,7},{6,4},{7,5},{8,10},{9,11},{10,... | collective-permute-start | bytes 227336 | tf_op jit(solution)/shard_map/ppermute | solution.py:386
  40.8 6.1 %collective-permute-start.4 = (f16[296,128]{1,0:T(8,128)(2,1)S(1)}, f16[296,128]{1,0:T(8,128)(2,1)S(1)}, u32[]{:S(2)}, u32[]{:S(2)}) collective-permute-start(f16[296,128]{1,0:T(8,128)(2,1)S(1)} %get-tuple-element.32), channel_id=1, source_target_pairs={{0,1},{1,0},{2,3},{3,2},{4,5},{5,4},{6,7},{7,6},{8,9},{9,8},{10,11... | collective-permute-start | bytes 227336 | tf_op jit(solution)/shard_map/ppermute | solution.py:386
  47.5 5.8 %collective-permute-start.13 = (f16[64,256]{1,0:T(8,128)(2,1)S(1)}, f16[64,256]{1,0:T(8,128)(2,1)S(1)}, u32[]{:S(2)}, u32[]{:S(2)}) collective-permute-start(f16[64,256]{1,0:T(8,128)(2,1)S(1)} %get-tuple-element.41), channel_id=1, source_target_pairs={{0,24},{8,16},{16,8},{24,0},{1,25},{9,17},{17,9},{25,1},{2,26},{10... | collective-permute-start | bytes 98312 | tf_op jit(solution)/shard_map/ppermute | solution.py:515
  51.0 4.8 %collective-permute-start.12 = (f16[64,256]{1,0:T(8,128)(2,1)S(1)}, f16[64,256]{1,0:T(8,128)(2,1)S(1)}, u32[]{:S(2)}, u32[]{:S(2)}) collective-permute-start(f16[64,256]{1,0:T(8,128)(2,1)S(1)} %get-tuple-element.42), channel_id=1, source_target_pairs={{0,16},{8,24},{16,0},{24,8},{1,17},{9,25},{17,1},{25,9},{2,18},{10... | collective-permute-start | bytes 98312 | tf_op jit(solution)/shard_map/ppermute | solution.py:515
  51.0 4.8 %collective-permute-start.11 = (f16[64,256]{1,0:T(8,128)(2,1)S(1)}, f16[64,256]{1,0:T(8,128)(2,1)S(1)}, u32[]{:S(2)}, u32[]{:S(2)}) collective-permute-start(f16[64,256]{1,0:T(8,128)(2,1)S(1)} %get-tuple-element.43), channel_id=1, source_target_pairs={{0,8},{8,0},{16,24},{24,16},{1,9},{9,1},{17,25},{25,17},{2,10},{10... | collective-permute-start | bytes 98312 | tf_op jit(solution)/shard_map/ppermute | solution.py:515
  56.1 5.2 %collective-permute-start.16 = (f32[64,256]{1,0:T(8,128)S(1)}, f32[64,256]{1,0:T(8,128)S(1)}, u32[]{:S(2)}, u32[]{:S(2)}) collective-permute-start(f32[64,256]{1,0:T(8,128)S(1)} %shard_map.72), channel_id=1, source_target_pairs={{0,5},{1,4},{2,7},{3,6},{4,1},{5,0},{6,3},{7,2},{8,13},{9,12},{10,... | collective-permute-start | bytes 196616 | tf_op jit(solution)/shard_map/ppermute | solution.py:386
  57.1 4.5 %collective-permute-start.15 = (f32[64,256]{1,0:T(8,128)S(1)}, f32[64,256]{1,0:T(8,128)S(1)}, u32[]{:S(2)}, u32[]{:S(2)}) collective-permute-start(f32[64,256]{1,0:T(8,128)S(1)} %shard_map.72), channel_id=1, source_target_pairs={{0,4},{1,5},{2,6},{3,7},{4,0},{5,1},{6,2},{7,3},{8,12},{9,13},{10,... | collective-permute-start | bytes 196616 | tf_op jit(solution)/shard_map/ppermute | solution.py:386
  58.7 4.3 %collective-permute-start.14 = (f32[64,256]{1,0:T(8,128)S(1)}, f32[64,256]{1,0:T(8,128)S(1)}, u32[]{:S(2)}, u32[]{:S(2)}) collective-permute-start(f32[64,256]{1,0:T(8,128)S(1)} %shard_map.72), channel_id=1, source_target_pairs={{0,1},{1,0},{2,3},{3,2},{4,5},{5,4},{6,7},{7,6},{8,9},{9,8},{10,11... | collective-permute-start | bytes 196616 | tf_op jit(solution)/shard_map/ppermute | solution.py:386
  63.0 1.3 %collective-permute-start.17 = (f32[64,256]{1,0:T(8,128)S(1)}, f32[64,256]{1,0:T(8,128)S(1)}, u32[]{:S(2)}, u32[]{:S(2)}) collective-permute-start(f32[64,256]{1,0:T(8,128)S(1)} %add_add_fusion), channel_id=1, source_target_pairs={{0,2},{1,3},{2,0},{3,1},{4,6},{5,7},{6,4},{7,5},{8,10},{9,11},{10,... | collective-permute-start | bytes 196616 | tf_op jit(solution)/shard_map/ppermute | solution.py:386

commit v14 on v13

--- a/solution.py
+++ b/solution.py
@@ -33,7 +33,6 @@
 levels = 17
 
 vmem = pl.BlockSpec(memory_space=pltpu.VMEM)
-smem = pl.BlockSpec(memory_space=pltpu.SMEM)
 hbm = pl.BlockSpec(memory_space=pl.ANY)
 params = pltpu.CompilerParams(vmem_limit_bytes=24 * 1024 * 1024)
 
@@ -68,27 +67,18 @@
         count = potential_ref.shape[1]
         out_ref[pl.ds(row, count), :] = potential_ref[i] * potential_gain
         row += count
-    lane = lax.broadcasted_iota(jnp.int32, (1, nz), 1)
-    numbers = jnp.zeros((1, nz), jnp.float32)
-    for a in range(atoms):
-        for p in range(projs):
-            numbers = jnp.where(lane == a * projs + p, energies_ref[a, p], numbers)
-    high = numbers.astype(jnp.bfloat16).astype(jnp.float32)
-    low = (numbers - high) * remainder_gain
-    count = atoms * projs
-    numbers = high + pltpu.roll(low, count, 1)
-    for a in range(atoms):
-        for d in range(2):
-            here = centers_ref[d, a].astype(jnp.float32)
-            numbers = jnp.where(lane == 2 * count + 2 * a + d, here, numbers)
-    out_ref[pl.ds(row, 1), :] = numbers
-    out_ref[pl.ds(row + 1, rows - row - 1), :] = jnp.zeros((rows - row - 1, nz), jnp.float32)
+    out_ref[pl.ds(row, rows - row), :] = jnp.zeros((rows - row, nz), jnp.float32)
+    energies = energies_ref[...]
+    high = energies.astype(jnp.bfloat16).astype(jnp.float32)
+    out_ref[pl.ds(row, atoms), :projs] = high
+    out_ref[pl.ds(row + atoms, atoms), :projs] = (energies - high) * remainder_gain
+    out_ref[pl.ds(row + 2 * atoms, 2), :atoms] = centers_ref[...].astype(jnp.float32)
 
 
 def filter_kernel(slabs_y, cells_x, cells_y, each, atoms, projs, slabs, *refs):
     inputs, (first, rounded_out) = refs[:-10], refs[-10:-8]
     second, partial, diagonal, coeffs, numbers, rounded_ref, arrived, sent = refs[-8:]
-    group = numbers.shape[0]
+    group, number_rows, _ = numbers.shape
     nz = first.shape[-1]
     count_x, count_y = diagonal.shape[0], diagonal.shape[1]
     tiles = len(offsets_x)
@@ -123,13 +113,15 @@
     if slabs is None:
         copies = [
             pltpu.make_async_copy(
-                inputs[0].at[:, slab_cells * each + number_row, :], numbers, arrived.at[0]
+                inputs[0].at[:, pl.ds(slab_cells * each + number_row, number_rows), :],
+                numbers,
+                arrived.at[0],
             )
         ]
     else:
         copies = [
             pltpu.make_async_copy(
-                rows_of(g, True, number_row, 1), numbers.at[pl.ds(g, 1), :], arrived.at[g]
+                rows_of(g, True, number_row, number_rows), numbers.at[g], arrived.at[g]
             )
             for g in range(group)
         ]
@@ -196,7 +188,7 @@
                 partial[x, y] = along_z[x] + diagonal[x, y] * cells[x] + along(cells, x)
             return carry
 
-        lax.fori_loop(0, count_y, xz_part, 0, unroll=4)
+        lax.fori_loop(0, count_y, xz_part, 0, unroll=6)
 
         def y_part(x, carry):
             cells = [source[ring + x, ring + y] for y in range(count_y)]
@@ -205,13 +197,12 @@
                 target[ring + x, ring + y] = finish(total, target, ring + x, ring + y)
             return carry
 
-        lax.fori_loop(0, count_x, y_part, 0, unroll=2)
+        lax.fori_loop(0, count_x, y_part, 0, unroll=4)
 
         def place_of(g, a):
-            at = 2 * atoms * projs + 2 * a
             return (
-                ring + numbers[g, at].astype(jnp.int32),
-                ring + numbers[g, at + 1].astype(jnp.int32),
+                ring + numbers[g, 2 * atoms, a].astype(jnp.int32),
+                ring + numbers[g, 2 * atoms + 1, a].astype(jnp.int32),
             )
 
         def gather_part(g):
@@ -224,9 +215,8 @@
                         term = tile * shared_row(g, (a * tiles + t) * projs + p)
                         totals[p] = term if t == 0 else totals[p] + term
                 for p in range(projs):
-                    k = a * projs + p
-                    energy = numbers[g, k] + numbers[g, atoms * projs + k] * (1.0 / remainder_gain)
-                    coeffs[g, k] = jnp.broadcast_to(
+                    energy = numbers[g, a, p] + numbers[g, atoms + a, p] * (1.0 / remainder_gain)
+                    coeffs[g, a * projs + p] = jnp.broadcast_to(
                         jnp.sum(totals[p], axis=-1, keepdims=True)
                         * (energy * (gain / projector_gain / projector_gain)),
                         (each, nz),
@@ -403,7 +393,8 @@
     by_swaps = group <= 8 and each % 8 == 0 and slabs_x > 1
     by_swaps = by_swaps and group & (group - 1) == 0 and bands & (bands - 1) == 0
 
-    rows = atoms * projs * tiles + slab_cells + 1
+    number_rows = 2 * atoms + 2
+    rows = atoms * projs * tiles + slab_cells + number_rows
     rows += -rows % 8
     piece_rows = slab_cells * each
     chunks = (orbitals * orbital_gain).astype(jnp.float16)
@@ -411,7 +402,7 @@
     chunks = chunks.transpose(1, 0, 2, 3).reshape(group, piece_rows, nz)
     shared = pl.pallas_call(
         share_kernel,
-        in_specs=[hbm, smem, smem, vmem, vmem],
+        in_specs=[hbm, vmem, vmem, vmem, vmem],
         out_specs=vmem,
         out_shape=jax.ShapeDtypeStruct((rows, nz), jnp.float32),
         compiler_params=params,
@@ -456,7 +447,7 @@
             pltpu.VMEM(grid + (each, nz), jnp.float32),
             pltpu.VMEM(grid + (1, nz), jnp.float32),
             pltpu.VMEM((group, atoms * projs, each, nz), jnp.float32),
-            pltpu.SMEM((group, nz), jnp.float32),
+            pltpu.SMEM((group, number_rows, nz), jnp.float32),
             pltpu.VMEM(rounded_shape, jnp.bfloat16),
             pltpu.SemaphoreType.DMA((group,)),
             pltpu.SemaphoreType.DMA((bands,)),

time: 65.2 us -> 64.8 us (level)
    pallas_call x1, Pallas kernels: 0.68 us -> 0.02 us  [local(): pl.pallas_call(share_kernel, in_specs=[hbm, vmem, vmem, vmem, vmem], out_...]
where the time goes in v14:
time: 64.8 us; the launch traced here: 64.6 us
  starting transfers between devices  27.1 us (42%)
  waiting for transfers between devices  24.5 us (38%)
  Pallas kernels  8.73 us (13%)
  other arithmetic  2.91 us (4%)
  between operations  1.02 us (2%)
    ppermute x15, waiting for transfers between devices, swap(): return lax.ppermute(block, plane, [(i, i ^ value) for i in range(group)])  20.7 us
    ppermute x15, starting transfers between devices, swap(): return lax.ppermute(block, plane, [(i, i ^ value) for i in range(group)])  17 us
    pallas_call x1, Pallas kernels, local(): pl.pallas_call(functools.partial(filter_kernel, slabs_y, cells_x, cells_y...  6.44 us
    all_to_all x1, starting transfers between devices, local(): matrix = lax.all_to_all(rounded, every, 0, 0)  5.71 us
    ppermute x3, starting transfers between devices, local(): lax.ppermute(sums[k].astype(jnp.float16), 'band', [(i, i ^ k) for i in ra...  4.45 us
    ppermute x3, waiting for transfers between devices, local(): lax.ppermute(sums[k].astype(jnp.float16), 'band', [(i, i ^ k) for i in ra...  3.8 us
    convert_element_type x1, other arithmetic, local(): chunks = (orbitals * orbital_gain).astype(jnp.float16)  1.46 us
  transfers between devices with their start and end apart: 19, of which 13 were waited for; matrix products, arithmetic and copies ran while one was open for 1% of the time, Pallas kernels for 2%

profile of v14, /device:TPU:0, one launch (start us, length us, event | category | flops | bytes accessed | tf_op | source)
XLA Modules:
  0.0 64.6 jit_solution(8077729177727992158)
XLA Ops:
  0.7 1.5 %multiply_convert_fusion = f16[64,6,6,128]{3,0,2,1:T(8,128)(2,1)S(1)} fusion(f32[64,6,6,128]{3,0,2,1:T(8,128)} %param.5), kind=kLoop, calls=%fused_computation | loop fusion | flops 589824 | bytes 1769472 | tf_op jit(solution)/shard_map/convert_element_type | solution.py:400
  2.7 4.0 %collective-permute-start.2 = (f16[704,128]{1,0:T(8,128)(2,1)S(1)}, f16[704,128]{1,0:T(8,128)(2,1)S(1)}, u32[]{:S(2)}, u32[]{:S(2)}) collective-permute-start(f16[704,128]{1,0:T(8,128)(2,1)S(1)} %get-tuple-element.44), channel_id=1, source_target_pairs={{0,5},{1,4},{2,7},{3,6},{4,1},{5,0},{6,3},{7,2},{8,13},{9,12},{10,... | collective-permute-start | bytes 540680 | tf_op jit(solution)/shard_map/ppermute | solution.py:376
  6.7 0.5 collective-permute-start.1
  7.3 4.7 %collective-permute-done.2 = f16[704,128]{1,0:T(8,128)(2,1)S(1)} collective-permute-done((f16[704,128]{1,0:T(8,128)(2,1)S(1)}, f16[704,128]{1,0:T(8,128)(2,1)S(1)}, u32[]{:S(2)}, u32[]{:S(2)}) %collective-permute-start.2) | collective-permute-done | bytes 180256 | tf_op jit(solution)/shard_map/ppermute | solution.py:376
  12.1 3.3 %collective-permute-done.1 = f16[704,128]{1,0:T(8,128)(2,1)S(1)} collective-permute-done((f16[704,128]{1,0:T(8,128)(2,1)S(1)}, f16[704,128]{1,0:T(8,128)(2,1)S(1)}, u32[]{:S(2)}, u32[]{:S(2)}) %collective-permute-start.1) | collective-permute-done | bytes 180256 | tf_op jit(solution)/shard_map/ppermute | solution.py:376
  15.8 1.7 %collective-permute-done.3 = f16[4,416,128]{2,1,0:T(8,128)(2,1)S(1)} collective-permute-done((f16[4,416,128]{2,1,0:T(8,128)(2,1)S(1)}, f16[4,416,128]{2,1,0:T(8,128)(2,1)S(1)}, u32[]{:S(2)}, u32[]{:S(2)}) %collective-permute-start.3) | collective-permute-done | bytes 426016 | tf_op jit(solution)/shard_map/ppermute | solution.py:376
  17.5 6.4 %shard_map.69 = (f32[26,14,8,128]{3,2,1,0:T(8,128)S(1)}, bf16[32,8,1152]{2,1,0:T(8,128)(2,1)}) custom-call(f32[1,288,128]{2,1,0:T(8,128)S(1)} %get-tuple-element.40.refs_0_, f32[1,128,128]{2,1,0:T(8,128)S(1)} %bitcast.93, f32[1,704,128]{2,1,0:T(8,128)S(1)} %bitcast_convert_fusion.2.refs_2_, f32[1,704,128]{2,1,0:T(8,128)S(1)} %bitcast_convert_fusion.1.refs_3_, ...), custom_call_target="tpu_custom_call" | custom-call | flops 47185920 | bytes 2359296 | tf_op jit(solution)/shard_map/pallas_call | solution.py:437
  23.9 5.7 %all-to-all-start = ((bf16[32,8,1152]{2,1,0:T(8,128)(2,1)}), bf16[32,8,1152]{2,1,0:T(8,128)(2,1)S(1)}, u32[]{:S(2)}, u32[]{:S(2)}) async-start(bf16[32,8,1152]{2,1,0:T(8,128)(2,1)} %get-tuple-element.15), calls=%async_computation | async-start | bytes 1179648 | tf_op jit(solution)/shard_map/all_to_all | solution.py:463
  29.7 0.4 shard_map.70.refs_0_
  30.3 2.5 %collective-permute-start.10 = (f16[296,128]{1,0:T(8,128)(2,1)S(1)}, f16[296,128]{1,0:T(8,128)(2,1)S(1)}, u32[]{:S(2)}, u32[]{:S(2)}) collective-permute-start(f16[296,128]{1,0:T(8,128)(2,1)S(1)} %get-tuple-element.26), channel_id=1, source_target_pairs={{0,7},{1,6},{2,5},{3,4},{4,3},{5,2},{6,1},{7,0},{8,15},{9,14},{10,... | collective-permute-start | bytes 227336 | tf_op jit(solution)/shard_map/ppermute | solution.py:376
  32.8 0.5 collective-permute-start.9
  33.3 1.5 %collective-permute-start.8 = (f16[296,128]{1,0:T(8,128)(2,1)S(1)}, f16[296,128]{1,0:T(8,128)(2,1)S(1)}, u32[]{:S(2)}, u32[]{:S(2)}) collective-permute-start(f16[296,128]{1,0:T(8,128)(2,1)S(1)} %get-tuple-element.28), channel_id=1, source_target_pairs={{0,5},{1,4},{2,7},{3,6},{4,1},{5,0},{6,3},{7,2},{8,13},{9,12},{10,... | collective-permute-start | bytes 227336 | tf_op jit(solution)/shard_map/ppermute | solution.py:376
  35.0 1.0 %collective-permute-start.6 = (f16[296,128]{1,0:T(8,128)(2,1)S(1)}, f16[296,128]{1,0:T(8,128)(2,1)S(1)}, u32[]{:S(2)}, u32[]{:S(2)}) collective-permute-start(f16[296,128]{1,0:T(8,128)(2,1)S(1)} %get-tuple-element.30), channel_id=1, source_target_pairs={{0,3},{1,2},{2,1},{3,0},{4,7},{5,6},{6,5},{7,4},{8,11},{9,10},{10,... | collective-permute-start | bytes 227336 | tf_op jit(solution)/shard_map/ppermute | solution.py:376
  36.0 2.9 %collective-permute-done.10 = f16[296,128]{1,0:T(8,128)(2,1)S(1)} collective-permute-done((f16[296,128]{1,0:T(8,128)(2,1)S(1)}, f16[296,128]{1,0:T(8,128)(2,1)S(1)}, u32[]{:S(2)}, u32[]{:S(2)}) %collective-permute-start.10) | collective-permute-done | bytes 75808 | tf_op jit(solution)/shard_map/ppermute | solution.py:376
  38.9 1.5 %collective-permute-start.5 = (f16[296,128]{1,0:T(8,128)(2,1)S(1)}, f16[296,128]{1,0:T(8,128)(2,1)S(1)}, u32[]{:S(2)}, u32[]{:S(2)}) collective-permute-start(f16[296,128]{1,0:T(8,128)(2,1)S(1)} %get-tuple-element.31), channel_id=1, source_target_pairs={{0,2},{1,3},{2,0},{3,1},{4,6},{5,7},{6,4},{7,5},{8,10},{9,11},{10,... | collective-permute-start | bytes 227336 | tf_op jit(solution)/shard_map/ppermute | solution.py:376
  40.4 1.5 %collective-permute-start.4 = (f16[296,128]{1,0:T(8,128)(2,1)S(1)}, f16[296,128]{1,0:T(8,128)(2,1)S(1)}, u32[]{:S(2)}, u32[]{:S(2)}) collective-permute-start(f16[296,128]{1,0:T(8,128)(2,1)S(1)} %get-tuple-element.32), channel_id=1, source_target_pairs={{0,1},{1,0},{2,3},{3,2},{4,5},{5,4},{6,7},{7,6},{8,9},{9,8},{10,11... | collective-permute-start | bytes 227336 | tf_op jit(solution)/shard_map/ppermute | solution.py:376
  41.9 2.6 %collective-permute-done.8 = f16[296,128]{1,0:T(8,128)(2,1)S(1)} collective-permute-done((f16[296,128]{1,0:T(8,128)(2,1)S(1)}, f16[296,128]{1,0:T(8,128)(2,1)S(1)}, u32[]{:S(2)}, u32[]{:S(2)}) %collective-permute-start.8) | collective-permute-done | bytes 75808 | tf_op jit(solution)/shard_map/ppermute | solution.py:376
  44.5 0.6 collective-permute-done.7
  45.1 1.5 %collective-permute-done.4 = f16[296,128]{1,0:T(8,128)(2,1)S(1)} collective-permute-done((f16[296,128]{1,0:T(8,128)(2,1)S(1)}, f16[296,128]{1,0:T(8,128)(2,1)S(1)}, u32[]{:S(2)}, u32[]{:S(2)}) %collective-permute-start.4) | collective-permute-done | bytes 75808 | tf_op jit(solution)/shard_map/ppermute | solution.py:376
  46.5 0.5 shard_map.71.own_ref
  47.1 3.5 %collective-permute-start.13 = (f16[64,256]{1,0:T(8,128)(2,1)S(1)}, f16[64,256]{1,0:T(8,128)(2,1)S(1)}, u32[]{:S(2)}, u32[]{:S(2)}) collective-permute-start(f16[64,256]{1,0:T(8,128)(2,1)S(1)} %get-tuple-element.41), channel_id=1, source_target_pairs={{0,24},{8,16},{16,8},{24,0},{1,25},{9,17},{17,9},{25,1},{2,26},{10... | collective-permute-start | bytes 98312 | tf_op jit(solution)/shard_map/ppermute | solution.py:506
  50.7 0.9 %collective-permute-start.11 = (f16[64,256]{1,0:T(8,128)(2,1)S(1)}, f16[64,256]{1,0:T(8,128)(2,1)S(1)}, u32[]{:S(2)}, u32[]{:S(2)}) collective-permute-start(f16[64,256]{1,0:T(8,128)(2,1)S(1)} %get-tuple-element.43), channel_id=1, source_target_pairs={{0,8},{8,0},{16,24},{24,16},{1,9},{9,1},{17,25},{25,17},{2,10},{10... | collective-permute-start | bytes 98312 | tf_op jit(solution)/shard_map/ppermute | solution.py:506
  51.7 1.2 %collective-permute-done.13 = f16[64,256]{1,0:T(8,128)(2,1)S(1)} collective-permute-done((f16[64,256]{1,0:T(8,128)(2,1)S(1)}, f16[64,256]{1,0:T(8,128)(2,1)S(1)}, u32[]{:S(2)}, u32[]{:S(2)}) %collective-permute-start.13) | collective-permute-done | bytes 32800 | tf_op jit(solution)/shard_map/ppermute | solution.py:506
  52.9 2.6 %collective-permute-done.12 = f16[64,256]{1,0:T(8,128)(2,1)S(1)} collective-permute-done((f16[64,256]{1,0:T(8,128)(2,1)S(1)}, f16[64,256]{1,0:T(8,128)(2,1)S(1)}, u32[]{:S(2)}, u32[]{:S(2)}) %collective-permute-start.12) | collective-permute-done | bytes 32800 | tf_op jit(solution)/shard_map/ppermute | solution.py:506
  55.7 1.1 %collective-permute-start.16 = (f32[64,256]{1,0:T(8,128)S(1)}, f32[64,256]{1,0:T(8,128)S(1)}, u32[]{:S(2)}, u32[]{:S(2)}) collective-permute-start(f32[64,256]{1,0:T(8,128)S(1)} %shard_map.72), channel_id=1, source_target_pairs={{0,5},{1,4},{2,7},{3,6},{4,1},{5,0},{6,3},{7,2},{8,13},{9,12},{10,... | collective-permute-start | bytes 196616 | tf_op jit(solution)/shard_map/ppermute | solution.py:376
  56.8 1.6 %collective-permute-start.15 = (f32[64,256]{1,0:T(8,128)S(1)}, f32[64,256]{1,0:T(8,128)S(1)}, u32[]{:S(2)}, u32[]{:S(2)}) collective-permute-start(f32[64,256]{1,0:T(8,128)S(1)} %shard_map.72), channel_id=1, source_target_pairs={{0,4},{1,5},{2,6},{3,7},{4,0},{5,1},{6,2},{7,3},{8,12},{9,13},{10,... | collective-permute-start | bytes 196616 | tf_op jit(solution)/shard_map/ppermute | solution.py:376
  58.4 0.8 %collective-permute-start.14 = (f32[64,256]{1,0:T(8,128)S(1)}, f32[64,256]{1,0:T(8,128)S(1)}, u32[]{:S(2)}, u32[]{:S(2)}) collective-permute-start(f32[64,256]{1,0:T(8,128)S(1)} %shard_map.72), channel_id=1, source_target_pairs={{0,1},{1,0},{2,3},{3,2},{4,5},{5,4},{6,7},{7,6},{8,9},{9,8},{10,11... | collective-permute-start | bytes 196616 | tf_op jit(solution)/shard_map/ppermute | solution.py:376
  59.2 1.1 %shard_map.73 = f32[36,64,128]{2,1,0:T(8,128)} custom-call(f32[8,296,128]{2,1,0:T(8,128)S(1)} %shard_map.70.refs_0_, f32[1,296,128]{2,1,0:T(8,128)S(1)} %bitcast_convert_fusion.9.refs_1_, f32[1,296,128]{2,1,0:T(8,128)S(1)} %get-tuple-element.52.refs_2_, f32[1,296,128]{2,1,0:T(8,128)S(1)} %get-tuple-element.51.refs_3_, ...), custom_call_target="tpu_custom_call" | custom-call | tf_op jit(solution)/shard_map/pallas_call | solution.py:483
  60.3 0.5 collective-permute-done.16
  61.3 1.3 %collective-permute-done.14 = f32[64,256]{1,0:T(8,128)S(1)} collective-permute-done((f32[64,256]{1,0:T(8,128)S(1)}, f32[64,256]{1,0:T(8,128)S(1)}, u32[]{:S(2)}, u32[]{:S(2)}) %collective-permute-start.14) | collective-permute-done | bytes 65568 | tf_op jit(solution)/shard_map/ppermute | solution.py:376
  62.7 1.2 %collective-permute-done.17 = f32[64,256]{1,0:T(8,128)S(1)} collective-permute-done((f32[64,256]{1,0:T(8,128)S(1)}, f32[64,256]{1,0:T(8,128)S(1)}, u32[]{:S(2)}, u32[]{:S(2)}) %collective-permute-start.17) | collective-permute-done | bytes 65568 | tf_op jit(solution)/shard_map/ppermute | solution.py:376
  64.0 0.6 add.52
  (48 shorter events, 2.3 us)
Async XLA Ops:
  0.7 1.6 %copy-start = (f32[4,4,5,128]{3,1,2,0:T(4,128)S(1)}, f32[4,4,5,128]{3,1,2,0:T(4,128)}, u32[]{:S(2)}) copy-start(f32[4,4,5,128]{3,1,2,0:T(4,128)} %param.7) | copy-start | bytes 122884
  0.7 1.6 %copy-start.1 = (f32[6,6,128]{2,1,0:T(8,128)S(1)}, f32[6,6,128]{2,1,0:T(8,128)}, u32[]{:S(2)}) copy-start(f32[6,6,128]{2,1,0:T(8,128)} %potential_ref.1) | copy-start | bytes 55300
  0.7 1.6 %copy-start.2 = (f32[4,4]{1,0:T(4,128)S(1)}, f32[4,4]{1,0:T(4,128)}, u32[]{:S(2)}) copy-start(f32[4,4]{1,0:T(4,128)} %energies_ref.1) | copy-start | bytes 196
  0.7 1.6 %copy-start.3 = (s32[4,2]{0,1:T(2,128)S(1)}, s32[4,2]{0,1:T(2,128)}, u32[]{:S(2)}) copy-start(s32[4,2]{0,1:T(2,128)} %param.9) | copy-start | bytes 100
  2.7 9.3 %collective-permute-start.2 = (f16[704,128]{1,0:T(8,128)(2,1)S(1)}, f16[704,128]{1,0:T(8,128)(2,1)S(1)}, u32[]{:S(2)}, u32[]{:S(2)}) collective-permute-start(f16[704,128]{1,0:T(8,128)(2,1)S(1)} %get-tuple-element.44), channel_id=1, source_target_pairs={{0,5},{1,4},{2,7},{3,6},{4,1},{5,0},{6,3},{7,2},{8,13},{9,12},{10,... | collective-permute-start | bytes 540680 | tf_op jit(solution)/shard_map/ppermute | solution.py:376
  6.7 8.7 %collective-permute-start.1 = (f16[704,128]{1,0:T(8,128)(2,1)S(1)}, f16[704,128]{1,0:T(8,128)(2,1)S(1)}, u32[]{:S(2)}, u32[]{:S(2)}) collective-permute-start(f16[704,128]{1,0:T(8,128)(2,1)S(1)} %get-tuple-element.45), channel_id=1, source_target_pairs={{0,4},{1,5},{2,6},{3,7},{4,0},{5,1},{6,2},{7,3},{8,12},{9,13},{10,... | collective-permute-start | bytes 540680 | tf_op jit(solution)/shard_map/ppermute | solution.py:376
  7.2 8.2 %collective-permute-start = (f16[704,128]{1,0:T(8,128)(2,1)S(1)}, f16[704,128]{1,0:T(8,128)(2,1)S(1)}, u32[]{:S(2)}, u32[]{:S(2)}) collective-permute-start(f16[704,128]{1,0:T(8,128)(2,1)S(1)} %get-tuple-element.46), channel_id=1, source_target_pairs={{0,1},{1,0},{2,3},{3,2},{4,5},{5,4},{6,7},{7,6},{8,9},{9,8},{10,11... | collective-permute-start | bytes 540680 | tf_op jit(solution)/shard_map/ppermute | solution.py:376
  15.6 1.8 %collective-permute-start.3 = (f16[4,416,128]{2,1,0:T(8,128)(2,1)S(1)}, f16[4,416,128]{2,1,0:T(8,128)(2,1)S(1)}, u32[]{:S(2)}, u32[]{:S(2)}) collective-permute-start(f16[4,416,128]{2,1,0:T(8,128)(2,1)S(1)} %pad_maximum_fusion), channel_id=1, source_target_pairs={{0,2},{1,3},{2,0},{3,1},{4,6},{5,7},{6,4},{7,5},{8,10},{9,11},{10,... | collective-permute-start | bytes 1277960 | tf_op jit(solution)/shard_map/ppermute | solution.py:376
  23.9 22.6 %all-to-all-start = ((bf16[32,8,1152]{2,1,0:T(8,128)(2,1)}), bf16[32,8,1152]{2,1,0:T(8,128)(2,1)S(1)}, u32[]{:S(2)}, u32[]{:S(2)}) async-start(bf16[32,8,1152]{2,1,0:T(8,128)(2,1)} %get-tuple-element.15), calls=%async_computation | async-start | bytes 1179648 | tf_op jit(solution)/shard_map/all_to_all | solution.py:463
  30.3 8.6 %collective-permute-start.10 = (f16[296,128]{1,0:T(8,128)(2,1)S(1)}, f16[296,128]{1,0:T(8,128)(2,1)S(1)}, u32[]{:S(2)}, u32[]{:S(2)}) collective-permute-start(f16[296,128]{1,0:T(8,128)(2,1)S(1)} %get-tuple-element.26), channel_id=1, source_target_pairs={{0,7},{1,6},{2,5},{3,4},{4,3},{5,2},{6,1},{7,0},{8,15},{9,14},{10,... | collective-permute-start | bytes 227336 | tf_op jit(solution)/shard_map/ppermute | solution.py:376
  32.8 7.6 %collective-permute-start.9 = (f16[296,128]{1,0:T(8,128)(2,1)S(1)}, f16[296,128]{1,0:T(8,128)(2,1)S(1)}, u32[]{:S(2)}, u32[]{:S(2)}) collective-permute-start(f16[296,128]{1,0:T(8,128)(2,1)S(1)} %get-tuple-element.27), channel_id=1, source_target_pairs={{0,6},{1,7},{2,4},{3,5},{4,2},{5,3},{6,0},{7,1},{8,14},{9,15},{10,... | collective-permute-start | bytes 227336 | tf_op jit(solution)/shard_map/ppermute | solution.py:376
  33.3 11.2 %collective-permute-start.8 = (f16[296,128]{1,0:T(8,128)(2,1)S(1)}, f16[296,128]{1,0:T(8,128)(2,1)S(1)}, u32[]{:S(2)}, u32[]{:S(2)}) collective-permute-start(f16[296,128]{1,0:T(8,128)(2,1)S(1)} %get-tuple-element.28), channel_id=1, source_target_pairs={{0,5},{1,4},{2,7},{3,6},{4,1},{5,0},{6,3},{7,2},{8,13},{9,12},{10,... | collective-permute-start | bytes 227336 | tf_op jit(solution)/shard_map/ppermute | solution.py:376
  34.8 10.3 %collective-permute-start.7 = (f16[296,128]{1,0:T(8,128)(2,1)S(1)}, f16[296,128]{1,0:T(8,128)(2,1)S(1)}, u32[]{:S(2)}, u32[]{:S(2)}) collective-permute-start(f16[296,128]{1,0:T(8,128)(2,1)S(1)} %get-tuple-element.29), channel_id=1, source_target_pairs={{0,4},{1,5},{2,6},{3,7},{4,0},{5,1},{6,2},{7,3},{8,12},{9,13},{10,... | collective-permute-start | bytes 227336 | tf_op jit(solution)/shard_map/ppermute | solution.py:376
  35.0 10.0 %collective-permute-start.6 = (f16[296,128]{1,0:T(8,128)(2,1)S(1)}, f16[296,128]{1,0:T(8,128)(2,1)S(1)}, u32[]{:S(2)}, u32[]{:S(2)}) collective-permute-start(f16[296,128]{1,0:T(8,128)(2,1)S(1)} %get-tuple-element.30), channel_id=1, source_target_pairs={{0,3},{1,2},{2,1},{3,0},{4,7},{5,6},{6,5},{7,4},{8,11},{9,10},{10,... | collective-permute-start | bytes 227336 | tf_op jit(solution)/shard_map/ppermute | solution.py:376
  38.9 6.2 %collective-permute-start.5 = (f16[296,128]{1,0:T(8,128)(2,1)S(1)}, f16[296,128]{1,0:T(8,128)(2,1)S(1)}, u32[]{:S(2)}, u32[]{:S(2)}) collective-permute-start(f16[296,128]{1,0:T(8,128)(2,1)S(1)} %get-tuple-element.31), channel_id=1, source_target_pairs={{0,2},{1,3},{2,0},{3,1},{4,6},{5,7},{6,4},{7,5},{8,10},{9,11},{10,... | collective-permute-start | bytes 227336 | tf_op jit(solution)/shard_map/ppermute | solution.py:376
  40.4 6.1 %collective-permute-start.4 = (f16[296,128]{1,0:T(8,128)(2,1)S(1)}, f16[296,128]{1,0:T(8,128)(2,1)S(1)}, u32[]{:S(2)}, u32[]{:S(2)}) collective-permute-start(f16[296,128]{1,0:T(8,128)(2,1)S(1)} %get-tuple-element.32), channel_id=1, source_target_pairs={{0,1},{1,0},{2,3},{3,2},{4,5},{5,4},{6,7},{7,6},{8,9},{9,8},{10,11... | collective-permute-start | bytes 227336 | tf_op jit(solution)/shard_map/ppermute | solution.py:376
  47.1 5.8 %collective-permute-start.13 = (f16[64,256]{1,0:T(8,128)(2,1)S(1)}, f16[64,256]{1,0:T(8,128)(2,1)S(1)}, u32[]{:S(2)}, u32[]{:S(2)}) collective-permute-start(f16[64,256]{1,0:T(8,128)(2,1)S(1)} %get-tuple-element.41), channel_id=1, source_target_pairs={{0,24},{8,16},{16,8},{24,0},{1,25},{9,17},{17,9},{25,1},{2,26},{10... | collective-permute-start | bytes 98312 | tf_op jit(solution)/shard_map/ppermute | solution.py:506
  50.7 4.8 %collective-permute-start.12 = (f16[64,256]{1,0:T(8,128)(2,1)S(1)}, f16[64,256]{1,0:T(8,128)(2,1)S(1)}, u32[]{:S(2)}, u32[]{:S(2)}) collective-permute-start(f16[64,256]{1,0:T(8,128)(2,1)S(1)} %get-tuple-element.42), channel_id=1, source_target_pairs={{0,16},{8,24},{16,0},{24,8},{1,17},{9,25},{17,1},{25,9},{2,18},{10... | collective-permute-start | bytes 98312 | tf_op jit(solution)/shard_map/ppermute | solution.py:506
  50.7 4.8 %collective-permute-start.11 = (f16[64,256]{1,0:T(8,128)(2,1)S(1)}, f16[64,256]{1,0:T(8,128)(2,1)S(1)}, u32[]{:S(2)}, u32[]{:S(2)}) collective-permute-start(f16[64,256]{1,0:T(8,128)(2,1)S(1)} %get-tuple-element.43), channel_id=1, source_target_pairs={{0,8},{8,0},{16,24},{24,16},{1,9},{9,1},{17,25},{25,17},{2,10},{10... | collective-permute-start | bytes 98312 | tf_op jit(solution)/shard_map/ppermute | solution.py:506
  55.7 5.2 %collective-permute-start.16 = (f32[64,256]{1,0:T(8,128)S(1)}, f32[64,256]{1,0:T(8,128)S(1)}, u32[]{:S(2)}, u32[]{:S(2)}) collective-permute-start(f32[64,256]{1,0:T(8,128)S(1)} %shard_map.72), channel_id=1, source_target_pairs={{0,5},{1,4},{2,7},{3,6},{4,1},{5,0},{6,3},{7,2},{8,13},{9,12},{10,... | collective-permute-start | bytes 196616 | tf_op jit(solution)/shard_map/ppermute | solution.py:376
  56.8 4.5 %collective-permute-start.15 = (f32[64,256]{1,0:T(8,128)S(1)}, f32[64,256]{1,0:T(8,128)S(1)}, u32[]{:S(2)}, u32[]{:S(2)}) collective-permute-start(f32[64,256]{1,0:T(8,128)S(1)} %shard_map.72), channel_id=1, source_target_pairs={{0,4},{1,5},{2,6},{3,7},{4,0},{5,1},{6,2},{7,3},{8,12},{9,13},{10,... | collective-permute-start | bytes 196616 | tf_op jit(solution)/shard_map/ppermute | solution.py:376
  58.4 4.3 %collective-permute-start.14 = (f32[64,256]{1,0:T(8,128)S(1)}, f32[64,256]{1,0:T(8,128)S(1)}, u32[]{:S(2)}, u32[]{:S(2)}) collective-permute-start(f32[64,256]{1,0:T(8,128)S(1)} %shard_map.72), channel_id=1, source_target_pairs={{0,1},{1,0},{2,3},{3,2},{4,5},{5,4},{6,7},{7,6},{8,9},{9,8},{10,11... | collective-permute-start | bytes 196616 | tf_op jit(solution)/shard_map/ppermute | solution.py:376
  62.6 1.3 %collective-permute-start.17 = (f32[64,256]{1,0:T(8,128)S(1)}, f32[64,256]{1,0:T(8,128)S(1)}, u32[]{:S(2)}, u32[]{:S(2)}) collective-permute-start(f32[64,256]{1,0:T(8,128)S(1)} %add_add_fusion), channel_id=1, source_target_pairs={{0,2},{1,3},{2,0},{3,1},{4,6},{5,7},{6,4},{7,5},{8,10},{9,11},{10,... | collective-permute-start | bytes 196616 | tf_op jit(solution)/shard_map/ppermute | solution.py:376

commit v15 on v14

--- a/solution.py
+++ b/solution.py
@@ -471,10 +471,14 @@
     )(values)
     narrow = field.astype(jnp.float16)
     if by_swaps:
-        came = [swap(narrow[v], v) for v in range(1, group)]
-        came, matrix = lax.optimization_barrier((came, matrix))
-        pieces = [field] + [block.astype(jnp.float32)[None] for block in came]
-        places = [(v, 0, v) for v in range(group)]
+        came = [swap(jnp.stack([narrow[v], narrow[v | near]]), v) for v in far]
+        first, matrix = lax.optimization_barrier((came[:-1], matrix))
+        came = first + came[-1:]
+        came.append(swap(jnp.stack([narrow[near]] + [block[1] for block in came]), near))
+        pieces = [field] + [block.astype(jnp.float32) for block in came]
+        places = [(0, 0, 0), (len(pieces) - 1, 0, near)]
+        for i, v in enumerate(far):
+            places += [(i + 1, 0, v), (len(pieces) - 1, i + 1, v | near)]
     else:
         pieces = [lax.all_to_all(narrow, plane, 0, 0).astype(jnp.float32)]
         places = [(0, g, g) for g in range(group)]
@@ -508,6 +512,7 @@
             ).astype(jnp.float32)
             for k in range(1, bands)
         ]
+        parts, pieces = lax.optimization_barrier((parts, pieces))
         gram = pl.pallas_call(
             functools.partial(rows_kernel, cells),
             in_specs=[vmem] * bands,

time: 64.8 us -> 64.1 us (0.989)
  starting transfers between devices: 27.1 us -> 23.1 us
  waiting for transfers between devices: 24.5 us -> 27.5 us
    ppermute x15 -> x12, starting transfers between devices: 17 us -> 12.9 us  [swap(): return lax.ppermute(block, plane, [(i, i ^ value) for i in range(group)])]
    ppermute x15 -> x12, waiting for transfers between devices: 20.7 us -> 23.8 us  [swap(): return lax.ppermute(block, plane, [(i, i ^ value) for i in range(group)])]
    ppermute x3, waiting for transfers between devices: 3.8 us -> 2.62 us  [local(): lax.ppermute(sums[k].astype(jnp.float16), 'band', [(i, i ^ k) for i in ra...]
    all_to_all x1, waiting for transfers between devices: 0.01 us -> 1 us  [local(): matrix = lax.all_to_all(rounded, every, 0, 0)]
  transfers between devices with their start and end apart: 19 -> 16, of which waited for: 13 -> 14; matrix products, arithmetic and copies ran while one was open for 1% -> 1% of each run, Pallas kernels for 2% -> 3%
where the time goes in v15:
time: 64.1 us; the launch traced here: 63.9 us
  waiting for transfers between devices  27.5 us (43%)
  starting transfers between devices  23.1 us (36%)
  Pallas kernels  8.72 us (14%)
  other arithmetic  3.19 us (5%)
  between operations  1.05 us (2%)
    ppermute x12, waiting for transfers between devices, swap(): return lax.ppermute(block, plane, [(i, i ^ value) for i in range(group)])  23.8 us
    ppermute x12, starting transfers between devices, swap(): return lax.ppermute(block, plane, [(i, i ^ value) for i in range(group)])  12.9 us
    pallas_call x1, Pallas kernels, local(): pl.pallas_call(functools.partial(filter_kernel, slabs_y, cells_x, cells_y...  6.44 us
    all_to_all x1, starting transfers between devices, local(): matrix = lax.all_to_all(rounded, every, 0, 0)  5.71 us
    ppermute x3, starting transfers between devices, local(): lax.ppermute(sums[k].astype(jnp.float16), 'band', [(i, i ^ k) for i in ra...  4.45 us
    ppermute x3, waiting for transfers between devices, local(): lax.ppermute(sums[k].astype(jnp.float16), 'band', [(i, i ^ k) for i in ra...  2.62 us
    convert_element_type x1, other arithmetic, local(): chunks = (orbitals * orbital_gain).astype(jnp.float16)  1.46 us
  transfers between devices with their start and end apart: 16, of which 14 were waited for; matrix products, arithmetic and copies ran while one was open for 1% of the time, Pallas kernels for 3%

profile of v15, /device:TPU:0, one launch (start us, length us, event | category | flops | bytes accessed | tf_op | source)
XLA Modules:
  0.0 63.9 jit_solution(14794253957682009939)
XLA Ops:
  0.7 1.5 %multiply_convert_fusion = f16[64,6,6,128]{3,0,2,1:T(8,128)(2,1)S(1)} fusion(f32[64,6,6,128]{3,0,2,1:T(8,128)} %param.5), kind=kLoop, calls=%fused_computation | loop fusion | flops 589824 | bytes 1769472 | tf_op jit(solution)/shard_map/convert_element_type | solution.py:400
  2.7 4.0 %collective-permute-start.2 = (f16[704,128]{1,0:T(8,128)(2,1)S(1)}, f16[704,128]{1,0:T(8,128)(2,1)S(1)}, u32[]{:S(2)}, u32[]{:S(2)}) collective-permute-start(f16[704,128]{1,0:T(8,128)(2,1)S(1)} %get-tuple-element.50), channel_id=1, source_target_pairs={{0,5},{1,4},{2,7},{3,6},{4,1},{5,0},{6,3},{7,2},{8,13},{9,12},{10,... | collective-permute-start | bytes 540680 | tf_op jit(solution)/shard_map/ppermute | solution.py:376
  6.7 0.5 collective-permute-start.1
  7.3 4.7 %collective-permute-done.2 = f16[704,128]{1,0:T(8,128)(2,1)S(1)} collective-permute-done((f16[704,128]{1,0:T(8,128)(2,1)S(1)}, f16[704,128]{1,0:T(8,128)(2,1)S(1)}, u32[]{:S(2)}, u32[]{:S(2)}) %collective-permute-start.2) | collective-permute-done | bytes 180256 | tf_op jit(solution)/shard_map/ppermute | solution.py:376
  12.1 3.3 %collective-permute-done.1 = f16[704,128]{1,0:T(8,128)(2,1)S(1)} collective-permute-done((f16[704,128]{1,0:T(8,128)(2,1)S(1)}, f16[704,128]{1,0:T(8,128)(2,1)S(1)}, u32[]{:S(2)}, u32[]{:S(2)}) %collective-permute-start.1) | collective-permute-done | bytes 180256 | tf_op jit(solution)/shard_map/ppermute | solution.py:376
  15.8 1.7 %collective-permute-done.3 = f16[4,416,128]{2,1,0:T(8,128)(2,1)S(1)} collective-permute-done((f16[4,416,128]{2,1,0:T(8,128)(2,1)S(1)}, f16[4,416,128]{2,1,0:T(8,128)(2,1)S(1)}, u32[]{:S(2)}, u32[]{:S(2)}) %collective-permute-start.3) | collective-permute-done | bytes 426016 | tf_op jit(solution)/shard_map/ppermute | solution.py:376
  17.5 6.4 %shard_map.69 = (f32[26,14,8,128]{3,2,1,0:T(8,128)S(1)}, bf16[32,8,1152]{2,1,0:T(8,128)(2,1)}) custom-call(f32[1,288,128]{2,1,0:T(8,128)S(1)} %get-tuple-element.46.refs_0_, f32[1,128,128]{2,1,0:T(8,128)S(1)} %bitcast.58, f32[1,704,128]{2,1,0:T(8,128)S(1)} %bitcast_convert_fusion.2.refs_2_, f32[1,704,128]{2,1,0:T(8,128)S(1)} %bitcast_convert_fusion.1.refs_3_, ...), custom_call_target="tpu_custom_call" | custom-call | flops 47185920 | bytes 2359296 | tf_op jit(solution)/shard_map/pallas_call | solution.py:437
  23.9 5.7 %all-to-all-start = ((bf16[32,8,1152]{2,1,0:T(8,128)(2,1)}), bf16[32,8,1152]{2,1,0:T(8,128)(2,1)S(1)}, u32[]{:S(2)}, u32[]{:S(2)}) async-start(bf16[32,8,1152]{2,1,0:T(8,128)(2,1)} %get-tuple-element.18), calls=%async_computation | async-start | bytes 1179648 | tf_op jit(solution)/shard_map/all_to_all | solution.py:463
  29.7 0.4 shard_map.70.refs_0_
  30.4 1.8 %collective-permute-start.4 = (f16[2,296,128]{2,1,0:T(8,128)(2,1)S(1)}, f16[2,296,128]{2,1,0:T(8,128)(2,1)S(1)}, u32[]{:S(2)}, u32[]{:S(2)}) collective-permute-start(f16[2,296,128]{2,1,0:T(8,128)(2,1)S(1)} %pad_maximum_fusion.5), channel_id=1, source_target_pairs={{0,1},{1,0},{2,3},{3,2},{4,5},{5,4},{6,7},{7,6},{8,9},{9,8},{10,11... | collective-permute-start | bytes 454664 | tf_op jit(solution)/shard_map/ppermute | solution.py:376
  32.2 1.5 %collective-permute-start.9 = (f16[2,296,128]{2,1,0:T(8,128)(2,1)S(1)}, f16[2,296,128]{2,1,0:T(8,128)(2,1)S(1)}, u32[]{:S(2)}, u32[]{:S(2)}) collective-permute-start(f16[2,296,128]{2,1,0:T(8,128)(2,1)S(1)} %pad_maximum_fusion.7), channel_id=1, source_target_pairs={{0,5},{1,4},{2,7},{3,6},{4,1},{5,0},{6,3},{7,2},{8,13},{9,12},{10,... | collective-permute-start | bytes 454664 | tf_op jit(solution)/shard_map/ppermute | solution.py:376
  33.8 0.3 collective-permute-start.5
  34.1 8.1 %collective-permute-done.9 = f16[2,296,128]{2,1,0:T(8,128)(2,1)S(1)} collective-permute-done((f16[2,296,128]{2,1,0:T(8,128)(2,1)S(1)}, f16[2,296,128]{2,1,0:T(8,128)(2,1)S(1)}, u32[]{:S(2)}, u32[]{:S(2)}) %collective-permute-start.9) | collective-permute-done | bytes 151584 | tf_op jit(solution)/shard_map/ppermute | solution.py:376
  42.3 2.3 %collective-permute-done.4 = f16[2,296,128]{2,1,0:T(8,128)(2,1)S(1)} collective-permute-done((f16[2,296,128]{2,1,0:T(8,128)(2,1)S(1)}, f16[2,296,128]{2,1,0:T(8,128)(2,1)S(1)}, u32[]{:S(2)}, u32[]{:S(2)}) %collective-permute-start.4) | collective-permute-done | bytes 151584 | tf_op jit(solution)/shard_map/ppermute | solution.py:376
  44.6 0.5 collective-permute-done.5
  45.1 1.0 %all-to-all-done = bf16[32,8,1152]{2,1,0:T(8,128)(2,1)S(1)} async-done(((bf16[32,8,1152]{2,1,0:T(8,128)(2,1)}), bf16[32,8,1152]{2,1,0:T(8,128)(2,1)S(1)}, u32[]{:S(2)}, u32[]{:S(2)}) %all-to-all-start) | async-done | bytes 589856 | tf_op jit(solution)/shard_map/all_to_all | solution.py:463
  46.2 1.0 %collective-permute-start.10 = (f16[4,296,128]{2,1,0:T(8,128)(2,1)S(1)}, f16[4,296,128]{2,1,0:T(8,128)(2,1)S(1)}, u32[]{:S(2)}, u32[]{:S(2)}) collective-permute-start(f16[4,296,128]{2,1,0:T(8,128)(2,1)S(1)} %pad_maximum_fusion.1), channel_id=1, source_target_pairs={{0,2},{1,3},{2,0},{3,1},{4,6},{5,7},{6,4},{7,5},{8,10},{9,11},{10,... | collective-permute-start | bytes 909320 | tf_op jit(solution)/shard_map/ppermute | solution.py:376
  47.2 0.5 shard_map.71.own_ref
  47.8 1.9 %collective-permute-start.8 = (f16[64,256]{1,0:T(8,128)(2,1)S(1)}, f16[64,256]{1,0:T(8,128)(2,1)S(1)}, u32[]{:S(2)}, u32[]{:S(2)}) collective-permute-start(f16[64,256]{1,0:T(8,128)(2,1)S(1)} %get-tuple-element.47), channel_id=1, source_target_pairs={{0,24},{8,16},{16,8},{24,0},{1,25},{9,17},{17,9},{25,1},{2,26},{10... | collective-permute-start | bytes 98312 | tf_op jit(solution)/shard_map/ppermute | solution.py:510
  49.8 0.7 %collective-permute-start.7 = (f16[64,256]{1,0:T(8,128)(2,1)S(1)}, f16[64,256]{1,0:T(8,128)(2,1)S(1)}, u32[]{:S(2)}, u32[]{:S(2)}) collective-permute-start(f16[64,256]{1,0:T(8,128)(2,1)S(1)} %get-tuple-element.48), channel_id=1, source_target_pairs={{0,16},{8,24},{16,0},{24,8},{1,17},{9,25},{17,1},{25,9},{2,18},{10... | collective-permute-start | bytes 98312 | tf_op jit(solution)/shard_map/ppermute | solution.py:510
  50.4 1.8 %collective-permute-start.6 = (f16[64,256]{1,0:T(8,128)(2,1)S(1)}, f16[64,256]{1,0:T(8,128)(2,1)S(1)}, u32[]{:S(2)}, u32[]{:S(2)}) collective-permute-start(f16[64,256]{1,0:T(8,128)(2,1)S(1)} %get-tuple-element.49), channel_id=1, source_target_pairs={{0,8},{8,0},{16,24},{24,16},{1,9},{9,1},{17,25},{25,17},{2,10},{10... | collective-permute-start | bytes 98312 | tf_op jit(solution)/shard_map/ppermute | solution.py:510
  52.4 1.2 %collective-permute-done.8 = f16[64,256]{1,0:T(8,128)(2,1)S(1)} collective-permute-done((f16[64,256]{1,0:T(8,128)(2,1)S(1)}, f16[64,256]{1,0:T(8,128)(2,1)S(1)}, u32[]{:S(2)}, u32[]{:S(2)}) %collective-permute-start.8) | collective-permute-done | bytes 32800 | tf_op jit(solution)/shard_map/ppermute | solution.py:510
  53.6 1.1 %collective-permute-done.7 = f16[64,256]{1,0:T(8,128)(2,1)S(1)} collective-permute-done((f16[64,256]{1,0:T(8,128)(2,1)S(1)}, f16[64,256]{1,0:T(8,128)(2,1)S(1)}, u32[]{:S(2)}, u32[]{:S(2)}) %collective-permute-start.7) | collective-permute-done | bytes 32800 | tf_op jit(solution)/shard_map/ppermute | solution.py:510
  55.3 1.4 %collective-permute-start.13 = (f32[64,256]{1,0:T(8,128)S(1)}, f32[64,256]{1,0:T(8,128)S(1)}, u32[]{:S(2)}, u32[]{:S(2)}) collective-permute-start(f32[64,256]{1,0:T(8,128)S(1)} %shard_map.72), channel_id=1, source_target_pairs={{0,5},{1,4},{2,7},{3,6},{4,1},{5,0},{6,3},{7,2},{8,13},{9,12},{10,... | collective-permute-start | bytes 196616 | tf_op jit(solution)/shard_map/ppermute | solution.py:376
  56.7 1.0 %collective-permute-start.12 = (f32[64,256]{1,0:T(8,128)S(1)}, f32[64,256]{1,0:T(8,128)S(1)}, u32[]{:S(2)}, u32[]{:S(2)}) collective-permute-start(f32[64,256]{1,0:T(8,128)S(1)} %shard_map.72), channel_id=1, source_target_pairs={{0,4},{1,5},{2,6},{3,7},{4,0},{5,1},{6,2},{7,3},{8,12},{9,13},{10,... | collective-permute-start | bytes 196616 | tf_op jit(solution)/shard_map/ppermute | solution.py:376
  57.7 1.1 %collective-permute-start.11 = (f32[64,256]{1,0:T(8,128)S(1)}, f32[64,256]{1,0:T(8,128)S(1)}, u32[]{:S(2)}, u32[]{:S(2)}) collective-permute-start(f32[64,256]{1,0:T(8,128)S(1)} %shard_map.72), channel_id=1, source_target_pairs={{0,1},{1,0},{2,3},{3,2},{4,5},{5,4},{6,7},{7,6},{8,9},{9,8},{10,11... | collective-permute-start | bytes 196616 | tf_op jit(solution)/shard_map/ppermute | solution.py:376
  58.8 1.1 %shard_map.73 = f32[36,64,128]{2,1,0:T(8,128)} custom-call(f32[8,296,128]{2,1,0:T(8,128)S(1)} %shard_map.70.refs_0_, f32[2,296,128]{2,1,0:T(8,128)S(1)} %convert_element_type.87.refs_1_, f32[2,296,128]{2,1,0:T(8,128)S(1)} %convert_element_type.88.refs_2_, f32[2,296,128]{2,1,0:T(8,128)S(1)} %convert_element_type.89.refs_3_, ...), custom_call_target="tpu_custom_call" | custom-call | tf_op jit(solution)/shard_map/pallas_call | solution.py:487
  59.9 0.6 collective-permute-done.13
  60.4 0.7 %collective-permute-done.12 = f32[64,256]{1,0:T(8,128)S(1)} collective-permute-done((f32[64,256]{1,0:T(8,128)S(1)}, f32[64,256]{1,0:T(8,128)S(1)}, u32[]{:S(2)}, u32[]{:S(2)}) %collective-permute-start.12) | collective-permute-done | bytes 65568 | tf_op jit(solution)/shard_map/ppermute | solution.py:376
  61.1 0.8 %collective-permute-done.11 = f32[64,256]{1,0:T(8,128)S(1)} collective-permute-done((f32[64,256]{1,0:T(8,128)S(1)}, f32[64,256]{1,0:T(8,128)S(1)}, u32[]{:S(2)}, u32[]{:S(2)}) %collective-permute-start.11) | collective-permute-done | bytes 65568 | tf_op jit(solution)/shard_map/ppermute | solution.py:376
  62.0 1.2 %collective-permute-done.14 = f32[64,256]{1,0:T(8,128)S(1)} collective-permute-done((f32[64,256]{1,0:T(8,128)S(1)}, f32[64,256]{1,0:T(8,128)S(1)}, u32[]{:S(2)}, u32[]{:S(2)}) %collective-permute-start.14) | collective-permute-done | bytes 65568 | tf_op jit(solution)/shard_map/ppermute | solution.py:376
  63.3 0.6 add.52
  (49 shorter events, 2.2 us)
Async XLA Ops:
  0.7 1.6 %copy-start = (f32[4,4,5,128]{3,1,2,0:T(4,128)S(1)}, f32[4,4,5,128]{3,1,2,0:T(4,128)}, u32[]{:S(2)}) copy-start(f32[4,4,5,128]{3,1,2,0:T(4,128)} %param.7) | copy-start | bytes 122884
  0.7 1.6 %copy-start.1 = (f32[6,6,128]{2,1,0:T(8,128)S(1)}, f32[6,6,128]{2,1,0:T(8,128)}, u32[]{:S(2)}) copy-start(f32[6,6,128]{2,1,0:T(8,128)} %potential_ref.1) | copy-start | bytes 55300
  0.7 1.6 %copy-start.2 = (f32[4,4]{1,0:T(4,128)S(1)}, f32[4,4]{1,0:T(4,128)}, u32[]{:S(2)}) copy-start(f32[4,4]{1,0:T(4,128)} %energies_ref.1) | copy-start | bytes 196
  0.7 1.6 %copy-start.3 = (s32[4,2]{0,1:T(2,128)S(1)}, s32[4,2]{0,1:T(2,128)}, u32[]{:S(2)}) copy-start(s32[4,2]{0,1:T(2,128)} %param.9) | copy-start | bytes 100
  2.7 9.3 %collective-permute-start.2 = (f16[704,128]{1,0:T(8,128)(2,1)S(1)}, f16[704,128]{1,0:T(8,128)(2,1)S(1)}, u32[]{:S(2)}, u32[]{:S(2)}) collective-permute-start(f16[704,128]{1,0:T(8,128)(2,1)S(1)} %get-tuple-element.50), channel_id=1, source_target_pairs={{0,5},{1,4},{2,7},{3,6},{4,1},{5,0},{6,3},{7,2},{8,13},{9,12},{10,... | collective-permute-start | bytes 540680 | tf_op jit(solution)/shard_map/ppermute | solution.py:376
  6.7 8.7 %collective-permute-start.1 = (f16[704,128]{1,0:T(8,128)(2,1)S(1)}, f16[704,128]{1,0:T(8,128)(2,1)S(1)}, u32[]{:S(2)}, u32[]{:S(2)}) collective-permute-start(f16[704,128]{1,0:T(8,128)(2,1)S(1)} %get-tuple-element.51), channel_id=1, source_target_pairs={{0,4},{1,5},{2,6},{3,7},{4,0},{5,1},{6,2},{7,3},{8,12},{9,13},{10,... | collective-permute-start | bytes 540680 | tf_op jit(solution)/shard_map/ppermute | solution.py:376
  7.2 8.2 %collective-permute-start = (f16[704,128]{1,0:T(8,128)(2,1)S(1)}, f16[704,128]{1,0:T(8,128)(2,1)S(1)}, u32[]{:S(2)}, u32[]{:S(2)}) collective-permute-start(f16[704,128]{1,0:T(8,128)(2,1)S(1)} %get-tuple-element.52), channel_id=1, source_target_pairs={{0,1},{1,0},{2,3},{3,2},{4,5},{5,4},{6,7},{7,6},{8,9},{9,8},{10,11... | collective-permute-start | bytes 540680 | tf_op jit(solution)/shard_map/ppermute | solution.py:376
  15.6 1.8 %collective-permute-start.3 = (f16[4,416,128]{2,1,0:T(8,128)(2,1)S(1)}, f16[4,416,128]{2,1,0:T(8,128)(2,1)S(1)}, u32[]{:S(2)}, u32[]{:S(2)}) collective-permute-start(f16[4,416,128]{2,1,0:T(8,128)(2,1)S(1)} %pad_maximum_fusion), channel_id=1, source_target_pairs={{0,2},{1,3},{2,0},{3,1},{4,6},{5,7},{6,4},{7,5},{8,10},{9,11},{10,... | collective-permute-start | bytes 1277960 | tf_op jit(solution)/shard_map/ppermute | solution.py:376
  23.9 22.1 %all-to-all-start = ((bf16[32,8,1152]{2,1,0:T(8,128)(2,1)}), bf16[32,8,1152]{2,1,0:T(8,128)(2,1)S(1)}, u32[]{:S(2)}, u32[]{:S(2)}) async-start(bf16[32,8,1152]{2,1,0:T(8,128)(2,1)} %get-tuple-element.18), calls=%async_computation | async-start | bytes 1179648 | tf_op jit(solution)/shard_map/all_to_all | solution.py:463
  30.4 14.2 %collective-permute-start.4 = (f16[2,296,128]{2,1,0:T(8,128)(2,1)S(1)}, f16[2,296,128]{2,1,0:T(8,128)(2,1)S(1)}, u32[]{:S(2)}, u32[]{:S(2)}) collective-permute-start(f16[2,296,128]{2,1,0:T(8,128)(2,1)S(1)} %pad_maximum_fusion.5), channel_id=1, source_target_pairs={{0,1},{1,0},{2,3},{3,2},{4,5},{5,4},{6,7},{7,6},{8,9},{9,8},{10,11... | collective-permute-start | bytes 454664 | tf_op jit(solution)/shard_map/ppermute | solution.py:376
  32.2 10.0 %collective-permute-start.9 = (f16[2,296,128]{2,1,0:T(8,128)(2,1)S(1)}, f16[2,296,128]{2,1,0:T(8,128)(2,1)S(1)}, u32[]{:S(2)}, u32[]{:S(2)}) collective-permute-start(f16[2,296,128]{2,1,0:T(8,128)(2,1)S(1)} %pad_maximum_fusion.7), channel_id=1, source_target_pairs={{0,5},{1,4},{2,7},{3,6},{4,1},{5,0},{6,3},{7,2},{8,13},{9,12},{10,... | collective-permute-start | bytes 454664 | tf_op jit(solution)/shard_map/ppermute | solution.py:376
  33.8 11.3 %collective-permute-start.5 = (f16[2,296,128]{2,1,0:T(8,128)(2,1)S(1)}, f16[2,296,128]{2,1,0:T(8,128)(2,1)S(1)}, u32[]{:S(2)}, u32[]{:S(2)}) collective-permute-start(f16[2,296,128]{2,1,0:T(8,128)(2,1)S(1)} %pad_maximum_fusion.6), channel_id=1, source_target_pairs={{0,4},{1,5},{2,6},{3,7},{4,0},{5,1},{6,2},{7,3},{8,12},{9,13},{10,... | collective-permute-start | bytes 454664 | tf_op jit(solution)/shard_map/ppermute | solution.py:376
  46.2 8.8 %collective-permute-start.10 = (f16[4,296,128]{2,1,0:T(8,128)(2,1)S(1)}, f16[4,296,128]{2,1,0:T(8,128)(2,1)S(1)}, u32[]{:S(2)}, u32[]{:S(2)}) collective-permute-start(f16[4,296,128]{2,1,0:T(8,128)(2,1)S(1)} %pad_maximum_fusion.1), channel_id=1, source_target_pairs={{0,2},{1,3},{2,0},{3,1},{4,6},{5,7},{6,4},{7,5},{8,10},{9,11},{10,... | collective-permute-start | bytes 909320 | tf_op jit(solution)/shard_map/ppermute | solution.py:376
  47.8 5.8 %collective-permute-start.8 = (f16[64,256]{1,0:T(8,128)(2,1)S(1)}, f16[64,256]{1,0:T(8,128)(2,1)S(1)}, u32[]{:S(2)}, u32[]{:S(2)}) collective-permute-start(f16[64,256]{1,0:T(8,128)(2,1)S(1)} %get-tuple-element.47), channel_id=1, source_target_pairs={{0,24},{8,16},{16,8},{24,0},{1,25},{9,17},{17,9},{25,1},{2,26},{10... | collective-permute-start | bytes 98312 | tf_op jit(solution)/shard_map/ppermute | solution.py:510
  49.8 5.0 %collective-permute-start.7 = (f16[64,256]{1,0:T(8,128)(2,1)S(1)}, f16[64,256]{1,0:T(8,128)(2,1)S(1)}, u32[]{:S(2)}, u32[]{:S(2)}) collective-permute-start(f16[64,256]{1,0:T(8,128)(2,1)S(1)} %get-tuple-element.48), channel_id=1, source_target_pairs={{0,16},{8,24},{16,0},{24,8},{1,17},{9,25},{17,1},{25,9},{2,18},{10... | collective-permute-start | bytes 98312 | tf_op jit(solution)/shard_map/ppermute | solution.py:510
  50.4 4.6 %collective-permute-start.6 = (f16[64,256]{1,0:T(8,128)(2,1)S(1)}, f16[64,256]{1,0:T(8,128)(2,1)S(1)}, u32[]{:S(2)}, u32[]{:S(2)}) collective-permute-start(f16[64,256]{1,0:T(8,128)(2,1)S(1)} %get-tuple-element.49), channel_id=1, source_target_pairs={{0,8},{8,0},{16,24},{24,16},{1,9},{9,1},{17,25},{25,17},{2,10},{10... | collective-permute-start | bytes 98312 | tf_op jit(solution)/shard_map/ppermute | solution.py:510
  55.3 5.2 %collective-permute-start.13 = (f32[64,256]{1,0:T(8,128)S(1)}, f32[64,256]{1,0:T(8,128)S(1)}, u32[]{:S(2)}, u32[]{:S(2)}) collective-permute-start(f32[64,256]{1,0:T(8,128)S(1)} %shard_map.72), channel_id=1, source_target_pairs={{0,5},{1,4},{2,7},{3,6},{4,1},{5,0},{6,3},{7,2},{8,13},{9,12},{10,... | collective-permute-start | bytes 196616 | tf_op jit(solution)/shard_map/ppermute | solution.py:376
  56.7 4.5 %collective-permute-start.12 = (f32[64,256]{1,0:T(8,128)S(1)}, f32[64,256]{1,0:T(8,128)S(1)}, u32[]{:S(2)}, u32[]{:S(2)}) collective-permute-start(f32[64,256]{1,0:T(8,128)S(1)} %shard_map.72), channel_id=1, source_target_pairs={{0,4},{1,5},{2,6},{3,7},{4,0},{5,1},{6,2},{7,3},{8,12},{9,13},{10,... | collective-permute-start | bytes 196616 | tf_op jit(solution)/shard_map/ppermute | solution.py:376
  57.7 4.3 %collective-permute-start.11 = (f32[64,256]{1,0:T(8,128)S(1)}, f32[64,256]{1,0:T(8,128)S(1)}, u32[]{:S(2)}, u32[]{:S(2)}) collective-permute-start(f32[64,256]{1,0:T(8,128)S(1)} %shard_map.72), channel_id=1, source_target_pairs={{0,1},{1,0},{2,3},{3,2},{4,5},{5,4},{6,7},{7,6},{8,9},{9,8},{10,11... | collective-permute-start | bytes 196616 | tf_op jit(solution)/shard_map/ppermute | solution.py:376
  61.9 1.3 %collective-permute-start.14 = (f32[64,256]{1,0:T(8,128)S(1)}, f32[64,256]{1,0:T(8,128)S(1)}, u32[]{:S(2)}, u32[]{:S(2)}) collective-permute-start(f32[64,256]{1,0:T(8,128)S(1)} %add_add_fusion), channel_id=1, source_target_pairs={{0,2},{1,3},{2,0},{3,1},{4,6},{5,7},{6,4},{7,5},{8,10},{9,11},{10,... | collective-permute-start | bytes 196616 | tf_op jit(solution)/shard_map/ppermute | solution.py:376

commit v16 on v15

--- a/solution.py
+++ b/solution.py
@@ -472,8 +472,8 @@
     narrow = field.astype(jnp.float16)
     if by_swaps:
         came = [swap(jnp.stack([narrow[v], narrow[v | near]]), v) for v in far]
-        first, matrix = lax.optimization_barrier((came[:-1], matrix))
-        came = first + came[-1:]
+        others, matrix = lax.optimization_barrier((came[1:], matrix))
+        came = came[:1] + others
         came.append(swap(jnp.stack([narrow[near]] + [block[1] for block in came]), near))
         pieces = [field] + [block.astype(jnp.float32) for block in came]
         places = [(0, 0, 0), (len(pieces) - 1, 0, near)]

time: 64.1 us -> 64.1 us (level)
    all_to_all x1, waiting for transfers between devices: 1 us -> 0.01 us  [local(): matrix = lax.all_to_all(rounded, every, 0, 0)]
    ppermute x12, waiting for transfers between devices: 23.8 us -> 24.7 us  [swap(): return lax.ppermute(block, plane, [(i, i ^ value) for i in range(group)])]
  transfers between devices with their start and end apart: 16 -> 16, of which waited for: 14 -> 11; matrix products, arithmetic and copies ran while one was open for 1% -> 1% of each run, Pallas kernels for 3% -> 3%
where the time goes in v16:
time: 64.1 us; the launch traced here: 63.9 us
  waiting for transfers between devices  27.7 us (43%)
  starting transfers between devices  22.8 us (36%)
  Pallas kernels  8.72 us (14%)
  other arithmetic  3.19 us (5%)
  between operations  1.07 us (2%)
    ppermute x12, waiting for transfers between devices, swap(): return lax.ppermute(block, plane, [(i, i ^ value) for i in range(group)])  24.7 us
    ppermute x12, starting transfers between devices, swap(): return lax.ppermute(block, plane, [(i, i ^ value) for i in range(group)])  12.6 us
    pallas_call x1, Pallas kernels, local(): pl.pallas_call(functools.partial(filter_kernel, slabs_y, cells_x, cells_y...  6.44 us
    all_to_all x1, starting transfers between devices, local(): matrix = lax.all_to_all(rounded, every, 0, 0)  5.71 us
    ppermute x3, starting transfers between devices, local(): lax.ppermute(sums[k].astype(jnp.float16), 'band', [(i, i ^ k) for i in ra...  4.45 us
    ppermute x3, waiting for transfers between devices, local(): lax.ppermute(sums[k].astype(jnp.float16), 'band', [(i, i ^ k) for i in ra...  3.01 us
    convert_element_type x1, other arithmetic, local(): chunks = (orbitals * orbital_gain).astype(jnp.float16)  1.46 us
  transfers between devices with their start and end apart: 16, of which 11 were waited for; matrix products, arithmetic and copies ran while one was open for 1% of the time, Pallas kernels for 3%

profile of v16, /device:TPU:0, one launch (start us, length us, event | category | flops | bytes accessed | tf_op | source)
XLA Modules:
  0.0 63.9 jit_solution(1711381094164212780)
XLA Ops:
  0.7 1.5 %multiply_convert_fusion = f16[64,6,6,128]{3,0,2,1:T(8,128)(2,1)S(1)} fusion(f32[64,6,6,128]{3,0,2,1:T(8,128)} %param.5), kind=kLoop, calls=%fused_computation | loop fusion | flops 589824 | bytes 1769472 | tf_op jit(solution)/shard_map/convert_element_type | solution.py:400
  2.6 0.1 fusion.2
  2.7 4.0 %collective-permute-start.2 = (f16[704,128]{1,0:T(8,128)(2,1)S(1)}, f16[704,128]{1,0:T(8,128)(2,1)S(1)}, u32[]{:S(2)}, u32[]{:S(2)}) collective-permute-start(f16[704,128]{1,0:T(8,128)(2,1)S(1)} %get-tuple-element.50), channel_id=1, source_target_pairs={{0,5},{1,4},{2,7},{3,6},{4,1},{5,0},{6,3},{7,2},{8,13},{9,12},{10,... | collective-permute-start | bytes 540680 | tf_op jit(solution)/shard_map/ppermute | solution.py:376
  6.7 0.5 collective-permute-start.1
  7.3 4.7 %collective-permute-done.2 = f16[704,128]{1,0:T(8,128)(2,1)S(1)} collective-permute-done((f16[704,128]{1,0:T(8,128)(2,1)S(1)}, f16[704,128]{1,0:T(8,128)(2,1)S(1)}, u32[]{:S(2)}, u32[]{:S(2)}) %collective-permute-start.2) | collective-permute-done | bytes 180256 | tf_op jit(solution)/shard_map/ppermute | solution.py:376
  12.1 3.3 %collective-permute-done.1 = f16[704,128]{1,0:T(8,128)(2,1)S(1)} collective-permute-done((f16[704,128]{1,0:T(8,128)(2,1)S(1)}, f16[704,128]{1,0:T(8,128)(2,1)S(1)}, u32[]{:S(2)}, u32[]{:S(2)}) %collective-permute-start.1) | collective-permute-done | bytes 180256 | tf_op jit(solution)/shard_map/ppermute | solution.py:376
  15.4 0.1 pad_maximum_fusion
  15.8 1.7 %collective-permute-done.3 = f16[4,416,128]{2,1,0:T(8,128)(2,1)S(1)} collective-permute-done((f16[4,416,128]{2,1,0:T(8,128)(2,1)S(1)}, f16[4,416,128]{2,1,0:T(8,128)(2,1)S(1)}, u32[]{:S(2)}, u32[]{:S(2)}) %collective-permute-start.3) | collective-permute-done | bytes 426016 | tf_op jit(solution)/shard_map/ppermute | solution.py:376
  17.5 6.4 %shard_map.69 = (f32[26,14,8,128]{3,2,1,0:T(8,128)S(1)}, bf16[32,8,1152]{2,1,0:T(8,128)(2,1)}) custom-call(f32[1,288,128]{2,1,0:T(8,128)S(1)} %get-tuple-element.46.refs_0_, f32[1,128,128]{2,1,0:T(8,128)S(1)} %bitcast.58, f32[1,704,128]{2,1,0:T(8,128)S(1)} %bitcast_convert_fusion.2.refs_2_, f32[1,704,128]{2,1,0:T(8,128)S(1)} %bitcast_convert_fusion.1.refs_3_, ...), custom_call_target="tpu_custom_call" | custom-call | flops 47185920 | bytes 2359296 | tf_op jit(solution)/shard_map/pallas_call | solution.py:437
  23.9 5.7 %all-to-all-start = ((bf16[32,8,1152]{2,1,0:T(8,128)(2,1)}), bf16[32,8,1152]{2,1,0:T(8,128)(2,1)S(1)}, u32[]{:S(2)}, u32[]{:S(2)}) async-start(bf16[32,8,1152]{2,1,0:T(8,128)(2,1)} %get-tuple-element.18), calls=%async_computation | async-start | bytes 1179648 | tf_op jit(solution)/shard_map/all_to_all | solution.py:463
  29.7 0.4 shard_map.70.refs_0_
  30.4 1.8 %collective-permute-start.4 = (f16[2,296,128]{2,1,0:T(8,128)(2,1)S(1)}, f16[2,296,128]{2,1,0:T(8,128)(2,1)S(1)}, u32[]{:S(2)}, u32[]{:S(2)}) collective-permute-start(f16[2,296,128]{2,1,0:T(8,128)(2,1)S(1)} %pad_maximum_fusion.5), channel_id=1, source_target_pairs={{0,4},{1,5},{2,6},{3,7},{4,0},{5,1},{6,2},{7,3},{8,12},{9,13},{10,... | collective-permute-start | bytes 454664 | tf_op jit(solution)/shard_map/ppermute | solution.py:376
  32.2 1.5 %collective-permute-start.9 = (f16[2,296,128]{2,1,0:T(8,128)(2,1)S(1)}, f16[2,296,128]{2,1,0:T(8,128)(2,1)S(1)}, u32[]{:S(2)}, u32[]{:S(2)}) collective-permute-start(f16[2,296,128]{2,1,0:T(8,128)(2,1)S(1)} %pad_maximum_fusion.7), channel_id=1, source_target_pairs={{0,1},{1,0},{2,3},{3,2},{4,5},{5,4},{6,7},{7,6},{8,9},{9,8},{10,11... | collective-permute-start | bytes 454664 | tf_op jit(solution)/shard_map/ppermute | solution.py:376
  33.8 0.3 collective-permute-start.5
  34.1 7.1 %collective-permute-done.9 = f16[2,296,128]{2,1,0:T(8,128)(2,1)S(1)} collective-permute-done((f16[2,296,128]{2,1,0:T(8,128)(2,1)S(1)}, f16[2,296,128]{2,1,0:T(8,128)(2,1)S(1)}, u32[]{:S(2)}, u32[]{:S(2)}) %collective-permute-start.9) | collective-permute-done | bytes 151584 | tf_op jit(solution)/shard_map/ppermute | solution.py:376
  41.3 5.1 %collective-permute-done.5 = f16[2,296,128]{2,1,0:T(8,128)(2,1)S(1)} collective-permute-done((f16[2,296,128]{2,1,0:T(8,128)(2,1)S(1)}, f16[2,296,128]{2,1,0:T(8,128)(2,1)S(1)}, u32[]{:S(2)}, u32[]{:S(2)}) %collective-permute-start.5) | collective-permute-done | bytes 151584 | tf_op jit(solution)/shard_map/ppermute | solution.py:376
  46.6 0.7 %collective-permute-start.10 = (f16[4,296,128]{2,1,0:T(8,128)(2,1)S(1)}, f16[4,296,128]{2,1,0:T(8,128)(2,1)S(1)}, u32[]{:S(2)}, u32[]{:S(2)}) collective-permute-start(f16[4,296,128]{2,1,0:T(8,128)(2,1)S(1)} %pad_maximum_fusion.1), channel_id=1, source_target_pairs={{0,2},{1,3},{2,0},{3,1},{4,6},{5,7},{6,4},{7,5},{8,10},{9,11},{10,... | collective-permute-start | bytes 909320 | tf_op jit(solution)/shard_map/ppermute | solution.py:376
  47.2 0.5 shard_map.71.own_ref
  47.8 2.7 %collective-permute-start.8 = (f16[64,256]{1,0:T(8,128)(2,1)S(1)}, f16[64,256]{1,0:T(8,128)(2,1)S(1)}, u32[]{:S(2)}, u32[]{:S(2)}) collective-permute-start(f16[64,256]{1,0:T(8,128)(2,1)S(1)} %get-tuple-element.47), channel_id=1, source_target_pairs={{0,24},{8,16},{16,8},{24,0},{1,25},{9,17},{17,9},{25,1},{2,26},{10... | collective-permute-start | bytes 98312 | tf_op jit(solution)/shard_map/ppermute | solution.py:510
  50.6 1.7 %collective-permute-start.6 = (f16[64,256]{1,0:T(8,128)(2,1)S(1)}, f16[64,256]{1,0:T(8,128)(2,1)S(1)}, u32[]{:S(2)}, u32[]{:S(2)}) collective-permute-start(f16[64,256]{1,0:T(8,128)(2,1)S(1)} %get-tuple-element.49), channel_id=1, source_target_pairs={{0,8},{8,0},{16,24},{24,16},{1,9},{9,1},{17,25},{25,17},{2,10},{10... | collective-permute-start | bytes 98312 | tf_op jit(solution)/shard_map/ppermute | solution.py:510
  52.4 1.6 %collective-permute-done.8 = f16[64,256]{1,0:T(8,128)(2,1)S(1)} collective-permute-done((f16[64,256]{1,0:T(8,128)(2,1)S(1)}, f16[64,256]{1,0:T(8,128)(2,1)S(1)}, u32[]{:S(2)}, u32[]{:S(2)}) %collective-permute-start.8) | collective-permute-done | bytes 32800 | tf_op jit(solution)/shard_map/ppermute | solution.py:510
  53.9 1.5 %collective-permute-done.7 = f16[64,256]{1,0:T(8,128)(2,1)S(1)} collective-permute-done((f16[64,256]{1,0:T(8,128)(2,1)S(1)}, f16[64,256]{1,0:T(8,128)(2,1)S(1)}, u32[]{:S(2)}, u32[]{:S(2)}) %collective-permute-start.7) | collective-permute-done | bytes 32800 | tf_op jit(solution)/shard_map/ppermute | solution.py:510
  55.5 0.2 shard_map.72
  55.7 1.0 %collective-permute-start.13 = (f32[64,256]{1,0:T(8,128)S(1)}, f32[64,256]{1,0:T(8,128)S(1)}, u32[]{:S(2)}, u32[]{:S(2)}) collective-permute-start(f32[64,256]{1,0:T(8,128)S(1)} %shard_map.72), channel_id=1, source_target_pairs={{0,5},{1,4},{2,7},{3,6},{4,1},{5,0},{6,3},{7,2},{8,13},{9,12},{10,... | collective-permute-start | bytes 196616 | tf_op jit(solution)/shard_map/ppermute | solution.py:376
  56.7 1.0 %collective-permute-start.12 = (f32[64,256]{1,0:T(8,128)S(1)}, f32[64,256]{1,0:T(8,128)S(1)}, u32[]{:S(2)}, u32[]{:S(2)}) collective-permute-start(f32[64,256]{1,0:T(8,128)S(1)} %shard_map.72), channel_id=1, source_target_pairs={{0,4},{1,5},{2,6},{3,7},{4,0},{5,1},{6,2},{7,3},{8,12},{9,13},{10,... | collective-permute-start | bytes 196616 | tf_op jit(solution)/shard_map/ppermute | solution.py:376
  57.6 1.6 %collective-permute-start.11 = (f32[64,256]{1,0:T(8,128)S(1)}, f32[64,256]{1,0:T(8,128)S(1)}, u32[]{:S(2)}, u32[]{:S(2)}) collective-permute-start(f32[64,256]{1,0:T(8,128)S(1)} %shard_map.72), channel_id=1, source_target_pairs={{0,1},{1,0},{2,3},{3,2},{4,5},{5,4},{6,7},{7,6},{8,9},{9,8},{10,11... | collective-permute-start | bytes 196616 | tf_op jit(solution)/shard_map/ppermute | solution.py:376
  59.2 1.1 %shard_map.73 = f32[36,64,128]{2,1,0:T(8,128)} custom-call(f32[8,296,128]{2,1,0:T(8,128)S(1)} %shard_map.70.refs_0_, f32[2,296,128]{2,1,0:T(8,128)S(1)} %convert_element_type.87.refs_1_, f32[2,296,128]{2,1,0:T(8,128)S(1)} %convert_element_type.88.refs_2_, f32[2,296,128]{2,1,0:T(8,128)S(1)} %convert_element_type.89.refs_3_, ...), custom_call_target="tpu_custom_call" | custom-call | tf_op jit(solution)/shard_map/pallas_call | solution.py:487
  60.3 0.6 collective-permute-done.13
  60.9 0.3 collective-permute-done.12
  61.1 0.8 %collective-permute-done.11 = f32[64,256]{1,0:T(8,128)S(1)} collective-permute-done((f32[64,256]{1,0:T(8,128)S(1)}, f32[64,256]{1,0:T(8,128)S(1)}, u32[]{:S(2)}, u32[]{:S(2)}) %collective-permute-start.11) | collective-permute-done | bytes 65568 | tf_op jit(solution)/shard_map/ppermute | solution.py:376
  62.0 1.2 %collective-permute-done.14 = f32[64,256]{1,0:T(8,128)S(1)} collective-permute-done((f32[64,256]{1,0:T(8,128)S(1)}, f32[64,256]{1,0:T(8,128)S(1)}, u32[]{:S(2)}, u32[]{:S(2)}) %collective-permute-start.14) | collective-permute-done | bytes 65568 | tf_op jit(solution)/shard_map/ppermute | solution.py:376
  63.2 0.6 add.52
  (49 shorter events, 1.5 us)
Async XLA Ops:
  0.7 1.6 %copy-start = (f32[4,4,5,128]{3,1,2,0:T(4,128)S(1)}, f32[4,4,5,128]{3,1,2,0:T(4,128)}, u32[]{:S(2)}) copy-start(f32[4,4,5,128]{3,1,2,0:T(4,128)} %param.7) | copy-start | bytes 122884
  0.7 1.6 %copy-start.1 = (f32[6,6,128]{2,1,0:T(8,128)S(1)}, f32[6,6,128]{2,1,0:T(8,128)}, u32[]{:S(2)}) copy-start(f32[6,6,128]{2,1,0:T(8,128)} %potential_ref.1) | copy-start | bytes 55300
  0.7 1.6 %copy-start.2 = (f32[4,4]{1,0:T(4,128)S(1)}, f32[4,4]{1,0:T(4,128)}, u32[]{:S(2)}) copy-start(f32[4,4]{1,0:T(4,128)} %energies_ref.1) | copy-start | bytes 196
  0.7 1.6 %copy-start.3 = (s32[4,2]{0,1:T(2,128)S(1)}, s32[4,2]{0,1:T(2,128)}, u32[]{:S(2)}) copy-start(s32[4,2]{0,1:T(2,128)} %param.9) | copy-start | bytes 100
  2.7 9.3 %collective-permute-start.2 = (f16[704,128]{1,0:T(8,128)(2,1)S(1)}, f16[704,128]{1,0:T(8,128)(2,1)S(1)}, u32[]{:S(2)}, u32[]{:S(2)}) collective-permute-start(f16[704,128]{1,0:T(8,128)(2,1)S(1)} %get-tuple-element.50), channel_id=1, source_target_pairs={{0,5},{1,4},{2,7},{3,6},{4,1},{5,0},{6,3},{7,2},{8,13},{9,12},{10,... | collective-permute-start | bytes 540680 | tf_op jit(solution)/shard_map/ppermute | solution.py:376
  6.7 8.7 %collective-permute-start.1 = (f16[704,128]{1,0:T(8,128)(2,1)S(1)}, f16[704,128]{1,0:T(8,128)(2,1)S(1)}, u32[]{:S(2)}, u32[]{:S(2)}) collective-permute-start(f16[704,128]{1,0:T(8,128)(2,1)S(1)} %get-tuple-element.51), channel_id=1, source_target_pairs={{0,4},{1,5},{2,6},{3,7},{4,0},{5,1},{6,2},{7,3},{8,12},{9,13},{10,... | collective-permute-start | bytes 540680 | tf_op jit(solution)/shard_map/ppermute | solution.py:376
  7.2 8.2 %collective-permute-start = (f16[704,128]{1,0:T(8,128)(2,1)S(1)}, f16[704,128]{1,0:T(8,128)(2,1)S(1)}, u32[]{:S(2)}, u32[]{:S(2)}) collective-permute-start(f16[704,128]{1,0:T(8,128)(2,1)S(1)} %get-tuple-element.52), channel_id=1, source_target_pairs={{0,1},{1,0},{2,3},{3,2},{4,5},{5,4},{6,7},{7,6},{8,9},{9,8},{10,11... | collective-permute-start | bytes 540680 | tf_op jit(solution)/shard_map/ppermute | solution.py:376
  15.6 1.8 %collective-permute-start.3 = (f16[4,416,128]{2,1,0:T(8,128)(2,1)S(1)}, f16[4,416,128]{2,1,0:T(8,128)(2,1)S(1)}, u32[]{:S(2)}, u32[]{:S(2)}) collective-permute-start(f16[4,416,128]{2,1,0:T(8,128)(2,1)S(1)} %pad_maximum_fusion), channel_id=1, source_target_pairs={{0,2},{1,3},{2,0},{3,1},{4,6},{5,7},{6,4},{7,5},{8,10},{9,11},{10,... | collective-permute-start | bytes 1277960 | tf_op jit(solution)/shard_map/ppermute | solution.py:376
  23.9 22.5 %all-to-all-start = ((bf16[32,8,1152]{2,1,0:T(8,128)(2,1)}), bf16[32,8,1152]{2,1,0:T(8,128)(2,1)S(1)}, u32[]{:S(2)}, u32[]{:S(2)}) async-start(bf16[32,8,1152]{2,1,0:T(8,128)(2,1)} %get-tuple-element.18), calls=%async_computation | async-start | bytes 1179648 | tf_op jit(solution)/shard_map/all_to_all | solution.py:463
  30.4 10.9 %collective-permute-start.4 = (f16[2,296,128]{2,1,0:T(8,128)(2,1)S(1)}, f16[2,296,128]{2,1,0:T(8,128)(2,1)S(1)}, u32[]{:S(2)}, u32[]{:S(2)}) collective-permute-start(f16[2,296,128]{2,1,0:T(8,128)(2,1)S(1)} %pad_maximum_fusion.5), channel_id=1, source_target_pairs={{0,4},{1,5},{2,6},{3,7},{4,0},{5,1},{6,2},{7,3},{8,12},{9,13},{10,... | collective-permute-start | bytes 454664 | tf_op jit(solution)/shard_map/ppermute | solution.py:376
  32.2 9.0 %collective-permute-start.9 = (f16[2,296,128]{2,1,0:T(8,128)(2,1)S(1)}, f16[2,296,128]{2,1,0:T(8,128)(2,1)S(1)}, u32[]{:S(2)}, u32[]{:S(2)}) collective-permute-start(f16[2,296,128]{2,1,0:T(8,128)(2,1)S(1)} %pad_maximum_fusion.7), channel_id=1, source_target_pairs={{0,1},{1,0},{2,3},{3,2},{4,5},{5,4},{6,7},{7,6},{8,9},{9,8},{10,11... | collective-permute-start | bytes 454664 | tf_op jit(solution)/shard_map/ppermute | solution.py:376
  33.8 12.6 %collective-permute-start.5 = (f16[2,296,128]{2,1,0:T(8,128)(2,1)S(1)}, f16[2,296,128]{2,1,0:T(8,128)(2,1)S(1)}, u32[]{:S(2)}, u32[]{:S(2)}) collective-permute-start(f16[2,296,128]{2,1,0:T(8,128)(2,1)S(1)} %pad_maximum_fusion.6), channel_id=1, source_target_pairs={{0,5},{1,4},{2,7},{3,6},{4,1},{5,0},{6,3},{7,2},{8,13},{9,12},{10,... | collective-permute-start | bytes 454664 | tf_op jit(solution)/shard_map/ppermute | solution.py:376
  46.6 8.9 %collective-permute-start.10 = (f16[4,296,128]{2,1,0:T(8,128)(2,1)S(1)}, f16[4,296,128]{2,1,0:T(8,128)(2,1)S(1)}, u32[]{:S(2)}, u32[]{:S(2)}) collective-permute-start(f16[4,296,128]{2,1,0:T(8,128)(2,1)S(1)} %pad_maximum_fusion.1), channel_id=1, source_target_pairs={{0,2},{1,3},{2,0},{3,1},{4,6},{5,7},{6,4},{7,5},{8,10},{9,11},{10,... | collective-permute-start | bytes 909320 | tf_op jit(solution)/shard_map/ppermute | solution.py:376
  47.8 6.1 %collective-permute-start.8 = (f16[64,256]{1,0:T(8,128)(2,1)S(1)}, f16[64,256]{1,0:T(8,128)(2,1)S(1)}, u32[]{:S(2)}, u32[]{:S(2)}) collective-permute-start(f16[64,256]{1,0:T(8,128)(2,1)S(1)} %get-tuple-element.47), channel_id=1, source_target_pairs={{0,24},{8,16},{16,8},{24,0},{1,25},{9,17},{17,9},{25,1},{2,26},{10... | collective-permute-start | bytes 98312 | tf_op jit(solution)/shard_map/ppermute | solution.py:510
  50.6 4.8 %collective-permute-start.7 = (f16[64,256]{1,0:T(8,128)(2,1)S(1)}, f16[64,256]{1,0:T(8,128)(2,1)S(1)}, u32[]{:S(2)}, u32[]{:S(2)}) collective-permute-start(f16[64,256]{1,0:T(8,128)(2,1)S(1)} %get-tuple-element.48), channel_id=1, source_target_pairs={{0,16},{8,24},{16,0},{24,8},{1,17},{9,25},{17,1},{25,9},{2,18},{10... | collective-permute-start | bytes 98312 | tf_op jit(solution)/shard_map/ppermute | solution.py:510
  50.6 4.8 %collective-permute-start.6 = (f16[64,256]{1,0:T(8,128)(2,1)S(1)}, f16[64,256]{1,0:T(8,128)(2,1)S(1)}, u32[]{:S(2)}, u32[]{:S(2)}) collective-permute-start(f16[64,256]{1,0:T(8,128)(2,1)S(1)} %get-tuple-element.49), channel_id=1, source_target_pairs={{0,8},{8,0},{16,24},{24,16},{1,9},{9,1},{17,25},{25,17},{2,10},{10... | collective-permute-start | bytes 98312 | tf_op jit(solution)/shard_map/ppermute | solution.py:510
  55.7 5.2 %collective-permute-start.13 = (f32[64,256]{1,0:T(8,128)S(1)}, f32[64,256]{1,0:T(8,128)S(1)}, u32[]{:S(2)}, u32[]{:S(2)}) collective-permute-start(f32[64,256]{1,0:T(8,128)S(1)} %shard_map.72), channel_id=1, source_target_pairs={{0,5},{1,4},{2,7},{3,6},{4,1},{5,0},{6,3},{7,2},{8,13},{9,12},{10,... | collective-permute-start | bytes 196616 | tf_op jit(solution)/shard_map/ppermute | solution.py:376
  56.7 4.5 %collective-permute-start.12 = (f32[64,256]{1,0:T(8,128)S(1)}, f32[64,256]{1,0:T(8,128)S(1)}, u32[]{:S(2)}, u32[]{:S(2)}) collective-permute-start(f32[64,256]{1,0:T(8,128)S(1)} %shard_map.72), channel_id=1, source_target_pairs={{0,4},{1,5},{2,6},{3,7},{4,0},{5,1},{6,2},{7,3},{8,12},{9,13},{10,... | collective-permute-start | bytes 196616 | tf_op jit(solution)/shard_map/ppermute | solution.py:376
  57.6 4.3 %collective-permute-start.11 = (f32[64,256]{1,0:T(8,128)S(1)}, f32[64,256]{1,0:T(8,128)S(1)}, u32[]{:S(2)}, u32[]{:S(2)}) collective-permute-start(f32[64,256]{1,0:T(8,128)S(1)} %shard_map.72), channel_id=1, source_target_pairs={{0,1},{1,0},{2,3},{3,2},{4,5},{5,4},{6,7},{7,6},{8,9},{9,8},{10,11... | collective-permute-start | bytes 196616 | tf_op jit(solution)/shard_map/ppermute | solution.py:376
  61.9 1.3 %collective-permute-start.14 = (f32[64,256]{1,0:T(8,128)S(1)}, f32[64,256]{1,0:T(8,128)S(1)}, u32[]{:S(2)}, u32[]{:S(2)}) collective-permute-start(f32[64,256]{1,0:T(8,128)S(1)} %add_add_fusion), channel_id=1, source_target_pairs={{0,2},{1,3},{2,0},{3,1},{4,6},{5,7},{6,4},{7,5},{8,10},{9,11},{10,... | collective-permute-start | bytes 196616 | tf_op jit(solution)/shard_map/ppermute | solution.py:376

commit v17 on v16

--- a/solution.py
+++ b/solution.py
@@ -416,15 +416,18 @@
 
         came = [swap(jnp.concatenate([chunk_for(v), narrow, chunk_for(v ^ near)]), v) for v in far]
         mine = jnp.concatenate([narrow, chunk_for(near)])
-        crossed = swap(jnp.stack([mine] + [block[piece_rows:] for block in came]), near)
-        operands = [chunk_for(0)[None], narrow[None]] + [block[None] for block in came] + [crossed]
+        passed = {0: mine, **{v: block[piece_rows:] for v, block in zip(far, came)}}
+        operands = [chunk_for(0)[None], narrow[None]] + [block[None] for block in came]
+        slabs = {0: ((0, 0, 0), (1, 0, 0))}
+        for i, v in enumerate(far):
+            slabs[v] = ((2 + i, 0, 0), (2 + i, 0, piece_rows))
+        for part in ([0], far[-1:], far[:-1]):
+            if part:
+                for i, v in enumerate(part):
+                    slabs[v ^ near] = ((len(operands), i, rows), (len(operands), i, 0))
+                operands.append(swap(jnp.stack([passed[v] for v in part]), near))
         operands = [block.astype(jnp.float32) for block in operands]
         operands[1] = shared[None]
-        last = len(operands) - 1
-        slabs = {0: ((0, 0, 0), (1, 0, 0)), near: ((last, 0, rows), (last, 0, 0))}
-        for i, v in enumerate(far):
-            slabs[v] = ((2 + i, 0, 0), (2 + i, 0, piece_rows))
-            slabs[v ^ near] = ((last, 1 + i, rows), (last, 1 + i, 0))
     else:
         sent = jnp.concatenate([chunks, jnp.broadcast_to(narrow[None], (group, rows, nz))], axis=1)
         operands = [lax.all_to_all(sent, plane, 0, 0).astype(jnp.float32)]

time: 64.1 us -> 63.7 us (level)
    ppermute x12 -> x14, waiting for transfers between devices: 24.7 us -> 24.1 us  [swap(): return lax.ppermute(block, plane, [(i, i ^ value) for i in range(group)])]
    ppermute x12 -> x14, starting transfers between devices: 12.6 us -> 12.7 us  [swap(): return lax.ppermute(block, plane, [(i, i ^ value) for i in range(group)])]
  transfers between devices with their start and end apart: 16 -> 18, of which waited for: 11 -> 12; matrix products, arithmetic and copies ran while one was open for 1% -> 1% of each run, Pallas kernels for 3% -> 3%
where the time goes in v17:
time: 63.7 us; the launch traced here: 63.5 us
  waiting for transfers between devices  27.2 us (43%)
  starting transfers between devices  23 us (36%)
  Pallas kernels  8.75 us (14%)
  other arithmetic  3.11 us (5%)
  between operations  1.1 us (2%)
    ppermute x14, waiting for transfers between devices, swap(): return lax.ppermute(block, plane, [(i, i ^ value) for i in range(group)])  24.1 us
    ppermute x14, starting transfers between devices, swap(): return lax.ppermute(block, plane, [(i, i ^ value) for i in range(group)])  12.7 us
    pallas_call x1, Pallas kernels, local(): pl.pallas_call(functools.partial(filter_kernel, slabs_y, cells_x, cells_y...  6.46 us
    all_to_all x1, starting transfers between devices, local(): matrix = lax.all_to_all(rounded, every, 0, 0)  5.76 us
    ppermute x3, starting transfers between devices, local(): lax.ppermute(sums[k].astype(jnp.float16), 'band', [(i, i ^ k) for i in ra...  4.45 us
    ppermute x3, waiting for transfers between devices, local(): lax.ppermute(sums[k].astype(jnp.float16), 'band', [(i, i ^ k) for i in ra...  3 us
    convert_element_type x1, other arithmetic, local(): chunks = (orbitals * orbital_gain).astype(jnp.float16)  1.46 us
  transfers between devices with their start and end apart: 18, of which 12 were waited for; matrix products, arithmetic and copies ran while one was open for 1% of the time, Pallas kernels for 3%

profile of v17, /device:TPU:0, one launch (start us, length us, event | category | flops | bytes accessed | tf_op | source)
XLA Modules:
  0.0 63.5 jit_solution(13465397938817504911)
XLA Ops:
  0.7 1.5 %multiply_convert_fusion = f16[64,6,6,128]{3,0,2,1:T(8,128)(2,1)S(1)} fusion(f32[64,6,6,128]{3,0,2,1:T(8,128)} %param.5), kind=kLoop, calls=%fused_computation | loop fusion | flops 589824 | bytes 1769472 | tf_op jit(solution)/shard_map/convert_element_type | solution.py:400
  2.6 0.1 fusion.2
  2.7 4.0 %collective-permute-start.2 = (f16[704,128]{1,0:T(8,128)(2,1)S(1)}, f16[704,128]{1,0:T(8,128)(2,1)S(1)}, u32[]{:S(2)}, u32[]{:S(2)}) collective-permute-start(f16[704,128]{1,0:T(8,128)(2,1)S(1)} %get-tuple-element.50), channel_id=1, source_target_pairs={{0,5},{1,4},{2,7},{3,6},{4,1},{5,0},{6,3},{7,2},{8,13},{9,12},{10,... | collective-permute-start | bytes 540680 | tf_op jit(solution)/shard_map/ppermute | solution.py:376
  6.8 0.6 collective-permute-start.1
  7.4 0.6 %collective-permute-done.3 = f16[1,416,128]{2,1,0:T(8,128)(2,1)S(1)} collective-permute-done((f16[1,416,128]{2,1,0:T(8,128)(2,1)S(1)}, f16[1,416,128]{2,1,0:T(8,128)(2,1)S(1)}, u32[]{:S(2)}, u32[]{:S(2)}) %collective-permute-start.3) | collective-permute-done | bytes 106528 | tf_op jit(solution)/shard_map/ppermute | solution.py:376
  8.1 3.9 %collective-permute-done.2 = f16[704,128]{1,0:T(8,128)(2,1)S(1)} collective-permute-done((f16[704,128]{1,0:T(8,128)(2,1)S(1)}, f16[704,128]{1,0:T(8,128)(2,1)S(1)}, u32[]{:S(2)}, u32[]{:S(2)}) %collective-permute-start.2) | collective-permute-done | bytes 180256 | tf_op jit(solution)/shard_map/ppermute | solution.py:376
  12.2 3.2 %collective-permute-done.1 = f16[704,128]{1,0:T(8,128)(2,1)S(1)} collective-permute-done((f16[704,128]{1,0:T(8,128)(2,1)S(1)}, f16[704,128]{1,0:T(8,128)(2,1)S(1)}, u32[]{:S(2)}, u32[]{:S(2)}) %collective-permute-start.1) | collective-permute-done | bytes 180256 | tf_op jit(solution)/shard_map/ppermute | solution.py:376
  15.7 1.3 %collective-permute-done.5 = f16[2,416,128]{2,1,0:T(8,128)(2,1)S(1)} collective-permute-done((f16[2,416,128]{2,1,0:T(8,128)(2,1)S(1)}, f16[2,416,128]{2,1,0:T(8,128)(2,1)S(1)}, u32[]{:S(2)}, u32[]{:S(2)}) %collective-permute-start.5) | collective-permute-done | bytes 213024 | tf_op jit(solution)/shard_map/ppermute | solution.py:376
  17.0 6.5 %shard_map.69 = (f32[26,14,8,128]{3,2,1,0:T(8,128)S(1)}, bf16[32,8,1152]{2,1,0:T(8,128)(2,1)}) custom-call(f32[1,288,128]{2,1,0:T(8,128)S(1)} %get-tuple-element.46.refs_0_, f32[1,128,128]{2,1,0:T(8,128)S(1)} %bitcast.58, f32[1,704,128]{2,1,0:T(8,128)S(1)} %bitcast_convert_fusion.2.refs_2_, f32[1,704,128]{2,1,0:T(8,128)S(1)} %bitcast_convert_fusion.1.refs_3_, ...), custom_call_target="tpu_custom_call" | custom-call | flops 47185920 | bytes 2359296 | tf_op jit(solution)/shard_map/pallas_call | solution.py:440
  23.5 5.8 %all-to-all-start = ((bf16[32,8,1152]{2,1,0:T(8,128)(2,1)}), bf16[32,8,1152]{2,1,0:T(8,128)(2,1)S(1)}, u32[]{:S(2)}, u32[]{:S(2)}) async-start(bf16[32,8,1152]{2,1,0:T(8,128)(2,1)} %get-tuple-element.18), calls=%async_computation | async-start | bytes 1179648 | tf_op jit(solution)/shard_map/all_to_all | solution.py:466
  29.3 0.4 shard_map.70.refs_0_
  30.0 1.8 %collective-permute-start.6 = (f16[2,296,128]{2,1,0:T(8,128)(2,1)S(1)}, f16[2,296,128]{2,1,0:T(8,128)(2,1)S(1)}, u32[]{:S(2)}, u32[]{:S(2)}) collective-permute-start(f16[2,296,128]{2,1,0:T(8,128)(2,1)S(1)} %pad_maximum_fusion.5), channel_id=1, source_target_pairs={{0,4},{1,5},{2,6},{3,7},{4,0},{5,1},{6,2},{7,3},{8,12},{9,13},{10,... | collective-permute-start | bytes 454664 | tf_op jit(solution)/shard_map/ppermute | solution.py:376
  31.8 1.5 %collective-permute-start.11 = (f16[2,296,128]{2,1,0:T(8,128)(2,1)S(1)}, f16[2,296,128]{2,1,0:T(8,128)(2,1)S(1)}, u32[]{:S(2)}, u32[]{:S(2)}) collective-permute-start(f16[2,296,128]{2,1,0:T(8,128)(2,1)S(1)} %pad_maximum_fusion.7), channel_id=1, source_target_pairs={{0,1},{1,0},{2,3},{3,2},{4,5},{5,4},{6,7},{7,6},{8,9},{9,8},{10,11... | collective-permute-start | bytes 454664 | tf_op jit(solution)/shard_map/ppermute | solution.py:376
  33.4 0.3 collective-permute-start.7
  33.7 7.1 %collective-permute-done.11 = f16[2,296,128]{2,1,0:T(8,128)(2,1)S(1)} collective-permute-done((f16[2,296,128]{2,1,0:T(8,128)(2,1)S(1)}, f16[2,296,128]{2,1,0:T(8,128)(2,1)S(1)}, u32[]{:S(2)}, u32[]{:S(2)}) %collective-permute-start.11) | collective-permute-done | bytes 151584 | tf_op jit(solution)/shard_map/ppermute | solution.py:376
  40.9 5.1 %collective-permute-done.7 = f16[2,296,128]{2,1,0:T(8,128)(2,1)S(1)} collective-permute-done((f16[2,296,128]{2,1,0:T(8,128)(2,1)S(1)}, f16[2,296,128]{2,1,0:T(8,128)(2,1)S(1)}, u32[]{:S(2)}, u32[]{:S(2)}) %collective-permute-start.7) | collective-permute-done | bytes 151584 | tf_op jit(solution)/shard_map/ppermute | solution.py:376
  46.2 0.7 %collective-permute-start.12 = (f16[4,296,128]{2,1,0:T(8,128)(2,1)S(1)}, f16[4,296,128]{2,1,0:T(8,128)(2,1)S(1)}, u32[]{:S(2)}, u32[]{:S(2)}) collective-permute-start(f16[4,296,128]{2,1,0:T(8,128)(2,1)S(1)} %pad_maximum_fusion), channel_id=1, source_target_pairs={{0,2},{1,3},{2,0},{3,1},{4,6},{5,7},{6,4},{7,5},{8,10},{9,11},{10,... | collective-permute-start | bytes 909320 | tf_op jit(solution)/shard_map/ppermute | solution.py:376
  46.8 0.5 shard_map.71.own_ref
  47.4 2.7 %collective-permute-start.10 = (f16[64,256]{1,0:T(8,128)(2,1)S(1)}, f16[64,256]{1,0:T(8,128)(2,1)S(1)}, u32[]{:S(2)}, u32[]{:S(2)}) collective-permute-start(f16[64,256]{1,0:T(8,128)(2,1)S(1)} %get-tuple-element.47), channel_id=1, source_target_pairs={{0,24},{8,16},{16,8},{24,0},{1,25},{9,17},{17,9},{25,1},{2,26},{10... | collective-permute-start | bytes 98312 | tf_op jit(solution)/shard_map/ppermute | solution.py:513
  50.2 1.7 %collective-permute-start.8 = (f16[64,256]{1,0:T(8,128)(2,1)S(1)}, f16[64,256]{1,0:T(8,128)(2,1)S(1)}, u32[]{:S(2)}, u32[]{:S(2)}) collective-permute-start(f16[64,256]{1,0:T(8,128)(2,1)S(1)} %get-tuple-element.49), channel_id=1, source_target_pairs={{0,8},{8,0},{16,24},{24,16},{1,9},{9,1},{17,25},{25,17},{2,10},{10... | collective-permute-start | bytes 98312 | tf_op jit(solution)/shard_map/ppermute | solution.py:513
  52.0 1.6 %collective-permute-done.10 = f16[64,256]{1,0:T(8,128)(2,1)S(1)} collective-permute-done((f16[64,256]{1,0:T(8,128)(2,1)S(1)}, f16[64,256]{1,0:T(8,128)(2,1)S(1)}, u32[]{:S(2)}, u32[]{:S(2)}) %collective-permute-start.10) | collective-permute-done | bytes 32800 | tf_op jit(solution)/shard_map/ppermute | solution.py:513
  53.6 1.4 %collective-permute-done.9 = f16[64,256]{1,0:T(8,128)(2,1)S(1)} collective-permute-done((f16[64,256]{1,0:T(8,128)(2,1)S(1)}, f16[64,256]{1,0:T(8,128)(2,1)S(1)}, u32[]{:S(2)}, u32[]{:S(2)}) %collective-permute-start.9) | collective-permute-done | bytes 32800 | tf_op jit(solution)/shard_map/ppermute | solution.py:513
  55.1 0.2 shard_map.72
  55.3 1.0 %collective-permute-start.15 = (f32[64,256]{1,0:T(8,128)S(1)}, f32[64,256]{1,0:T(8,128)S(1)}, u32[]{:S(2)}, u32[]{:S(2)}) collective-permute-start(f32[64,256]{1,0:T(8,128)S(1)} %shard_map.72), channel_id=1, source_target_pairs={{0,5},{1,4},{2,7},{3,6},{4,1},{5,0},{6,3},{7,2},{8,13},{9,12},{10,... | collective-permute-start | bytes 196616 | tf_op jit(solution)/shard_map/ppermute | solution.py:376
  56.3 1.0 %collective-permute-start.14 = (f32[64,256]{1,0:T(8,128)S(1)}, f32[64,256]{1,0:T(8,128)S(1)}, u32[]{:S(2)}, u32[]{:S(2)}) collective-permute-start(f32[64,256]{1,0:T(8,128)S(1)} %shard_map.72), channel_id=1, source_target_pairs={{0,4},{1,5},{2,6},{3,7},{4,0},{5,1},{6,2},{7,3},{8,12},{9,13},{10,... | collective-permute-start | bytes 196616 | tf_op jit(solution)/shard_map/ppermute | solution.py:376
  57.2 1.6 %collective-permute-start.13 = (f32[64,256]{1,0:T(8,128)S(1)}, f32[64,256]{1,0:T(8,128)S(1)}, u32[]{:S(2)}, u32[]{:S(2)}) collective-permute-start(f32[64,256]{1,0:T(8,128)S(1)} %shard_map.72), channel_id=1, source_target_pairs={{0,1},{1,0},{2,3},{3,2},{4,5},{5,4},{6,7},{7,6},{8,9},{9,8},{10,11... | collective-permute-start | bytes 196616 | tf_op jit(solution)/shard_map/ppermute | solution.py:376
  58.8 1.1 %shard_map.73 = f32[36,64,128]{2,1,0:T(8,128)} custom-call(f32[8,296,128]{2,1,0:T(8,128)S(1)} %shard_map.70.refs_0_, f32[2,296,128]{2,1,0:T(8,128)S(1)} %convert_element_type.95.refs_1_, f32[2,296,128]{2,1,0:T(8,128)S(1)} %convert_element_type.96.refs_2_, f32[2,296,128]{2,1,0:T(8,128)S(1)} %convert_element_type.97.refs_3_, ...), custom_call_target="tpu_custom_call" | custom-call | tf_op jit(solution)/shard_map/pallas_call | solution.py:490
  59.9 0.6 collective-permute-done.15
  60.5 0.3 collective-permute-done.14
  60.7 0.8 %collective-permute-done.13 = f32[64,256]{1,0:T(8,128)S(1)} collective-permute-done((f32[64,256]{1,0:T(8,128)S(1)}, f32[64,256]{1,0:T(8,128)S(1)}, u32[]{:S(2)}, u32[]{:S(2)}) %collective-permute-start.13) | collective-permute-done | bytes 65568 | tf_op jit(solution)/shard_map/ppermute | solution.py:376
  61.6 1.2 %collective-permute-done.16 = f32[64,256]{1,0:T(8,128)S(1)} collective-permute-done((f32[64,256]{1,0:T(8,128)S(1)}, f32[64,256]{1,0:T(8,128)S(1)}, u32[]{:S(2)}, u32[]{:S(2)}) %collective-permute-start.16) | collective-permute-done | bytes 65568 | tf_op jit(solution)/shard_map/ppermute | solution.py:376
  62.8 0.6 %add.52 = f32[64,256]{1,0:T(8,128)} add(f32[64,256]{1,0:T(8,128)S(1)} %add_add_fusion, f32[64,256]{1,0:T(8,128)S(1)} %collective-permute-done.16) | non-fusion elementwise | flops 16384 | bytes 196608 | tf_op jit(solution)/shard_map/add | solution.py:534
  (55 shorter events, 1.6 us)
Async XLA Ops:
  0.7 1.6 %copy-start = (f32[4,4,5,128]{3,1,2,0:T(4,128)S(1)}, f32[4,4,5,128]{3,1,2,0:T(4,128)}, u32[]{:S(2)}) copy-start(f32[4,4,5,128]{3,1,2,0:T(4,128)} %param.7) | copy-start | bytes 122884
  0.7 1.6 %copy-start.1 = (f32[6,6,128]{2,1,0:T(8,128)S(1)}, f32[6,6,128]{2,1,0:T(8,128)}, u32[]{:S(2)}) copy-start(f32[6,6,128]{2,1,0:T(8,128)} %potential_ref.1) | copy-start | bytes 55300
  0.7 1.6 %copy-start.2 = (f32[4,4]{1,0:T(4,128)S(1)}, f32[4,4]{1,0:T(4,128)}, u32[]{:S(2)}) copy-start(f32[4,4]{1,0:T(4,128)} %energies_ref.1) | copy-start | bytes 196
  0.7 1.6 %copy-start.3 = (s32[4,2]{0,1:T(2,128)S(1)}, s32[4,2]{0,1:T(2,128)}, u32[]{:S(2)}) copy-start(s32[4,2]{0,1:T(2,128)} %param.9) | copy-start | bytes 100
  2.7 9.3 %collective-permute-start.2 = (f16[704,128]{1,0:T(8,128)(2,1)S(1)}, f16[704,128]{1,0:T(8,128)(2,1)S(1)}, u32[]{:S(2)}, u32[]{:S(2)}) collective-permute-start(f16[704,128]{1,0:T(8,128)(2,1)S(1)} %get-tuple-element.50), channel_id=1, source_target_pairs={{0,5},{1,4},{2,7},{3,6},{4,1},{5,0},{6,3},{7,2},{8,13},{9,12},{10,... | collective-permute-start | bytes 540680 | tf_op jit(solution)/shard_map/ppermute | solution.py:376
  6.7 1.4 %collective-permute-start.3 = (f16[1,416,128]{2,1,0:T(8,128)(2,1)S(1)}, f16[1,416,128]{2,1,0:T(8,128)(2,1)S(1)}, u32[]{:S(2)}, u32[]{:S(2)}) collective-permute-start(f16[1,416,128]{2,1,0:T(8,128)(2,1)S(1)} %maximum_bitcast_fusion), channel_id=1, source_target_pairs={{0,2},{1,3},{2,0},{3,1},{4,6},{5,7},{6,4},{7,5},{8,10},{9,11},{10,... | collective-permute-start | bytes 319496 | tf_op jit(solution)/shard_map/ppermute | solution.py:376
  6.8 8.5 %collective-permute-start.1 = (f16[704,128]{1,0:T(8,128)(2,1)S(1)}, f16[704,128]{1,0:T(8,128)(2,1)S(1)}, u32[]{:S(2)}, u32[]{:S(2)}) collective-permute-start(f16[704,128]{1,0:T(8,128)(2,1)S(1)} %get-tuple-element.51), channel_id=1, source_target_pairs={{0,4},{1,5},{2,6},{3,7},{4,0},{5,1},{6,2},{7,3},{8,12},{9,13},{10,... | collective-permute-start | bytes 540680 | tf_op jit(solution)/shard_map/ppermute | solution.py:376
  7.4 8.0 %collective-permute-start = (f16[704,128]{1,0:T(8,128)(2,1)S(1)}, f16[704,128]{1,0:T(8,128)(2,1)S(1)}, u32[]{:S(2)}, u32[]{:S(2)}) collective-permute-start(f16[704,128]{1,0:T(8,128)(2,1)S(1)} %get-tuple-element.52), channel_id=1, source_target_pairs={{0,1},{1,0},{2,3},{3,2},{4,5},{5,4},{6,7},{7,6},{8,9},{9,8},{10,11... | collective-permute-start | bytes 540680 | tf_op jit(solution)/shard_map/ppermute | solution.py:376
  12.1 3.6 %collective-permute-start.4 = (f16[1,416,128]{2,1,0:T(8,128)(2,1)S(1)}, f16[1,416,128]{2,1,0:T(8,128)(2,1)S(1)}, u32[]{:S(2)}, u32[]{:S(2)}) collective-permute-start(f16[1,416,128]{2,1,0:T(8,128)(2,1)S(1)} %slice_bitcast_fusion.2), channel_id=1, source_target_pairs={{0,2},{1,3},{2,0},{3,1},{4,6},{5,7},{6,4},{7,5},{8,10},{9,11},{10,... | collective-permute-start | bytes 319496 | tf_op jit(solution)/shard_map/ppermute | solution.py:376
  15.5 1.5 %collective-permute-start.5 = (f16[2,416,128]{2,1,0:T(8,128)(2,1)S(1)}, f16[2,416,128]{2,1,0:T(8,128)(2,1)S(1)}, u32[]{:S(2)}, u32[]{:S(2)}) collective-permute-start(f16[2,416,128]{2,1,0:T(8,128)(2,1)S(1)} %pad_maximum_fusion.4), channel_id=1, source_target_pairs={{0,2},{1,3},{2,0},{3,1},{4,6},{5,7},{6,4},{7,5},{8,10},{9,11},{10,... | collective-permute-start | bytes 638984 | tf_op jit(solution)/shard_map/ppermute | solution.py:376
  23.5 22.5 %all-to-all-start = ((bf16[32,8,1152]{2,1,0:T(8,128)(2,1)}), bf16[32,8,1152]{2,1,0:T(8,128)(2,1)S(1)}, u32[]{:S(2)}, u32[]{:S(2)}) async-start(bf16[32,8,1152]{2,1,0:T(8,128)(2,1)} %get-tuple-element.18), calls=%async_computation | async-start | bytes 1179648 | tf_op jit(solution)/shard_map/all_to_all | solution.py:466
  30.0 10.9 %collective-permute-start.6 = (f16[2,296,128]{2,1,0:T(8,128)(2,1)S(1)}, f16[2,296,128]{2,1,0:T(8,128)(2,1)S(1)}, u32[]{:S(2)}, u32[]{:S(2)}) collective-permute-start(f16[2,296,128]{2,1,0:T(8,128)(2,1)S(1)} %pad_maximum_fusion.5), channel_id=1, source_target_pairs={{0,4},{1,5},{2,6},{3,7},{4,0},{5,1},{6,2},{7,3},{8,12},{9,13},{10,... | collective-permute-start | bytes 454664 | tf_op jit(solution)/shard_map/ppermute | solution.py:376
  31.8 9.0 %collective-permute-start.11 = (f16[2,296,128]{2,1,0:T(8,128)(2,1)S(1)}, f16[2,296,128]{2,1,0:T(8,128)(2,1)S(1)}, u32[]{:S(2)}, u32[]{:S(2)}) collective-permute-start(f16[2,296,128]{2,1,0:T(8,128)(2,1)S(1)} %pad_maximum_fusion.7), channel_id=1, source_target_pairs={{0,1},{1,0},{2,3},{3,2},{4,5},{5,4},{6,7},{7,6},{8,9},{9,8},{10,11... | collective-permute-start | bytes 454664 | tf_op jit(solution)/shard_map/ppermute | solution.py:376
  33.4 12.6 %collective-permute-start.7 = (f16[2,296,128]{2,1,0:T(8,128)(2,1)S(1)}, f16[2,296,128]{2,1,0:T(8,128)(2,1)S(1)}, u32[]{:S(2)}, u32[]{:S(2)}) collective-permute-start(f16[2,296,128]{2,1,0:T(8,128)(2,1)S(1)} %pad_maximum_fusion.6), channel_id=1, source_target_pairs={{0,5},{1,4},{2,7},{3,6},{4,1},{5,0},{6,3},{7,2},{8,13},{9,12},{10,... | collective-permute-start | bytes 454664 | tf_op jit(solution)/shard_map/ppermute | solution.py:376
  46.2 8.9 %collective-permute-start.12 = (f16[4,296,128]{2,1,0:T(8,128)(2,1)S(1)}, f16[4,296,128]{2,1,0:T(8,128)(2,1)S(1)}, u32[]{:S(2)}, u32[]{:S(2)}) collective-permute-start(f16[4,296,128]{2,1,0:T(8,128)(2,1)S(1)} %pad_maximum_fusion), channel_id=1, source_target_pairs={{0,2},{1,3},{2,0},{3,1},{4,6},{5,7},{6,4},{7,5},{8,10},{9,11},{10,... | collective-permute-start | bytes 909320 | tf_op jit(solution)/shard_map/ppermute | solution.py:376
  47.4 6.1 %collective-permute-start.10 = (f16[64,256]{1,0:T(8,128)(2,1)S(1)}, f16[64,256]{1,0:T(8,128)(2,1)S(1)}, u32[]{:S(2)}, u32[]{:S(2)}) collective-permute-start(f16[64,256]{1,0:T(8,128)(2,1)S(1)} %get-tuple-element.47), channel_id=1, source_target_pairs={{0,24},{8,16},{16,8},{24,0},{1,25},{9,17},{17,9},{25,1},{2,26},{10... | collective-permute-start | bytes 98312 | tf_op jit(solution)/shard_map/ppermute | solution.py:513
  50.2 4.8 %collective-permute-start.9 = (f16[64,256]{1,0:T(8,128)(2,1)S(1)}, f16[64,256]{1,0:T(8,128)(2,1)S(1)}, u32[]{:S(2)}, u32[]{:S(2)}) collective-permute-start(f16[64,256]{1,0:T(8,128)(2,1)S(1)} %get-tuple-element.48), channel_id=1, source_target_pairs={{0,16},{8,24},{16,0},{24,8},{1,17},{9,25},{17,1},{25,9},{2,18},{10... | collective-permute-start | bytes 98312 | tf_op jit(solution)/shard_map/ppermute | solution.py:513
  50.2 4.8 %collective-permute-start.8 = (f16[64,256]{1,0:T(8,128)(2,1)S(1)}, f16[64,256]{1,0:T(8,128)(2,1)S(1)}, u32[]{:S(2)}, u32[]{:S(2)}) collective-permute-start(f16[64,256]{1,0:T(8,128)(2,1)S(1)} %get-tuple-element.49), channel_id=1, source_target_pairs={{0,8},{8,0},{16,24},{24,16},{1,9},{9,1},{17,25},{25,17},{2,10},{10... | collective-permute-start | bytes 98312 | tf_op jit(solution)/shard_map/ppermute | solution.py:513
  55.3 5.2 %collective-permute-start.15 = (f32[64,256]{1,0:T(8,128)S(1)}, f32[64,256]{1,0:T(8,128)S(1)}, u32[]{:S(2)}, u32[]{:S(2)}) collective-permute-start(f32[64,256]{1,0:T(8,128)S(1)} %shard_map.72), channel_id=1, source_target_pairs={{0,5},{1,4},{2,7},{3,6},{4,1},{5,0},{6,3},{7,2},{8,13},{9,12},{10,... | collective-permute-start | bytes 196616 | tf_op jit(solution)/shard_map/ppermute | solution.py:376
  56.3 4.5 %collective-permute-start.14 = (f32[64,256]{1,0:T(8,128)S(1)}, f32[64,256]{1,0:T(8,128)S(1)}, u32[]{:S(2)}, u32[]{:S(2)}) collective-permute-start(f32[64,256]{1,0:T(8,128)S(1)} %shard_map.72), channel_id=1, source_target_pairs={{0,4},{1,5},{2,6},{3,7},{4,0},{5,1},{6,2},{7,3},{8,12},{9,13},{10,... | collective-permute-start | bytes 196616 | tf_op jit(solution)/shard_map/ppermute | solution.py:376
  57.2 4.3 %collective-permute-start.13 = (f32[64,256]{1,0:T(8,128)S(1)}, f32[64,256]{1,0:T(8,128)S(1)}, u32[]{:S(2)}, u32[]{:S(2)}) collective-permute-start(f32[64,256]{1,0:T(8,128)S(1)} %shard_map.72), channel_id=1, source_target_pairs={{0,1},{1,0},{2,3},{3,2},{4,5},{5,4},{6,7},{7,6},{8,9},{9,8},{10,11... | collective-permute-start | bytes 196616 | tf_op jit(solution)/shard_map/ppermute | solution.py:376
  61.5 1.3 %collective-permute-start.16 = (f32[64,256]{1,0:T(8,128)S(1)}, f32[64,256]{1,0:T(8,128)S(1)}, u32[]{:S(2)}, u32[]{:S(2)}) collective-permute-start(f32[64,256]{1,0:T(8,128)S(1)} %add_add_fusion), channel_id=1, source_target_pairs={{0,2},{1,3},{2,0},{3,1},{4,6},{5,7},{6,4},{7,5},{8,10},{9,11},{10,... | collective-permute-start | bytes 196616 | tf_op jit(solution)/shard_map/ppermute | solution.py:376

commit v18 on v17

--- a/solution.py
+++ b/solution.py
@@ -188,7 +188,7 @@
                 partial[x, y] = along_z[x] + diagonal[x, y] * cells[x] + along(cells, x)
             return carry
 
-        lax.fori_loop(0, count_y, xz_part, 0, unroll=6)
+        lax.fori_loop(0, count_y, xz_part, 0, unroll=4)
 
         def y_part(x, carry):
             cells = [source[ring + x, ring + y] for y in range(count_y)]
@@ -197,7 +197,7 @@
                 target[ring + x, ring + y] = finish(total, target, ring + x, ring + y)
             return carry
 
-        lax.fori_loop(0, count_x, y_part, 0, unroll=4)
+        lax.fori_loop(0, count_x, y_part, 0, unroll=2)
 
         def place_of(g, a):
             return (
@@ -476,17 +476,11 @@
     if by_swaps:
         came = [swap(jnp.stack([narrow[v], narrow[v | near]]), v) for v in far]
         others, matrix = lax.optimization_barrier((came[1:], matrix))
-        came = came[:1] + others
-        came.append(swap(jnp.stack([narrow[near]] + [block[1] for block in came]), near))
-        pieces = [field] + [block.astype(jnp.float32) for block in came]
-        places = [(0, 0, 0), (len(pieces) - 1, 0, near)]
-        for i, v in enumerate(far):
-            places += [(i + 1, 0, v), (len(pieces) - 1, i + 1, v | near)]
     else:
         pieces = [lax.all_to_all(narrow, plane, 0, 0).astype(jnp.float32)]
         places = [(0, g, g) for g in range(group)]
 
-    def unpack(pieces):
+    def unpack(pieces, places):
         return pl.pallas_call(
             functools.partial(unpack_kernel, each, slabs_y, places),
             in_specs=[vmem] * len(pieces),
@@ -515,7 +509,6 @@
             ).astype(jnp.float32)
             for k in range(1, bands)
         ]
-        parts, pieces = lax.optimization_barrier((parts, pieces))
         gram = pl.pallas_call(
             functools.partial(rows_kernel, cells),
             in_specs=[vmem] * bands,
@@ -523,6 +516,13 @@
             out_shape=jax.ShapeDtypeStruct((band_orbitals, total_orbitals), jnp.float32),
             compiler_params=params,
         )(sums, *parts)
+        beside, gram = lax.optimization_barrier((came[0], gram))
+        came = [beside] + others
+        came.append(swap(jnp.stack([narrow[near]] + [block[1] for block in came]), near))
+        pieces = [field] + [block.astype(jnp.float32) for block in came]
+        places = [(0, 0, 0), (len(pieces) - 1, 0, near)]
+        for i, v in enumerate(far):
+            places += [(i + 1, 0, v), (len(pieces) - 1, i + 1, v | near)]
         terms = {v: swap(gram, v) for v in far}
         terms[0] = gram
         bit = 1
@@ -530,8 +530,9 @@
             if any(v ^ bit in terms for v in terms):
                 terms = {v: terms[v] + terms[v ^ bit] for v in terms if not v & bit}
             bit *= 2
-        gram, filtered = lax.optimization_barrier((terms[0], unpack(pieces)))
-        gram = gram + swap(gram, near)
+        gram = terms[0]
+        other, filtered = lax.optimization_barrier((swap(gram, near), unpack(pieces, places)))
+        gram = gram + other
     else:
         sums = lax.dot_general(
             matrix, matrix, (((1,), (1,)), ((), ())), preferred_element_type=jnp.float32
@@ -540,7 +541,7 @@
         rows = jnp.sum(parts, axis=0) / cells
         gram = lax.all_to_all(jnp.broadcast_to(rows[None], (group,) + rows.shape), plane, 0, 0)
         gram = gram.reshape(band_orbitals, total_orbitals)
-        filtered = unpack(pieces)
+        filtered = unpack(pieces, places)
 
     filtered = filtered.reshape(cells_x, cells_y, band_orbitals, nz).transpose(2, 0, 1, 3)
     return (filtered, gram)

time: 63.7 us -> 63.7 us (level)
  starting transfers between devices: 23 us -> 22.3 us
    ppermute x3, waiting for transfers between devices: 3 us -> 3.64 us  [local(): lax.ppermute(sums[k].astype(jnp.float16), 'band', [(i, i ^ k) for i in ra...]
  transfers between devices with their start and end apart: 18 -> 18, of which waited for: 12 -> 10; matrix products, arithmetic and copies ran while one was open for 1% -> 2% of each run, Pallas kernels for 3% -> 4%
where the time goes in v18:
time: 63.7 us; the launch traced here: 63.4 us
  waiting for transfers between devices  27.5 us (43%)
  starting transfers between devices  22.3 us (35%)
  Pallas kernels  8.96 us (14%)
  other arithmetic  3.11 us (5%)
  between operations  1.12 us (2%)
    ppermute x14, waiting for transfers between devices, swap(): return lax.ppermute(block, plane, [(i, i ^ value) for i in range(group)])  23.8 us
    ppermute x14, starting transfers between devices, swap(): return lax.ppermute(block, plane, [(i, i ^ value) for i in range(group)])  12.1 us
    pallas_call x1, Pallas kernels, local(): pl.pallas_call(functools.partial(filter_kernel, slabs_y, cells_x, cells_y...  6.66 us
    all_to_all x1, starting transfers between devices, local(): matrix = lax.all_to_all(rounded, every, 0, 0)  5.74 us
    ppermute x3, starting transfers between devices, local(): lax.ppermute(sums[k].astype(jnp.float16), 'band', [(i, i ^ k) for i in ra...  4.45 us
    ppermute x3, waiting for transfers between devices, local(): lax.ppermute(sums[k].astype(jnp.float16), 'band', [(i, i ^ k) for i in ra...  3.64 us
    convert_element_type x1, other arithmetic, local(): chunks = (orbitals * orbital_gain).astype(jnp.float16)  1.46 us
  transfers between devices with their start and end apart: 18, of which 10 were waited for; matrix products, arithmetic and copies ran while one was open for 2% of the time, Pallas kernels for 4%

profile of v18, /device:TPU:0, one launch (start us, length us, event | category | flops | bytes accessed | tf_op | source)
XLA Modules:
  0.0 63.4 jit_solution(4093752096953626688)
XLA Ops:
  0.7 1.5 %multiply_convert_fusion = f16[64,6,6,128]{3,0,2,1:T(8,128)(2,1)S(1)} fusion(f32[64,6,6,128]{3,0,2,1:T(8,128)} %param.5), kind=kLoop, calls=%fused_computation | loop fusion | flops 589824 | bytes 1769472 | tf_op jit(solution)/shard_map/convert_element_type | solution.py:400
  2.2 0.1 copy.9
  2.4 0.1 dynamic-slice_bitcast_fusion
  2.6 0.1 fusion.2
  2.7 4.0 %collective-permute-start.2 = (f16[704,128]{1,0:T(8,128)(2,1)S(1)}, f16[704,128]{1,0:T(8,128)(2,1)S(1)}, u32[]{:S(2)}, u32[]{:S(2)}) collective-permute-start(f16[704,128]{1,0:T(8,128)(2,1)S(1)} %get-tuple-element.38), channel_id=1, source_target_pairs={{0,5},{1,4},{2,7},{3,6},{4,1},{5,0},{6,3},{7,2},{8,13},{9,12},{10,... | collective-permute-start | bytes 540680 | tf_op jit(solution)/shard_map/ppermute | solution.py:376
  6.8 0.6 collective-permute-start.1
  7.4 0.6 %collective-permute-done.3 = f16[1,416,128]{2,1,0:T(8,128)(2,1)S(1)} collective-permute-done((f16[1,416,128]{2,1,0:T(8,128)(2,1)S(1)}, f16[1,416,128]{2,1,0:T(8,128)(2,1)S(1)}, u32[]{:S(2)}, u32[]{:S(2)}) %collective-permute-start.3) | collective-permute-done | bytes 106528 | tf_op jit(solution)/shard_map/ppermute | solution.py:376
  8.1 3.9 %collective-permute-done.2 = f16[704,128]{1,0:T(8,128)(2,1)S(1)} collective-permute-done((f16[704,128]{1,0:T(8,128)(2,1)S(1)}, f16[704,128]{1,0:T(8,128)(2,1)S(1)}, u32[]{:S(2)}, u32[]{:S(2)}) %collective-permute-start.2) | collective-permute-done | bytes 180256 | tf_op jit(solution)/shard_map/ppermute | solution.py:376
  12.2 3.2 %collective-permute-done.1 = f16[704,128]{1,0:T(8,128)(2,1)S(1)} collective-permute-done((f16[704,128]{1,0:T(8,128)(2,1)S(1)}, f16[704,128]{1,0:T(8,128)(2,1)S(1)}, u32[]{:S(2)}, u32[]{:S(2)}) %collective-permute-start.1) | collective-permute-done | bytes 180256 | tf_op jit(solution)/shard_map/ppermute | solution.py:376
  15.7 1.3 %collective-permute-done.5 = f16[2,416,128]{2,1,0:T(8,128)(2,1)S(1)} collective-permute-done((f16[2,416,128]{2,1,0:T(8,128)(2,1)S(1)}, f16[2,416,128]{2,1,0:T(8,128)(2,1)S(1)}, u32[]{:S(2)}, u32[]{:S(2)}) %collective-permute-start.5) | collective-permute-done | bytes 213024 | tf_op jit(solution)/shard_map/ppermute | solution.py:376
  17.0 6.7 %shard_map.69 = (f32[26,14,8,128]{3,2,1,0:T(8,128)S(1)}, bf16[32,8,1152]{2,1,0:T(8,128)(2,1)}) custom-call(f32[1,288,128]{2,1,0:T(8,128)S(1)} %get-tuple-element.34.refs_0_, f32[1,128,128]{2,1,0:T(8,128)S(1)} %bitcast.58, f32[1,704,128]{2,1,0:T(8,128)S(1)} %bitcast_convert_fusion.2.refs_2_, f32[1,704,128]{2,1,0:T(8,128)S(1)} %bitcast_convert_fusion.1.refs_3_, ...), custom_call_target="tpu_custom_call" | custom-call | flops 47185920 | bytes 2359296 | tf_op jit(solution)/shard_map/pallas_call | solution.py:440
  23.7 5.7 %all-to-all-start = ((bf16[32,8,1152]{2,1,0:T(8,128)(2,1)}), bf16[32,8,1152]{2,1,0:T(8,128)(2,1)S(1)}, u32[]{:S(2)}, u32[]{:S(2)}) async-start(bf16[32,8,1152]{2,1,0:T(8,128)(2,1)} %get-tuple-element.12), calls=%async_computation | async-start | bytes 1179648 | tf_op jit(solution)/shard_map/all_to_all | solution.py:466
  29.5 0.4 shard_map.70.refs_0_
  30.2 1.8 %collective-permute-start.7 = (f16[2,296,128]{2,1,0:T(8,128)(2,1)S(1)}, f16[2,296,128]{2,1,0:T(8,128)(2,1)S(1)}, u32[]{:S(2)}, u32[]{:S(2)}) collective-permute-start(f16[2,296,128]{2,1,0:T(8,128)(2,1)S(1)} %pad_maximum_fusion.6), channel_id=1, source_target_pairs={{0,4},{1,5},{2,6},{3,7},{4,0},{5,1},{6,2},{7,3},{8,12},{9,13},{10,... | collective-permute-start | bytes 454664 | tf_op jit(solution)/shard_map/ppermute | solution.py:376
  32.0 1.5 %collective-permute-start.8 = (f16[2,296,128]{2,1,0:T(8,128)(2,1)S(1)}, f16[2,296,128]{2,1,0:T(8,128)(2,1)S(1)}, u32[]{:S(2)}, u32[]{:S(2)}) collective-permute-start(f16[2,296,128]{2,1,0:T(8,128)(2,1)S(1)} %pad_maximum_fusion.7), channel_id=1, source_target_pairs={{0,5},{1,4},{2,7},{3,6},{4,1},{5,0},{6,3},{7,2},{8,13},{9,12},{10,... | collective-permute-start | bytes 454664 | tf_op jit(solution)/shard_map/ppermute | solution.py:376
  33.6 0.3 collective-permute-start.6
  33.9 6.8 %collective-permute-done.7 = f16[2,296,128]{2,1,0:T(8,128)(2,1)S(1)} collective-permute-done((f16[2,296,128]{2,1,0:T(8,128)(2,1)S(1)}, f16[2,296,128]{2,1,0:T(8,128)(2,1)S(1)}, u32[]{:S(2)}, u32[]{:S(2)}) %collective-permute-start.7) | collective-permute-done | bytes 151584 | tf_op jit(solution)/shard_map/ppermute | solution.py:376
  40.8 5.4 %collective-permute-done.8 = f16[2,296,128]{2,1,0:T(8,128)(2,1)S(1)} collective-permute-done((f16[2,296,128]{2,1,0:T(8,128)(2,1)S(1)}, f16[2,296,128]{2,1,0:T(8,128)(2,1)S(1)}, u32[]{:S(2)}, u32[]{:S(2)}) %collective-permute-start.8) | collective-permute-done | bytes 151584 | tf_op jit(solution)/shard_map/ppermute | solution.py:376
  46.2 0.5 shard_map.71.own_ref
  46.8 3.3 %collective-permute-start.11 = (f16[64,256]{1,0:T(8,128)(2,1)S(1)}, f16[64,256]{1,0:T(8,128)(2,1)S(1)}, u32[]{:S(2)}, u32[]{:S(2)}) collective-permute-start(f16[64,256]{1,0:T(8,128)(2,1)S(1)} %get-tuple-element.35), channel_id=1, source_target_pairs={{0,24},{8,16},{16,8},{24,0},{1,25},{9,17},{17,9},{25,1},{2,26},{10... | collective-permute-start | bytes 98312 | tf_op jit(solution)/shard_map/ppermute | solution.py:507
  50.1 1.1 %collective-permute-start.9 = (f16[64,256]{1,0:T(8,128)(2,1)S(1)}, f16[64,256]{1,0:T(8,128)(2,1)S(1)}, u32[]{:S(2)}, u32[]{:S(2)}) collective-permute-start(f16[64,256]{1,0:T(8,128)(2,1)S(1)} %get-tuple-element.37), channel_id=1, source_target_pairs={{0,8},{8,0},{16,24},{24,16},{1,9},{9,1},{17,25},{25,17},{2,10},{10... | collective-permute-start | bytes 98312 | tf_op jit(solution)/shard_map/ppermute | solution.py:507
  51.3 1.5 %collective-permute-done.11 = f16[64,256]{1,0:T(8,128)(2,1)S(1)} collective-permute-done((f16[64,256]{1,0:T(8,128)(2,1)S(1)}, f16[64,256]{1,0:T(8,128)(2,1)S(1)}, u32[]{:S(2)}, u32[]{:S(2)}) %collective-permute-start.11) | collective-permute-done | bytes 32800 | tf_op jit(solution)/shard_map/ppermute | solution.py:507
  52.8 2.1 %collective-permute-done.10 = f16[64,256]{1,0:T(8,128)(2,1)S(1)} collective-permute-done((f16[64,256]{1,0:T(8,128)(2,1)S(1)}, f16[64,256]{1,0:T(8,128)(2,1)S(1)}, u32[]{:S(2)}, u32[]{:S(2)}) %collective-permute-start.10) | collective-permute-done | bytes 32800 | tf_op jit(solution)/shard_map/ppermute | solution.py:507
  55.0 0.2 shard_map.72
  55.2 0.6 collective-permute-start.14
  55.8 1.3 %collective-permute-start.13 = (f32[64,256]{1,0:T(8,128)S(1)}, f32[64,256]{1,0:T(8,128)S(1)}, u32[]{:S(2)}, u32[]{:S(2)}) collective-permute-start(f32[64,256]{1,0:T(8,128)S(1)} %shard_map.72), channel_id=1, source_target_pairs={{0,4},{1,5},{2,6},{3,7},{4,0},{5,1},{6,2},{7,3},{8,12},{9,13},{10,... | collective-permute-start | bytes 196616 | tf_op jit(solution)/shard_map/ppermute | solution.py:376
  57.1 1.6 %collective-permute-start.12 = (f32[64,256]{1,0:T(8,128)S(1)}, f32[64,256]{1,0:T(8,128)S(1)}, u32[]{:S(2)}, u32[]{:S(2)}) collective-permute-start(f32[64,256]{1,0:T(8,128)S(1)} %shard_map.72), channel_id=1, source_target_pairs={{0,1},{1,0},{2,3},{3,2},{4,5},{5,4},{6,7},{7,6},{8,9},{9,8},{10,11... | collective-permute-start | bytes 196616 | tf_op jit(solution)/shard_map/ppermute | solution.py:376
  58.7 0.1 pad_maximum_fusion
  58.9 1.5 %collective-permute-done.14 = f32[64,256]{1,0:T(8,128)S(1)} collective-permute-done((f32[64,256]{1,0:T(8,128)S(1)}, f32[64,256]{1,0:T(8,128)S(1)}, u32[]{:S(2)}, u32[]{:S(2)}) %collective-permute-start.14) | collective-permute-done | bytes 65568 | tf_op jit(solution)/shard_map/ppermute | solution.py:376
  60.4 1.0 %collective-permute-done.12 = f32[64,256]{1,0:T(8,128)S(1)} collective-permute-done((f32[64,256]{1,0:T(8,128)S(1)}, f32[64,256]{1,0:T(8,128)S(1)}, u32[]{:S(2)}, u32[]{:S(2)}) %collective-permute-start.12) | collective-permute-done | bytes 65568 | tf_op jit(solution)/shard_map/ppermute | solution.py:376
  61.6 1.1 %shard_map.73 = f32[36,64,128]{2,1,0:T(8,128)} custom-call(f32[8,296,128]{2,1,0:T(8,128)S(1)} %shard_map.70.refs_0_, f32[2,296,128]{2,1,0:T(8,128)S(1)} %convert_element_type.95.refs_1_, f32[2,296,128]{2,1,0:T(8,128)S(1)} %convert_element_type.96.refs_2_, f32[2,296,128]{2,1,0:T(8,128)S(1)} %convert_element_type.97.refs_3_, ...), custom_call_target="tpu_custom_call" | custom-call | tf_op jit(solution)/shard_map/pallas_call | solution.py:484
  62.8 0.6 %add.52 = f32[64,256]{1,0:T(8,128)} add(f32[64,256]{1,0:T(8,128)S(1)} %add_add_fusion, f32[64,256]{1,0:T(8,128)S(1)} %collective-permute-done.15) | non-fusion elementwise | flops 16384 | bytes 196608 | tf_op jit(solution)/shard_map/add | solution.py:535
  (55 shorter events, 1.4 us)
Async XLA Ops:
  0.7 1.6 %copy-start = (f32[4,4,5,128]{3,1,2,0:T(4,128)S(1)}, f32[4,4,5,128]{3,1,2,0:T(4,128)}, u32[]{:S(2)}) copy-start(f32[4,4,5,128]{3,1,2,0:T(4,128)} %param.7) | copy-start | bytes 122884
  0.7 1.6 %copy-start.1 = (f32[6,6,128]{2,1,0:T(8,128)S(1)}, f32[6,6,128]{2,1,0:T(8,128)}, u32[]{:S(2)}) copy-start(f32[6,6,128]{2,1,0:T(8,128)} %potential_ref.1) | copy-start | bytes 55300
  0.7 1.6 %copy-start.2 = (f32[4,4]{1,0:T(4,128)S(1)}, f32[4,4]{1,0:T(4,128)}, u32[]{:S(2)}) copy-start(f32[4,4]{1,0:T(4,128)} %energies_ref.1) | copy-start | bytes 196
  0.7 1.6 %copy-start.3 = (s32[4,2]{0,1:T(2,128)S(1)}, s32[4,2]{0,1:T(2,128)}, u32[]{:S(2)}) copy-start(s32[4,2]{0,1:T(2,128)} %param.9) | copy-start | bytes 100
  2.7 9.3 %collective-permute-start.2 = (f16[704,128]{1,0:T(8,128)(2,1)S(1)}, f16[704,128]{1,0:T(8,128)(2,1)S(1)}, u32[]{:S(2)}, u32[]{:S(2)}) collective-permute-start(f16[704,128]{1,0:T(8,128)(2,1)S(1)} %get-tuple-element.38), channel_id=1, source_target_pairs={{0,5},{1,4},{2,7},{3,6},{4,1},{5,0},{6,3},{7,2},{8,13},{9,12},{10,... | collective-permute-start | bytes 540680 | tf_op jit(solution)/shard_map/ppermute | solution.py:376
  6.7 1.4 %collective-permute-start.3 = (f16[1,416,128]{2,1,0:T(8,128)(2,1)S(1)}, f16[1,416,128]{2,1,0:T(8,128)(2,1)S(1)}, u32[]{:S(2)}, u32[]{:S(2)}) collective-permute-start(f16[1,416,128]{2,1,0:T(8,128)(2,1)S(1)} %maximum_bitcast_fusion), channel_id=1, source_target_pairs={{0,2},{1,3},{2,0},{3,1},{4,6},{5,7},{6,4},{7,5},{8,10},{9,11},{10,... | collective-permute-start | bytes 319496 | tf_op jit(solution)/shard_map/ppermute | solution.py:376
  6.8 8.5 %collective-permute-start.1 = (f16[704,128]{1,0:T(8,128)(2,1)S(1)}, f16[704,128]{1,0:T(8,128)(2,1)S(1)}, u32[]{:S(2)}, u32[]{:S(2)}) collective-permute-start(f16[704,128]{1,0:T(8,128)(2,1)S(1)} %get-tuple-element.39), channel_id=1, source_target_pairs={{0,4},{1,5},{2,6},{3,7},{4,0},{5,1},{6,2},{7,3},{8,12},{9,13},{10,... | collective-permute-start | bytes 540680 | tf_op jit(solution)/shard_map/ppermute | solution.py:376
  7.4 8.0 %collective-permute-start = (f16[704,128]{1,0:T(8,128)(2,1)S(1)}, f16[704,128]{1,0:T(8,128)(2,1)S(1)}, u32[]{:S(2)}, u32[]{:S(2)}) collective-permute-start(f16[704,128]{1,0:T(8,128)(2,1)S(1)} %get-tuple-element.40), channel_id=1, source_target_pairs={{0,1},{1,0},{2,3},{3,2},{4,5},{5,4},{6,7},{7,6},{8,9},{9,8},{10,11... | collective-permute-start | bytes 540680 | tf_op jit(solution)/shard_map/ppermute | solution.py:376
  12.1 3.6 %collective-permute-start.4 = (f16[1,416,128]{2,1,0:T(8,128)(2,1)S(1)}, f16[1,416,128]{2,1,0:T(8,128)(2,1)S(1)}, u32[]{:S(2)}, u32[]{:S(2)}) collective-permute-start(f16[1,416,128]{2,1,0:T(8,128)(2,1)S(1)} %slice_bitcast_fusion.2), channel_id=1, source_target_pairs={{0,2},{1,3},{2,0},{3,1},{4,6},{5,7},{6,4},{7,5},{8,10},{9,11},{10,... | collective-permute-start | bytes 319496 | tf_op jit(solution)/shard_map/ppermute | solution.py:376
  15.5 1.5 %collective-permute-start.5 = (f16[2,416,128]{2,1,0:T(8,128)(2,1)S(1)}, f16[2,416,128]{2,1,0:T(8,128)(2,1)S(1)}, u32[]{:S(2)}, u32[]{:S(2)}) collective-permute-start(f16[2,416,128]{2,1,0:T(8,128)(2,1)S(1)} %pad_maximum_fusion.4), channel_id=1, source_target_pairs={{0,2},{1,3},{2,0},{3,1},{4,6},{5,7},{6,4},{7,5},{8,10},{9,11},{10,... | collective-permute-start | bytes 638984 | tf_op jit(solution)/shard_map/ppermute | solution.py:376
  23.7 22.5 %all-to-all-start = ((bf16[32,8,1152]{2,1,0:T(8,128)(2,1)}), bf16[32,8,1152]{2,1,0:T(8,128)(2,1)S(1)}, u32[]{:S(2)}, u32[]{:S(2)}) async-start(bf16[32,8,1152]{2,1,0:T(8,128)(2,1)} %get-tuple-element.12), calls=%async_computation | async-start | bytes 1179648 | tf_op jit(solution)/shard_map/all_to_all | solution.py:466
  30.2 10.6 %collective-permute-start.7 = (f16[2,296,128]{2,1,0:T(8,128)(2,1)S(1)}, f16[2,296,128]{2,1,0:T(8,128)(2,1)S(1)}, u32[]{:S(2)}, u32[]{:S(2)}) collective-permute-start(f16[2,296,128]{2,1,0:T(8,128)(2,1)S(1)} %pad_maximum_fusion.6), channel_id=1, source_target_pairs={{0,4},{1,5},{2,6},{3,7},{4,0},{5,1},{6,2},{7,3},{8,12},{9,13},{10,... | collective-permute-start | bytes 454664 | tf_op jit(solution)/shard_map/ppermute | solution.py:376
  32.0 14.2 %collective-permute-start.8 = (f16[2,296,128]{2,1,0:T(8,128)(2,1)S(1)}, f16[2,296,128]{2,1,0:T(8,128)(2,1)S(1)}, u32[]{:S(2)}, u32[]{:S(2)}) collective-permute-start(f16[2,296,128]{2,1,0:T(8,128)(2,1)S(1)} %pad_maximum_fusion.7), channel_id=1, source_target_pairs={{0,5},{1,4},{2,7},{3,6},{4,1},{5,0},{6,3},{7,2},{8,13},{9,12},{10,... | collective-permute-start | bytes 454664 | tf_op jit(solution)/shard_map/ppermute | solution.py:376
  33.6 21.6 %collective-permute-start.6 = (f16[2,296,128]{2,1,0:T(8,128)(2,1)S(1)}, f16[2,296,128]{2,1,0:T(8,128)(2,1)S(1)}, u32[]{:S(2)}, u32[]{:S(2)}) collective-permute-start(f16[2,296,128]{2,1,0:T(8,128)(2,1)S(1)} %pad_maximum_fusion.5), channel_id=1, source_target_pairs={{0,1},{1,0},{2,3},{3,2},{4,5},{5,4},{6,7},{7,6},{8,9},{9,8},{10,11... | collective-permute-start | bytes 454664 | tf_op jit(solution)/shard_map/ppermute | solution.py:376
  46.8 6.0 %collective-permute-start.11 = (f16[64,256]{1,0:T(8,128)(2,1)S(1)}, f16[64,256]{1,0:T(8,128)(2,1)S(1)}, u32[]{:S(2)}, u32[]{:S(2)}) collective-permute-start(f16[64,256]{1,0:T(8,128)(2,1)S(1)} %get-tuple-element.35), channel_id=1, source_target_pairs={{0,24},{8,16},{16,8},{24,0},{1,25},{9,17},{17,9},{25,1},{2,26},{10... | collective-permute-start | bytes 98312 | tf_op jit(solution)/shard_map/ppermute | solution.py:507
  50.1 4.8 %collective-permute-start.10 = (f16[64,256]{1,0:T(8,128)(2,1)S(1)}, f16[64,256]{1,0:T(8,128)(2,1)S(1)}, u32[]{:S(2)}, u32[]{:S(2)}) collective-permute-start(f16[64,256]{1,0:T(8,128)(2,1)S(1)} %get-tuple-element.36), channel_id=1, source_target_pairs={{0,16},{8,24},{16,0},{24,8},{1,17},{9,25},{17,1},{25,9},{2,18},{10... | collective-permute-start | bytes 98312 | tf_op jit(solution)/shard_map/ppermute | solution.py:507
  50.1 4.8 %collective-permute-start.9 = (f16[64,256]{1,0:T(8,128)(2,1)S(1)}, f16[64,256]{1,0:T(8,128)(2,1)S(1)}, u32[]{:S(2)}, u32[]{:S(2)}) collective-permute-start(f16[64,256]{1,0:T(8,128)(2,1)S(1)} %get-tuple-element.37), channel_id=1, source_target_pairs={{0,8},{8,0},{16,24},{24,16},{1,9},{9,1},{17,25},{25,17},{2,10},{10... | collective-permute-start | bytes 98312 | tf_op jit(solution)/shard_map/ppermute | solution.py:507
  55.2 5.2 %collective-permute-start.14 = (f32[64,256]{1,0:T(8,128)S(1)}, f32[64,256]{1,0:T(8,128)S(1)}, u32[]{:S(2)}, u32[]{:S(2)}) collective-permute-start(f32[64,256]{1,0:T(8,128)S(1)} %shard_map.72), channel_id=1, source_target_pairs={{0,5},{1,4},{2,7},{3,6},{4,1},{5,0},{6,3},{7,2},{8,13},{9,12},{10,... | collective-permute-start | bytes 196616 | tf_op jit(solution)/shard_map/ppermute | solution.py:376
  55.8 4.6 %collective-permute-start.13 = (f32[64,256]{1,0:T(8,128)S(1)}, f32[64,256]{1,0:T(8,128)S(1)}, u32[]{:S(2)}, u32[]{:S(2)}) collective-permute-start(f32[64,256]{1,0:T(8,128)S(1)} %shard_map.72), channel_id=1, source_target_pairs={{0,4},{1,5},{2,6},{3,7},{4,0},{5,1},{6,2},{7,3},{8,12},{9,13},{10,... | collective-permute-start | bytes 196616 | tf_op jit(solution)/shard_map/ppermute | solution.py:376
  57.1 4.3 %collective-permute-start.12 = (f32[64,256]{1,0:T(8,128)S(1)}, f32[64,256]{1,0:T(8,128)S(1)}, u32[]{:S(2)}, u32[]{:S(2)}) collective-permute-start(f32[64,256]{1,0:T(8,128)S(1)} %shard_map.72), channel_id=1, source_target_pairs={{0,1},{1,0},{2,3},{3,2},{4,5},{5,4},{6,7},{7,6},{8,9},{9,8},{10,11... | collective-permute-start | bytes 196616 | tf_op jit(solution)/shard_map/ppermute | solution.py:376
  58.8 2.8 %collective-permute-start.16 = (f16[4,296,128]{2,1,0:T(8,128)(2,1)S(1)}, f16[4,296,128]{2,1,0:T(8,128)(2,1)S(1)}, u32[]{:S(2)}, u32[]{:S(2)}) collective-permute-start(f16[4,296,128]{2,1,0:T(8,128)(2,1)S(1)} %pad_maximum_fusion), channel_id=1, source_target_pairs={{0,2},{1,3},{2,0},{3,1},{4,6},{5,7},{6,4},{7,5},{8,10},{9,11},{10,... | collective-permute-start | bytes 909320 | tf_op jit(solution)/shard_map/ppermute | solution.py:376
  61.4 1.3 %collective-permute-start.15 = (f32[64,256]{1,0:T(8,128)S(1)}, f32[64,256]{1,0:T(8,128)S(1)}, u32[]{:S(2)}, u32[]{:S(2)}) collective-permute-start(f32[64,256]{1,0:T(8,128)S(1)} %add_add_fusion), channel_id=1, source_target_pairs={{0,2},{1,3},{2,0},{3,1},{4,6},{5,7},{6,4},{7,5},{8,10},{9,11},{10,... | collective-permute-start | bytes 196616 | tf_op jit(solution)/shard_map/ppermute | solution.py:376

commit v19 on v18

--- a/solution.py
+++ b/solution.py
@@ -188,7 +188,7 @@
                 partial[x, y] = along_z[x] + diagonal[x, y] * cells[x] + along(cells, x)
             return carry
 
-        lax.fori_loop(0, count_y, xz_part, 0, unroll=4)
+        lax.fori_loop(0, count_y, xz_part, 0, unroll=6)
 
         def y_part(x, carry):
             cells = [source[ring + x, ring + y] for y in range(count_y)]
@@ -197,7 +197,7 @@
                 target[ring + x, ring + y] = finish(total, target, ring + x, ring + y)
             return carry
 
-        lax.fori_loop(0, count_x, y_part, 0, unroll=2)
+        lax.fori_loop(0, count_x, y_part, 0, unroll=4)
 
         def place_of(g, a):
             return (
@@ -474,8 +474,10 @@
     )(values)
     narrow = field.astype(jnp.float16)
     if by_swaps:
-        came = [swap(jnp.stack([narrow[v], narrow[v | near]]), v) for v in far]
-        others, matrix = lax.optimization_barrier((came[1:], matrix))
+        came = {v: swap(jnp.stack([narrow[v], narrow[v | near]]), v) for v in far}
+        along_x = [v for v in far if v % slabs_y == 0]
+        along_y = [v for v in far if v % slabs_y > 0]
+        tied, matrix = lax.optimization_barrier(([came[v] for v in along_x], matrix))
     else:
         pieces = [lax.all_to_all(narrow, plane, 0, 0).astype(jnp.float32)]
         places = [(0, g, g) for g in range(group)]
@@ -516,8 +518,9 @@
             out_shape=jax.ShapeDtypeStruct((band_orbitals, total_orbitals), jnp.float32),
             compiler_params=params,
         )(sums, *parts)
-        beside, gram = lax.optimization_barrier((came[0], gram))
-        came = [beside] + others
+        free, gram = lax.optimization_barrier(([came[v] for v in along_y], gram))
+        came = dict(zip(along_x + along_y, tied + free))
+        came = [came[v] for v in far]
         came.append(swap(jnp.stack([narrow[near]] + [block[1] for block in came]), near))
         pieces = [field] + [block.astype(jnp.float32) for block in came]
         places = [(0, 0, 0), (len(pieces) - 1, 0, near)]

time: 63.7 us -> 63 us (0.989)
    all_to_all x1, waiting for transfers between devices: 0.01 us -> 5.09 us  [local(): matrix = lax.all_to_all(rounded, every, 0, 0)]
    ppermute x14, waiting for transfers between devices: 23.8 us -> 18.9 us  [swap(): return lax.ppermute(block, plane, [(i, i ^ value) for i in range(group)])]
    ppermute x3, waiting for transfers between devices: 3.64 us -> 2.98 us  [local(): lax.ppermute(sums[k].astype(jnp.float16), 'band', [(i, i ^ k) for i in ra...]
  transfers between devices with their start and end apart: 18 -> 18, of which waited for: 10 -> 11; matrix products, arithmetic and copies ran while one was open for 2% -> 2% of each run, Pallas kernels for 4% -> 4%
where the time goes in v19:
time: 63 us; the launch traced here: 62.7 us
  waiting for transfers between devices  27 us (43%)
  starting transfers between devices  22.4 us (36%)
  Pallas kernels  8.75 us (14%)
  other arithmetic  3.11 us (5%)
  between operations  1.12 us (2%)
    ppermute x14, waiting for transfers between devices, swap(): return lax.ppermute(block, plane, [(i, i ^ value) for i in range(group)])  18.9 us
    ppermute x14, starting transfers between devices, swap(): return lax.ppermute(block, plane, [(i, i ^ value) for i in range(group)])  12.2 us
    pallas_call x1, Pallas kernels, local(): pl.pallas_call(functools.partial(filter_kernel, slabs_y, cells_x, cells_y...  6.46 us
    all_to_all x1, starting transfers between devices, local(): matrix = lax.all_to_all(rounded, every, 0, 0)  5.75 us
    all_to_all x1, waiting for transfers between devices, local(): matrix = lax.all_to_all(rounded, every, 0, 0)  5.09 us
    ppermute x3, starting transfers between devices, local(): lax.ppermute(sums[k].astype(jnp.float16), 'band', [(i, i ^ k) for i in ra...  4.47 us
    ppermute x3, waiting for transfers between devices, local(): lax.ppermute(sums[k].astype(jnp.float16), 'band', [(i, i ^ k) for i in ra...  2.98 us
    convert_element_type x1, other arithmetic, local(): chunks = (orbitals * orbital_gain).astype(jnp.float16)  1.46 us
  transfers between devices with their start and end apart: 18, of which 11 were waited for; matrix products, arithmetic and copies ran while one was open for 2% of the time, Pallas kernels for 4%

profile of v19, /device:TPU:0, one launch (start us, length us, event | category | flops | bytes accessed | tf_op | source)
XLA Modules:
  0.0 62.7 jit_solution(5028953690028554622)
XLA Ops:
  0.7 1.5 %multiply_convert_fusion = f16[64,6,6,128]{3,0,2,1:T(8,128)(2,1)S(1)} fusion(f32[64,6,6,128]{3,0,2,1:T(8,128)} %param.5), kind=kLoop, calls=%fused_computation | loop fusion | flops 589824 | bytes 1769472 | tf_op jit(solution)/shard_map/convert_element_type | solution.py:400
  2.2 0.1 copy.9
  2.4 0.1 dynamic-slice_bitcast_fusion
  2.6 0.1 fusion.2
  2.7 4.0 %collective-permute-start.2 = (f16[704,128]{1,0:T(8,128)(2,1)S(1)}, f16[704,128]{1,0:T(8,128)(2,1)S(1)}, u32[]{:S(2)}, u32[]{:S(2)}) collective-permute-start(f16[704,128]{1,0:T(8,128)(2,1)S(1)} %get-tuple-element.38), channel_id=1, source_target_pairs={{0,5},{1,4},{2,7},{3,6},{4,1},{5,0},{6,3},{7,2},{8,13},{9,12},{10,... | collective-permute-start | bytes 540680 | tf_op jit(solution)/shard_map/ppermute | solution.py:376
  6.8 0.6 collective-permute-start.1
  7.4 0.6 %collective-permute-done.3 = f16[1,416,128]{2,1,0:T(8,128)(2,1)S(1)} collective-permute-done((f16[1,416,128]{2,1,0:T(8,128)(2,1)S(1)}, f16[1,416,128]{2,1,0:T(8,128)(2,1)S(1)}, u32[]{:S(2)}, u32[]{:S(2)}) %collective-permute-start.3) | collective-permute-done | bytes 106528 | tf_op jit(solution)/shard_map/ppermute | solution.py:376
  8.1 3.9 %collective-permute-done.2 = f16[704,128]{1,0:T(8,128)(2,1)S(1)} collective-permute-done((f16[704,128]{1,0:T(8,128)(2,1)S(1)}, f16[704,128]{1,0:T(8,128)(2,1)S(1)}, u32[]{:S(2)}, u32[]{:S(2)}) %collective-permute-start.2) | collective-permute-done | bytes 180256 | tf_op jit(solution)/shard_map/ppermute | solution.py:376
  12.2 3.2 %collective-permute-done.1 = f16[704,128]{1,0:T(8,128)(2,1)S(1)} collective-permute-done((f16[704,128]{1,0:T(8,128)(2,1)S(1)}, f16[704,128]{1,0:T(8,128)(2,1)S(1)}, u32[]{:S(2)}, u32[]{:S(2)}) %collective-permute-start.1) | collective-permute-done | bytes 180256 | tf_op jit(solution)/shard_map/ppermute | solution.py:376
  15.7 1.3 %collective-permute-done.5 = f16[2,416,128]{2,1,0:T(8,128)(2,1)S(1)} collective-permute-done((f16[2,416,128]{2,1,0:T(8,128)(2,1)S(1)}, f16[2,416,128]{2,1,0:T(8,128)(2,1)S(1)}, u32[]{:S(2)}, u32[]{:S(2)}) %collective-permute-start.5) | collective-permute-done | bytes 213024 | tf_op jit(solution)/shard_map/ppermute | solution.py:376
  17.0 6.5 %shard_map.69 = (f32[26,14,8,128]{3,2,1,0:T(8,128)S(1)}, bf16[32,8,1152]{2,1,0:T(8,128)(2,1)}) custom-call(f32[1,288,128]{2,1,0:T(8,128)S(1)} %get-tuple-element.34.refs_0_, f32[1,128,128]{2,1,0:T(8,128)S(1)} %bitcast.58, f32[1,704,128]{2,1,0:T(8,128)S(1)} %bitcast_convert_fusion.2.refs_2_, f32[1,704,128]{2,1,0:T(8,128)S(1)} %bitcast_convert_fusion.1.refs_3_, ...), custom_call_target="tpu_custom_call" | custom-call | flops 47185920 | bytes 2359296 | tf_op jit(solution)/shard_map/pallas_call | solution.py:440
  23.5 5.8 %all-to-all-start = ((bf16[32,8,1152]{2,1,0:T(8,128)(2,1)}), bf16[32,8,1152]{2,1,0:T(8,128)(2,1)S(1)}, u32[]{:S(2)}, u32[]{:S(2)}) async-start(bf16[32,8,1152]{2,1,0:T(8,128)(2,1)} %get-tuple-element.12), calls=%async_computation | async-start | bytes 1179648 | tf_op jit(solution)/shard_map/all_to_all | solution.py:466
  29.3 0.4 shard_map.70.refs_0_
  30.0 1.8 %collective-permute-start.8 = (f16[2,296,128]{2,1,0:T(8,128)(2,1)S(1)}, f16[2,296,128]{2,1,0:T(8,128)(2,1)S(1)}, u32[]{:S(2)}, u32[]{:S(2)}) collective-permute-start(f16[2,296,128]{2,1,0:T(8,128)(2,1)S(1)} %pad_maximum_fusion.7), channel_id=1, source_target_pairs={{0,4},{1,5},{2,6},{3,7},{4,0},{5,1},{6,2},{7,3},{8,12},{9,13},{10,... | collective-permute-start | bytes 454664 | tf_op jit(solution)/shard_map/ppermute | solution.py:376
  31.8 1.5 %collective-permute-start.6 = (f16[2,296,128]{2,1,0:T(8,128)(2,1)S(1)}, f16[2,296,128]{2,1,0:T(8,128)(2,1)S(1)}, u32[]{:S(2)}, u32[]{:S(2)}) collective-permute-start(f16[2,296,128]{2,1,0:T(8,128)(2,1)S(1)} %pad_maximum_fusion.5), channel_id=1, source_target_pairs={{0,1},{1,0},{2,3},{3,2},{4,5},{5,4},{6,7},{7,6},{8,9},{9,8},{10,11... | collective-permute-start | bytes 454664 | tf_op jit(solution)/shard_map/ppermute | solution.py:376
  33.4 0.3 collective-permute-start.7
  33.7 6.8 %collective-permute-done.8 = f16[2,296,128]{2,1,0:T(8,128)(2,1)S(1)} collective-permute-done((f16[2,296,128]{2,1,0:T(8,128)(2,1)S(1)}, f16[2,296,128]{2,1,0:T(8,128)(2,1)S(1)}, u32[]{:S(2)}, u32[]{:S(2)}) %collective-permute-start.8) | collective-permute-done | bytes 151584 | tf_op jit(solution)/shard_map/ppermute | solution.py:376
  40.6 5.1 %all-to-all-done = bf16[32,8,1152]{2,1,0:T(8,128)(2,1)S(1)} async-done(((bf16[32,8,1152]{2,1,0:T(8,128)(2,1)}), bf16[32,8,1152]{2,1,0:T(8,128)(2,1)S(1)}, u32[]{:S(2)}, u32[]{:S(2)}) %all-to-all-start) | async-done | bytes 589856 | tf_op jit(solution)/shard_map/all_to_all | solution.py:466
  45.7 0.5 shard_map.71.own_ref
  46.3 1.3 %collective-permute-start.11 = (f16[64,256]{1,0:T(8,128)(2,1)S(1)}, f16[64,256]{1,0:T(8,128)(2,1)S(1)}, u32[]{:S(2)}, u32[]{:S(2)}) collective-permute-start(f16[64,256]{1,0:T(8,128)(2,1)S(1)} %get-tuple-element.35), channel_id=1, source_target_pairs={{0,24},{8,16},{16,8},{24,0},{1,25},{9,17},{17,9},{25,1},{2,26},{10... | collective-permute-start | bytes 98312 | tf_op jit(solution)/shard_map/ppermute | solution.py:509
  47.6 1.0 %collective-permute-start.10 = (f16[64,256]{1,0:T(8,128)(2,1)S(1)}, f16[64,256]{1,0:T(8,128)(2,1)S(1)}, u32[]{:S(2)}, u32[]{:S(2)}) collective-permute-start(f16[64,256]{1,0:T(8,128)(2,1)S(1)} %get-tuple-element.36), channel_id=1, source_target_pairs={{0,16},{8,24},{16,0},{24,8},{1,17},{9,25},{17,1},{25,9},{2,18},{10... | collective-permute-start | bytes 98312 | tf_op jit(solution)/shard_map/ppermute | solution.py:509
  48.7 2.1 %collective-permute-start.9 = (f16[64,256]{1,0:T(8,128)(2,1)S(1)}, f16[64,256]{1,0:T(8,128)(2,1)S(1)}, u32[]{:S(2)}, u32[]{:S(2)}) collective-permute-start(f16[64,256]{1,0:T(8,128)(2,1)S(1)} %get-tuple-element.37), channel_id=1, source_target_pairs={{0,8},{8,0},{16,24},{24,16},{1,9},{9,1},{17,25},{25,17},{2,10},{10... | collective-permute-start | bytes 98312 | tf_op jit(solution)/shard_map/ppermute | solution.py:509
  50.8 1.8 %collective-permute-done.11 = f16[64,256]{1,0:T(8,128)(2,1)S(1)} collective-permute-done((f16[64,256]{1,0:T(8,128)(2,1)S(1)}, f16[64,256]{1,0:T(8,128)(2,1)S(1)}, u32[]{:S(2)}, u32[]{:S(2)}) %collective-permute-start.11) | collective-permute-done | bytes 32800 | tf_op jit(solution)/shard_map/ppermute | solution.py:509
  52.5 1.2 %collective-permute-done.10 = f16[64,256]{1,0:T(8,128)(2,1)S(1)} collective-permute-done((f16[64,256]{1,0:T(8,128)(2,1)S(1)}, f16[64,256]{1,0:T(8,128)(2,1)S(1)}, u32[]{:S(2)}, u32[]{:S(2)}) %collective-permute-start.10) | collective-permute-done | bytes 32800 | tf_op jit(solution)/shard_map/ppermute | solution.py:509
  53.8 0.2 shard_map.72
  54.0 1.6 %collective-permute-start.14 = (f32[64,256]{1,0:T(8,128)S(1)}, f32[64,256]{1,0:T(8,128)S(1)}, u32[]{:S(2)}, u32[]{:S(2)}) collective-permute-start(f32[64,256]{1,0:T(8,128)S(1)} %shard_map.72), channel_id=1, source_target_pairs={{0,5},{1,4},{2,7},{3,6},{4,1},{5,0},{6,3},{7,2},{8,13},{9,12},{10,... | collective-permute-start | bytes 196616 | tf_op jit(solution)/shard_map/ppermute | solution.py:376
  55.6 0.9 %collective-permute-start.13 = (f32[64,256]{1,0:T(8,128)S(1)}, f32[64,256]{1,0:T(8,128)S(1)}, u32[]{:S(2)}, u32[]{:S(2)}) collective-permute-start(f32[64,256]{1,0:T(8,128)S(1)} %shard_map.72), channel_id=1, source_target_pairs={{0,4},{1,5},{2,6},{3,7},{4,0},{5,1},{6,2},{7,3},{8,12},{9,13},{10,... | collective-permute-start | bytes 196616 | tf_op jit(solution)/shard_map/ppermute | solution.py:376
  56.4 1.1 %collective-permute-start.12 = (f32[64,256]{1,0:T(8,128)S(1)}, f32[64,256]{1,0:T(8,128)S(1)}, u32[]{:S(2)}, u32[]{:S(2)}) collective-permute-start(f32[64,256]{1,0:T(8,128)S(1)} %shard_map.72), channel_id=1, source_target_pairs={{0,1},{1,0},{2,3},{3,2},{4,5},{5,4},{6,7},{7,6},{8,9},{9,8},{10,11... | collective-permute-start | bytes 196616 | tf_op jit(solution)/shard_map/ppermute | solution.py:376
  57.8 2.0 %collective-permute-done.14 = f32[64,256]{1,0:T(8,128)S(1)} collective-permute-done((f32[64,256]{1,0:T(8,128)S(1)}, f32[64,256]{1,0:T(8,128)S(1)}, u32[]{:S(2)}, u32[]{:S(2)}) %collective-permute-start.14) | collective-permute-done | bytes 65568 | tf_op jit(solution)/shard_map/ppermute | solution.py:376
  59.9 0.9 %collective-permute-done.12 = f32[64,256]{1,0:T(8,128)S(1)} collective-permute-done((f32[64,256]{1,0:T(8,128)S(1)}, f32[64,256]{1,0:T(8,128)S(1)}, u32[]{:S(2)}, u32[]{:S(2)}) %collective-permute-start.12) | collective-permute-done | bytes 65568 | tf_op jit(solution)/shard_map/ppermute | solution.py:376
  61.0 1.1 %shard_map.73 = f32[36,64,128]{2,1,0:T(8,128)} custom-call(f32[8,296,128]{2,1,0:T(8,128)S(1)} %shard_map.70.refs_0_, f32[2,296,128]{2,1,0:T(8,128)S(1)} %convert_element_type.95.refs_1_, f32[2,296,128]{2,1,0:T(8,128)S(1)} %convert_element_type.96.refs_2_, f32[2,296,128]{2,1,0:T(8,128)S(1)} %convert_element_type.97.refs_3_, ...), custom_call_target="tpu_custom_call" | custom-call | tf_op jit(solution)/shard_map/pallas_call | solution.py:486
  62.1 0.6 %add.52 = f32[64,256]{1,0:T(8,128)} add(f32[64,256]{1,0:T(8,128)S(1)} %add_add_fusion, f32[64,256]{1,0:T(8,128)S(1)} %collective-permute-done.15) | non-fusion elementwise | flops 16384 | bytes 196608 | tf_op jit(solution)/shard_map/add | solution.py:538
  (55 shorter events, 1.5 us)
Async XLA Ops:
  0.7 1.6 %copy-start = (f32[4,4,5,128]{3,1,2,0:T(4,128)S(1)}, f32[4,4,5,128]{3,1,2,0:T(4,128)}, u32[]{:S(2)}) copy-start(f32[4,4,5,128]{3,1,2,0:T(4,128)} %param.7) | copy-start | bytes 122884
  0.7 1.6 %copy-start.1 = (f32[6,6,128]{2,1,0:T(8,128)S(1)}, f32[6,6,128]{2,1,0:T(8,128)}, u32[]{:S(2)}) copy-start(f32[6,6,128]{2,1,0:T(8,128)} %potential_ref.1) | copy-start | bytes 55300
  0.7 1.6 %copy-start.2 = (f32[4,4]{1,0:T(4,128)S(1)}, f32[4,4]{1,0:T(4,128)}, u32[]{:S(2)}) copy-start(f32[4,4]{1,0:T(4,128)} %energies_ref.1) | copy-start | bytes 196
  0.7 1.6 %copy-start.3 = (s32[4,2]{0,1:T(2,128)S(1)}, s32[4,2]{0,1:T(2,128)}, u32[]{:S(2)}) copy-start(s32[4,2]{0,1:T(2,128)} %param.9) | copy-start | bytes 100
  2.7 9.3 %collective-permute-start.2 = (f16[704,128]{1,0:T(8,128)(2,1)S(1)}, f16[704,128]{1,0:T(8,128)(2,1)S(1)}, u32[]{:S(2)}, u32[]{:S(2)}) collective-permute-start(f16[704,128]{1,0:T(8,128)(2,1)S(1)} %get-tuple-element.38), channel_id=1, source_target_pairs={{0,5},{1,4},{2,7},{3,6},{4,1},{5,0},{6,3},{7,2},{8,13},{9,12},{10,... | collective-permute-start | bytes 540680 | tf_op jit(solution)/shard_map/ppermute | solution.py:376
  6.7 1.4 %collective-permute-start.3 = (f16[1,416,128]{2,1,0:T(8,128)(2,1)S(1)}, f16[1,416,128]{2,1,0:T(8,128)(2,1)S(1)}, u32[]{:S(2)}, u32[]{:S(2)}) collective-permute-start(f16[1,416,128]{2,1,0:T(8,128)(2,1)S(1)} %maximum_bitcast_fusion), channel_id=1, source_target_pairs={{0,2},{1,3},{2,0},{3,1},{4,6},{5,7},{6,4},{7,5},{8,10},{9,11},{10,... | collective-permute-start | bytes 319496 | tf_op jit(solution)/shard_map/ppermute | solution.py:376
  6.8 8.5 %collective-permute-start.1 = (f16[704,128]{1,0:T(8,128)(2,1)S(1)}, f16[704,128]{1,0:T(8,128)(2,1)S(1)}, u32[]{:S(2)}, u32[]{:S(2)}) collective-permute-start(f16[704,128]{1,0:T(8,128)(2,1)S(1)} %get-tuple-element.39), channel_id=1, source_target_pairs={{0,4},{1,5},{2,6},{3,7},{4,0},{5,1},{6,2},{7,3},{8,12},{9,13},{10,... | collective-permute-start | bytes 540680 | tf_op jit(solution)/shard_map/ppermute | solution.py:376
  7.4 8.0 %collective-permute-start = (f16[704,128]{1,0:T(8,128)(2,1)S(1)}, f16[704,128]{1,0:T(8,128)(2,1)S(1)}, u32[]{:S(2)}, u32[]{:S(2)}) collective-permute-start(f16[704,128]{1,0:T(8,128)(2,1)S(1)} %get-tuple-element.40), channel_id=1, source_target_pairs={{0,1},{1,0},{2,3},{3,2},{4,5},{5,4},{6,7},{7,6},{8,9},{9,8},{10,11... | collective-permute-start | bytes 540680 | tf_op jit(solution)/shard_map/ppermute | solution.py:376
  12.1 3.6 %collective-permute-start.4 = (f16[1,416,128]{2,1,0:T(8,128)(2,1)S(1)}, f16[1,416,128]{2,1,0:T(8,128)(2,1)S(1)}, u32[]{:S(2)}, u32[]{:S(2)}) collective-permute-start(f16[1,416,128]{2,1,0:T(8,128)(2,1)S(1)} %slice_bitcast_fusion.2), channel_id=1, source_target_pairs={{0,2},{1,3},{2,0},{3,1},{4,6},{5,7},{6,4},{7,5},{8,10},{9,11},{10,... | collective-permute-start | bytes 319496 | tf_op jit(solution)/shard_map/ppermute | solution.py:376
  15.5 1.5 %collective-permute-start.5 = (f16[2,416,128]{2,1,0:T(8,128)(2,1)S(1)}, f16[2,416,128]{2,1,0:T(8,128)(2,1)S(1)}, u32[]{:S(2)}, u32[]{:S(2)}) collective-permute-start(f16[2,416,128]{2,1,0:T(8,128)(2,1)S(1)} %pad_maximum_fusion.4), channel_id=1, source_target_pairs={{0,2},{1,3},{2,0},{3,1},{4,6},{5,7},{6,4},{7,5},{8,10},{9,11},{10,... | collective-permute-start | bytes 638984 | tf_op jit(solution)/shard_map/ppermute | solution.py:376
  23.5 22.2 %all-to-all-start = ((bf16[32,8,1152]{2,1,0:T(8,128)(2,1)}), bf16[32,8,1152]{2,1,0:T(8,128)(2,1)S(1)}, u32[]{:S(2)}, u32[]{:S(2)}) async-start(bf16[32,8,1152]{2,1,0:T(8,128)(2,1)} %get-tuple-element.12), calls=%async_computation | async-start | bytes 1179648 | tf_op jit(solution)/shard_map/all_to_all | solution.py:466
  30.0 10.6 %collective-permute-start.8 = (f16[2,296,128]{2,1,0:T(8,128)(2,1)S(1)}, f16[2,296,128]{2,1,0:T(8,128)(2,1)S(1)}, u32[]{:S(2)}, u32[]{:S(2)}) collective-permute-start(f16[2,296,128]{2,1,0:T(8,128)(2,1)S(1)} %pad_maximum_fusion.7), channel_id=1, source_target_pairs={{0,4},{1,5},{2,6},{3,7},{4,0},{5,1},{6,2},{7,3},{8,12},{9,13},{10,... | collective-permute-start | bytes 454664 | tf_op jit(solution)/shard_map/ppermute | solution.py:376
  31.8 22.1 %collective-permute-start.6 = (f16[2,296,128]{2,1,0:T(8,128)(2,1)S(1)}, f16[2,296,128]{2,1,0:T(8,128)(2,1)S(1)}, u32[]{:S(2)}, u32[]{:S(2)}) collective-permute-start(f16[2,296,128]{2,1,0:T(8,128)(2,1)S(1)} %pad_maximum_fusion.5), channel_id=1, source_target_pairs={{0,1},{1,0},{2,3},{3,2},{4,5},{5,4},{6,7},{7,6},{8,9},{9,8},{10,11... | collective-permute-start | bytes 454664 | tf_op jit(solution)/shard_map/ppermute | solution.py:376
  33.4 20.6 %collective-permute-start.7 = (f16[2,296,128]{2,1,0:T(8,128)(2,1)S(1)}, f16[2,296,128]{2,1,0:T(8,128)(2,1)S(1)}, u32[]{:S(2)}, u32[]{:S(2)}) collective-permute-start(f16[2,296,128]{2,1,0:T(8,128)(2,1)S(1)} %pad_maximum_fusion.6), channel_id=1, source_target_pairs={{0,5},{1,4},{2,7},{3,6},{4,1},{5,0},{6,3},{7,2},{8,13},{9,12},{10,... | collective-permute-start | bytes 454664 | tf_op jit(solution)/shard_map/ppermute | solution.py:376
  46.3 6.2 %collective-permute-start.11 = (f16[64,256]{1,0:T(8,128)(2,1)S(1)}, f16[64,256]{1,0:T(8,128)(2,1)S(1)}, u32[]{:S(2)}, u32[]{:S(2)}) collective-permute-start(f16[64,256]{1,0:T(8,128)(2,1)S(1)} %get-tuple-element.35), channel_id=1, source_target_pairs={{0,24},{8,16},{16,8},{24,0},{1,25},{9,17},{17,9},{25,1},{2,26},{10... | collective-permute-start | bytes 98312 | tf_op jit(solution)/shard_map/ppermute | solution.py:509
  47.6 6.1 %collective-permute-start.10 = (f16[64,256]{1,0:T(8,128)(2,1)S(1)}, f16[64,256]{1,0:T(8,128)(2,1)S(1)}, u32[]{:S(2)}, u32[]{:S(2)}) collective-permute-start(f16[64,256]{1,0:T(8,128)(2,1)S(1)} %get-tuple-element.36), channel_id=1, source_target_pairs={{0,16},{8,24},{16,0},{24,8},{1,17},{9,25},{17,1},{25,9},{2,18},{10... | collective-permute-start | bytes 98312 | tf_op jit(solution)/shard_map/ppermute | solution.py:509
  48.7 5.1 %collective-permute-start.9 = (f16[64,256]{1,0:T(8,128)(2,1)S(1)}, f16[64,256]{1,0:T(8,128)(2,1)S(1)}, u32[]{:S(2)}, u32[]{:S(2)}) collective-permute-start(f16[64,256]{1,0:T(8,128)(2,1)S(1)} %get-tuple-element.37), channel_id=1, source_target_pairs={{0,8},{8,0},{16,24},{24,16},{1,9},{9,1},{17,25},{25,17},{2,10},{10... | collective-permute-start | bytes 98312 | tf_op jit(solution)/shard_map/ppermute | solution.py:509
  54.0 5.8 %collective-permute-start.14 = (f32[64,256]{1,0:T(8,128)S(1)}, f32[64,256]{1,0:T(8,128)S(1)}, u32[]{:S(2)}, u32[]{:S(2)}) collective-permute-start(f32[64,256]{1,0:T(8,128)S(1)} %shard_map.72), channel_id=1, source_target_pairs={{0,5},{1,4},{2,7},{3,6},{4,1},{5,0},{6,3},{7,2},{8,13},{9,12},{10,... | collective-permute-start | bytes 196616 | tf_op jit(solution)/shard_map/ppermute | solution.py:376
  55.6 4.3 %collective-permute-start.13 = (f32[64,256]{1,0:T(8,128)S(1)}, f32[64,256]{1,0:T(8,128)S(1)}, u32[]{:S(2)}, u32[]{:S(2)}) collective-permute-start(f32[64,256]{1,0:T(8,128)S(1)} %shard_map.72), channel_id=1, source_target_pairs={{0,4},{1,5},{2,6},{3,7},{4,0},{5,1},{6,2},{7,3},{8,12},{9,13},{10,... | collective-permute-start | bytes 196616 | tf_op jit(solution)/shard_map/ppermute | solution.py:376
  56.4 4.3 %collective-permute-start.12 = (f32[64,256]{1,0:T(8,128)S(1)}, f32[64,256]{1,0:T(8,128)S(1)}, u32[]{:S(2)}, u32[]{:S(2)}) collective-permute-start(f32[64,256]{1,0:T(8,128)S(1)} %shard_map.72), channel_id=1, source_target_pairs={{0,1},{1,0},{2,3},{3,2},{4,5},{5,4},{6,7},{7,6},{8,9},{9,8},{10,11... | collective-permute-start | bytes 196616 | tf_op jit(solution)/shard_map/ppermute | solution.py:376
  57.7 3.2 %collective-permute-start.16 = (f16[4,296,128]{2,1,0:T(8,128)(2,1)S(1)}, f16[4,296,128]{2,1,0:T(8,128)(2,1)S(1)}, u32[]{:S(2)}, u32[]{:S(2)}) collective-permute-start(f16[4,296,128]{2,1,0:T(8,128)(2,1)S(1)} %pad_maximum_fusion), channel_id=1, source_target_pairs={{0,2},{1,3},{2,0},{3,1},{4,6},{5,7},{6,4},{7,5},{8,10},{9,11},{10,... | collective-permute-start | bytes 909320 | tf_op jit(solution)/shard_map/ppermute | solution.py:376
  60.7 1.3 %collective-permute-start.15 = (f32[64,256]{1,0:T(8,128)S(1)}, f32[64,256]{1,0:T(8,128)S(1)}, u32[]{:S(2)}, u32[]{:S(2)}) collective-permute-start(f32[64,256]{1,0:T(8,128)S(1)} %add_add_fusion), channel_id=1, source_target_pairs={{0,2},{1,3},{2,0},{3,1},{4,6},{5,7},{6,4},{7,5},{8,10},{9,11},{10,... | collective-permute-start | bytes 196616 | tf_op jit(solution)/shard_map/ppermute | solution.py:376

commit v20 on v19

--- a/solution.py
+++ b/solution.py
@@ -509,7 +509,7 @@
             lax.ppermute(
                 sums[k].astype(jnp.float16), "band", [(i, i ^ k) for i in range(bands)]
             ).astype(jnp.float32)
-            for k in range(1, bands)
+            for k in range(bands - 1, 0, -1)
         ]
         gram = pl.pallas_call(
             functools.partial(rows_kernel, cells),

time: 63 us -> 64 us (1.016)
  waiting for transfers between devices: 27 us -> 28 us
where the time goes in v20:
time: 64 us; the launch traced here: 63.8 us
  waiting for transfers between devices  28 us (44%)
  starting transfers between devices  22.4 us (35%)
  Pallas kernels  8.74 us (14%)
  other arithmetic  3.11 us (5%)
  between operations  1.12 us (2%)
    ppermute x14, waiting for transfers between devices, swap(): return lax.ppermute(block, plane, [(i, i ^ value) for i in range(group)])  19.4 us
    ppermute x14, starting transfers between devices, swap(): return lax.ppermute(block, plane, [(i, i ^ value) for i in range(group)])  12.2 us
    pallas_call x1, Pallas kernels, local(): pl.pallas_call(functools.partial(filter_kernel, slabs_y, cells_x, cells_y...  6.46 us
    all_to_all x1, starting transfers between devices, local(): matrix = lax.all_to_all(rounded, every, 0, 0)  5.76 us
    all_to_all x1, waiting for transfers between devices, local(): matrix = lax.all_to_all(rounded, every, 0, 0)  5.09 us
    ppermute x3, starting transfers between devices, local(): lax.ppermute(sums[k].astype(jnp.float16), 'band', [(i, i ^ k) for i in ra...  4.47 us
    ppermute x3, waiting for transfers between devices, local(): lax.ppermute(sums[k].astype(jnp.float16), 'band', [(i, i ^ k) for i in ra...  3.58 us
    convert_element_type x1, other arithmetic, local(): chunks = (orbitals * orbital_gain).astype(jnp.float16)  1.46 us
  transfers between devices with their start and end apart: 18, of which 11 were waited for; matrix products, arithmetic and copies ran while one was open for 2% of the time, Pallas kernels for 4%

profile of v20, /device:TPU:0, one launch (start us, length us, event | category | flops | bytes accessed | tf_op | source)
XLA Modules:
  0.0 63.8 jit_solution(5330869740524153690)
XLA Ops:
  0.7 1.5 %multiply_convert_fusion = f16[64,6,6,128]{3,0,2,1:T(8,128)(2,1)S(1)} fusion(f32[64,6,6,128]{3,0,2,1:T(8,128)} %param.5), kind=kLoop, calls=%fused_computation | loop fusion | flops 589824 | bytes 1769472 | tf_op jit(solution)/shard_map/convert_element_type | solution.py:400
  2.4 0.1 dynamic-slice_bitcast_fusion
  2.6 0.1 fusion.2
  2.7 4.0 %collective-permute-start.2 = (f16[704,128]{1,0:T(8,128)(2,1)S(1)}, f16[704,128]{1,0:T(8,128)(2,1)S(1)}, u32[]{:S(2)}, u32[]{:S(2)}) collective-permute-start(f16[704,128]{1,0:T(8,128)(2,1)S(1)} %get-tuple-element.38), channel_id=1, source_target_pairs={{0,5},{1,4},{2,7},{3,6},{4,1},{5,0},{6,3},{7,2},{8,13},{9,12},{10,... | collective-permute-start | bytes 540680 | tf_op jit(solution)/shard_map/ppermute | solution.py:376
  6.8 0.6 collective-permute-start.1
  7.4 0.6 %collective-permute-done.3 = f16[1,416,128]{2,1,0:T(8,128)(2,1)S(1)} collective-permute-done((f16[1,416,128]{2,1,0:T(8,128)(2,1)S(1)}, f16[1,416,128]{2,1,0:T(8,128)(2,1)S(1)}, u32[]{:S(2)}, u32[]{:S(2)}) %collective-permute-start.3) | collective-permute-done | bytes 106528 | tf_op jit(solution)/shard_map/ppermute | solution.py:376
  8.1 3.9 %collective-permute-done.2 = f16[704,128]{1,0:T(8,128)(2,1)S(1)} collective-permute-done((f16[704,128]{1,0:T(8,128)(2,1)S(1)}, f16[704,128]{1,0:T(8,128)(2,1)S(1)}, u32[]{:S(2)}, u32[]{:S(2)}) %collective-permute-start.2) | collective-permute-done | bytes 180256 | tf_op jit(solution)/shard_map/ppermute | solution.py:376
  12.2 3.2 %collective-permute-done.1 = f16[704,128]{1,0:T(8,128)(2,1)S(1)} collective-permute-done((f16[704,128]{1,0:T(8,128)(2,1)S(1)}, f16[704,128]{1,0:T(8,128)(2,1)S(1)}, u32[]{:S(2)}, u32[]{:S(2)}) %collective-permute-start.1) | collective-permute-done | bytes 180256 | tf_op jit(solution)/shard_map/ppermute | solution.py:376
  15.7 1.3 %collective-permute-done.5 = f16[2,416,128]{2,1,0:T(8,128)(2,1)S(1)} collective-permute-done((f16[2,416,128]{2,1,0:T(8,128)(2,1)S(1)}, f16[2,416,128]{2,1,0:T(8,128)(2,1)S(1)}, u32[]{:S(2)}, u32[]{:S(2)}) %collective-permute-start.5) | collective-permute-done | bytes 213024 | tf_op jit(solution)/shard_map/ppermute | solution.py:376
  17.0 6.5 %shard_map.69 = (f32[26,14,8,128]{3,2,1,0:T(8,128)S(1)}, bf16[32,8,1152]{2,1,0:T(8,128)(2,1)}) custom-call(f32[1,288,128]{2,1,0:T(8,128)S(1)} %get-tuple-element.34.refs_0_, f32[1,128,128]{2,1,0:T(8,128)S(1)} %bitcast.58, f32[1,704,128]{2,1,0:T(8,128)S(1)} %bitcast_convert_fusion.2.refs_2_, f32[1,704,128]{2,1,0:T(8,128)S(1)} %bitcast_convert_fusion.1.refs_3_, ...), custom_call_target="tpu_custom_call" | custom-call | flops 47185920 | bytes 2359296 | tf_op jit(solution)/shard_map/pallas_call | solution.py:440
  23.5 5.8 %all-to-all-start = ((bf16[32,8,1152]{2,1,0:T(8,128)(2,1)}), bf16[32,8,1152]{2,1,0:T(8,128)(2,1)S(1)}, u32[]{:S(2)}, u32[]{:S(2)}) async-start(bf16[32,8,1152]{2,1,0:T(8,128)(2,1)} %get-tuple-element.12), calls=%async_computation | async-start | bytes 1179648 | tf_op jit(solution)/shard_map/all_to_all | solution.py:466
  29.3 0.4 shard_map.70.refs_0_
  30.0 1.8 %collective-permute-start.8 = (f16[2,296,128]{2,1,0:T(8,128)(2,1)S(1)}, f16[2,296,128]{2,1,0:T(8,128)(2,1)S(1)}, u32[]{:S(2)}, u32[]{:S(2)}) collective-permute-start(f16[2,296,128]{2,1,0:T(8,128)(2,1)S(1)} %pad_maximum_fusion.7), channel_id=1, source_target_pairs={{0,4},{1,5},{2,6},{3,7},{4,0},{5,1},{6,2},{7,3},{8,12},{9,13},{10,... | collective-permute-start | bytes 454664 | tf_op jit(solution)/shard_map/ppermute | solution.py:376
  31.8 1.5 %collective-permute-start.6 = (f16[2,296,128]{2,1,0:T(8,128)(2,1)S(1)}, f16[2,296,128]{2,1,0:T(8,128)(2,1)S(1)}, u32[]{:S(2)}, u32[]{:S(2)}) collective-permute-start(f16[2,296,128]{2,1,0:T(8,128)(2,1)S(1)} %pad_maximum_fusion.5), channel_id=1, source_target_pairs={{0,1},{1,0},{2,3},{3,2},{4,5},{5,4},{6,7},{7,6},{8,9},{9,8},{10,11... | collective-permute-start | bytes 454664 | tf_op jit(solution)/shard_map/ppermute | solution.py:376
  33.4 0.3 collective-permute-start.7
  33.7 6.8 %collective-permute-done.8 = f16[2,296,128]{2,1,0:T(8,128)(2,1)S(1)} collective-permute-done((f16[2,296,128]{2,1,0:T(8,128)(2,1)S(1)}, f16[2,296,128]{2,1,0:T(8,128)(2,1)S(1)}, u32[]{:S(2)}, u32[]{:S(2)}) %collective-permute-start.8) | collective-permute-done | bytes 151584 | tf_op jit(solution)/shard_map/ppermute | solution.py:376
  40.6 5.1 %all-to-all-done = bf16[32,8,1152]{2,1,0:T(8,128)(2,1)S(1)} async-done(((bf16[32,8,1152]{2,1,0:T(8,128)(2,1)}), bf16[32,8,1152]{2,1,0:T(8,128)(2,1)S(1)}, u32[]{:S(2)}, u32[]{:S(2)}) %all-to-all-start) | async-done | bytes 589856 | tf_op jit(solution)/shard_map/all_to_all | solution.py:466
  45.7 0.5 shard_map.71.own_ref
  46.3 0.9 %collective-permute-start.11 = (f16[64,256]{1,0:T(8,128)(2,1)S(1)}, f16[64,256]{1,0:T(8,128)(2,1)S(1)}, u32[]{:S(2)}, u32[]{:S(2)}) collective-permute-start(f16[64,256]{1,0:T(8,128)(2,1)S(1)} %get-tuple-element.35), channel_id=1, source_target_pairs={{0,8},{8,0},{16,24},{24,16},{1,9},{9,1},{17,25},{25,17},{2,10},{10... | collective-permute-start | bytes 98312 | tf_op jit(solution)/shard_map/ppermute | solution.py:509
  47.2 1.4 %collective-permute-start.10 = (f16[64,256]{1,0:T(8,128)(2,1)S(1)}, f16[64,256]{1,0:T(8,128)(2,1)S(1)}, u32[]{:S(2)}, u32[]{:S(2)}) collective-permute-start(f16[64,256]{1,0:T(8,128)(2,1)S(1)} %get-tuple-element.36), channel_id=1, source_target_pairs={{0,16},{8,24},{16,0},{24,8},{1,17},{9,25},{17,1},{25,9},{2,18},{10... | collective-permute-start | bytes 98312 | tf_op jit(solution)/shard_map/ppermute | solution.py:509
  48.6 2.2 %collective-permute-start.9 = (f16[64,256]{1,0:T(8,128)(2,1)S(1)}, f16[64,256]{1,0:T(8,128)(2,1)S(1)}, u32[]{:S(2)}, u32[]{:S(2)}) collective-permute-start(f16[64,256]{1,0:T(8,128)(2,1)S(1)} %get-tuple-element.37), channel_id=1, source_target_pairs={{0,24},{8,16},{16,8},{24,0},{1,25},{9,17},{17,9},{25,1},{2,26},{10... | collective-permute-start | bytes 98312 | tf_op jit(solution)/shard_map/ppermute | solution.py:509
  50.8 2.6 %collective-permute-done.10 = f16[64,256]{1,0:T(8,128)(2,1)S(1)} collective-permute-done((f16[64,256]{1,0:T(8,128)(2,1)S(1)}, f16[64,256]{1,0:T(8,128)(2,1)S(1)}, u32[]{:S(2)}, u32[]{:S(2)}) %collective-permute-start.10) | collective-permute-done | bytes 32800 | tf_op jit(solution)/shard_map/ppermute | solution.py:509
  53.4 0.9 %collective-permute-done.9 = f16[64,256]{1,0:T(8,128)(2,1)S(1)} collective-permute-done((f16[64,256]{1,0:T(8,128)(2,1)S(1)}, f16[64,256]{1,0:T(8,128)(2,1)S(1)}, u32[]{:S(2)}, u32[]{:S(2)}) %collective-permute-start.9) | collective-permute-done | bytes 32800 | tf_op jit(solution)/shard_map/ppermute | solution.py:509
  54.4 0.2 shard_map.72
  54.6 2.1 %collective-permute-start.14 = (f32[64,256]{1,0:T(8,128)S(1)}, f32[64,256]{1,0:T(8,128)S(1)}, u32[]{:S(2)}, u32[]{:S(2)}) collective-permute-start(f32[64,256]{1,0:T(8,128)S(1)} %shard_map.72), channel_id=1, source_target_pairs={{0,5},{1,4},{2,7},{3,6},{4,1},{5,0},{6,3},{7,2},{8,13},{9,12},{10,... | collective-permute-start | bytes 196616 | tf_op jit(solution)/shard_map/ppermute | solution.py:376
  56.7 0.8 %collective-permute-start.13 = (f32[64,256]{1,0:T(8,128)S(1)}, f32[64,256]{1,0:T(8,128)S(1)}, u32[]{:S(2)}, u32[]{:S(2)}) collective-permute-start(f32[64,256]{1,0:T(8,128)S(1)} %shard_map.72), channel_id=1, source_target_pairs={{0,4},{1,5},{2,6},{3,7},{4,0},{5,1},{6,2},{7,3},{8,12},{9,13},{10,... | collective-permute-start | bytes 196616 | tf_op jit(solution)/shard_map/ppermute | solution.py:376
  57.5 0.6 collective-permute-start.12
  58.4 1.4 %collective-permute-done.14 = f32[64,256]{1,0:T(8,128)S(1)} collective-permute-done((f32[64,256]{1,0:T(8,128)S(1)}, f32[64,256]{1,0:T(8,128)S(1)}, u32[]{:S(2)}, u32[]{:S(2)}) %collective-permute-start.14) | collective-permute-done | bytes 65568 | tf_op jit(solution)/shard_map/ppermute | solution.py:376
  59.8 1.2 %collective-permute-done.13 = f32[64,256]{1,0:T(8,128)S(1)} collective-permute-done((f32[64,256]{1,0:T(8,128)S(1)}, f32[64,256]{1,0:T(8,128)S(1)}, u32[]{:S(2)}, u32[]{:S(2)}) %collective-permute-start.13) | collective-permute-done | bytes 65568 | tf_op jit(solution)/shard_map/ppermute | solution.py:376
  60.9 0.8 %collective-permute-done.12 = f32[64,256]{1,0:T(8,128)S(1)} collective-permute-done((f32[64,256]{1,0:T(8,128)S(1)}, f32[64,256]{1,0:T(8,128)S(1)}, u32[]{:S(2)}, u32[]{:S(2)}) %collective-permute-start.12) | collective-permute-done | bytes 65568 | tf_op jit(solution)/shard_map/ppermute | solution.py:376
  62.0 1.1 %shard_map.73 = f32[36,64,128]{2,1,0:T(8,128)} custom-call(f32[8,296,128]{2,1,0:T(8,128)S(1)} %shard_map.70.refs_0_, f32[2,296,128]{2,1,0:T(8,128)S(1)} %convert_element_type.95.refs_1_, f32[2,296,128]{2,1,0:T(8,128)S(1)} %convert_element_type.96.refs_2_, f32[2,296,128]{2,1,0:T(8,128)S(1)} %convert_element_type.97.refs_3_, ...), custom_call_target="tpu_custom_call" | custom-call | tf_op jit(solution)/shard_map/pallas_call | solution.py:486
  63.1 0.6 %add.52 = f32[64,256]{1,0:T(8,128)} add(f32[64,256]{1,0:T(8,128)S(1)} %add_add_fusion, f32[64,256]{1,0:T(8,128)S(1)} %collective-permute-done.15) | non-fusion elementwise | flops 16384 | bytes 196608 | tf_op jit(solution)/shard_map/add | solution.py:538
  (55 shorter events, 1.6 us)
Async XLA Ops:
  0.7 1.6 %copy-start = (f32[4,4,5,128]{3,1,2,0:T(4,128)S(1)}, f32[4,4,5,128]{3,1,2,0:T(4,128)}, u32[]{:S(2)}) copy-start(f32[4,4,5,128]{3,1,2,0:T(4,128)} %param.7) | copy-start | bytes 122884
  0.7 1.6 %copy-start.1 = (f32[6,6,128]{2,1,0:T(8,128)S(1)}, f32[6,6,128]{2,1,0:T(8,128)}, u32[]{:S(2)}) copy-start(f32[6,6,128]{2,1,0:T(8,128)} %potential_ref.1) | copy-start | bytes 55300
  0.7 1.6 %copy-start.2 = (f32[4,4]{1,0:T(4,128)S(1)}, f32[4,4]{1,0:T(4,128)}, u32[]{:S(2)}) copy-start(f32[4,4]{1,0:T(4,128)} %energies_ref.1) | copy-start | bytes 196
  0.7 1.6 %copy-start.3 = (s32[4,2]{0,1:T(2,128)S(1)}, s32[4,2]{0,1:T(2,128)}, u32[]{:S(2)}) copy-start(s32[4,2]{0,1:T(2,128)} %param.9) | copy-start | bytes 100
  2.7 9.3 %collective-permute-start.2 = (f16[704,128]{1,0:T(8,128)(2,1)S(1)}, f16[704,128]{1,0:T(8,128)(2,1)S(1)}, u32[]{:S(2)}, u32[]{:S(2)}) collective-permute-start(f16[704,128]{1,0:T(8,128)(2,1)S(1)} %get-tuple-element.38), channel_id=1, source_target_pairs={{0,5},{1,4},{2,7},{3,6},{4,1},{5,0},{6,3},{7,2},{8,13},{9,12},{10,... | collective-permute-start | bytes 540680 | tf_op jit(solution)/shard_map/ppermute | solution.py:376
  6.7 1.4 %collective-permute-start.3 = (f16[1,416,128]{2,1,0:T(8,128)(2,1)S(1)}, f16[1,416,128]{2,1,0:T(8,128)(2,1)S(1)}, u32[]{:S(2)}, u32[]{:S(2)}) collective-permute-start(f16[1,416,128]{2,1,0:T(8,128)(2,1)S(1)} %maximum_bitcast_fusion), channel_id=1, source_target_pairs={{0,2},{1,3},{2,0},{3,1},{4,6},{5,7},{6,4},{7,5},{8,10},{9,11},{10,... | collective-permute-start | bytes 319496 | tf_op jit(solution)/shard_map/ppermute | solution.py:376
  6.8 8.5 %collective-permute-start.1 = (f16[704,128]{1,0:T(8,128)(2,1)S(1)}, f16[704,128]{1,0:T(8,128)(2,1)S(1)}, u32[]{:S(2)}, u32[]{:S(2)}) collective-permute-start(f16[704,128]{1,0:T(8,128)(2,1)S(1)} %get-tuple-element.39), channel_id=1, source_target_pairs={{0,4},{1,5},{2,6},{3,7},{4,0},{5,1},{6,2},{7,3},{8,12},{9,13},{10,... | collective-permute-start | bytes 540680 | tf_op jit(solution)/shard_map/ppermute | solution.py:376
  7.4 8.0 %collective-permute-start = (f16[704,128]{1,0:T(8,128)(2,1)S(1)}, f16[704,128]{1,0:T(8,128)(2,1)S(1)}, u32[]{:S(2)}, u32[]{:S(2)}) collective-permute-start(f16[704,128]{1,0:T(8,128)(2,1)S(1)} %get-tuple-element.40), channel_id=1, source_target_pairs={{0,1},{1,0},{2,3},{3,2},{4,5},{5,4},{6,7},{7,6},{8,9},{9,8},{10,11... | collective-permute-start | bytes 540680 | tf_op jit(solution)/shard_map/ppermute | solution.py:376
  12.1 3.6 %collective-permute-start.4 = (f16[1,416,128]{2,1,0:T(8,128)(2,1)S(1)}, f16[1,416,128]{2,1,0:T(8,128)(2,1)S(1)}, u32[]{:S(2)}, u32[]{:S(2)}) collective-permute-start(f16[1,416,128]{2,1,0:T(8,128)(2,1)S(1)} %slice_bitcast_fusion.2), channel_id=1, source_target_pairs={{0,2},{1,3},{2,0},{3,1},{4,6},{5,7},{6,4},{7,5},{8,10},{9,11},{10,... | collective-permute-start | bytes 319496 | tf_op jit(solution)/shard_map/ppermute | solution.py:376
  15.5 1.5 %collective-permute-start.5 = (f16[2,416,128]{2,1,0:T(8,128)(2,1)S(1)}, f16[2,416,128]{2,1,0:T(8,128)(2,1)S(1)}, u32[]{:S(2)}, u32[]{:S(2)}) collective-permute-start(f16[2,416,128]{2,1,0:T(8,128)(2,1)S(1)} %pad_maximum_fusion.4), channel_id=1, source_target_pairs={{0,2},{1,3},{2,0},{3,1},{4,6},{5,7},{6,4},{7,5},{8,10},{9,11},{10,... | collective-permute-start | bytes 638984 | tf_op jit(solution)/shard_map/ppermute | solution.py:376
  23.5 22.2 %all-to-all-start = ((bf16[32,8,1152]{2,1,0:T(8,128)(2,1)}), bf16[32,8,1152]{2,1,0:T(8,128)(2,1)S(1)}, u32[]{:S(2)}, u32[]{:S(2)}) async-start(bf16[32,8,1152]{2,1,0:T(8,128)(2,1)} %get-tuple-element.12), calls=%async_computation | async-start | bytes 1179648 | tf_op jit(solution)/shard_map/all_to_all | solution.py:466
  30.0 10.6 %collective-permute-start.8 = (f16[2,296,128]{2,1,0:T(8,128)(2,1)S(1)}, f16[2,296,128]{2,1,0:T(8,128)(2,1)S(1)}, u32[]{:S(2)}, u32[]{:S(2)}) collective-permute-start(f16[2,296,128]{2,1,0:T(8,128)(2,1)S(1)} %pad_maximum_fusion.7), channel_id=1, source_target_pairs={{0,4},{1,5},{2,6},{3,7},{4,0},{5,1},{6,2},{7,3},{8,12},{9,13},{10,... | collective-permute-start | bytes 454664 | tf_op jit(solution)/shard_map/ppermute | solution.py:376
  31.8 22.7 %collective-permute-start.6 = (f16[2,296,128]{2,1,0:T(8,128)(2,1)S(1)}, f16[2,296,128]{2,1,0:T(8,128)(2,1)S(1)}, u32[]{:S(2)}, u32[]{:S(2)}) collective-permute-start(f16[2,296,128]{2,1,0:T(8,128)(2,1)S(1)} %pad_maximum_fusion.5), channel_id=1, source_target_pairs={{0,1},{1,0},{2,3},{3,2},{4,5},{5,4},{6,7},{7,6},{8,9},{9,8},{10,11... | collective-permute-start | bytes 454664 | tf_op jit(solution)/shard_map/ppermute | solution.py:376
  33.4 21.2 %collective-permute-start.7 = (f16[2,296,128]{2,1,0:T(8,128)(2,1)S(1)}, f16[2,296,128]{2,1,0:T(8,128)(2,1)S(1)}, u32[]{:S(2)}, u32[]{:S(2)}) collective-permute-start(f16[2,296,128]{2,1,0:T(8,128)(2,1)S(1)} %pad_maximum_fusion.6), channel_id=1, source_target_pairs={{0,5},{1,4},{2,7},{3,6},{4,1},{5,0},{6,3},{7,2},{8,13},{9,12},{10,... | collective-permute-start | bytes 454664 | tf_op jit(solution)/shard_map/ppermute | solution.py:376
  46.3 4.5 %collective-permute-start.11 = (f16[64,256]{1,0:T(8,128)(2,1)S(1)}, f16[64,256]{1,0:T(8,128)(2,1)S(1)}, u32[]{:S(2)}, u32[]{:S(2)}) collective-permute-start(f16[64,256]{1,0:T(8,128)(2,1)S(1)} %get-tuple-element.35), channel_id=1, source_target_pairs={{0,8},{8,0},{16,24},{24,16},{1,9},{9,1},{17,25},{25,17},{2,10},{10... | collective-permute-start | bytes 98312 | tf_op jit(solution)/shard_map/ppermute | solution.py:509
  47.2 6.2 %collective-permute-start.10 = (f16[64,256]{1,0:T(8,128)(2,1)S(1)}, f16[64,256]{1,0:T(8,128)(2,1)S(1)}, u32[]{:S(2)}, u32[]{:S(2)}) collective-permute-start(f16[64,256]{1,0:T(8,128)(2,1)S(1)} %get-tuple-element.36), channel_id=1, source_target_pairs={{0,16},{8,24},{16,0},{24,8},{1,17},{9,25},{17,1},{25,9},{2,18},{10... | collective-permute-start | bytes 98312 | tf_op jit(solution)/shard_map/ppermute | solution.py:509
  48.6 5.8 %collective-permute-start.9 = (f16[64,256]{1,0:T(8,128)(2,1)S(1)}, f16[64,256]{1,0:T(8,128)(2,1)S(1)}, u32[]{:S(2)}, u32[]{:S(2)}) collective-permute-start(f16[64,256]{1,0:T(8,128)(2,1)S(1)} %get-tuple-element.37), channel_id=1, source_target_pairs={{0,24},{8,16},{16,8},{24,0},{1,25},{9,17},{17,9},{25,1},{2,26},{10... | collective-permute-start | bytes 98312 | tf_op jit(solution)/shard_map/ppermute | solution.py:509
  54.6 5.2 %collective-permute-start.14 = (f32[64,256]{1,0:T(8,128)S(1)}, f32[64,256]{1,0:T(8,128)S(1)}, u32[]{:S(2)}, u32[]{:S(2)}) collective-permute-start(f32[64,256]{1,0:T(8,128)S(1)} %shard_map.72), channel_id=1, source_target_pairs={{0,5},{1,4},{2,7},{3,6},{4,1},{5,0},{6,3},{7,2},{8,13},{9,12},{10,... | collective-permute-start | bytes 196616 | tf_op jit(solution)/shard_map/ppermute | solution.py:376
  56.7 4.3 %collective-permute-start.13 = (f32[64,256]{1,0:T(8,128)S(1)}, f32[64,256]{1,0:T(8,128)S(1)}, u32[]{:S(2)}, u32[]{:S(2)}) collective-permute-start(f32[64,256]{1,0:T(8,128)S(1)} %shard_map.72), channel_id=1, source_target_pairs={{0,4},{1,5},{2,6},{3,7},{4,0},{5,1},{6,2},{7,3},{8,12},{9,13},{10,... | collective-permute-start | bytes 196616 | tf_op jit(solution)/shard_map/ppermute | solution.py:376
  57.5 4.3 %collective-permute-start.12 = (f32[64,256]{1,0:T(8,128)S(1)}, f32[64,256]{1,0:T(8,128)S(1)}, u32[]{:S(2)}, u32[]{:S(2)}) collective-permute-start(f32[64,256]{1,0:T(8,128)S(1)} %shard_map.72), channel_id=1, source_target_pairs={{0,1},{1,0},{2,3},{3,2},{4,5},{5,4},{6,7},{7,6},{8,9},{9,8},{10,11... | collective-permute-start | bytes 196616 | tf_op jit(solution)/shard_map/ppermute | solution.py:376
  58.3 3.7 %collective-permute-start.16 = (f16[4,296,128]{2,1,0:T(8,128)(2,1)S(1)}, f16[4,296,128]{2,1,0:T(8,128)(2,1)S(1)}, u32[]{:S(2)}, u32[]{:S(2)}) collective-permute-start(f16[4,296,128]{2,1,0:T(8,128)(2,1)S(1)} %pad_maximum_fusion), channel_id=1, source_target_pairs={{0,2},{1,3},{2,0},{3,1},{4,6},{5,7},{6,4},{7,5},{8,10},{9,11},{10,... | collective-permute-start | bytes 909320 | tf_op jit(solution)/shard_map/ppermute | solution.py:376
  61.8 1.3 %collective-permute-start.15 = (f32[64,256]{1,0:T(8,128)S(1)}, f32[64,256]{1,0:T(8,128)S(1)}, u32[]{:S(2)}, u32[]{:S(2)}) collective-permute-start(f32[64,256]{1,0:T(8,128)S(1)} %add_add_fusion), channel_id=1, source_target_pairs={{0,2},{1,3},{2,0},{3,1},{4,6},{5,7},{6,4},{7,5},{8,10},{9,11},{10,... | collective-permute-start | bytes 196616 | tf_op jit(solution)/shard_map/ppermute | solution.py:376

commit v21 on v19

--- a/solution.py
+++ b/solution.py
@@ -474,9 +474,11 @@
     )(values)
     narrow = field.astype(jnp.float16)
     if by_swaps:
-        came = {v: swap(jnp.stack([narrow[v], narrow[v | near]]), v) for v in far}
         along_x = [v for v in far if v % slabs_y == 0]
         along_y = [v for v in far if v % slabs_y > 0]
+        came = {v: swap(jnp.stack([narrow[v], narrow[v | near]]), v) for v in along_x}
+        came, narrow = lax.optimization_barrier((came, narrow))
+        came |= {v: swap(jnp.stack([narrow[v], narrow[v | near]]), v) for v in along_y}
         tied, matrix = lax.optimization_barrier(([came[v] for v in along_x], matrix))
     else:
         pieces = [lax.all_to_all(narrow, plane, 0, 0).astype(jnp.float32)]

time: 63 us -> 63 us (level)
  starting transfers between devices: 22.4 us -> 23.2 us
  waiting for transfers between devices: 27 us -> 26.2 us
    all_to_all x1, waiting for transfers between devices: 5.09 us -> 2.97 us  [local(): matrix = lax.all_to_all(rounded, every, 0, 0)]
    ppermute x14, waiting for transfers between devices: 18.9 us -> 20.3 us  [swap(): return lax.ppermute(block, plane, [(i, i ^ value) for i in range(group)])]
    ppermute x14, starting transfers between devices: 12.2 us -> 13 us  [swap(): return lax.ppermute(block, plane, [(i, i ^ value) for i in range(group)])]
where the time goes in v21:
time: 63 us; the launch traced here: 62.8 us
  waiting for transfers between devices  26.2 us (42%)
  starting transfers between devices  23.2 us (37%)
  Pallas kernels  8.75 us (14%)
  other arithmetic  3.11 us (5%)
  between operations  1.12 us (2%)
    ppermute x14, waiting for transfers between devices, swap(): return lax.ppermute(block, plane, [(i, i ^ value) for i in range(group)])  20.3 us
    ppermute x14, starting transfers between devices, swap(): return lax.ppermute(block, plane, [(i, i ^ value) for i in range(group)])  13 us
    pallas_call x1, Pallas kernels, local(): pl.pallas_call(functools.partial(filter_kernel, slabs_y, cells_x, cells_y...  6.45 us
    all_to_all x1, starting transfers between devices, local(): matrix = lax.all_to_all(rounded, every, 0, 0)  5.76 us
    ppermute x3, starting transfers between devices, local(): lax.ppermute(sums[k].astype(jnp.float16), 'band', [(i, i ^ k) for i in ra...  4.45 us
    all_to_all x1, waiting for transfers between devices, local(): matrix = lax.all_to_all(rounded, every, 0, 0)  2.97 us
    ppermute x3, waiting for transfers between devices, local(): lax.ppermute(sums[k].astype(jnp.float16), 'band', [(i, i ^ k) for i in ra...  2.94 us
    convert_element_type x1, other arithmetic, local(): chunks = (orbitals * orbital_gain).astype(jnp.float16)  1.46 us
  transfers between devices with their start and end apart: 18, of which 11 were waited for; matrix products, arithmetic and copies ran while one was open for 2% of the time, Pallas kernels for 4%

profile of v21, /device:TPU:0, one launch (start us, length us, event | category | flops | bytes accessed | tf_op | source)
XLA Modules:
  0.0 62.8 jit_solution(229171157349253551)
XLA Ops:
  0.7 1.5 %multiply_convert_fusion = f16[64,6,6,128]{3,0,2,1:T(8,128)(2,1)S(1)} fusion(f32[64,6,6,128]{3,0,2,1:T(8,128)} %param.5), kind=kLoop, calls=%fused_computation | loop fusion | flops 589824 | bytes 1769472 | tf_op jit(solution)/shard_map/convert_element_type | solution.py:400
  2.4 0.1 dynamic-slice_bitcast_fusion
  2.6 0.1 fusion.2
  2.7 4.0 %collective-permute-start.2 = (f16[704,128]{1,0:T(8,128)(2,1)S(1)}, f16[704,128]{1,0:T(8,128)(2,1)S(1)}, u32[]{:S(2)}, u32[]{:S(2)}) collective-permute-start(f16[704,128]{1,0:T(8,128)(2,1)S(1)} %get-tuple-element.42), channel_id=1, source_target_pairs={{0,5},{1,4},{2,7},{3,6},{4,1},{5,0},{6,3},{7,2},{8,13},{9,12},{10,... | collective-permute-start | bytes 540680 | tf_op jit(solution)/shard_map/ppermute | solution.py:376
  6.8 0.6 collective-permute-start.1
  7.4 0.6 %collective-permute-done.3 = f16[1,416,128]{2,1,0:T(8,128)(2,1)S(1)} collective-permute-done((f16[1,416,128]{2,1,0:T(8,128)(2,1)S(1)}, f16[1,416,128]{2,1,0:T(8,128)(2,1)S(1)}, u32[]{:S(2)}, u32[]{:S(2)}) %collective-permute-start.3) | collective-permute-done | bytes 106528 | tf_op jit(solution)/shard_map/ppermute | solution.py:376
  8.1 3.9 %collective-permute-done.2 = f16[704,128]{1,0:T(8,128)(2,1)S(1)} collective-permute-done((f16[704,128]{1,0:T(8,128)(2,1)S(1)}, f16[704,128]{1,0:T(8,128)(2,1)S(1)}, u32[]{:S(2)}, u32[]{:S(2)}) %collective-permute-start.2) | collective-permute-done | bytes 180256 | tf_op jit(solution)/shard_map/ppermute | solution.py:376
  12.2 3.2 %collective-permute-done.1 = f16[704,128]{1,0:T(8,128)(2,1)S(1)} collective-permute-done((f16[704,128]{1,0:T(8,128)(2,1)S(1)}, f16[704,128]{1,0:T(8,128)(2,1)S(1)}, u32[]{:S(2)}, u32[]{:S(2)}) %collective-permute-start.1) | collective-permute-done | bytes 180256 | tf_op jit(solution)/shard_map/ppermute | solution.py:376
  15.7 1.3 %collective-permute-done.5 = f16[2,416,128]{2,1,0:T(8,128)(2,1)S(1)} collective-permute-done((f16[2,416,128]{2,1,0:T(8,128)(2,1)S(1)}, f16[2,416,128]{2,1,0:T(8,128)(2,1)S(1)}, u32[]{:S(2)}, u32[]{:S(2)}) %collective-permute-start.5) | collective-permute-done | bytes 213024 | tf_op jit(solution)/shard_map/ppermute | solution.py:376
  17.0 6.5 %shard_map.69 = (f32[26,14,8,128]{3,2,1,0:T(8,128)S(1)}, bf16[32,8,1152]{2,1,0:T(8,128)(2,1)}) custom-call(f32[1,288,128]{2,1,0:T(8,128)S(1)} %get-tuple-element.38.refs_0_, f32[1,128,128]{2,1,0:T(8,128)S(1)} %bitcast.58, f32[1,704,128]{2,1,0:T(8,128)S(1)} %bitcast_convert_fusion.2.refs_2_, f32[1,704,128]{2,1,0:T(8,128)S(1)} %bitcast_convert_fusion.1.refs_3_, ...), custom_call_target="tpu_custom_call" | custom-call | flops 47185920 | bytes 2359296 | tf_op jit(solution)/shard_map/pallas_call | solution.py:440
  23.5 5.8 %all-to-all-start = ((bf16[32,8,1152]{2,1,0:T(8,128)(2,1)}), bf16[32,8,1152]{2,1,0:T(8,128)(2,1)S(1)}, u32[]{:S(2)}, u32[]{:S(2)}) async-start(bf16[32,8,1152]{2,1,0:T(8,128)(2,1)} %get-tuple-element.16), calls=%async_computation | async-start | bytes 1179648 | tf_op jit(solution)/shard_map/all_to_all | solution.py:466
  29.3 0.4 shard_map.70.refs_0_
  29.9 1.8 %collective-permute-start.6 = (f16[2,296,128]{2,1,0:T(8,128)(2,1)S(1)}, f16[2,296,128]{2,1,0:T(8,128)(2,1)S(1)}, u32[]{:S(2)}, u32[]{:S(2)}) collective-permute-start(f16[2,296,128]{2,1,0:T(8,128)(2,1)S(1)} %pad_maximum_fusion.5), channel_id=1, source_target_pairs={{0,4},{1,5},{2,6},{3,7},{4,0},{5,1},{6,2},{7,3},{8,12},{9,13},{10,... | collective-permute-start | bytes 454664 | tf_op jit(solution)/shard_map/ppermute | solution.py:376
  31.7 8.2 %collective-permute-done.6 = f16[2,296,128]{2,1,0:T(8,128)(2,1)S(1)} collective-permute-done((f16[2,296,128]{2,1,0:T(8,128)(2,1)S(1)}, f16[2,296,128]{2,1,0:T(8,128)(2,1)S(1)}, u32[]{:S(2)}, u32[]{:S(2)}) %collective-permute-start.6) | collective-permute-done | bytes 151584 | tf_op jit(solution)/shard_map/ppermute | solution.py:376
  40.0 2.2 %collective-permute-start.7 = (f16[2,296,128]{2,1,0:T(8,128)(2,1)S(1)}, f16[2,296,128]{2,1,0:T(8,128)(2,1)S(1)}, u32[]{:S(2)}, u32[]{:S(2)}) collective-permute-start(f16[2,296,128]{2,1,0:T(8,128)(2,1)S(1)} %pad_maximum_fusion.6), channel_id=1, source_target_pairs={{0,1},{1,0},{2,3},{3,2},{4,5},{5,4},{6,7},{7,6},{8,9},{9,8},{10,11... | collective-permute-start | bytes 454664 | tf_op jit(solution)/shard_map/ppermute | solution.py:376
  42.3 0.4 collective-permute-start.8
  42.7 3.0 %all-to-all-done = bf16[32,8,1152]{2,1,0:T(8,128)(2,1)S(1)} async-done(((bf16[32,8,1152]{2,1,0:T(8,128)(2,1)}), bf16[32,8,1152]{2,1,0:T(8,128)(2,1)S(1)}, u32[]{:S(2)}, u32[]{:S(2)}) %all-to-all-start) | async-done | bytes 589856 | tf_op jit(solution)/shard_map/all_to_all | solution.py:466
  45.7 0.5 shard_map.71.own_ref
  46.3 1.3 %collective-permute-start.11 = (f16[64,256]{1,0:T(8,128)(2,1)S(1)}, f16[64,256]{1,0:T(8,128)(2,1)S(1)}, u32[]{:S(2)}, u32[]{:S(2)}) collective-permute-start(f16[64,256]{1,0:T(8,128)(2,1)S(1)} %get-tuple-element.39), channel_id=1, source_target_pairs={{0,24},{8,16},{16,8},{24,0},{1,25},{9,17},{17,9},{25,1},{2,26},{10... | collective-permute-start | bytes 98312 | tf_op jit(solution)/shard_map/ppermute | solution.py:511
  47.6 0.9 %collective-permute-start.10 = (f16[64,256]{1,0:T(8,128)(2,1)S(1)}, f16[64,256]{1,0:T(8,128)(2,1)S(1)}, u32[]{:S(2)}, u32[]{:S(2)}) collective-permute-start(f16[64,256]{1,0:T(8,128)(2,1)S(1)} %get-tuple-element.40), channel_id=1, source_target_pairs={{0,16},{8,24},{16,0},{24,8},{1,17},{9,25},{17,1},{25,9},{2,18},{10... | collective-permute-start | bytes 98312 | tf_op jit(solution)/shard_map/ppermute | solution.py:511
  48.5 2.2 %collective-permute-start.9 = (f16[64,256]{1,0:T(8,128)(2,1)S(1)}, f16[64,256]{1,0:T(8,128)(2,1)S(1)}, u32[]{:S(2)}, u32[]{:S(2)}) collective-permute-start(f16[64,256]{1,0:T(8,128)(2,1)S(1)} %get-tuple-element.41), channel_id=1, source_target_pairs={{0,8},{8,0},{16,24},{24,16},{1,9},{9,1},{17,25},{25,17},{2,10},{10... | collective-permute-start | bytes 98312 | tf_op jit(solution)/shard_map/ppermute | solution.py:511
  50.7 1.8 %collective-permute-done.11 = f16[64,256]{1,0:T(8,128)(2,1)S(1)} collective-permute-done((f16[64,256]{1,0:T(8,128)(2,1)S(1)}, f16[64,256]{1,0:T(8,128)(2,1)S(1)}, u32[]{:S(2)}, u32[]{:S(2)}) %collective-permute-start.11) | collective-permute-done | bytes 32800 | tf_op jit(solution)/shard_map/ppermute | solution.py:511
  52.5 1.2 %collective-permute-done.10 = f16[64,256]{1,0:T(8,128)(2,1)S(1)} collective-permute-done((f16[64,256]{1,0:T(8,128)(2,1)S(1)}, f16[64,256]{1,0:T(8,128)(2,1)S(1)}, u32[]{:S(2)}, u32[]{:S(2)}) %collective-permute-start.10) | collective-permute-done | bytes 32800 | tf_op jit(solution)/shard_map/ppermute | solution.py:511
  53.7 0.2 shard_map.72
  53.9 1.7 %collective-permute-start.14 = (f32[64,256]{1,0:T(8,128)S(1)}, f32[64,256]{1,0:T(8,128)S(1)}, u32[]{:S(2)}, u32[]{:S(2)}) collective-permute-start(f32[64,256]{1,0:T(8,128)S(1)} %shard_map.72), channel_id=1, source_target_pairs={{0,5},{1,4},{2,7},{3,6},{4,1},{5,0},{6,3},{7,2},{8,13},{9,12},{10,... | collective-permute-start | bytes 196616 | tf_op jit(solution)/shard_map/ppermute | solution.py:376
  55.6 0.9 %collective-permute-start.13 = (f32[64,256]{1,0:T(8,128)S(1)}, f32[64,256]{1,0:T(8,128)S(1)}, u32[]{:S(2)}, u32[]{:S(2)}) collective-permute-start(f32[64,256]{1,0:T(8,128)S(1)} %shard_map.72), channel_id=1, source_target_pairs={{0,4},{1,5},{2,6},{3,7},{4,0},{5,1},{6,2},{7,3},{8,12},{9,13},{10,... | collective-permute-start | bytes 196616 | tf_op jit(solution)/shard_map/ppermute | solution.py:376
  56.5 1.0 %collective-permute-start.12 = (f32[64,256]{1,0:T(8,128)S(1)}, f32[64,256]{1,0:T(8,128)S(1)}, u32[]{:S(2)}, u32[]{:S(2)}) collective-permute-start(f32[64,256]{1,0:T(8,128)S(1)} %shard_map.72), channel_id=1, source_target_pairs={{0,1},{1,0},{2,3},{3,2},{4,5},{5,4},{6,7},{7,6},{8,9},{9,8},{10,11... | collective-permute-start | bytes 196616 | tf_op jit(solution)/shard_map/ppermute | solution.py:376
  57.7 1.9 %collective-permute-done.14 = f32[64,256]{1,0:T(8,128)S(1)} collective-permute-done((f32[64,256]{1,0:T(8,128)S(1)}, f32[64,256]{1,0:T(8,128)S(1)}, u32[]{:S(2)}, u32[]{:S(2)}) %collective-permute-start.14) | collective-permute-done | bytes 65568 | tf_op jit(solution)/shard_map/ppermute | solution.py:376
  59.6 0.2 collective-permute-done.13
  59.9 0.9 %collective-permute-done.12 = f32[64,256]{1,0:T(8,128)S(1)} collective-permute-done((f32[64,256]{1,0:T(8,128)S(1)}, f32[64,256]{1,0:T(8,128)S(1)}, u32[]{:S(2)}, u32[]{:S(2)}) %collective-permute-start.12) | collective-permute-done | bytes 65568 | tf_op jit(solution)/shard_map/ppermute | solution.py:376
  61.0 1.1 %shard_map.73 = f32[36,64,128]{2,1,0:T(8,128)} custom-call(f32[8,296,128]{2,1,0:T(8,128)S(1)} %shard_map.70.refs_0_, f32[2,296,128]{2,1,0:T(8,128)S(1)} %convert_element_type.95.refs_1_, f32[2,296,128]{2,1,0:T(8,128)S(1)} %convert_element_type.96.refs_2_, f32[2,296,128]{2,1,0:T(8,128)S(1)} %convert_element_type.97.refs_3_, ...), custom_call_target="tpu_custom_call" | custom-call | tf_op jit(solution)/shard_map/pallas_call | solution.py:488
  62.1 0.6 %add.52 = f32[64,256]{1,0:T(8,128)} add(f32[64,256]{1,0:T(8,128)S(1)} %add_add_fusion, f32[64,256]{1,0:T(8,128)S(1)} %collective-permute-done.15) | non-fusion elementwise | flops 16384 | bytes 196608 | tf_op jit(solution)/shard_map/add | solution.py:540
  (56 shorter events, 1.6 us)
Async XLA Ops:
  0.7 1.6 %copy-start = (f32[4,4,5,128]{3,1,2,0:T(4,128)S(1)}, f32[4,4,5,128]{3,1,2,0:T(4,128)}, u32[]{:S(2)}) copy-start(f32[4,4,5,128]{3,1,2,0:T(4,128)} %param.7) | copy-start | bytes 122884
  0.7 1.6 %copy-start.1 = (f32[6,6,128]{2,1,0:T(8,128)S(1)}, f32[6,6,128]{2,1,0:T(8,128)}, u32[]{:S(2)}) copy-start(f32[6,6,128]{2,1,0:T(8,128)} %potential_ref.1) | copy-start | bytes 55300
  0.7 1.6 %copy-start.2 = (f32[4,4]{1,0:T(4,128)S(1)}, f32[4,4]{1,0:T(4,128)}, u32[]{:S(2)}) copy-start(f32[4,4]{1,0:T(4,128)} %energies_ref.1) | copy-start | bytes 196
  0.7 1.6 %copy-start.3 = (s32[4,2]{0,1:T(2,128)S(1)}, s32[4,2]{0,1:T(2,128)}, u32[]{:S(2)}) copy-start(s32[4,2]{0,1:T(2,128)} %param.9) | copy-start | bytes 100
  2.7 9.3 %collective-permute-start.2 = (f16[704,128]{1,0:T(8,128)(2,1)S(1)}, f16[704,128]{1,0:T(8,128)(2,1)S(1)}, u32[]{:S(2)}, u32[]{:S(2)}) collective-permute-start(f16[704,128]{1,0:T(8,128)(2,1)S(1)} %get-tuple-element.42), channel_id=1, source_target_pairs={{0,5},{1,4},{2,7},{3,6},{4,1},{5,0},{6,3},{7,2},{8,13},{9,12},{10,... | collective-permute-start | bytes 540680 | tf_op jit(solution)/shard_map/ppermute | solution.py:376
  6.7 1.4 %collective-permute-start.3 = (f16[1,416,128]{2,1,0:T(8,128)(2,1)S(1)}, f16[1,416,128]{2,1,0:T(8,128)(2,1)S(1)}, u32[]{:S(2)}, u32[]{:S(2)}) collective-permute-start(f16[1,416,128]{2,1,0:T(8,128)(2,1)S(1)} %maximum_bitcast_fusion), channel_id=1, source_target_pairs={{0,2},{1,3},{2,0},{3,1},{4,6},{5,7},{6,4},{7,5},{8,10},{9,11},{10,... | collective-permute-start | bytes 319496 | tf_op jit(solution)/shard_map/ppermute | solution.py:376
  6.8 8.5 %collective-permute-start.1 = (f16[704,128]{1,0:T(8,128)(2,1)S(1)}, f16[704,128]{1,0:T(8,128)(2,1)S(1)}, u32[]{:S(2)}, u32[]{:S(2)}) collective-permute-start(f16[704,128]{1,0:T(8,128)(2,1)S(1)} %get-tuple-element.43), channel_id=1, source_target_pairs={{0,4},{1,5},{2,6},{3,7},{4,0},{5,1},{6,2},{7,3},{8,12},{9,13},{10,... | collective-permute-start | bytes 540680 | tf_op jit(solution)/shard_map/ppermute | solution.py:376
  7.4 8.0 %collective-permute-start = (f16[704,128]{1,0:T(8,128)(2,1)S(1)}, f16[704,128]{1,0:T(8,128)(2,1)S(1)}, u32[]{:S(2)}, u32[]{:S(2)}) collective-permute-start(f16[704,128]{1,0:T(8,128)(2,1)S(1)} %get-tuple-element.44), channel_id=1, source_target_pairs={{0,1},{1,0},{2,3},{3,2},{4,5},{5,4},{6,7},{7,6},{8,9},{9,8},{10,11... | collective-permute-start | bytes 540680 | tf_op jit(solution)/shard_map/ppermute | solution.py:376
  12.1 3.6 %collective-permute-start.4 = (f16[1,416,128]{2,1,0:T(8,128)(2,1)S(1)}, f16[1,416,128]{2,1,0:T(8,128)(2,1)S(1)}, u32[]{:S(2)}, u32[]{:S(2)}) collective-permute-start(f16[1,416,128]{2,1,0:T(8,128)(2,1)S(1)} %slice_bitcast_fusion.2), channel_id=1, source_target_pairs={{0,2},{1,3},{2,0},{3,1},{4,6},{5,7},{6,4},{7,5},{8,10},{9,11},{10,... | collective-permute-start | bytes 319496 | tf_op jit(solution)/shard_map/ppermute | solution.py:376
  15.5 1.5 %collective-permute-start.5 = (f16[2,416,128]{2,1,0:T(8,128)(2,1)S(1)}, f16[2,416,128]{2,1,0:T(8,128)(2,1)S(1)}, u32[]{:S(2)}, u32[]{:S(2)}) collective-permute-start(f16[2,416,128]{2,1,0:T(8,128)(2,1)S(1)} %pad_maximum_fusion.4), channel_id=1, source_target_pairs={{0,2},{1,3},{2,0},{3,1},{4,6},{5,7},{6,4},{7,5},{8,10},{9,11},{10,... | collective-permute-start | bytes 638984 | tf_op jit(solution)/shard_map/ppermute | solution.py:376
  23.5 22.2 %all-to-all-start = ((bf16[32,8,1152]{2,1,0:T(8,128)(2,1)}), bf16[32,8,1152]{2,1,0:T(8,128)(2,1)S(1)}, u32[]{:S(2)}, u32[]{:S(2)}) async-start(bf16[32,8,1152]{2,1,0:T(8,128)(2,1)} %get-tuple-element.16), calls=%async_computation | async-start | bytes 1179648 | tf_op jit(solution)/shard_map/all_to_all | solution.py:466
  29.9 10.0 %collective-permute-start.6 = (f16[2,296,128]{2,1,0:T(8,128)(2,1)S(1)}, f16[2,296,128]{2,1,0:T(8,128)(2,1)S(1)}, u32[]{:S(2)}, u32[]{:S(2)}) collective-permute-start(f16[2,296,128]{2,1,0:T(8,128)(2,1)S(1)} %pad_maximum_fusion.5), channel_id=1, source_target_pairs={{0,4},{1,5},{2,6},{3,7},{4,0},{5,1},{6,2},{7,3},{8,12},{9,13},{10,... | collective-permute-start | bytes 454664 | tf_op jit(solution)/shard_map/ppermute | solution.py:376
  40.0 13.9 %collective-permute-start.7 = (f16[2,296,128]{2,1,0:T(8,128)(2,1)S(1)}, f16[2,296,128]{2,1,0:T(8,128)(2,1)S(1)}, u32[]{:S(2)}, u32[]{:S(2)}) collective-permute-start(f16[2,296,128]{2,1,0:T(8,128)(2,1)S(1)} %pad_maximum_fusion.6), channel_id=1, source_target_pairs={{0,1},{1,0},{2,3},{3,2},{4,5},{5,4},{6,7},{7,6},{8,9},{9,8},{10,11... | collective-permute-start | bytes 454664 | tf_op jit(solution)/shard_map/ppermute | solution.py:376
  42.3 11.7 %collective-permute-start.8 = (f16[2,296,128]{2,1,0:T(8,128)(2,1)S(1)}, f16[2,296,128]{2,1,0:T(8,128)(2,1)S(1)}, u32[]{:S(2)}, u32[]{:S(2)}) collective-permute-start(f16[2,296,128]{2,1,0:T(8,128)(2,1)S(1)} %pad_maximum_fusion.7), channel_id=1, source_target_pairs={{0,5},{1,4},{2,7},{3,6},{4,1},{5,0},{6,3},{7,2},{8,13},{9,12},{10,... | collective-permute-start | bytes 454664 | tf_op jit(solution)/shard_map/ppermute | solution.py:376
  46.3 6.3 %collective-permute-start.11 = (f16[64,256]{1,0:T(8,128)(2,1)S(1)}, f16[64,256]{1,0:T(8,128)(2,1)S(1)}, u32[]{:S(2)}, u32[]{:S(2)}) collective-permute-start(f16[64,256]{1,0:T(8,128)(2,1)S(1)} %get-tuple-element.39), channel_id=1, source_target_pairs={{0,24},{8,16},{16,8},{24,0},{1,25},{9,17},{17,9},{25,1},{2,26},{10... | collective-permute-start | bytes 98312 | tf_op jit(solution)/shard_map/ppermute | solution.py:511
  47.6 6.1 %collective-permute-start.10 = (f16[64,256]{1,0:T(8,128)(2,1)S(1)}, f16[64,256]{1,0:T(8,128)(2,1)S(1)}, u32[]{:S(2)}, u32[]{:S(2)}) collective-permute-start(f16[64,256]{1,0:T(8,128)(2,1)S(1)} %get-tuple-element.40), channel_id=1, source_target_pairs={{0,16},{8,24},{16,0},{24,8},{1,17},{9,25},{17,1},{25,9},{2,18},{10... | collective-permute-start | bytes 98312 | tf_op jit(solution)/shard_map/ppermute | solution.py:511
  48.5 5.2 %collective-permute-start.9 = (f16[64,256]{1,0:T(8,128)(2,1)S(1)}, f16[64,256]{1,0:T(8,128)(2,1)S(1)}, u32[]{:S(2)}, u32[]{:S(2)}) collective-permute-start(f16[64,256]{1,0:T(8,128)(2,1)S(1)} %get-tuple-element.41), channel_id=1, source_target_pairs={{0,8},{8,0},{16,24},{24,16},{1,9},{9,1},{17,25},{25,17},{2,10},{10... | collective-permute-start | bytes 98312 | tf_op jit(solution)/shard_map/ppermute | solution.py:511
  53.9 5.7 %collective-permute-start.14 = (f32[64,256]{1,0:T(8,128)S(1)}, f32[64,256]{1,0:T(8,128)S(1)}, u32[]{:S(2)}, u32[]{:S(2)}) collective-permute-start(f32[64,256]{1,0:T(8,128)S(1)} %shard_map.72), channel_id=1, source_target_pairs={{0,5},{1,4},{2,7},{3,6},{4,1},{5,0},{6,3},{7,2},{8,13},{9,12},{10,... | collective-permute-start | bytes 196616 | tf_op jit(solution)/shard_map/ppermute | solution.py:376
  55.6 4.3 %collective-permute-start.13 = (f32[64,256]{1,0:T(8,128)S(1)}, f32[64,256]{1,0:T(8,128)S(1)}, u32[]{:S(2)}, u32[]{:S(2)}) collective-permute-start(f32[64,256]{1,0:T(8,128)S(1)} %shard_map.72), channel_id=1, source_target_pairs={{0,4},{1,5},{2,6},{3,7},{4,0},{5,1},{6,2},{7,3},{8,12},{9,13},{10,... | collective-permute-start | bytes 196616 | tf_op jit(solution)/shard_map/ppermute | solution.py:376
  56.5 4.3 %collective-permute-start.12 = (f32[64,256]{1,0:T(8,128)S(1)}, f32[64,256]{1,0:T(8,128)S(1)}, u32[]{:S(2)}, u32[]{:S(2)}) collective-permute-start(f32[64,256]{1,0:T(8,128)S(1)} %shard_map.72), channel_id=1, source_target_pairs={{0,1},{1,0},{2,3},{3,2},{4,5},{5,4},{6,7},{7,6},{8,9},{9,8},{10,11... | collective-permute-start | bytes 196616 | tf_op jit(solution)/shard_map/ppermute | solution.py:376
  57.6 3.3 %collective-permute-start.16 = (f16[4,296,128]{2,1,0:T(8,128)(2,1)S(1)}, f16[4,296,128]{2,1,0:T(8,128)(2,1)S(1)}, u32[]{:S(2)}, u32[]{:S(2)}) collective-permute-start(f16[4,296,128]{2,1,0:T(8,128)(2,1)S(1)} %pad_maximum_fusion), channel_id=1, source_target_pairs={{0,2},{1,3},{2,0},{3,1},{4,6},{5,7},{6,4},{7,5},{8,10},{9,11},{10,... | collective-permute-start | bytes 909320 | tf_op jit(solution)/shard_map/ppermute | solution.py:376
  60.8 1.3 %collective-permute-start.15 = (f32[64,256]{1,0:T(8,128)S(1)}, f32[64,256]{1,0:T(8,128)S(1)}, u32[]{:S(2)}, u32[]{:S(2)}) collective-permute-start(f32[64,256]{1,0:T(8,128)S(1)} %add_add_fusion), channel_id=1, source_target_pairs={{0,2},{1,3},{2,0},{3,1},{4,6},{5,7},{6,4},{7,5},{8,10},{9,11},{10,... | collective-permute-start | bytes 196616 | tf_op jit(solution)/shard_map/ppermute | solution.py:376
